TPU v7x, 32 devices: a whole 2x2x4 slice. The times are simulated.
32 devices in a mesh: tile: 4 (over y, x), tm: 8 (over z, core).
Axes of the slice: x: 2, y: 2, z: 4, core: 2. Of those that a mesh axis runs over, the one named last changes fastest.
Arguments:
- histories: bfloat16 [4, 32, 128, 1024], P('tile', 'tm'), may hold values from -6 to 6
- gain_time: float32 [1024], replicated, may hold values from 0.25 to 1.75
- wq_time: bfloat16 [1024, 1024], replicated
- wkv_time: bfloat16 [1024, 512], replicated
- wo_time: bfloat16 [1024, 1024], replicated, may hold values from -0.1875 to 0.1875
- gain_space: float32 [1024], replicated, may hold values from 0.25 to 1.75
- wq_space: bfloat16 [1024, 1024], replicated
- wkv_space: bfloat16 [1024, 512], replicated
- wo_space: bfloat16 [1024, 1024], replicated, may hold values from -0.1875 to 0.1875
- neighbours: int32 [4, 4], P('tile'), may hold values from 0 to 3, as said below
- nbr_valid: int32 [4, 4], P('tile'), may hold values from 0 to 1, as said below
- agent_valid: int32 [4, 32], P('tile'), may hold values from 0 to 1
Outputs:
- updated: bfloat16 [4, 32, 128, 1024], P('tile', 'tm')
Inputs may be any that keep to these rules, and one draw needn't show every extreme that they name: `neighbours`: row i starts with tile i; the entries of a row are distinct tiles. `nbr_valid`: the first entry of every row is 1; row 0 is all ones; other rows keep differing shares of their entries.
All inputs are finite; a program needn't handle non-finite values.
Results may differ from a plain program's by a relative error of at most 0.014.
The roundings to bfloat16 on the way count: a program that leaves them out, or rounds other values in their place, can miss the bound.
Values may be sent and summed in bfloat16 or wider, within the bound.
No kernel may reach another device: no remote copies, remote signals or barrier semaphores. Data moves between devices by JAX's collectives and lax.ppermute only.
A program may use at most 128 MiB of HBM per device.

v0:
```python
import jax
import jax.numpy as jnp
from jax import lax
from jax.sharding import PartitionSpec as P

HEADS = 16
KV_HEADS = 4
HEAD_DIM = 64


def norm_rows(values, gain):
    wide = values.astype(jnp.float32)
    meansq = jnp.mean(wide * wide, axis=-1, keepdims=True)
    return (wide * lax.rsqrt(meansq + 1e-05) * gain).astype(jnp.bfloat16)


def temporal_block(history, gain, w_query, w_keyval, w_out):
    batch, nsteps, model_width = history.shape
    groups = HEADS // KV_HEADS
    normed = norm_rows(history, gain).reshape(batch * nsteps, model_width)
    queries = jnp.dot(normed, w_query, preferred_element_type=jnp.float32).astype(jnp.bfloat16)
    queries = queries.reshape(batch, nsteps, KV_HEADS, groups, HEAD_DIM)
    keyval = jnp.dot(normed, w_keyval, preferred_element_type=jnp.float32).astype(jnp.bfloat16)
    keyval = keyval.reshape(batch, nsteps, 2, KV_HEADS, HEAD_DIM)
    logit_scores = jnp.einsum(
        "bskgd,btkd->bkgst", queries, keyval[:, :, 0], preferred_element_type=jnp.float32
    )
    logit_scores = logit_scores * HEAD_DIM ** (-0.5)
    causal = jnp.arange(nsteps)[:, None] >= jnp.arange(nsteps)[None, :]
    logit_scores = jnp.where(causal, logit_scores, -1e30)
    row_top = jnp.max(logit_scores, axis=-1, keepdims=True)
    expd = jnp.where(causal, jnp.exp(logit_scores - row_top), 0.0)
    probs = (expd / jnp.sum(expd, axis=-1, keepdims=True)).astype(jnp.bfloat16)
    mixed = jnp.einsum(
        "bkgst,btkd->bskgd", probs, keyval[:, :, 1], preferred_element_type=jnp.float32
    )
    mixed = mixed.astype(jnp.bfloat16).reshape(batch * nsteps, model_width)
    projected = jnp.dot(mixed, w_out, preferred_element_type=jnp.float32)
    return (history.astype(jnp.float32) + projected.reshape(batch, nsteps, model_width)).astype(
        jnp.bfloat16
    )


def tile_update(running, kv_tile, key_weight, queries):
    row_top, denominator, weighted = running
    agent_count, local_steps = (kv_tile.shape[0], kv_tile.shape[1])
    key_values = kv_tile.reshape(agent_count, local_steps, 2, KV_HEADS, HEAD_DIM)
    logit_scores = jnp.einsum(
        "sakgd,bskd->skgab", queries, key_values[:, :, 0], preferred_element_type=jnp.float32
    )
    logit_scores = logit_scores * HEAD_DIM ** (-0.5)
    logit_scores = jnp.where(key_weight > 0, logit_scores, -1e30)
    new_top = jnp.maximum(row_top, jnp.max(logit_scores, axis=-1))
    expd = jnp.exp(logit_scores - new_top[..., None]) * key_weight
    factor = jnp.exp(row_top - new_top)
    denominator = denominator * factor + jnp.sum(expd, axis=-1)
    added = jnp.einsum(
        "skgab,bskd->skgad",
        expd.astype(jnp.bfloat16),
        key_values[:, :, 1],
        preferred_element_type=jnp.float32,
    )
    weighted = weighted * factor[..., None] + added
    return (new_top, denominator, weighted)


def per_device(
    histories,
    gain_time,
    wq_time,
    wkv_time,
    wo_time,
    gain_space,
    wq_space,
    wkv_space,
    wo_space,
    neighbours,
    nbr_valid,
    agent_valid,
):
    history = temporal_block(histories[0], gain_time, wq_time, wkv_time, wo_time)[None]
    timed = lax.all_to_all(history, "tm", split_axis=2, concat_axis=1, tiled=True)
    agents, local_steps, model_width = (timed.shape[1], timed.shape[2], timed.shape[3])
    groups = HEADS // KV_HEADS
    normed = norm_rows(timed[0], gain_space).reshape(agents * local_steps, model_width)
    queries = jnp.dot(normed, wq_space, preferred_element_type=jnp.float32).astype(jnp.bfloat16)
    queries = queries.reshape(agents, local_steps, KV_HEADS, groups, HEAD_DIM)
    queries = jnp.transpose(queries, (1, 0, 2, 3, 4))
    nbr_row = neighbours[0]
    valid_row = nbr_valid[0]
    alive_mask = agent_valid.astype(jnp.bfloat16)
    normed_block = normed.reshape(1, agents, local_steps, model_width)
    initial = (
        jnp.full((local_steps, KV_HEADS, groups, agents), -1e30, jnp.float32),
        jnp.zeros((local_steps, KV_HEADS, groups, agents), jnp.float32),
        jnp.zeros((local_steps, KV_HEADS, groups, agents, HEAD_DIM), jnp.float32),
    )
    row_block = normed_block[0]
    flat_rows = row_block.reshape(-1, model_width)
    result = jnp.dot(flat_rows, wkv_space, preferred_element_type=jnp.float32).astype(jnp.bfloat16)
    keyval = result.reshape(row_block.shape[0], row_block.shape[1], -1)[None]
    all_step_keyvalues, every_alive = (
        lax.all_gather(keyval, "tile", axis=0, tiled=True),
        lax.all_gather(alive_mask, "tile", axis=0, tiled=True),
    )
    chosen = jnp.take(all_step_keyvalues, nbr_row, axis=0)
    key_weights = valid_row.astype(jnp.float32)[:, None] * jnp.take(
        every_alive, nbr_row, axis=0
    ).astype(jnp.float32)

    def advance(inner, scan_item):
        return (tile_update(inner, scan_item[0], scan_item[1], queries), None)

    final = lax.scan(advance, initial, (chosen, key_weights))[0]
    row_top, denominator, weighted = final
    mixed = weighted / denominator[..., None]
    mixed = (
        jnp.transpose(mixed, (3, 0, 1, 2, 4))
        .astype(jnp.bfloat16)
        .reshape(agents * local_steps, model_width)
    )
    projected = jnp.dot(mixed, wo_space, preferred_element_type=jnp.float32)
    updated = (
        timed[0].astype(jnp.float32) + projected.reshape(agents, local_steps, model_width)
    ).astype(jnp.bfloat16)
    return lax.all_to_all(updated[None], "tm", split_axis=1, concat_axis=2, tiled=True)


def solution(mesh):
    return jax.shard_map(
        per_device,
        mesh=mesh,
        in_specs=(
            P("tile", "tm", None, None),
            P(),
            P(),
            P(),
            P(),
            P(),
            P(),
            P(),
            P(),
            P("tile", None),
            P("tile", None),
            P("tile", None),
        ),
        out_specs=P("tile", "tm", None, None),
        check_vma=False,
    )
```

profile of v0, /device:TPU:0, one launch (start us, length us, event | category | flops | bytes accessed | tf_op | source)
XLA Modules:
  0.0 210.6 jit_solution(16764752486686966595)
XLA Ops:
  6.6 1.7 fusion.28
  8.2 1.5 fusion.27
  9.8 1.5 convolution_convert_fusion.3
  11.3 1.3 convolution_convert_fusion.1
  12.6 2.2 %reshape.165 = bf16[4,128,2,4,64]{4,3,2,1,0:T(4,128)(2,1)S(1)} reshape(bf16[512,512]{1,0:T(8,128)(2,1)} %convolution_convert_fusion.3) | data formatting | bytes 1048576 | tf_op jit(solution)/shard_map/reshape | solution.py:24
  15.2 0.9 copy.100
  16.4 1.3 reshape.164
  17.7 0.8 fusion.24
  18.5 1.2 fusion.53
  20.2 0.7 copy-done.5
  20.9 0.7 copy-done.7
  21.6 1.3 fusion.40
  22.9 0.8 copy.77
  23.7 32.7 %all_to_all.27 = bf16[1,4,128,1024]{3,1,0,2:T(4,128)(2,1)S(1)} all-to-all(bf16[1,4,128,1024]{3,1,0,2:T(4,128)(2,1)S(1)} %copy.77), channel_id=1, replica_groups=mesh['tile'=4,'tm'=8] {'tm'}, dimensions={2} | all-to-all | bytes 2097152 | tf_op jit(solution)/shard_map/all_to_all | solution.py:82
  57.6 0.5 copy-done.10
  58.4 1.0 copy-done.8
  59.3 0.8 copy-done.12
  60.1 1.5 convolution_convert_fusion.2
  61.7 7.9 %all-gather = bf16[4,1,32]{2,1,0:T(2,128)(2,1)S(1)} all-gather(bf16[1,1,32]{2,1,0:T(2,128)(2,1)S(1)} %convert_bitcast_fusion), channel_id=1, replica_groups=mesh['tile'=4,'tm'=8] {'tile'}, dimensions={0}, use_global_device_ids=true | all-gather | bytes 320 | tf_op jit(solution)/shard_map/all_gather | solution.py:104
  69.6 0.6 gather_fusion
  70.3 3.2 %convolution_convert_fusion = bf16[512,1024]{1,0:T(8,128)(2,1)S(1)} fusion(bf16[512,1024]{1,0:T(8,128)(2,1)} %copy-done.8, bf16[1024,1024]{1,0:T(8,128)(2,1)} %param.20), kind=kOutput, calls=%fused_computation.61 | convolution fusion | flops 1074266112 | bytes 4194304 | tf_op jit(solution)/shard_map/dot_general | solution.py:86
  73.5 2.5 %reshape.127 = bf16[32,16,4,4,64]{4,3,2,1,0:T(4,128)(2,1)} reshape(bf16[512,1024]{1,0:T(8,128)(2,1)S(1)} %convolution_convert_fusion) | data formatting | bytes 2097152 | tf_op jit(solution)/shard_map/reshape | solution.py:87
  76.0 5.4 %copy.115 = bf16[32,16,4,4,64]{4,0,3,2,1:T(8,128)(2,1)} copy(bf16[32,16,4,4,64]{4,3,2,1,0:T(4,128)(2,1)} %reshape.127) | data formatting | bytes 2097152 | tf_op jit(solution)/shard_map/reshape | solution.py:87
  81.4 14.6 %all-gather.3.cloned.1.call-done = bf16[4,32,16,512]{3,2,1,0:T(8,128)(2,1)} async-done(((bf16[1,32,16,512]{3,2,1,0:T(8,128)(2,1)}), bf16[4,32,16,512]{3,2,1,0:T(8,128)(2,1)}) %all-gather.3.cloned.1.call-update) | async-done | bytes 2097168 | tf_op jit(solution)/shard_map/all_gather | solution.py:103
  96.0 3.6 %gather_fusion.1 = bf16[4,32,16,512]{3,2,1,0:T(8,128)(2,1)} fusion(bf16[4,32,16,512]{3,2,1,0:T(8,128)(2,1)} %all-gather.3.cloned.1.call-done, s32[1024]{0:T(1024)S(1)} %pad_clamp_fusion), kind=kCustom, calls=%fused_computation.1 | custom fusion | bytes 4194320 | tf_op jit(solution)/shard_map/jit(_take)/gather | solution.py:106
  99.6 3.2 %broadcast_select_fusion = bf16[4,32,16,512]{3,2,1,0:T(8,128)(2,1)} fusion(bf16[4,32,16,512]{3,2,1,0:T(8,128)(2,1)} %gather_fusion.1, pred[4]{0:T(512)(128)(4,1)S(1)} %compare_and_fusion), kind=kLoop, calls=%fused_computation.58 | loop fusion | flops 1048576 | bytes 4194308 | tf_op jit(solution)/shard_map/jit(_take)/select_n | solution.py:106
  102.8 56.1 %while.15 = (s32[]{:T(128)}, f32[16,4,4,32]{3,2,1,0:T(4,128)S(1)}, f32[16,4,4,32]{3,2,1,0:T(4,128)S(1)}, f32[16,4,4,32,64]{4,3,2,1,0:T(8,128)}, f32[4,32]{1,0:T(...) while((s32[]{:T(128)}, f32[16,4,4,32]{3,2,1,0:T(4,128)S(1)}, ...), condition=%wide.region_7.8_spmd.clone, body=%wide.region_4.0_spmd.clone.sunk | while | flops 72130592 | bytes 33555276 | solution.py:114
  102.8 1.1 constant_dynamic-slice_fusion.2
  103.9 0.5 reshape.167
  104.4 0.6 fusion.73
  105.0 1.0 copy-done.4
  106.0 3.4 %bitcast_reduce_fusion.2 = (f32[16,4,4,32]{3,2,1,0:T(4,128)S(1)}, f32[16,4,32,32,4]{3,2,4,1,0:T(8,128)S(1)}) fusion(pred[32]{0:T(512)(128)(4,1)S(1)} %get-tuple-element.146, bf16[16,32,4,4,64]{4,1,3,2,0:T(8,128)(2,1)S(1)} %copy-done.4, bf16[32,16,1,4,64]{4,3,2,1,0:T(4,128)(2,1)S(1)} %get-tuple-element.147), kind=kOutput, calls=%fused_computation.3.clone.1 | convolution fusion | flops 34332672 | bytes 2392096 | tf_op jit(solution)/shard_map/while/body/eval_jaxpr/sakgd,bskd->skgab/dot_general | solution.py:48
  109.4 1.7 fusion.74
  111.6 3.3 %fusion.76 = f32[16,4,4,32,64]{4,3,2,1,0:T(8,128)S(1)} fusion(f32[16,4,4,32,64]{4,3,2,1,0:T(8,128)S(1)} %copy-done.2, f32[16,4,32,32,4]{3,2,4,1,0:T(8,128)S(1)} %get-tuple-element.149, f32[16,4,4,32]{3,2,1,0:T(4,128)S(1)} %get-tuple-element.152, f32[32]{0:T(128)S(1)} %get-tuple-element.150, f32[16,4,4,32]{3,2,1,0:T(4,128)S(1)} %select_maximum_fusion.2, ...), kind=kOutput, calls=%fused_computation.7.clone.1 | convolution fusion | flops 36438016 | bytes 5570721 | tf_op jit(solution)/shard_map/while/body/eval_jaxpr/skgab,bskd->skgad/dot_general | solution.py:57
  114.9 1.9 copy-done.3
  116.8 1.1 constant_dynamic-slice_fusion.2
  117.9 0.5 reshape.167
  118.5 0.6 fusion.73
  119.1 1.0 copy-done.4
  120.1 3.4 %bitcast_reduce_fusion.2 = (f32[16,4,4,32]{3,2,1,0:T(4,128)S(1)}, f32[16,4,32,32,4]{3,2,4,1,0:T(8,128)S(1)}) fusion(pred[32]{0:T(512)(128)(4,1)S(1)} %get-tuple-element.146, bf16[16,32,4,4,64]{4,1,3,2,0:T(8,128)(2,1)S(1)} %copy-done.4, bf16[32,16,1,4,64]{4,3,2,1,0:T(4,128)(2,1)S(1)} %get-tuple-element.147), kind=kOutput, calls=%fused_computation.3.clone.1 | convolution fusion | flops 34332672 | bytes 2392096 | tf_op jit(solution)/shard_map/while/body/eval_jaxpr/sakgd,bskd->skgab/dot_general | solution.py:48
  123.5 1.7 fusion.74
  125.7 3.3 %fusion.76 = f32[16,4,4,32,64]{4,3,2,1,0:T(8,128)S(1)} fusion(f32[16,4,4,32,64]{4,3,2,1,0:T(8,128)S(1)} %copy-done.2, f32[16,4,32,32,4]{3,2,4,1,0:T(8,128)S(1)} %get-tuple-element.149, f32[16,4,4,32]{3,2,1,0:T(4,128)S(1)} %get-tuple-element.152, f32[32]{0:T(128)S(1)} %get-tuple-element.150, f32[16,4,4,32]{3,2,1,0:T(4,128)S(1)} %select_maximum_fusion.2, ...), kind=kOutput, calls=%fused_computation.7.clone.1 | convolution fusion | flops 36438016 | bytes 5570721 | tf_op jit(solution)/shard_map/while/body/eval_jaxpr/skgab,bskd->skgad/dot_general | solution.py:57
  129.0 1.9 copy-done.3
  130.9 1.1 constant_dynamic-slice_fusion.2
  132.0 0.5 reshape.167
  132.5 0.6 fusion.73
  133.1 1.0 copy-done.4
  134.1 3.4 %bitcast_reduce_fusion.2 = (f32[16,4,4,32]{3,2,1,0:T(4,128)S(1)}, f32[16,4,32,32,4]{3,2,4,1,0:T(8,128)S(1)}) fusion(pred[32]{0:T(512)(128)(4,1)S(1)} %get-tuple-element.146, bf16[16,32,4,4,64]{4,1,3,2,0:T(8,128)(2,1)S(1)} %copy-done.4, bf16[32,16,1,4,64]{4,3,2,1,0:T(4,128)(2,1)S(1)} %get-tuple-element.147), kind=kOutput, calls=%fused_computation.3.clone.1 | convolution fusion | flops 34332672 | bytes 2392096 | tf_op jit(solution)/shard_map/while/body/eval_jaxpr/sakgd,bskd->skgab/dot_general | solution.py:48
  137.5 1.7 fusion.74
  139.7 3.3 %fusion.76 = f32[16,4,4,32,64]{4,3,2,1,0:T(8,128)S(1)} fusion(f32[16,4,4,32,64]{4,3,2,1,0:T(8,128)S(1)} %copy-done.2, f32[16,4,32,32,4]{3,2,4,1,0:T(8,128)S(1)} %get-tuple-element.149, f32[16,4,4,32]{3,2,1,0:T(4,128)S(1)} %get-tuple-element.152, f32[32]{0:T(128)S(1)} %get-tuple-element.150, f32[16,4,4,32]{3,2,1,0:T(4,128)S(1)} %select_maximum_fusion.2, ...), kind=kOutput, calls=%fused_computation.7.clone.1 | convolution fusion | flops 36438016 | bytes 5570721 | tf_op jit(solution)/shard_map/while/body/eval_jaxpr/skgab,bskd->skgad/dot_general | solution.py:57
  143.0 1.9 copy-done.3
  144.9 1.1 constant_dynamic-slice_fusion.2
  146.5 0.6 fusion.73
  147.1 1.0 copy-done.4
  148.1 3.4 %bitcast_reduce_fusion.2 = (f32[16,4,4,32]{3,2,1,0:T(4,128)S(1)}, f32[16,4,32,32,4]{3,2,4,1,0:T(8,128)S(1)}) fusion(pred[32]{0:T(512)(128)(4,1)S(1)} %get-tuple-element.146, bf16[16,32,4,4,64]{4,1,3,2,0:T(8,128)(2,1)S(1)} %copy-done.4, bf16[32,16,1,4,64]{4,3,2,1,0:T(4,128)(2,1)S(1)} %get-tuple-element.147), kind=kOutput, calls=%fused_computation.3.clone.1 | convolution fusion | flops 34332672 | bytes 2392096 | tf_op jit(solution)/shard_map/while/body/eval_jaxpr/sakgd,bskd->skgab/dot_general | solution.py:48
  151.5 1.7 fusion.74
  153.7 3.3 %fusion.76 = f32[16,4,4,32,64]{4,3,2,1,0:T(8,128)S(1)} fusion(f32[16,4,4,32,64]{4,3,2,1,0:T(8,128)S(1)} %copy-done.2, f32[16,4,32,32,4]{3,2,4,1,0:T(8,128)S(1)} %get-tuple-element.149, f32[16,4,4,32]{3,2,1,0:T(4,128)S(1)} %get-tuple-element.152, f32[32]{0:T(128)S(1)} %get-tuple-element.150, f32[16,4,4,32]{3,2,1,0:T(4,128)S(1)} %select_maximum_fusion.2, ...), kind=kOutput, calls=%fused_computation.7.clone.1 | convolution fusion | flops 36438016 | bytes 5570721 | tf_op jit(solution)/shard_map/while/body/eval_jaxpr/skgab,bskd->skgad/dot_general | solution.py:57
  157.0 1.9 copy-done.3
  158.9 2.9 %fusion.32 = bf16[32,16,4,4,64]{4,0,3,2,1:T(8,128)(2,1)S(1)} fusion(f32[16,4,4,32,64]{4,3,2,1,0:T(8,128)} %get-tuple-element.43, f32[16,4,4,32]{3,2,1,0:T(4,128)S(1)} %get-tuple-element.44), kind=kLoop, calls=%fused_computation.56 | loop fusion | flops 1048576 | bytes 3178496 | tf_op jit(solution)/shard_map/convert_element_type | solution.py:119
  161.8 2.4 %copy.83 = bf16[32,16,4,4,64]{4,3,2,1,0:T(4,128)(2,1)} copy(bf16[32,16,4,4,64]{4,0,3,2,1:T(8,128)(2,1)S(1)} %fusion.32) | data formatting | bytes 2097152 | tf_op jit(solution)/shard_map/convert_element_type | solution.py:119
  164.2 3.8 %dot_general.42 = bf16[32,16,1024]{2,1,0:T(8,128)(2,1)S(1)} reshape(bf16[32,16,4,4,64]{4,3,2,1,0:T(4,128)(2,1)} %copy.83) | data formatting | bytes 2097152 | tf_op jit(solution)/shard_map/dot_general | solution.py:122
  168.1 3.6 %fusion.43 = bf16[1,32,16,1024]{3,2,0,1:T(8,128)(2,1)S(1)} fusion(bf16[32,16,1024]{2,1,0:T(8,128)(2,1)S(1)} %dot_general.42, bf16[1024,1024]{1,0:T(8,128)(2,1)} %param.22, f32[1,8,4,16,1024]{4,3,2,1,0:T(8,128)} %copy-done.6), kind=kOutput, calls=%fused_computation.64 | convolution fusion | flops 1074790400 | bytes 6291456 | tf_op jit(solution)/shard_map/dot_general | solution.py:122
  171.7 31.0 %all_to_all.28 = bf16[1,32,16,1024]{3,2,0,1:T(8,128)(2,1)S(1)} all-to-all(bf16[1,32,16,1024]{3,2,0,1:T(8,128)(2,1)S(1)} %fusion.43), channel_id=1, replica_groups=mesh['tile'=4,'tm'=8] {'tm'}, dimensions={1} | all-to-all | bytes 2097152 | tf_op jit(solution)/shard_map/all_to_all | solution.py:126
  202.7 1.0 copy.85
  (79 shorter events, 5.4 us)
Async XLA Ops:
  6.5 4.8 %copy-start = (bf16[1024,1024]{1,0:T(8,128)(2,1)S(1)}, bf16[1024,1024]{1,0:T(8,128)(2,1)}, u32[]{:S(2)}) copy-start(bf16[1024,1024]{1,0:T(8,128)(2,1)} %param.16) | copy-start | bytes 6291460
  6.5 3.3 %copy-start.11 = (bf16[1024,512]{1,0:T(8,128)(2,1)S(1)}, bf16[1024,512]{1,0:T(8,128)(2,1)}, u32[]{:S(2)}) copy-start(bf16[1024,512]{1,0:T(8,128)(2,1)} %param.17) | copy-start | bytes 3145732
  6.5 89.5 %all-gather.3.cloned.1.call-start = ((), (), s32[]{:S(2)}) async-start(), calls=%async_computation.2 | async-start | bytes 2621440 | tf_op jit(solution)/shard_map/all_gather | solution.py:103
  18.5 1.2 copy-start.9
  19.7 1.2 copy-start.5
  19.7 1.9 copy-start.7
  57.4 0.7 copy-start.10
  58.1 3.5 %copy-start.6 = (f32[1,8,4,16,1024]{4,3,2,1,0:T(8,128)}, f32[1,8,4,16,1024]{4,3,2,1,0:T(8,128)S(1)}, u32[]{:S(2)}) copy-start(f32[1,8,4,16,1024]{4,3,2,1,0:T(8,128)S(1)} %copy.79) | copy-start | bytes 6291460
  58.1 2.0 copy-start.12
  58.4 1.0 copy-start.8
  60.1 1.6 copy-start.13
  60.1 9.5 %copy-start.14 = (s32[1,4]{1,0:T(1,128)S(1)}, s32[1,4]{1,0:T(1,128)}, u32[]{:S(2)}) copy-start(s32[1,4]{1,0:T(1,128)} %param.23) | copy-start | bytes 52
  60.1 10.1 %copy-start.15 = (s32[1,4]{1,0:T(1,128)S(1)}, s32[1,4]{1,0:T(1,128)}, u32[]{:S(2)}) copy-start(s32[1,4]{1,0:T(1,128)} %param.24) | copy-start | bytes 52
  104.4 1.6 copy-start.4
  109.4 2.2 %copy-start.2 = (f32[16,4,4,32,64]{4,3,2,1,0:T(8,128)S(1)}, f32[16,4,4,32,64]{4,3,2,1,0:T(8,128)}, u32[]{:S(2)}) copy-start(f32[16,4,4,32,64]{4,3,2,1,0:T(8,128)} %get-tuple-element.166) | copy-start | bytes 6291460 | tf_op jit(solution)/shard_map/while
  114.9 1.9 copy-start.3
  118.5 1.6 copy-start.4
  123.5 2.2 %copy-start.2 = (f32[16,4,4,32,64]{4,3,2,1,0:T(8,128)S(1)}, f32[16,4,4,32,64]{4,3,2,1,0:T(8,128)}, u32[]{:S(2)}) copy-start(f32[16,4,4,32,64]{4,3,2,1,0:T(8,128)} %get-tuple-element.166) | copy-start | bytes 6291460 | tf_op jit(solution)/shard_map/while
  128.9 1.9 copy-start.3
  132.5 1.6 copy-start.4
  137.5 2.2 %copy-start.2 = (f32[16,4,4,32,64]{4,3,2,1,0:T(8,128)S(1)}, f32[16,4,4,32,64]{4,3,2,1,0:T(8,128)}, u32[]{:S(2)}) copy-start(f32[16,4,4,32,64]{4,3,2,1,0:T(8,128)} %get-tuple-element.166) | copy-start | bytes 6291460 | tf_op jit(solution)/shard_map/while
  143.0 1.9 copy-start.3
  146.5 1.6 copy-start.4
  151.5 2.2 %copy-start.2 = (f32[16,4,4,32,64]{4,3,2,1,0:T(8,128)S(1)}, f32[16,4,4,32,64]{4,3,2,1,0:T(8,128)}, u32[]{:S(2)}) copy-start(f32[16,4,4,32,64]{4,3,2,1,0:T(8,128)} %get-tuple-element.166) | copy-start | bytes 6291460 | tf_op jit(solution)/shard_map/while
  157.0 1.9 copy-start.3
  168.1 35.7 %copy-start.1 = (bf16[1024,1024]{1,0:T(8,128)(2,1)S(1)}, bf16[1024,1024]{1,0:T(8,128)(2,1)}, u32[]{:S(2)}) copy-start(bf16[1024,1024]{1,0:T(8,128)(2,1)} %param.16) | copy-start | bytes 6291460
Sparse Core Ops, SparseCore 0:
  61.8 34.2 all-gather.2
where the time goes:
time: 212 us; the launch traced here: 211 us
  blocking collectives  71.6 us (34%)
  local copies, waits for them, and re-layouts  51 us (24%)
  matrix products  40.1 us (19%)
  other arithmetic  19.2 us (9%)
  waiting for transfers between devices  14.7 us (7%)
  between operations  13.7 us (6%)
    all_to_all x1, blocking collectives, per_device(): lax.all_to_all(history, 'tm', split_axis=2, concat_axis=1, tiled=True)  32.7 us
    all_to_all x1, blocking collectives, per_device(): lax.all_to_all(updated[None], 'tm', split_axis=1, concat_axis=2, tiled=True)  31 us
    all_gather x1, waiting for transfers between devices, per_device(): lax.all_gather(keyval, 'tile', axis=0, tiled=True)  14.6 us
    dot_general x4, matrix products, tile_update(): jnp.einsum('sakgd,bskd->skgab', queries, key_values[:, :, 0], preferred_e...  13.4 us
    dot_general x4, matrix products, tile_update(): jnp.einsum('skgab,bskd->skgad', expd.astype(jnp.bfloat16), key_values[:,...  13.1 us
    while x28, local copies, waits for them, and re-layouts  13 us
    all_gather x1, blocking collectives, per_device(): lax.all_gather(alive_mask, 'tile', axis=0, tiled=True)  7.93 us
    reshape x2, local copies, waits for them, and re-layouts, per_device(): queries = queries.reshape(agents, local_steps, KV_HEADS, groups, HEAD_DIM)  7.89 us
  transfers between devices with their start and end apart: 1, of which 1 were waited for; matrix products, arithmetic and copies ran while one was open for 6% of the time, Pallas kernels for 0%

commit v1 on v0

v1 whole, which is shorter than its diff:
```python
import functools

import jax
import jax.numpy as jnp
from jax import lax
from jax.experimental import pallas as pl
from jax.experimental.pallas import tpu as pltpu
from jax.sharding import Mesh
from jax.sharding import PartitionSpec as P

HEADS = 16
KV_HEADS = 4
HEAD_DIM = 64
GROUPS = HEADS // KV_HEADS
KEYS = KV_HEADS * HEAD_DIM
WIDE = GROUPS * HEAD_DIM
SCALE = HEAD_DIM ** (-0.5)
NEG = -1e30
LANES = 128
COLS = 256
HALVES = 2
VMEM_BYTES = 56 * 1024 * 1024
F32 = jnp.float32
BF16 = jnp.bfloat16
ROWS_BY_COLS = (((1,), (1,)), ((), ()))


def norm_rows(values, gain):
    wide = values.astype(F32)
    meansq = jnp.mean(wide * wide, axis=-1, keepdims=True)
    return (wide * lax.rsqrt(meansq + 1e-05) * gain).astype(BF16)


def to_blocks(values, agents, steps, local):
    split = values.reshape(agents, steps // local, local, values.shape[-1])
    return jnp.transpose(split, (1, 0, 2, 3)).reshape(steps // local, agents * local, values.shape[-1])


def from_blocks(values, agents, steps, local):
    split = values.reshape(steps // local, agents, local, values.shape[-1])
    return jnp.transpose(split, (1, 0, 2, 3)).reshape(agents * steps, values.shape[-1])


def time_kernel(
    agents, steps, local, blocked,
    hist, gain_t, gain_s, wq_hbm, wkv_hbm, wo_hbm, wkv2_hbm,
    mid, second, kv_out,
    wq, wkv, wo, wkv2, normed, query, keyval, mix, sems,
):
    rows, width = hist.shape
    loads = [
        pltpu.make_async_copy(source, target, sems.at[i])
        for i, (source, target) in enumerate(
            ((wq_hbm, wq), (wkv_hbm, wkv), (wo_hbm, wo), (wkv2_hbm, wkv2))
        )
    ]
    for load in loads:
        load.start()
    for a in range(agents):
        part = pl.ds(a * steps, steps)
        normed[part, :] = norm_rows(hist[part, :], gain_t[...])
    loads[0].wait()
    for c in range(0, width, COLS):
        query[:, c : c + COLS] = jnp.dot(
            normed[...], wq[:, c : c + COLS], preferred_element_type=F32
        ).astype(BF16)
    loads[1].wait()
    for c in range(0, 2 * KEYS, COLS):
        keyval[:, c : c + COLS] = jnp.dot(
            normed[...], wkv[:, c : c + COLS], preferred_element_type=F32
        ).astype(BF16)
    lane_head = lax.broadcasted_iota(jnp.int32, (steps, WIDE), 1) // HEAD_DIM
    causal = lax.broadcasted_iota(jnp.int32, (steps, steps), 0) >= lax.broadcasted_iota(
        jnp.int32, (steps, steps), 1
    )

    def spread(part):
        repeated = jnp.concatenate([part] * GROUPS, axis=1)
        zero = jnp.zeros_like(repeated)
        return jnp.concatenate(
            [jnp.where(lane_head == j, repeated, zero) for j in range(GROUPS)], axis=0
        )

    def one_agent(a, carry):
        part = pl.ds(pl.multiple_of(a * steps, steps), steps)
        for k in range(KV_HEADS):
            wide = slice(k * WIDE, (k + 1) * WIDE)
            keys = spread(keyval[part, k * HEAD_DIM : (k + 1) * HEAD_DIM])
            vals = spread(keyval[part, KEYS + k * HEAD_DIM : KEYS + (k + 1) * HEAD_DIM])
            scores = lax.dot_general(
                query[part, wide], keys, ROWS_BY_COLS, preferred_element_type=F32
            )
            expd, sums = [], []
            for j in range(GROUPS):
                head = jnp.where(causal, scores[:, j * steps : (j + 1) * steps] * SCALE, NEG)
                top = jnp.max(head, axis=-1, keepdims=True)
                grown = jnp.exp(head - top)
                sums.append(jnp.sum(grown, axis=-1, keepdims=True))
                expd.append(grown.astype(BF16))
            mixed = jnp.dot(jnp.concatenate(expd, axis=1), vals, preferred_element_type=F32)
            inverse = jnp.concatenate(
                [jnp.broadcast_to(1.0 / s, (steps, HEAD_DIM)) for s in sums], axis=1
            )
            mix[part, wide] = (mixed * inverse).astype(BF16)
        return carry

    lax.fori_loop(0, agents, one_agent, 0)
    loads[2].wait()
    for c in range(0, width, COLS):
        cols = slice(c, c + COLS)
        projected = jnp.dot(mix[...], wo[:, cols], preferred_element_type=F32)
        mid[:, cols] = (hist[:, cols].astype(F32) + projected).astype(BF16)
    for a in range(agents):
        part = pl.ds(a * steps, steps)
        second[part, :] = norm_rows(mid[part, :], gain_s[...])
    loads[3].wait()
    for c in range(0, 2 * KEYS, COLS):
        cols = slice(c, c + COLS)
        result = jnp.dot(second[...], wkv2[:, cols], preferred_element_type=F32)
        if blocked:
            kv_out[:, :, cols] = to_blocks(result, agents, steps, local).astype(BF16)
        else:
            kv_out[:, cols] = result.astype(BF16)


def query_kernel(agents, steps, local, blocked, second, wq, meta, out):
    width = second.shape[1]
    for c in range(0, width, COLS):
        cols = slice(c, c + COLS)
        result = jnp.dot(second[...], wq[:, cols], preferred_element_type=F32)
        if blocked:
            out[:, :, cols] = to_blocks(result, agents, steps, local).astype(BF16)
        else:
            out[:, cols] = result.astype(BF16)
    lines = jnp.broadcast_to(meta[0:1, :], (out.shape[-2], LANES)).astype(BF16)
    if blocked:
        out[:, :, width:] = jnp.broadcast_to(lines[None], (out.shape[0], out.shape[1], LANES))
    else:
        out[:, width:] = lines


def one_hot(shape, group, local, dtype=BF16):
    row = lax.broadcasted_iota(jnp.int32, shape, 0)
    col = lax.broadcasted_iota(jnp.int32, shape, 1)
    wanted = (row % group) * local + row // group
    return jnp.where(col == wanted, 1.0, 0.0).astype(dtype)


def space_kernel(
    local, block, q_in, own, other, weight, out, query, keyval, mix
):
    rows, width = out.shape
    group = block // local
    total = rows // local
    if local > 1:
        order = one_hot((block, block), group, local)

    def by_steps(source, target, offset, cols):
        for b in range(rows // block):
            piece = source[b * block : (b + 1) * block, cols]
            if local > 1:
                piece = jnp.dot(order, piece, preferred_element_type=F32).astype(BF16)
            target[:, offset + b * group : offset + (b + 1) * group, cols] = piece.reshape(
                local, group, piece.shape[1]
            )

    for c in range(0, width, COLS):
        by_steps(q_in, query, 0, slice(c, c + COLS))
    for c in range(0, 2 * KEYS, COLS):
        by_steps(own, keyval, 0, slice(c, c + COLS))
        by_steps(other, keyval, total, slice(c, c + COLS))

    def one_step(s, carry):
        mask = jnp.concatenate([weight[...]] * GROUPS, axis=0)
        for k in range(KV_HEADS):
            wide = slice(k * WIDE, (k + 1) * WIDE)
            heads = query[s, :, wide]
            heads = jnp.concatenate(
                [heads[:, j * HEAD_DIM : (j + 1) * HEAD_DIM] for j in range(GROUPS)], axis=0
            )
            keys = keyval[s, :, k * HEAD_DIM : (k + 1) * HEAD_DIM]
            vals = keyval[s, :, KEYS + k * HEAD_DIM : KEYS + (k + 1) * HEAD_DIM]
            scores = lax.dot_general(heads, keys, ROWS_BY_COLS, preferred_element_type=F32)
            scores = jnp.where(mask > 0, scores * SCALE, NEG)
            top = jnp.max(scores, axis=-1, keepdims=True)
            grown = jnp.exp(scores - top) * mask
            sums = jnp.sum(grown, axis=-1, keepdims=True)
            mixed = jnp.dot(grown.astype(BF16), vals, preferred_element_type=F32) / sums
            mixed = mixed.astype(BF16)
            mix[s, :, wide] = jnp.concatenate(
                [mixed[j * total : (j + 1) * total] for j in range(GROUPS)], axis=1
            )
        return carry

    lax.fori_loop(0, local, one_step, 0)
    for b in range(rows // block):
        for c in range(0, width, COLS):
            cols = slice(c, c + COLS)
            piece = mix[:, b * group : (b + 1) * group, cols].reshape(block, COLS)
            if local > 1:
                piece = lax.dot_general(
                    order, piece, (((0,), (0,)), ((), ())), preferred_element_type=F32
                ).astype(BF16)
            out[b * block : (b + 1) * block, cols] = piece


def out_kernel(agents, steps, local, blocked, mix, mid, wo, out):
    width = mid.shape[1]
    for c in range(0, width, COLS):
        cols = slice(c, c + COLS)
        projected = jnp.dot(mix[...], wo[:, cols], preferred_element_type=F32)
        if blocked:
            projected = from_blocks(projected, agents, steps, local)
        out[:, cols] = (mid[:, cols].astype(F32) + projected).astype(BF16)


def call(kernel, shapes, args, hbm=(), scratch=(), flops=0):
    moved = sum(a.size * a.dtype.itemsize for a in args)
    moved += sum(s.size * s.dtype.itemsize for s in shapes)
    return pl.pallas_call(
        kernel,
        out_shape=shapes if len(shapes) > 1 else shapes[0],
        in_specs=[
            pl.BlockSpec(memory_space=pl.ANY if i in hbm else pltpu.VMEM) for i in range(len(args))
        ],
        out_specs=[pl.BlockSpec(memory_space=pltpu.VMEM)] * len(shapes)
        if len(shapes) > 1
        else pl.BlockSpec(memory_space=pltpu.VMEM),
        scratch_shapes=list(scratch),
        compiler_params=pltpu.CompilerParams(vmem_limit_bytes=VMEM_BYTES),
        cost_estimate=pl.CostEstimate(flops=flops, bytes_accessed=moved, transcendentals=0),
    )(*args)


def per_device(
    histories,
    gain_time,
    wq_time,
    wkv_time,
    wo_time,
    gain_space,
    wq_space,
    wkv_space,
    wo_space,
    neighbours,
    nbr_valid,
    agent_valid,
):
    agents, steps, width = histories.shape[1:]
    tiles, rest = lax.axis_size("tile"), lax.axis_size("rest")
    spread = ("tile", "rest")
    parts = tiles * rest
    local = steps // parts
    rows = agents * steps
    blocked = local % 8 == 0
    struct = jax.ShapeDtypeStruct

    hist = histories.reshape(rows, width)
    kv_shape = (parts, agents * local, 2 * KEYS) if blocked else (rows, 2 * KEYS)
    mid, second, kv = call(
        functools.partial(time_kernel, agents, steps, local, blocked),
        [struct((rows, width), BF16), struct((rows, width), BF16), struct(kv_shape, BF16)],
        [hist, gain_time[None], gain_space[None], wq_time, wkv_time, wo_time, wkv_space],
        hbm=(3, 4, 5, 6),
        scratch=[
            pltpu.VMEM(wq_time.shape, BF16),
            pltpu.VMEM(wkv_time.shape, BF16),
            pltpu.VMEM(wo_time.shape, BF16),
            pltpu.VMEM(wkv_space.shape, BF16),
            pltpu.VMEM((rows, width), BF16),
            pltpu.VMEM((rows, width), BF16),
            pltpu.VMEM((rows, 2 * KEYS), BF16),
            pltpu.VMEM((rows, width), BF16),
            pltpu.SemaphoreType.DMA((4,)),
        ],
        flops=2 * rows * width * (2 * width + 4 * KEYS),
    )
    if not blocked:
        kv = to_blocks(kv, agents, steps, local)
    own = lax.all_to_all(kv, spread, split_axis=0, concat_axis=0, tiled=True)
    own = own.reshape(rows, 2 * KEYS)
    swap = [(h, HALVES - 1 - h) for h in range(HALVES)]
    other = lax.ppermute(own, "half", swap)

    listed = jnp.sum(
        jnp.where(
            neighbours[0][:, None] == jnp.arange(tiles)[None, :], nbr_valid[0][:, None], 0
        ),
        axis=0,
    )
    alive = agent_valid[0]
    meta = jnp.concatenate([alive, listed])
    meta = jnp.pad(meta, (0, LANES - meta.shape[0])).astype(F32)
    meta = jnp.broadcast_to(meta[None], (8, LANES))
    second, own = lax.optimization_barrier((second, own))
    q_shape = (parts, agents * local, width + LANES) if blocked else (rows, width + LANES)
    q = call(
        functools.partial(query_kernel, agents, steps, local, blocked),
        [struct(q_shape, BF16)],
        [second, wq_space, meta],
        flops=2 * rows * width * width,
    )
    if not blocked:
        q = to_blocks(q, agents, steps, local)
    q = lax.all_to_all(q, spread, split_axis=0, concat_axis=0, tiled=True)

    lines = q.reshape(tiles, rest, agents * local, width + LANES)[:, 0, 0, width:].astype(F32)
    group = rest * agents
    half = lax.axis_index("half")
    alive_all = lines[:, : HALVES * group].reshape(tiles, HALVES, group)
    alive_own = lax.dynamic_index_in_dim(alive_all, half, 1, keepdims=False)
    alive_other = lax.dynamic_index_in_dim(alive_all, 1 - half, 1, keepdims=False)
    listed_all = lines[:, HALVES * group : HALVES * group + tiles]
    weight = listed_all[:, None, :, None] * jnp.stack([alive_own, alive_other])[None]
    weight = jnp.repeat(weight.reshape(tiles, -1), group, axis=0)

    block = max(COLS, local) if rows % max(COLS, local) == 0 else rows
    mix = call(
        functools.partial(space_kernel, local, block),
        [struct((rows, width), BF16)],
        [q.reshape(rows, width + LANES), own, other, weight],
        scratch=[
            pltpu.VMEM((local, rows // local, width), BF16),
            pltpu.VMEM((local, HALVES * rows // local, 2 * KEYS), BF16),
            pltpu.VMEM((local, rows // local, width), BF16),
        ],
        flops=8 * rows * rows // local * width,
    )
    mix = lax.all_to_all(
        mix.reshape(parts, agents * local, width), spread, split_axis=0, concat_axis=0, tiled=True
    )
    if not blocked:
        mix = from_blocks(mix, agents, steps, local)
    out = call(
        functools.partial(out_kernel, agents, steps, local, blocked),
        [struct((rows, width), BF16)],
        [mix.reshape(rows, width), mid, wo_space],
        flops=2 * rows * width * width,
    )
    return out.reshape(1, agents, steps, width)


def solution(mesh):
    tiles, members = mesh.devices.shape
    split = Mesh(
        mesh.devices.reshape(tiles, HALVES, members // HALVES), ("tile", "half", "rest")
    )
    states = P("tile", ("half", "rest"), None, None)
    listing = P("tile", None)
    return jax.shard_map(
        per_device,
        mesh=split,
        in_specs=(states,) + (P(),) * 8 + (listing,) * 3,
        out_specs=states,
        check_vma=False,
    )
```

time: 212 us -> 105 us (0.50)
  blocking collectives: 71.6 us -> 20.5 us
  local copies, waits for them, and re-layouts: 51 us -> 1.85 us
  matrix products: 40.1 us -> 0 us
  Pallas kernels: 0 us -> 32.7 us
  waiting for transfers between devices: 14.7 us -> 36.5 us
  other arithmetic: 19.2 us -> 0.19 us
  between operations: 13.7 us -> 0.1 us
  starting transfers between devices: 0.01 us -> 12.7 us
    all_to_all x2 -> x1, blocking collectives: 63.7 us -> 20.5 us  [per_device(): lax.all_to_all(mix.reshape(parts, agents * local, width), spread, split_a...]
    dot_general x16 -> x0, matrix products: 40.1 us -> none  [the longest x4 13.4 us: tile_update(): jnp.einsum('sakgd,bskd->skgab', queries, key_values[:, :, 0], preferred_e...]
    all_to_all x0 -> x2, waiting for transfers between devices: none -> 36.5 us  [the longest x1 26.1 us: per_device(): q = lax.all_to_all(q, spread, split_axis=0, concat_axis=0, tiled=True)]
    pallas_call x0 -> x4, Pallas kernels: none -> 32.7 us  [call(): pl.pallas_call(kernel, out_shape=shapes if len(shapes) > 1 else shapes[0]...]
    all_gather x1 -> x0, waiting for transfers between devices: 14.6 us -> none  [per_device(): lax.all_gather(keyval, 'tile', axis=0, tiled=True)]
    reshape x8 -> x1, local copies, waits for them, and re-layouts: 13.6 us -> 0.08 us  [per_device(): alive_all = lines[:, :HALVES * group].reshape(tiles, HALVES, group)]
    while x28 -> x0, local copies, waits for them, and re-layouts: 13 us -> none
    all_to_all x0 -> x2, starting transfers between devices: none -> 9.99 us  [the longest x1 6.29 us: per_device(): own = lax.all_to_all(kv, spread, split_axis=0, concat_axis=0, tiled=True)]
  transfers between devices with their start and end apart: 1 -> 3, of which waited for: 1 -> 2; matrix products, arithmetic and copies ran while one was open for 6% -> 1% of each run, Pallas kernels for 0% -> 0%
where the time goes in v1:
time: 105 us; the launch traced here: 104 us
  waiting for transfers between devices  36.5 us (35%)
  Pallas kernels  32.7 us (31%)
  blocking collectives  20.5 us (20%)
  starting transfers between devices  12.7 us (12%)
  local copies, waits for them, and re-layouts  1.85 us (2%)
    pallas_call x4, Pallas kernels, call(): pl.pallas_call(kernel, out_shape=shapes if len(shapes) > 1 else shapes[0]...  32.7 us
    all_to_all x1, waiting for transfers between devices, per_device(): q = lax.all_to_all(q, spread, split_axis=0, concat_axis=0, tiled=True)  26.1 us
    all_to_all x1, blocking collectives, per_device(): lax.all_to_all(mix.reshape(parts, agents * local, width), spread, split_a...  20.5 us
    all_to_all x1, waiting for transfers between devices, per_device(): own = lax.all_to_all(kv, spread, split_axis=0, concat_axis=0, tiled=True)  10.4 us
    all_to_all x1, starting transfers between devices, per_device(): own = lax.all_to_all(kv, spread, split_axis=0, concat_axis=0, tiled=True)  6.29 us
    all_to_all x1, starting transfers between devices, per_device(): q = lax.all_to_all(q, spread, split_axis=0, concat_axis=0, tiled=True)  3.7 us
    ppermute x1, starting transfers between devices, per_device(): other = lax.ppermute(own, 'half', swap)  2.66 us
  transfers between devices with their start and end apart: 3, of which 2 were waited for; matrix products, arithmetic and copies ran while one was open for 1% of the time, Pallas kernels for 0%

profile of v1, /device:TPU:0, one launch (start us, length us, event | category | flops | bytes accessed | tf_op | source)
XLA Modules:
  0.0 104.5 jit_solution(15158646258539785592)
XLA Ops:
  0.0 0.0 copy-start.3
  0.0 0.0 copy-start.4
  0.0 0.0 copy-start.5
  0.0 13.7 %shard_map.118 = (bf16[512,1024]{1,0:T(8,128)(2,1)}, bf16[512,1024]{1,0:T(8,128)(2,1)}, bf16[16,32,512]{2,1,0:T(8,128)(2,1)}) custom-call(bf16[512,1024]{1,0:T(8,128)(2,1)} %bitcast.31, f32[1,1024]{1,0:T(1,128)} %bitcast.32, f32[1,1024]{1,0:T(1,128)} %bitcast.33, bf16[1024,1024]{1,0:T(8,128)(2,1)} %wq_hbm.1, bf16[1024,512]{1,0:T(8,128)(2,1)} %wkv_hbm.1, ...), custom_call_target="tpu_custom_call" | custom-call | flops 3221225472 | bytes 9969664 | tf_op jit(solution)/shard_map/pallas_call | solution.py:220
  13.7 6.3 %all-to-all-start = ((bf16[16,32,512]{2,1,0:T(8,128)(2,1)}), bf16[16,32,512]{2,1,0:T(8,128)(2,1)S(1)}, u32[]{:S(2)}, u32[]{:S(2)}) async-start(bf16[16,32,512]{2,1,0:T(8,128)(2,1)} %get-tuple-element.11), calls=%async_computation | async-start | bytes 1048576 | tf_op jit(solution)/shard_map/all_to_all | solution.py:280
  20.0 0.0 copy-done.3
  20.0 0.0 copy-done.4
  20.0 0.1 select_reduce_fusion
  20.1 0.0 copy-done.5
  20.1 0.1 pad_add_fusion
  20.2 10.4 %all-to-all-done = bf16[16,32,512]{2,1,0:T(8,128)(2,1)S(1)} async-done(((bf16[16,32,512]{2,1,0:T(8,128)(2,1)}), bf16[16,32,512]{2,1,0:T(8,128)(2,1)S(1)}, u32[]{:S(2)}, u32[]{:S(2)}) %all-to-all-start) | async-done | bytes 524320 | tf_op jit(solution)/shard_map/all_to_all | solution.py:280
  30.5 0.0 copy-start.1
  30.5 0.6 broadcast_in_dim.37.meta
  31.1 4.2 %shard_map.119 = bf16[16,32,1152]{2,1,0:T(8,128)(2,1)} custom-call(bf16[512,1024]{1,0:T(8,128)(2,1)} %get-tuple-element.12.second, bf16[1024,1024]{1,0:T(8,128)(2,1)} %wq.1, f32[8,128]{1,0:T(8,128)} %broadcast_in_dim.37.meta), custom_call_target="tpu_custom_call" | custom-call | flops 1073741824 | bytes 4329472 | tf_op jit(solution)/shard_map/pallas_call | solution.py:220
  35.3 3.7 %all-to-all-start.1 = ((bf16[16,32,1152]{2,1,0:T(8,128)(2,1)}), bf16[16,32,1152]{2,1,0:T(8,128)(2,1)S(1)}, u32[]{:S(2)}, u32[]{:S(2)}) async-start(bf16[16,32,1152]{2,1,0:T(8,128)(2,1)} %shard_map.119), calls=%async_computation.1 | async-start | bytes 2359296 | tf_op jit(solution)/shard_map/all_to_all | solution.py:305
  39.0 0.0 copy-done.1
  39.0 2.7 %collective-permute-start = (bf16[512,512]{1,0:T(8,128)(2,1)S(1)}, bf16[512,512]{1,0:T(8,128)(2,1)S(1)}, u32[]{:S(2)}, u32[]{:S(2)}) collective-permute-start(bf16[512,512]{1,0:T(8,128)(2,1)S(1)} %bitcast.25), channel_id=1, source_target_pairs={{0,4},{4,0},{1,5},{5,1},{2,6},{6,2},{3,7},{7,3},{8,12},{12,8},{9,1... | collective-permute-start | bytes 1572872 | tf_op jit(solution)/shard_map/ppermute | solution.py:283
  41.7 26.1 %all-to-all-done.1 = bf16[16,32,1152]{2,1,0:T(8,128)(2,1)S(1)} async-done(((bf16[16,32,1152]{2,1,0:T(8,128)(2,1)}), bf16[16,32,1152]{2,1,0:T(8,128)(2,1)S(1)}, u32[]{:S(2)}, u32[]{:S(2)}) %all-to-all-start.1) | async-done | bytes 1179680 | tf_op jit(solution)/shard_map/all_to_all | solution.py:305
  67.8 0.0 copy-start
  67.8 0.1 slice.10
  67.9 0.1 reshape.44
  68.0 0.1 mul.20
  68.1 0.1 mul.18
  68.2 0.1 mul.19
  68.3 0.0 collective-permute-done.other
  68.3 0.0 copy-start.2
  68.3 0.7 broadcast_in_dim.38
  68.9 0.0 copy-done
  68.9 0.1 copy-done.2
  69.1 10.4 %shard_map.120 = bf16[512,1024]{1,0:T(8,128)(2,1)} custom-call(bf16[512,1152]{1,0:T(8,128)(2,1)} %bitcast.22, bf16[512,512]{1,0:T(8,128)(2,1)} %bitcast.26, bf16[512,512]{1,0:T(8,128)(2,1)} %copy-done.2, f32[64,128]{1,0:T(8,128)} %bitcast.27), custom_call_target="tpu_custom_call" | custom-call | flops 268435456 | bytes 3309568 | tf_op jit(solution)/shard_map/pallas_call | solution.py:220
  79.5 20.5 %all_to_all.15 = bf16[16,32,1024]{2,1,0:T(8,128)(2,1)} all-to-all(bf16[16,32,1024]{2,1,0:T(8,128)(2,1)} %bitcast.23), channel_id=1, replica_groups=mesh['tile'=4,'half'=2,'rest'=4] {'tile','rest'}, dimensions={0} | all-to-all | bytes 2097152 | tf_op jit(solution)/shard_map/all_to_all | solution.py:329
  100.0 4.5 %shard_map.121 = bf16[512,1024]{1,0:T(8,128)(2,1)} custom-call(bf16[512,1024]{1,0:T(8,128)(2,1)} %bitcast.24, bf16[512,1024]{1,0:T(8,128)(2,1)} %get-tuple-element.14.mid, bf16[1024,1024]{1,0:T(8,128)(2,1)} %wo.1), custom_call_target="tpu_custom_call" | custom-call | flops 1073741824 | bytes 5242880 | tf_op jit(solution)/shard_map/pallas_call | solution.py:220
  (6 shorter events, 0.0 us)
Async XLA Ops:
  0.0 20.0 %copy-start.3 = (s32[1,4]{1,0:T(1,128)S(1)}, s32[1,4]{1,0:T(1,128)}, u32[]{:S(2)}) copy-start(s32[1,4]{1,0:T(1,128)} %param.22) | copy-start | bytes 52
  0.0 20.0 %copy-start.4 = (s32[1,4]{1,0:T(1,128)S(1)}, s32[1,4]{1,0:T(1,128)}, u32[]{:S(2)}) copy-start(s32[1,4]{1,0:T(1,128)} %param.21) | copy-start | bytes 52
  0.0 20.1 %copy-start.5 = (s32[1,32]{1,0:T(1,128)S(1)}, s32[1,32]{1,0:T(1,128)}, u32[]{:S(2)}) copy-start(s32[1,32]{1,0:T(1,128)} %param.23) | copy-start | bytes 388
  13.7 16.9 %all-to-all-start = ((bf16[16,32,512]{2,1,0:T(8,128)(2,1)}), bf16[16,32,512]{2,1,0:T(8,128)(2,1)S(1)}, u32[]{:S(2)}, u32[]{:S(2)}) async-start(bf16[16,32,512]{2,1,0:T(8,128)(2,1)} %get-tuple-element.11), calls=%async_computation | async-start | bytes 1048576 | tf_op jit(solution)/shard_map/all_to_all | solution.py:280
  30.5 8.5 %copy-start.1 = (bf16[16,32,512]{2,1,0:T(8,128)(2,1)}, bf16[16,32,512]{2,1,0:T(8,128)(2,1)S(1)}, u32[]{:S(2)}) copy-start(bf16[16,32,512]{2,1,0:T(8,128)(2,1)S(1)} %all-to-all-done) | copy-start | bytes 1572868
  35.3 32.5 %all-to-all-start.1 = ((bf16[16,32,1152]{2,1,0:T(8,128)(2,1)}), bf16[16,32,1152]{2,1,0:T(8,128)(2,1)S(1)}, u32[]{:S(2)}, u32[]{:S(2)}) async-start(bf16[16,32,1152]{2,1,0:T(8,128)(2,1)} %shard_map.119), calls=%async_computation.1 | async-start | bytes 2359296 | tf_op jit(solution)/shard_map/all_to_all | solution.py:305
  39.0 29.3 %collective-permute-start = (bf16[512,512]{1,0:T(8,128)(2,1)S(1)}, bf16[512,512]{1,0:T(8,128)(2,1)S(1)}, u32[]{:S(2)}, u32[]{:S(2)}) collective-permute-start(bf16[512,512]{1,0:T(8,128)(2,1)S(1)} %bitcast.25), channel_id=1, source_target_pairs={{0,4},{4,0},{1,5},{5,1},{2,6},{6,2},{3,7},{7,3},{8,12},{12,8},{9,1... | collective-permute-start | bytes 1572872 | tf_op jit(solution)/shard_map/ppermute | solution.py:283
  67.8 1.1 %copy-start = (bf16[16,32,1152]{2,1,0:T(8,128)(2,1)}, bf16[16,32,1152]{2,1,0:T(8,128)(2,1)S(1)}, u32[]{:S(2)}) copy-start(bf16[16,32,1152]{2,1,0:T(8,128)(2,1)S(1)} %all-to-all-done.1) | copy-start | bytes 3538948
  68.3 0.8 copy-start.2

commit v2 on v1

--- a/solution.py
+++ b/solution.py
@@ -1,4 +1,5 @@
 import functools
+import math
 
 import jax
 import jax.numpy as jnp
@@ -15,11 +16,12 @@
 KEYS = KV_HEADS * HEAD_DIM
 WIDE = GROUPS * HEAD_DIM
 SCALE = HEAD_DIM ** (-0.5)
+EXP2_SCALE = SCALE * math.log2(math.e)
 NEG = -1e30
 LANES = 128
 COLS = 256
 HALVES = 2
-VMEM_BYTES = 56 * 1024 * 1024
+MIB = 1024 * 1024
 F32 = jnp.float32
 BF16 = jnp.bfloat16
 ROWS_BY_COLS = (((1,), (1,)), ((), ()))
@@ -69,42 +71,30 @@
         keyval[:, c : c + COLS] = jnp.dot(
             normed[...], wkv[:, c : c + COLS], preferred_element_type=F32
         ).astype(BF16)
-    lane_head = lax.broadcasted_iota(jnp.int32, (steps, WIDE), 1) // HEAD_DIM
-    causal = lax.broadcasted_iota(jnp.int32, (steps, steps), 0) >= lax.broadcasted_iota(
+    causal = lax.broadcasted_iota(jnp.int32, (steps, steps), 0) <= lax.broadcasted_iota(
         jnp.int32, (steps, steps), 1
     )
-
-    def spread(part):
-        repeated = jnp.concatenate([part] * GROUPS, axis=1)
-        zero = jnp.zeros_like(repeated)
-        return jnp.concatenate(
-            [jnp.where(lane_head == j, repeated, zero) for j in range(GROUPS)], axis=0
-        )
-
-    def one_agent(a, carry):
-        part = pl.ds(pl.multiple_of(a * steps, steps), steps)
+    causal = jnp.concatenate([causal] * GROUPS, axis=1)
+    for a in range(agents):
+        part = slice(a * steps, (a + 1) * steps)
         for k in range(KV_HEADS):
             wide = slice(k * WIDE, (k + 1) * WIDE)
-            keys = spread(keyval[part, k * HEAD_DIM : (k + 1) * HEAD_DIM])
-            vals = spread(keyval[part, KEYS + k * HEAD_DIM : KEYS + (k + 1) * HEAD_DIM])
-            scores = lax.dot_general(
-                query[part, wide], keys, ROWS_BY_COLS, preferred_element_type=F32
-            )
-            expd, sums = [], []
-            for j in range(GROUPS):
-                head = jnp.where(causal, scores[:, j * steps : (j + 1) * steps] * SCALE, NEG)
-                top = jnp.max(head, axis=-1, keepdims=True)
-                grown = jnp.exp(head - top)
-                sums.append(jnp.sum(grown, axis=-1, keepdims=True))
-                expd.append(grown.astype(BF16))
-            mixed = jnp.dot(jnp.concatenate(expd, axis=1), vals, preferred_element_type=F32)
-            inverse = jnp.concatenate(
-                [jnp.broadcast_to(1.0 / s, (steps, HEAD_DIM)) for s in sums], axis=1
-            )
-            mix[part, wide] = (mixed * inverse).astype(BF16)
-        return carry
-
-    lax.fori_loop(0, agents, one_agent, 0)
+            keys = keyval[part, k * HEAD_DIM : (k + 1) * HEAD_DIM]
+            vals = keyval[part, KEYS + k * HEAD_DIM : KEYS + (k + 1) * HEAD_DIM]
+            heads = query[part, wide].T
+            heads = jnp.concatenate(
+                [heads[j * HEAD_DIM : (j + 1) * HEAD_DIM] for j in range(GROUPS)], axis=1
+            )
+            scores = jnp.dot(keys, heads, preferred_element_type=F32)
+            scores = jnp.where(causal, scores, NEG)
+            top = jnp.max(scores, axis=0, keepdims=True)
+            grown = jnp.exp2((scores - top) * EXP2_SCALE)
+            sums = jnp.sum(grown, axis=0, keepdims=True)
+            mixed = jnp.dot(vals.T, grown.astype(BF16), preferred_element_type=F32) * (1.0 / sums)
+            mixed = jnp.concatenate(
+                [mixed[:, j * steps : (j + 1) * steps] for j in range(GROUPS)], axis=0
+            )
+            mix[part, wide] = mixed.astype(BF16).T
     loads[2].wait()
     for c in range(0, width, COLS):
         cols = slice(c, c + COLS)
@@ -146,12 +136,34 @@
     return jnp.where(col == wanted, 1.0, 0.0).astype(dtype)
 
 
+def key_weights(notes, local, tiles, total):
+    rows = notes.shape[0]
+    group = total // tiles
+    shape = (total, rows)
+    row, col = (lax.broadcasted_iota(jnp.int32, shape, d) for d in range(2))
+    pick = jnp.where(col == row * local, 1.0, 0.0).astype(BF16)
+    lines = jnp.dot(pick, notes, preferred_element_type=F32).astype(BF16)
+    shape = (LANES, HALVES * total)
+    lane, key = (lax.broadcasted_iota(jnp.int32, shape, d) for d in range(2))
+    half, tile, agent = key // total, key % total // group, key % group
+    spread = jnp.where(lane == HALVES * group + tile, 1.0, 0.0).astype(BF16)
+    listed = jnp.dot(lines, spread, preferred_element_type=F32)
+    spread = jnp.where(lane == half * group + agent, 1.0, 0.0).astype(BF16)
+    alive = jnp.dot(lines, spread, preferred_element_type=F32)
+    shape = (total, HALVES * total)
+    row, key = (lax.broadcasted_iota(jnp.int32, shape, d) for d in range(2))
+    first = row == key % total // group * group
+    alive = jnp.sum(jnp.where(first, alive, 0.0), axis=0, keepdims=True)
+    return listed * alive
+
+
 def space_kernel(
-    local, block, q_in, own, other, weight, out, query, keyval, mix
+    local, block, tiles, q_in, own, other, out, query, keyval, mix
 ):
     rows, width = out.shape
     group = block // local
     total = rows // local
+    weight = key_weights(q_in[:, width:], local, tiles, total)
     if local > 1:
         order = one_hot((block, block), group, local)
 
@@ -171,7 +183,7 @@
         by_steps(other, keyval, total, slice(c, c + COLS))
 
     def one_step(s, carry):
-        mask = jnp.concatenate([weight[...]] * GROUPS, axis=0)
+        mask = jnp.concatenate([weight] * GROUPS, axis=0)
         for k in range(KV_HEADS):
             wide = slice(k * WIDE, (k + 1) * WIDE)
             heads = query[s, :, wide]
@@ -181,9 +193,9 @@
             keys = keyval[s, :, k * HEAD_DIM : (k + 1) * HEAD_DIM]
             vals = keyval[s, :, KEYS + k * HEAD_DIM : KEYS + (k + 1) * HEAD_DIM]
             scores = lax.dot_general(heads, keys, ROWS_BY_COLS, preferred_element_type=F32)
-            scores = jnp.where(mask > 0, scores * SCALE, NEG)
+            scores = jnp.where(mask > 0, scores, NEG)
             top = jnp.max(scores, axis=-1, keepdims=True)
-            grown = jnp.exp(scores - top) * mask
+            grown = jnp.exp2((scores - top) * EXP2_SCALE) * mask
             sums = jnp.sum(grown, axis=-1, keepdims=True)
             mixed = jnp.dot(grown.astype(BF16), vals, preferred_element_type=F32) / sums
             mixed = mixed.astype(BF16)
@@ -192,7 +204,7 @@
             )
         return carry
 
-    lax.fori_loop(0, local, one_step, 0)
+    lax.fori_loop(0, local, one_step, 0, unroll=2 if local % 2 == 0 else 1)
     for b in range(rows // block):
         for c in range(0, width, COLS):
             cols = slice(c, c + COLS)
@@ -214,7 +226,7 @@
         out[:, cols] = (mid[:, cols].astype(F32) + projected).astype(BF16)
 
 
-def call(kernel, shapes, args, hbm=(), scratch=(), flops=0):
+def call(kernel, shapes, args, hbm=(), scratch=(), flops=0, mib=16):
     moved = sum(a.size * a.dtype.itemsize for a in args)
     moved += sum(s.size * s.dtype.itemsize for s in shapes)
     return pl.pallas_call(
@@ -227,7 +239,7 @@
         if len(shapes) > 1
         else pl.BlockSpec(memory_space=pltpu.VMEM),
         scratch_shapes=list(scratch),
-        compiler_params=pltpu.CompilerParams(vmem_limit_bytes=VMEM_BYTES),
+        compiler_params=pltpu.CompilerParams(vmem_limit_bytes=mib * MIB),
         cost_estimate=pl.CostEstimate(flops=flops, bytes_accessed=moved, transcendentals=0),
     )(*args)
 
@@ -274,25 +286,23 @@
             pltpu.SemaphoreType.DMA((4,)),
         ],
         flops=2 * rows * width * (2 * width + 4 * KEYS),
+        mib=24,
     )
     if not blocked:
         kv = to_blocks(kv, agents, steps, local)
-    own = lax.all_to_all(kv, spread, split_axis=0, concat_axis=0, tiled=True)
-    own = own.reshape(rows, 2 * KEYS)
-    swap = [(h, HALVES - 1 - h) for h in range(HALVES)]
-    other = lax.ppermute(own, "half", swap)
-
     listed = jnp.sum(
         jnp.where(
             neighbours[0][:, None] == jnp.arange(tiles)[None, :], nbr_valid[0][:, None], 0
         ),
         axis=0,
     )
-    alive = agent_valid[0]
+    group = rest * agents
+    alive = jnp.where(lax.axis_index("half") == 0, agent_valid[0], jnp.roll(agent_valid[0], -group))
     meta = jnp.concatenate([alive, listed])
     meta = jnp.pad(meta, (0, LANES - meta.shape[0])).astype(F32)
     meta = jnp.broadcast_to(meta[None], (8, LANES))
-    second, own = lax.optimization_barrier((second, own))
+    own = lax.all_to_all(kv, spread, split_axis=0, concat_axis=0, tiled=True)
+    own = own.reshape(rows, 2 * KEYS)
     q_shape = (parts, agents * local, width + LANES) if blocked else (rows, width + LANES)
     q = call(
         functools.partial(query_kernel, agents, steps, local, blocked),
@@ -302,29 +312,23 @@
     )
     if not blocked:
         q = to_blocks(q, agents, steps, local)
+    q, own = lax.optimization_barrier((q, own))
+    swap = [(h, HALVES - 1 - h) for h in range(HALVES)]
+    other = lax.ppermute(own, "half", swap)
     q = lax.all_to_all(q, spread, split_axis=0, concat_axis=0, tiled=True)
-
-    lines = q.reshape(tiles, rest, agents * local, width + LANES)[:, 0, 0, width:].astype(F32)
-    group = rest * agents
-    half = lax.axis_index("half")
-    alive_all = lines[:, : HALVES * group].reshape(tiles, HALVES, group)
-    alive_own = lax.dynamic_index_in_dim(alive_all, half, 1, keepdims=False)
-    alive_other = lax.dynamic_index_in_dim(alive_all, 1 - half, 1, keepdims=False)
-    listed_all = lines[:, HALVES * group : HALVES * group + tiles]
-    weight = listed_all[:, None, :, None] * jnp.stack([alive_own, alive_other])[None]
-    weight = jnp.repeat(weight.reshape(tiles, -1), group, axis=0)
 
     block = max(COLS, local) if rows % max(COLS, local) == 0 else rows
     mix = call(
-        functools.partial(space_kernel, local, block),
+        functools.partial(space_kernel, local, block, tiles),
         [struct((rows, width), BF16)],
-        [q.reshape(rows, width + LANES), own, other, weight],
+        [q.reshape(rows, width + LANES), own, other],
         scratch=[
             pltpu.VMEM((local, rows // local, width), BF16),
             pltpu.VMEM((local, HALVES * rows // local, 2 * KEYS), BF16),
             pltpu.VMEM((local, rows // local, width), BF16),
         ],
         flops=8 * rows * rows // local * width,
+        mib=16 + 16 * GROUPS * HALVES * (rows // local) ** 2 // MIB,
     )
     mix = lax.all_to_all(
         mix.reshape(parts, agents * local, width), spread, split_axis=0, concat_axis=0, tiled=True

time: 105 us -> 98.7 us (0.940)
  Pallas kernels: 32.7 us -> 20.9 us
  local copies, waits for them, and re-layouts: 1.85 us -> 11.5 us
  waiting for transfers between devices: 36.5 us -> 32.8 us
    all_to_all x1, waiting for transfers between devices: 26.1 us -> 3.12 us  [per_device(): q = lax.all_to_all(q, spread, split_axis=0, concat_axis=0, tiled=True)]
    ppermute x1, waiting for transfers between devices: 0.01 us -> 23 us  [per_device(): other = lax.ppermute(own, 'half', swap)]
    pallas_call x4, Pallas kernels: 32.7 us -> 20.9 us  [call(): pl.pallas_call(kernel, out_shape=shapes if len(shapes) > 1 else shapes[0]...]
    unnamed x12 -> x32, local copies, waits for them, and re-layouts: 0.16 us -> 11.4 us
    all_to_all x1, waiting for transfers between devices: 10.4 us -> 6.66 us  [per_device(): own = lax.all_to_all(kv, spread, split_axis=0, concat_axis=0, tiled=True)]
  transfers between devices with their start and end apart: 3 -> 3, of which waited for: 2 -> 3; matrix products, arithmetic and copies ran while one was open for 1% -> 0% of each run, Pallas kernels for 0% -> 2%
where the time goes in v2:
time: 98.7 us; the launch traced here: 98.1 us
  waiting for transfers between devices  32.8 us (33%)
  Pallas kernels  20.9 us (21%)
  blocking collectives  20 us (20%)
  starting transfers between devices  12.6 us (13%)
  local copies, waits for them, and re-layouts  11.5 us (12%)
    ppermute x1, waiting for transfers between devices, per_device(): other = lax.ppermute(own, 'half', swap)  23 us
    pallas_call x4, Pallas kernels, call(): pl.pallas_call(kernel, out_shape=shapes if len(shapes) > 1 else shapes[0]...  20.9 us
    all_to_all x1, blocking collectives, per_device(): lax.all_to_all(mix.reshape(parts, agents * local, width), spread, split_a...  20 us
    unnamed x32, local copies, waits for them, and re-layouts  11.4 us
    all_to_all x1, waiting for transfers between devices, per_device(): own = lax.all_to_all(kv, spread, split_axis=0, concat_axis=0, tiled=True)  6.66 us
    all_to_all x1, starting transfers between devices, per_device(): own = lax.all_to_all(kv, spread, split_axis=0, concat_axis=0, tiled=True)  6.29 us
    all_to_all x1, starting transfers between devices, per_device(): q = lax.all_to_all(q, spread, split_axis=0, concat_axis=0, tiled=True)  3.7 us
    all_to_all x1, waiting for transfers between devices, per_device(): q = lax.all_to_all(q, spread, split_axis=0, concat_axis=0, tiled=True)  3.12 us
  transfers between devices with their start and end apart: 3, of which 3 were waited for; matrix products, arithmetic and copies ran while one was open for 0% of the time, Pallas kernels for 2%

profile of v2, /device:TPU:0, one launch (start us, length us, event | category | flops | bytes accessed | tf_op | source)
XLA Modules:
  0.0 98.1 jit_solution(15416237156712579708)
XLA Ops:
  0.0 0.0 copy-start.6
  0.0 1.6 %copy-done.6 = bf16[1024,1024]{1,0:T(8,128)(2,1)S(1)} copy-done((bf16[1024,1024]{1,0:T(8,128)(2,1)S(1)}, bf16[1024,1024]{1,0:T(8,128)(2,1)}, u32[]{:S(2)}) %copy-start.6) | copy-done | bytes 2097176
  1.6 0.0 copy-start.7
  1.6 1.6 %copy-done.7 = bf16[1024,1024]{1,0:T(8,128)(2,1)S(1)} copy-done((bf16[1024,1024]{1,0:T(8,128)(2,1)S(1)}, bf16[1024,1024]{1,0:T(8,128)(2,1)}, u32[]{:S(2)}) %copy-start.7) | copy-done | bytes 2097176
  3.2 0.0 copy-start.8
  3.2 1.2 %copy-done.8 = bf16[1,4,128,1024]{3,2,1,0:T(8,128)(2,1)S(1)} copy-done((bf16[1,4,128,1024]{3,2,1,0:T(8,128)(2,1)S(1)}, bf16[1,4,128,1024]{3,2,1,0:T(8,128)(2,1)}, u32[]{:S(2)}) %copy-start.8) | copy-done | bytes 1048600
  4.4 0.0 copy-start.9
  4.4 1.2 %copy-done.9 = bf16[1024,512]{1,0:T(8,128)(2,1)S(1)} copy-done((bf16[1024,512]{1,0:T(8,128)(2,1)S(1)}, bf16[1024,512]{1,0:T(8,128)(2,1)}, u32[]{:S(2)}) %copy-start.9) | copy-done | bytes 1048600
  5.6 0.0 copy-start.10
  5.6 1.2 %copy-done.10 = bf16[1024,512]{1,0:T(8,128)(2,1)S(1)} copy-done((bf16[1024,512]{1,0:T(8,128)(2,1)S(1)}, bf16[1024,512]{1,0:T(8,128)(2,1)}, u32[]{:S(2)}) %copy-start.10) | copy-done | bytes 1048600
  6.9 0.0 copy-start.11
  6.9 0.7 copy-done.11
  7.5 0.0 copy-start.12
  7.5 0.7 copy-done.12
  8.2 0.0 copy-start.14
  8.2 0.0 copy-start.15
  8.2 0.0 copy-start.13
  8.2 0.0 copy-start
  8.2 9.7 %shard_map.118 = (bf16[512,1024]{1,0:T(8,128)(2,1)S(1)}, bf16[512,1024]{1,0:T(8,128)(2,1)S(1)}, bf16[16,32,512]{2,1,0:T(8,128)(2,1)}) custom-call(bf16[512,1024]{1,0:T(8,128)(2,1)S(1)} %bitcast.21, f32[1,1024]{1,0:T(1,128)S(1)} %bitcast.22, f32[1,1024]{1,0:T(1,128)S(1)} %bitcast.23, bf16[1024,1024]{1,0:T(8,128)(2,1)S(1)} %copy-done.6, ...), custom_call_target="tpu_custom_call" | custom-call | flops 3221225472 | bytes 9969664 | tf_op jit(solution)/shard_map/pallas_call | solution.py:232
  18.0 0.0 copy-start.2
  18.0 0.9 copy-done.2
  18.9 0.0 copy-start.4
  18.9 1.0 copy-done.4
  19.9 6.3 %all-to-all-start = ((bf16[16,32,512]{2,1,0:T(8,128)(2,1)}), bf16[16,32,512]{2,1,0:T(8,128)(2,1)S(1)}, u32[]{:S(2)}, u32[]{:S(2)}) async-start(bf16[16,32,512]{2,1,0:T(8,128)(2,1)} %get-tuple-element.11), calls=%async_computation | async-start | bytes 1048576 | tf_op jit(solution)/shard_map/all_to_all | solution.py:304
  26.2 0.0 copy-done.14
  26.2 0.0 copy-done.15
  26.2 0.1 select_reduce_fusion
  26.3 0.0 copy-done.13
  26.3 0.1 slice_bitcast_fusion.1
  26.4 0.1 broadcast_select_fusion
  26.5 0.1 pad_add_fusion
  26.5 0.0 copy-done
  26.6 0.0 copy-start.5
  26.6 1.2 %copy-done.5 = bf16[512,1024]{1,0:T(8,128)(2,1)S(1)} copy-done((bf16[512,1024]{1,0:T(8,128)(2,1)S(1)}, bf16[512,1024]{1,0:T(8,128)(2,1)}, u32[]{:S(2)}) %copy-start.5) | copy-done | bytes 1048600
  27.8 2.3 %shard_map.119 = bf16[16,32,1152]{2,1,0:T(8,128)(2,1)} custom-call(bf16[512,1024]{1,0:T(8,128)(2,1)S(1)} %copy-done.5, bf16[1024,1024]{1,0:T(8,128)(2,1)S(1)} %copy-done, f32[8,128]{1,0:T(8,128)S(1)} %broadcast_in_dim.32.meta), custom_call_target="tpu_custom_call" | custom-call | flops 1073741824 | bytes 4329472 | tf_op jit(solution)/shard_map/pallas_call | solution.py:232
  30.1 6.7 %all-to-all-done = bf16[16,32,512]{2,1,0:T(8,128)(2,1)S(1)} async-done(((bf16[16,32,512]{2,1,0:T(8,128)(2,1)}), bf16[16,32,512]{2,1,0:T(8,128)(2,1)S(1)}, u32[]{:S(2)}, u32[]{:S(2)}) %all-to-all-start) | async-done | bytes 524320 | tf_op jit(solution)/shard_map/all_to_all | solution.py:304
  36.7 3.7 %all-to-all-start.1 = ((bf16[16,32,1152]{2,1,0:T(8,128)(2,1)}), bf16[16,32,1152]{2,1,0:T(8,128)(2,1)S(1)}, u32[]{:S(2)}, u32[]{:S(2)}) async-start(bf16[16,32,1152]{2,1,0:T(8,128)(2,1)} %shard_map.119), calls=%async_computation.1 | async-start | bytes 2359296 | tf_op jit(solution)/shard_map/all_to_all | solution.py:318
  40.4 2.6 %collective-permute-start = (bf16[512,512]{1,0:T(8,128)(2,1)S(1)}, bf16[512,512]{1,0:T(8,128)(2,1)S(1)}, u32[]{:S(2)}, u32[]{:S(2)}) collective-permute-start(bf16[512,512]{1,0:T(8,128)(2,1)S(1)} %bitcast.19), channel_id=1, source_target_pairs={{0,4},{4,0},{1,5},{5,1},{2,6},{6,2},{3,7},{7,3},{8,12},{12,8},{9,1... | collective-permute-start | bytes 1572872 | tf_op jit(solution)/shard_map/ppermute | solution.py:317
  43.1 23.0 %collective-permute-done.other = bf16[512,512]{1,0:T(8,128)(2,1)S(1)} collective-permute-done((bf16[512,512]{1,0:T(8,128)(2,1)S(1)}, bf16[512,512]{1,0:T(8,128)(2,1)S(1)}, u32[]{:S(2)}, u32[]{:S(2)}) %collective-permute-start) | collective-permute-done | bytes 524320 | tf_op jit(solution)/shard_map/ppermute | solution.py:317
  66.1 3.1 %all-to-all-done.1 = bf16[16,32,1152]{2,1,0:T(8,128)(2,1)S(1)} async-done(((bf16[16,32,1152]{2,1,0:T(8,128)(2,1)}), bf16[16,32,1152]{2,1,0:T(8,128)(2,1)S(1)}, u32[]{:S(2)}, u32[]{:S(2)}) %all-to-all-start.1) | async-done | bytes 1179680 | tf_op jit(solution)/shard_map/all_to_all | solution.py:318
  69.2 0.0 copy-start.1
  69.2 0.0 copy-start.3
  69.2 6.7 %shard_map.120 = bf16[512,1024]{1,0:T(8,128)(2,1)S(1)} custom-call(bf16[512,1152]{1,0:T(8,128)(2,1)S(1)} %bitcast.16, bf16[512,512]{1,0:T(8,128)(2,1)S(1)} %bitcast.20, bf16[512,512]{1,0:T(8,128)(2,1)S(1)} %collective-permute-done.other), custom_call_target="tpu_custom_call" | custom-call | flops 268435456 | bytes 3276800 | tf_op jit(solution)/shard_map/pallas_call | solution.py:232
  75.9 20.0 %all_to_all.15 = bf16[16,32,1024]{2,1,0:T(8,128)(2,1)S(1)} all-to-all(bf16[16,32,1024]{2,1,0:T(8,128)(2,1)S(1)} %bitcast.17), channel_id=1, replica_groups=mesh['tile'=4,'half'=2,'rest'=4] {'tile','rest'}, dimensions={0} | all-to-all | bytes 2097152 | tf_op jit(solution)/shard_map/all_to_all | solution.py:333
  95.9 0.0 copy-done.1
  95.9 0.0 copy-done.3
  95.9 2.2 %shard_map.121 = bf16[512,1024]{1,0:T(8,128)(2,1)} custom-call(bf16[512,1024]{1,0:T(8,128)(2,1)S(1)} %bitcast.18, bf16[512,1024]{1,0:T(8,128)(2,1)S(1)} %copy-done.3, bf16[1024,1024]{1,0:T(8,128)(2,1)S(1)} %copy-done.1), custom_call_target="tpu_custom_call" | custom-call | flops 1073741824 | bytes 5242880 | tf_op jit(solution)/shard_map/pallas_call | solution.py:232
  (2 shorter events, 0.0 us)
Async XLA Ops:
  0.0 1.6 %copy-start.6 = (bf16[1024,1024]{1,0:T(8,128)(2,1)S(1)}, bf16[1024,1024]{1,0:T(8,128)(2,1)}, u32[]{:S(2)}) copy-start(bf16[1024,1024]{1,0:T(8,128)(2,1)} %wq_hbm.1) | copy-start | bytes 6291460
  1.6 1.6 %copy-start.7 = (bf16[1024,1024]{1,0:T(8,128)(2,1)S(1)}, bf16[1024,1024]{1,0:T(8,128)(2,1)}, u32[]{:S(2)}) copy-start(bf16[1024,1024]{1,0:T(8,128)(2,1)} %wo_hbm.1) | copy-start | bytes 6291460
  3.2 1.2 %copy-start.8 = (bf16[1,4,128,1024]{3,2,1,0:T(8,128)(2,1)S(1)}, bf16[1,4,128,1024]{3,2,1,0:T(8,128)(2,1)}, u32[]{:S(2)}) copy-start(bf16[1,4,128,1024]{3,2,1,0:T(8,128)(2,1)} %param.12) | copy-start | bytes 3145732
  4.4 1.2 %copy-start.9 = (bf16[1024,512]{1,0:T(8,128)(2,1)S(1)}, bf16[1024,512]{1,0:T(8,128)(2,1)}, u32[]{:S(2)}) copy-start(bf16[1024,512]{1,0:T(8,128)(2,1)} %wkv_hbm.1) | copy-start | bytes 3145732
  5.6 1.2 %copy-start.10 = (bf16[1024,512]{1,0:T(8,128)(2,1)S(1)}, bf16[1024,512]{1,0:T(8,128)(2,1)}, u32[]{:S(2)}) copy-start(bf16[1024,512]{1,0:T(8,128)(2,1)} %wkv2_hbm.1) | copy-start | bytes 3145732
  6.9 0.7 copy-start.11
  7.5 0.7 copy-start.12
  8.2 18.0 %copy-start.14 = (s32[1,4]{1,0:T(1,128)S(1)}, s32[1,4]{1,0:T(1,128)}, u32[]{:S(2)}) copy-start(s32[1,4]{1,0:T(1,128)} %param.22) | copy-start | bytes 52
  8.2 18.0 %copy-start.15 = (s32[1,4]{1,0:T(1,128)S(1)}, s32[1,4]{1,0:T(1,128)}, u32[]{:S(2)}) copy-start(s32[1,4]{1,0:T(1,128)} %param.21) | copy-start | bytes 52
  8.2 18.1 %copy-start.13 = (s32[1,32]{1,0:T(1,128)S(1)}, s32[1,32]{1,0:T(1,128)}, u32[]{:S(2)}) copy-start(s32[1,32]{1,0:T(1,128)} %param.23) | copy-start | bytes 388
  8.2 18.3 %copy-start = (bf16[1024,1024]{1,0:T(8,128)(2,1)S(1)}, bf16[1024,1024]{1,0:T(8,128)(2,1)}, u32[]{:S(2)}) copy-start(bf16[1024,1024]{1,0:T(8,128)(2,1)} %wq.1) | copy-start | bytes 6291460
  18.0 1.0 copy-start.2
  18.9 1.0 copy-start.4
  19.9 16.9 %all-to-all-start = ((bf16[16,32,512]{2,1,0:T(8,128)(2,1)}), bf16[16,32,512]{2,1,0:T(8,128)(2,1)S(1)}, u32[]{:S(2)}, u32[]{:S(2)}) async-start(bf16[16,32,512]{2,1,0:T(8,128)(2,1)} %get-tuple-element.11), calls=%async_computation | async-start | bytes 1048576 | tf_op jit(solution)/shard_map/all_to_all | solution.py:304
  26.6 1.2 %copy-start.5 = (bf16[512,1024]{1,0:T(8,128)(2,1)S(1)}, bf16[512,1024]{1,0:T(8,128)(2,1)}, u32[]{:S(2)}) copy-start(bf16[512,1024]{1,0:T(8,128)(2,1)} %copy-done.4) | copy-start | bytes 3145732
  36.7 32.5 %all-to-all-start.1 = ((bf16[16,32,1152]{2,1,0:T(8,128)(2,1)}), bf16[16,32,1152]{2,1,0:T(8,128)(2,1)S(1)}, u32[]{:S(2)}, u32[]{:S(2)}) async-start(bf16[16,32,1152]{2,1,0:T(8,128)(2,1)} %shard_map.119), calls=%async_computation.1 | async-start | bytes 2359296 | tf_op jit(solution)/shard_map/all_to_all | solution.py:318
  40.4 25.6 %collective-permute-start = (bf16[512,512]{1,0:T(8,128)(2,1)S(1)}, bf16[512,512]{1,0:T(8,128)(2,1)S(1)}, u32[]{:S(2)}, u32[]{:S(2)}) collective-permute-start(bf16[512,512]{1,0:T(8,128)(2,1)S(1)} %bitcast.19), channel_id=1, source_target_pairs={{0,4},{4,0},{1,5},{5,1},{2,6},{6,2},{3,7},{7,3},{8,12},{12,8},{9,1... | collective-permute-start | bytes 1572872 | tf_op jit(solution)/shard_map/ppermute | solution.py:317
  69.2 26.7 %copy-start.1 = (bf16[1024,1024]{1,0:T(8,128)(2,1)S(1)}, bf16[1024,1024]{1,0:T(8,128)(2,1)}, u32[]{:S(2)}) copy-start(bf16[1024,1024]{1,0:T(8,128)(2,1)} %wo.1) | copy-start | bytes 6291460
  69.2 26.7 %copy-start.3 = (bf16[512,1024]{1,0:T(8,128)(2,1)S(1)}, bf16[512,1024]{1,0:T(8,128)(2,1)}, u32[]{:S(2)}) copy-start(bf16[512,1024]{1,0:T(8,128)(2,1)} %copy-done.2) | copy-start | bytes 3145732

commit v3 on v2

--- a/solution.py
+++ b/solution.py
@@ -45,28 +45,38 @@
 
 def time_kernel(
     agents, steps, local, blocked,
-    hist, gain_t, gain_s, wq_hbm, wkv_hbm, wo_hbm, wkv2_hbm,
-    mid, second, kv_out,
-    wq, wkv, wo, wkv2, normed, query, keyval, mix, sems,
+    hist_hbm, gain_t, gain_s, wq_hbm, wkv_hbm, wo_hbm, wkv2_hbm,
+    mid_hbm, kv_out,
+    hist, wq, wkv, wo, wkv2, normed, query, keyval, mix, mid, hist_sems, wq_sems, sems, out_sem,
 ):
     rows, width = hist.shape
+    hist_loads, wq_loads = [], []
+    for a in range(agents):
+        part = pl.ds(a * steps, steps)
+        hist_loads.append(
+            pltpu.make_async_copy(hist_hbm.at[part, :], hist.at[part, :], hist_sems.at[a])
+        )
+    for c in range(0, width, COLS):
+        cols = pl.ds(c, COLS)
+        wq_loads.append(
+            pltpu.make_async_copy(wq_hbm.at[:, cols], wq.at[:, cols], wq_sems.at[c // COLS])
+        )
     loads = [
         pltpu.make_async_copy(source, target, sems.at[i])
-        for i, (source, target) in enumerate(
-            ((wq_hbm, wq), (wkv_hbm, wkv), (wo_hbm, wo), (wkv2_hbm, wkv2))
-        )
+        for i, (source, target) in enumerate(((wkv_hbm, wkv), (wo_hbm, wo), (wkv2_hbm, wkv2)))
     ]
-    for load in loads:
+    for load in hist_loads + wq_loads + loads:
         load.start()
     for a in range(agents):
         part = pl.ds(a * steps, steps)
+        hist_loads[a].wait()
         normed[part, :] = norm_rows(hist[part, :], gain_t[...])
-    loads[0].wait()
-    for c in range(0, width, COLS):
+    for c in range(0, width, COLS):
+        wq_loads[c // COLS].wait()
         query[:, c : c + COLS] = jnp.dot(
             normed[...], wq[:, c : c + COLS], preferred_element_type=F32
         ).astype(BF16)
-    loads[1].wait()
+    loads[0].wait()
     for c in range(0, 2 * KEYS, COLS):
         keyval[:, c : c + COLS] = jnp.dot(
             normed[...], wkv[:, c : c + COLS], preferred_element_type=F32
@@ -95,26 +105,32 @@
                 [mixed[:, j * steps : (j + 1) * steps] for j in range(GROUPS)], axis=0
             )
             mix[part, wide] = mixed.astype(BF16).T
-    loads[2].wait()
+    loads[1].wait()
     for c in range(0, width, COLS):
         cols = slice(c, c + COLS)
         projected = jnp.dot(mix[...], wo[:, cols], preferred_element_type=F32)
         mid[:, cols] = (hist[:, cols].astype(F32) + projected).astype(BF16)
+    keep = pltpu.make_async_copy(mid, mid_hbm, out_sem)
+    keep.start()
     for a in range(agents):
         part = pl.ds(a * steps, steps)
-        second[part, :] = norm_rows(mid[part, :], gain_s[...])
-    loads[3].wait()
+        normed[part, :] = norm_rows(mid[part, :], gain_s[...])
+    loads[2].wait()
     for c in range(0, 2 * KEYS, COLS):
         cols = slice(c, c + COLS)
-        result = jnp.dot(second[...], wkv2[:, cols], preferred_element_type=F32)
+        result = jnp.dot(normed[...], wkv2[:, cols], preferred_element_type=F32)
         if blocked:
             kv_out[:, :, cols] = to_blocks(result, agents, steps, local).astype(BF16)
         else:
             kv_out[:, cols] = result.astype(BF16)
-
-
-def query_kernel(agents, steps, local, blocked, second, wq, meta, out):
-    width = second.shape[1]
+    keep.wait()
+
+
+def query_kernel(agents, steps, local, blocked, mid, gain, wq, meta, out, second):
+    width = mid.shape[1]
+    for a in range(agents):
+        part = pl.ds(a * steps, steps)
+        second[part, :] = norm_rows(mid[part, :], gain[...])
     for c in range(0, width, COLS):
         cols = slice(c, c + COLS)
         result = jnp.dot(second[...], wq[:, cols], preferred_element_type=F32)
@@ -226,22 +242,25 @@
         out[:, cols] = (mid[:, cols].astype(F32) + projected).astype(BF16)
 
 
-def call(kernel, shapes, args, hbm=(), scratch=(), flops=0, mib=16):
+def call(kernel, shapes, args, hbm=(), hbm_out=(), scratch=(), flops=0, mib=16):
     moved = sum(a.size * a.dtype.itemsize for a in args)
     moved += sum(s.size * s.dtype.itemsize for s in shapes)
-    return pl.pallas_call(
+
+    def specs(count, far):
+        return [
+            pl.BlockSpec(memory_space=pl.ANY if i in far else pltpu.VMEM) for i in range(count)
+        ]
+
+    results = pl.pallas_call(
         kernel,
-        out_shape=shapes if len(shapes) > 1 else shapes[0],
-        in_specs=[
-            pl.BlockSpec(memory_space=pl.ANY if i in hbm else pltpu.VMEM) for i in range(len(args))
-        ],
-        out_specs=[pl.BlockSpec(memory_space=pltpu.VMEM)] * len(shapes)
-        if len(shapes) > 1
-        else pl.BlockSpec(memory_space=pltpu.VMEM),
+        out_shape=list(shapes),
+        in_specs=specs(len(args), hbm),
+        out_specs=specs(len(shapes), hbm_out),
         scratch_shapes=list(scratch),
         compiler_params=pltpu.CompilerParams(vmem_limit_bytes=mib * MIB),
         cost_estimate=pl.CostEstimate(flops=flops, bytes_accessed=moved, transcendentals=0),
     )(*args)
+    return results if len(shapes) > 1 else results[0]
 
 
 def per_device(
@@ -269,12 +288,14 @@
 
     hist = histories.reshape(rows, width)
     kv_shape = (parts, agents * local, 2 * KEYS) if blocked else (rows, 2 * KEYS)
-    mid, second, kv = call(
+    mid, kv = call(
         functools.partial(time_kernel, agents, steps, local, blocked),
-        [struct((rows, width), BF16), struct((rows, width), BF16), struct(kv_shape, BF16)],
+        [struct((rows, width), BF16), struct(kv_shape, BF16)],
         [hist, gain_time[None], gain_space[None], wq_time, wkv_time, wo_time, wkv_space],
-        hbm=(3, 4, 5, 6),
+        hbm=(0, 3, 4, 5, 6),
+        hbm_out=(0,),
         scratch=[
+            pltpu.VMEM((rows, width), BF16),
             pltpu.VMEM(wq_time.shape, BF16),
             pltpu.VMEM(wkv_time.shape, BF16),
             pltpu.VMEM(wo_time.shape, BF16),
@@ -283,10 +304,14 @@
             pltpu.VMEM((rows, width), BF16),
             pltpu.VMEM((rows, 2 * KEYS), BF16),
             pltpu.VMEM((rows, width), BF16),
-            pltpu.SemaphoreType.DMA((4,)),
+            pltpu.VMEM((rows, width), BF16),
+            pltpu.SemaphoreType.DMA((agents,)),
+            pltpu.SemaphoreType.DMA((width // COLS,)),
+            pltpu.SemaphoreType.DMA((3,)),
+            pltpu.SemaphoreType.DMA,
         ],
         flops=2 * rows * width * (2 * width + 4 * KEYS),
-        mib=24,
+        mib=56,
     )
     if not blocked:
         kv = to_blocks(kv, agents, steps, local)
@@ -307,12 +332,12 @@
     q = call(
         functools.partial(query_kernel, agents, steps, local, blocked),
         [struct(q_shape, BF16)],
-        [second, wq_space, meta],
+        [mid, gain_space[None], wq_space, meta],
+        scratch=[pltpu.VMEM((rows, width), BF16)],
         flops=2 * rows * width * width,
     )
     if not blocked:
         q = to_blocks(q, agents, steps, local)
-    q, own = lax.optimization_barrier((q, own))
     swap = [(h, HALVES - 1 - h) for h in range(HALVES)]
     other = lax.ppermute(own, "half", swap)
     q = lax.all_to_all(q, spread, split_axis=0, concat_axis=0, tiled=True)

time: 98.7 us -> 92.8 us (0.940)
  local copies, waits for them, and re-layouts: 11.5 us -> 2.91 us
  Pallas kernels: 20.9 us -> 25.5 us
  waiting for transfers between devices: 32.8 us -> 31 us
    unnamed x32 -> x16, local copies, waits for them, and re-layouts: 11.4 us -> 2.83 us
    pallas_call x4, Pallas kernels: 20.9 us -> 25.5 us  [call(): pl.pallas_call(kernel, out_shape=list(shapes), in_specs=specs(len(args),...]
    all_to_all x1, waiting for transfers between devices: 6.66 us -> 4.9 us  [per_device(): own = lax.all_to_all(kv, spread, split_axis=0, concat_axis=0, tiled=True)]
  transfers between devices with their start and end apart: 3 -> 3, of which waited for: 3 -> 3; matrix products, arithmetic and copies ran while one was open for 0% -> 0% of each run, Pallas kernels for 2% -> 3%
where the time goes in v3:
time: 92.8 us; the launch traced here: 92.3 us
  waiting for transfers between devices  31 us (33%)
  Pallas kernels  25.5 us (27%)
  blocking collectives  20 us (22%)
  starting transfers between devices  12.7 us (14%)
  local copies, waits for them, and re-layouts  2.91 us (3%)
    pallas_call x4, Pallas kernels, call(): pl.pallas_call(kernel, out_shape=list(shapes), in_specs=specs(len(args),...  25.5 us
    ppermute x1, waiting for transfers between devices, per_device(): other = lax.ppermute(own, 'half', swap)  23 us
    all_to_all x1, blocking collectives, per_device(): lax.all_to_all(mix.reshape(parts, agents * local, width), spread, split_a...  20 us
    all_to_all x1, starting transfers between devices, per_device(): own = lax.all_to_all(kv, spread, split_axis=0, concat_axis=0, tiled=True)  6.31 us
    all_to_all x1, waiting for transfers between devices, per_device(): own = lax.all_to_all(kv, spread, split_axis=0, concat_axis=0, tiled=True)  4.9 us
    all_to_all x1, starting transfers between devices, per_device(): q = lax.all_to_all(q, spread, split_axis=0, concat_axis=0, tiled=True)  3.7 us
    all_to_all x1, waiting for transfers between devices, per_device(): q = lax.all_to_all(q, spread, split_axis=0, concat_axis=0, tiled=True)  3.12 us
    unnamed x16, local copies, waits for them, and re-layouts  2.83 us
  transfers between devices with their start and end apart: 3, of which 3 were waited for; matrix products, arithmetic and copies ran while one was open for 0% of the time, Pallas kernels for 3%

profile of v3, /device:TPU:0, one launch (start us, length us, event | category | flops | bytes accessed | tf_op | source)
XLA Modules:
  0.0 92.3 jit_solution(3070366333410016189)
XLA Ops:
  0.0 0.0 copy-start.6
  0.0 0.0 copy-start.7
  0.0 0.0 copy-start.5
  0.0 0.0 copy-start.4
  0.0 14.1 %shard_map.118 = (bf16[512,1024]{1,0:T(8,128)(2,1)}, bf16[16,32,512]{2,1,0:T(8,128)(2,1)}) custom-call(bf16[512,1024]{1,0:T(8,128)(2,1)} %bitcast.23, f32[1,1024]{1,0:T(1,128)} %bitcast.24, f32[1,1024]{1,0:T(1,128)} %bitcast.21, bf16[1024,1024]{1,0:T(8,128)(2,1)} %wq_hbm.1, bf16[1024,512]{1,0:T(8,128)(2,1)} %wkv_hbm.1, bf16[1024,1024]{1,0:T(8,128)(2,1)} %wo_hbm.1, ...), custom_call_target="tpu_custom_call" | custom-call | flops 3221225472 | bytes 8921088 | tf_op jit(solution)/shard_map/pallas_call | solution.py:254
  14.1 6.3 %all-to-all-start.1 = ((bf16[16,32,512]{2,1,0:T(8,128)(2,1)}), bf16[16,32,512]{2,1,0:T(8,128)(2,1)S(1)}, u32[]{:S(2)}, u32[]{:S(2)}) async-start(bf16[16,32,512]{2,1,0:T(8,128)(2,1)} %get-tuple-element.8), calls=%async_computation.1 | async-start | bytes 1048576 | tf_op jit(solution)/shard_map/all_to_all | solution.py:329
  20.4 0.0 copy-done.6
  20.4 0.0 copy-done.7
  20.5 0.1 select_reduce_fusion
  20.5 0.0 copy-done.5
  20.5 0.1 slice_bitcast_fusion.1
  20.6 0.1 broadcast_select_fusion
  20.7 0.1 pad_add_fusion
  20.8 0.0 copy-done.4
  20.8 0.0 copy-start
  20.8 1.2 %copy-done = bf16[512,1024]{1,0:T(8,128)(2,1)S(1)} copy-done((bf16[512,1024]{1,0:T(8,128)(2,1)S(1)}, bf16[512,1024]{1,0:T(8,128)(2,1)}, u32[]{:S(2)}) %copy-start) | copy-done | bytes 1048600
  22.0 0.0 copy-start.2
  22.0 1.6 %copy-done.2 = bf16[1024,1024]{1,0:T(8,128)(2,1)S(1)} copy-done((bf16[1024,1024]{1,0:T(8,128)(2,1)S(1)}, bf16[1024,1024]{1,0:T(8,128)(2,1)}, u32[]{:S(2)}) %copy-start.2) | copy-done | bytes 2097176
  23.6 2.5 %shard_map.119 = bf16[16,32,1152]{2,1,0:T(8,128)(2,1)} custom-call(bf16[512,1024]{1,0:T(8,128)(2,1)S(1)} %copy-done, f32[1,1024]{1,0:T(1,128)S(1)} %bitcast.22, bf16[1024,1024]{1,0:T(8,128)(2,1)S(1)} %copy-done.2, f32[8,128]{1,0:T(8,128)S(1)} %broadcast_in_dim.33.meta), custom_call_target="tpu_custom_call" | custom-call | flops 1073741824 | bytes 4333568 | tf_op jit(solution)/shard_map/pallas_call | solution.py:254
  26.1 4.9 %all-to-all-done.1 = bf16[16,32,512]{2,1,0:T(8,128)(2,1)S(1)} async-done(((bf16[16,32,512]{2,1,0:T(8,128)(2,1)}), bf16[16,32,512]{2,1,0:T(8,128)(2,1)S(1)}, u32[]{:S(2)}, u32[]{:S(2)}) %all-to-all-start.1) | async-done | bytes 524320 | tf_op jit(solution)/shard_map/all_to_all | solution.py:329
  31.0 3.7 %all-to-all-start = ((bf16[16,32,1152]{2,1,0:T(8,128)(2,1)}), bf16[16,32,1152]{2,1,0:T(8,128)(2,1)S(1)}, u32[]{:S(2)}, u32[]{:S(2)}) async-start(bf16[16,32,1152]{2,1,0:T(8,128)(2,1)} %shard_map.119), calls=%async_computation | async-start | bytes 2359296 | tf_op jit(solution)/shard_map/all_to_all | solution.py:343
  34.7 2.6 %collective-permute-start = (bf16[512,512]{1,0:T(8,128)(2,1)S(1)}, bf16[512,512]{1,0:T(8,128)(2,1)S(1)}, u32[]{:S(2)}, u32[]{:S(2)}) collective-permute-start(bf16[512,512]{1,0:T(8,128)(2,1)S(1)} %bitcast.19), channel_id=1, source_target_pairs={{0,4},{4,0},{1,5},{5,1},{2,6},{6,2},{3,7},{7,3},{8,12},{12,8},{9,1... | collective-permute-start | bytes 1572872 | tf_op jit(solution)/shard_map/ppermute | solution.py:342
  37.3 23.0 %collective-permute-done.other = bf16[512,512]{1,0:T(8,128)(2,1)S(1)} collective-permute-done((bf16[512,512]{1,0:T(8,128)(2,1)S(1)}, bf16[512,512]{1,0:T(8,128)(2,1)S(1)}, u32[]{:S(2)}, u32[]{:S(2)}) %collective-permute-start) | collective-permute-done | bytes 524320 | tf_op jit(solution)/shard_map/ppermute | solution.py:342
  60.3 3.1 %all-to-all-done = bf16[16,32,1152]{2,1,0:T(8,128)(2,1)S(1)} async-done(((bf16[16,32,1152]{2,1,0:T(8,128)(2,1)}), bf16[16,32,1152]{2,1,0:T(8,128)(2,1)S(1)}, u32[]{:S(2)}, u32[]{:S(2)}) %all-to-all-start) | async-done | bytes 1179680 | tf_op jit(solution)/shard_map/all_to_all | solution.py:343
  63.5 0.0 copy-start.1
  63.5 0.0 copy-start.3
  63.5 6.7 %shard_map.120 = bf16[512,1024]{1,0:T(8,128)(2,1)S(1)} custom-call(bf16[512,1152]{1,0:T(8,128)(2,1)S(1)} %bitcast.16, bf16[512,512]{1,0:T(8,128)(2,1)S(1)} %bitcast.20, bf16[512,512]{1,0:T(8,128)(2,1)S(1)} %collective-permute-done.other), custom_call_target="tpu_custom_call" | custom-call | flops 268435456 | bytes 3276800 | tf_op jit(solution)/shard_map/pallas_call | solution.py:254
  70.1 20.0 %all_to_all.15 = bf16[16,32,1024]{2,1,0:T(8,128)(2,1)S(1)} all-to-all(bf16[16,32,1024]{2,1,0:T(8,128)(2,1)S(1)} %bitcast.17), channel_id=1, replica_groups=mesh['tile'=4,'half'=2,'rest'=4] {'tile','rest'}, dimensions={0} | all-to-all | bytes 2097152 | tf_op jit(solution)/shard_map/all_to_all | solution.py:358
  90.1 0.0 copy-done.1
  90.1 0.0 copy-done.3
  90.1 2.2 %shard_map.121 = bf16[512,1024]{1,0:T(8,128)(2,1)} custom-call(bf16[512,1024]{1,0:T(8,128)(2,1)S(1)} %bitcast.18, bf16[512,1024]{1,0:T(8,128)(2,1)S(1)} %copy-done.1, bf16[1024,1024]{1,0:T(8,128)(2,1)S(1)} %copy-done.3), custom_call_target="tpu_custom_call" | custom-call | flops 1073741824 | bytes 5242880 | tf_op jit(solution)/shard_map/pallas_call | solution.py:254
  (2 shorter events, 0.0 us)
Async XLA Ops:
  0.0 20.4 %copy-start.6 = (s32[1,4]{1,0:T(1,128)S(1)}, s32[1,4]{1,0:T(1,128)}, u32[]{:S(2)}) copy-start(s32[1,4]{1,0:T(1,128)} %param.22) | copy-start | bytes 52
  0.0 20.4 %copy-start.7 = (s32[1,4]{1,0:T(1,128)S(1)}, s32[1,4]{1,0:T(1,128)}, u32[]{:S(2)}) copy-start(s32[1,4]{1,0:T(1,128)} %param.21) | copy-start | bytes 52
  0.0 20.5 %copy-start.5 = (s32[1,32]{1,0:T(1,128)S(1)}, s32[1,32]{1,0:T(1,128)}, u32[]{:S(2)}) copy-start(s32[1,32]{1,0:T(1,128)} %param.23) | copy-start | bytes 388
  0.0 20.8 %copy-start.4 = (f32[1024]{0:T(1024)S(1)}, f32[1024]{0:T(1024)}, u32[]{:S(2)}) copy-start(f32[1024]{0:T(1024)} %param.17) | copy-start | bytes 12292
  14.1 16.9 %all-to-all-start.1 = ((bf16[16,32,512]{2,1,0:T(8,128)(2,1)}), bf16[16,32,512]{2,1,0:T(8,128)(2,1)S(1)}, u32[]{:S(2)}, u32[]{:S(2)}) async-start(bf16[16,32,512]{2,1,0:T(8,128)(2,1)} %get-tuple-element.8), calls=%async_computation.1 | async-start | bytes 1048576 | tf_op jit(solution)/shard_map/all_to_all | solution.py:329
  20.8 1.2 %copy-start = (bf16[512,1024]{1,0:T(8,128)(2,1)S(1)}, bf16[512,1024]{1,0:T(8,128)(2,1)}, u32[]{:S(2)}) copy-start(bf16[512,1024]{1,0:T(8,128)(2,1)} %get-tuple-element.7.mid) | copy-start | bytes 3145732
  22.0 1.6 %copy-start.2 = (bf16[1024,1024]{1,0:T(8,128)(2,1)S(1)}, bf16[1024,1024]{1,0:T(8,128)(2,1)}, u32[]{:S(2)}) copy-start(bf16[1024,1024]{1,0:T(8,128)(2,1)} %wq.1) | copy-start | bytes 6291460
  31.0 32.5 %all-to-all-start = ((bf16[16,32,1152]{2,1,0:T(8,128)(2,1)}), bf16[16,32,1152]{2,1,0:T(8,128)(2,1)S(1)}, u32[]{:S(2)}, u32[]{:S(2)}) async-start(bf16[16,32,1152]{2,1,0:T(8,128)(2,1)} %shard_map.119), calls=%async_computation | async-start | bytes 2359296 | tf_op jit(solution)/shard_map/all_to_all | solution.py:343
  34.7 25.6 %collective-permute-start = (bf16[512,512]{1,0:T(8,128)(2,1)S(1)}, bf16[512,512]{1,0:T(8,128)(2,1)S(1)}, u32[]{:S(2)}, u32[]{:S(2)}) collective-permute-start(bf16[512,512]{1,0:T(8,128)(2,1)S(1)} %bitcast.19), channel_id=1, source_target_pairs={{0,4},{4,0},{1,5},{5,1},{2,6},{6,2},{3,7},{7,3},{8,12},{12,8},{9,1... | collective-permute-start | bytes 1572872 | tf_op jit(solution)/shard_map/ppermute | solution.py:342
  63.5 26.7 %copy-start.1 = (bf16[512,1024]{1,0:T(8,128)(2,1)S(1)}, bf16[512,1024]{1,0:T(8,128)(2,1)}, u32[]{:S(2)}) copy-start(bf16[512,1024]{1,0:T(8,128)(2,1)} %get-tuple-element.7.mid) | copy-start | bytes 3145732
  63.5 26.7 %copy-start.3 = (bf16[1024,1024]{1,0:T(8,128)(2,1)S(1)}, bf16[1024,1024]{1,0:T(8,128)(2,1)}, u32[]{:S(2)}) copy-start(bf16[1024,1024]{1,0:T(8,128)(2,1)} %wo.1) | copy-start | bytes 6291460

commit v4 on v3

--- a/solution.py
+++ b/solution.py
@@ -21,6 +21,7 @@
 LANES = 128
 COLS = 256
 HALVES = 2
+DEPTH = 2
 MIB = 1024 * 1024
 F32 = jnp.float32
 BF16 = jnp.bfloat16
@@ -41,6 +42,17 @@
 def from_blocks(values, agents, steps, local):
     split = values.reshape(steps // local, agents, local, values.shape[-1])
     return jnp.transpose(split, (1, 0, 2, 3)).reshape(agents * steps, values.shape[-1])
+
+
+def staggered(units, first, second, third):
+    scores, grown = {}, {}
+    for i in range(len(units) + 2 * DEPTH):
+        if i < len(units):
+            scores[i] = first(*units[i])
+        if 0 <= i - DEPTH < len(units):
+            grown[i - DEPTH] = second(scores.pop(i - DEPTH))
+        if 0 <= i - 2 * DEPTH < len(units):
+            third(units[i - 2 * DEPTH], *grown.pop(i - 2 * DEPTH))
 
 
 def time_kernel(
@@ -65,46 +77,59 @@
         pltpu.make_async_copy(source, target, sems.at[i])
         for i, (source, target) in enumerate(((wkv_hbm, wkv), (wo_hbm, wo), (wkv2_hbm, wkv2)))
     ]
-    for load in hist_loads + wq_loads + loads:
+    for load in hist_loads + loads[:1]:
         load.start()
     for a in range(agents):
         part = pl.ds(a * steps, steps)
         hist_loads[a].wait()
+        if a == 0:
+            for load in wq_loads:
+                load.start()
         normed[part, :] = norm_rows(hist[part, :], gain_t[...])
-    for c in range(0, width, COLS):
-        wq_loads[c // COLS].wait()
-        query[:, c : c + COLS] = jnp.dot(
-            normed[...], wq[:, c : c + COLS], preferred_element_type=F32
-        ).astype(BF16)
     loads[0].wait()
     for c in range(0, 2 * KEYS, COLS):
         keyval[:, c : c + COLS] = jnp.dot(
             normed[...], wkv[:, c : c + COLS], preferred_element_type=F32
         ).astype(BF16)
+    for load in loads[1:]:
+        load.start()
+    for c in range(0, width, COLS):
+        wq_loads[c // COLS].wait()
+        query[:, c : c + COLS] = jnp.dot(
+            normed[...], wq[:, c : c + COLS], preferred_element_type=F32
+        ).astype(BF16)
     causal = lax.broadcasted_iota(jnp.int32, (steps, steps), 0) <= lax.broadcasted_iota(
         jnp.int32, (steps, steps), 1
     )
     causal = jnp.concatenate([causal] * GROUPS, axis=1)
-    for a in range(agents):
+
+    def scores_of(a, k):
         part = slice(a * steps, (a + 1) * steps)
-        for k in range(KV_HEADS):
-            wide = slice(k * WIDE, (k + 1) * WIDE)
-            keys = keyval[part, k * HEAD_DIM : (k + 1) * HEAD_DIM]
-            vals = keyval[part, KEYS + k * HEAD_DIM : KEYS + (k + 1) * HEAD_DIM]
-            heads = query[part, wide].T
-            heads = jnp.concatenate(
-                [heads[j * HEAD_DIM : (j + 1) * HEAD_DIM] for j in range(GROUPS)], axis=1
-            )
-            scores = jnp.dot(keys, heads, preferred_element_type=F32)
-            scores = jnp.where(causal, scores, NEG)
-            top = jnp.max(scores, axis=0, keepdims=True)
-            grown = jnp.exp2((scores - top) * EXP2_SCALE)
-            sums = jnp.sum(grown, axis=0, keepdims=True)
-            mixed = jnp.dot(vals.T, grown.astype(BF16), preferred_element_type=F32) * (1.0 / sums)
-            mixed = jnp.concatenate(
-                [mixed[:, j * steps : (j + 1) * steps] for j in range(GROUPS)], axis=0
-            )
-            mix[part, wide] = mixed.astype(BF16).T
+        heads = query[part, k * WIDE : (k + 1) * WIDE].T
+        heads = jnp.concatenate(
+            [heads[j * HEAD_DIM : (j + 1) * HEAD_DIM] for j in range(GROUPS)], axis=1
+        )
+        keys = keyval[part, k * HEAD_DIM : (k + 1) * HEAD_DIM]
+        return jnp.dot(keys, heads, preferred_element_type=F32)
+
+    def grow(scores):
+        scores = jnp.where(causal, scores, NEG)
+        top = jnp.max(scores, axis=0, keepdims=True)
+        grown = jnp.exp2((scores - top) * EXP2_SCALE)
+        return grown.astype(BF16), jnp.sum(grown, axis=0, keepdims=True)
+
+    def values_of(unit, grown, sums):
+        a, k = unit
+        part = slice(a * steps, (a + 1) * steps)
+        vals = keyval[part, KEYS + k * HEAD_DIM : KEYS + (k + 1) * HEAD_DIM]
+        mixed = jnp.dot(vals.T, grown, preferred_element_type=F32) * (1.0 / sums)
+        mixed = jnp.concatenate(
+            [mixed[:, j * steps : (j + 1) * steps] for j in range(GROUPS)], axis=0
+        )
+        mix[part, k * WIDE : (k + 1) * WIDE] = mixed.astype(BF16).T
+
+    units = [(a, k) for a in range(agents) for k in range(KV_HEADS)]
+    staggered(units, scores_of, grow, values_of)
     loads[1].wait()
     for c in range(0, width, COLS):
         cols = slice(c, c + COLS)
@@ -173,54 +198,89 @@
     return listed * alive
 
 
+def by_steps(source, target, local, block, total, offset=0):
+    rows, width = source.shape[0], target.shape[-1]
+    group = block // local
+    order = one_hot((block, block), group, local)
+    for c in range(0, width, COLS):
+        cols = slice(c, c + COLS)
+        for b in range(rows // block):
+            piece = source[b * block : (b + 1) * block, cols]
+            if local > 1:
+                piece = jnp.dot(order, piece, preferred_element_type=F32).astype(BF16)
+            at = offset + b * group
+            target[:, at : at + group, cols] = piece.reshape(local, group, piece.shape[1])
+
+
+def keys_kernel(local, block, source, out):
+    by_steps(source, out, local, block, out.shape[1])
+
+
 def space_kernel(
-    local, block, tiles, q_in, own, other, out, query, keyval, mix
+    local, block, tiles, pair, q_in, own, other_in, out, query, other, mix
 ):
     rows, width = out.shape
     group = block // local
     total = rows // local
+    columns = pair * total
+    by_steps(q_in, query, local, block, total)
+    by_steps(other_in, other, local, block, total)
     weight = key_weights(q_in[:, width:], local, tiles, total)
-    if local > 1:
-        order = one_hot((block, block), group, local)
-
-    def by_steps(source, target, offset, cols):
-        for b in range(rows // block):
-            piece = source[b * block : (b + 1) * block, cols]
-            if local > 1:
-                piece = jnp.dot(order, piece, preferred_element_type=F32).astype(BF16)
-            target[:, offset + b * group : offset + (b + 1) * group, cols] = piece.reshape(
-                local, group, piece.shape[1]
-            )
-
-    for c in range(0, width, COLS):
-        by_steps(q_in, query, 0, slice(c, c + COLS))
-    for c in range(0, 2 * KEYS, COLS):
-        by_steps(own, keyval, 0, slice(c, c + COLS))
-        by_steps(other, keyval, total, slice(c, c + COLS))
-
-    def one_step(s, carry):
-        mask = jnp.concatenate([weight] * GROUPS, axis=0)
-        for k in range(KV_HEADS):
-            wide = slice(k * WIDE, (k + 1) * WIDE)
-            heads = query[s, :, wide]
-            heads = jnp.concatenate(
-                [heads[:, j * HEAD_DIM : (j + 1) * HEAD_DIM] for j in range(GROUPS)], axis=0
-            )
-            keys = keyval[s, :, k * HEAD_DIM : (k + 1) * HEAD_DIM]
-            vals = keyval[s, :, KEYS + k * HEAD_DIM : KEYS + (k + 1) * HEAD_DIM]
-            scores = lax.dot_general(heads, keys, ROWS_BY_COLS, preferred_element_type=F32)
-            scores = jnp.where(mask > 0, scores, NEG)
-            top = jnp.max(scores, axis=-1, keepdims=True)
-            grown = jnp.exp2((scores - top) * EXP2_SCALE) * mask
-            sums = jnp.sum(grown, axis=-1, keepdims=True)
-            mixed = jnp.dot(grown.astype(BF16), vals, preferred_element_type=F32) / sums
-            mixed = mixed.astype(BF16)
-            mix[s, :, wide] = jnp.concatenate(
-                [mixed[j * total : (j + 1) * total] for j in range(GROUPS)], axis=1
-            )
-        return carry
-
-    lax.fori_loop(0, local, one_step, 0, unroll=2 if local % 2 == 0 else 1)
+    together = GROUPS if columns <= LANES else 1
+    weight = jnp.concatenate([weight.T] * (pair * together), axis=1)
+    valid = weight > 0
+    lane = lax.broadcasted_iota(jnp.int32, (HEAD_DIM, columns), 1) // total
+
+    def both(s, part):
+        return jnp.concatenate([own[s, :, part], other[s, :, part]], axis=0)
+
+    def scores_of(p, k, heads):
+        turned = query[p * pair : (p + 1) * pair, :, k * WIDE : (k + 1) * WIDE]
+        turned = turned.reshape(columns, WIDE).T
+        turned = [turned[j * HEAD_DIM : (j + 1) * HEAD_DIM] for j in heads]
+        if pair > 1:
+            zero = jnp.zeros((HEAD_DIM, columns), BF16)
+            turned = [
+                jnp.concatenate([jnp.where(lane == s, t, zero) for s in range(pair)], axis=0)
+                for t in turned
+            ]
+        part = slice(k * HEAD_DIM, (k + 1) * HEAD_DIM)
+        keys = jnp.concatenate([both(p * pair + s, part) for s in range(pair)], axis=1)
+        return jnp.dot(keys, jnp.concatenate(turned, axis=1), preferred_element_type=F32)
+
+    def grow(scores):
+        scores = jnp.where(valid, scores, NEG)
+        top = jnp.max(scores, axis=0, keepdims=True)
+        grown = jnp.exp2((scores - top) * EXP2_SCALE) * weight
+        return grown.astype(BF16), jnp.sum(grown, axis=0, keepdims=True)
+
+    def values_of(unit, grown, sums):
+        p, k, heads = unit
+        part = slice(KEYS + k * HEAD_DIM, KEYS + (k + 1) * HEAD_DIM)
+        vals = jnp.concatenate([both(p * pair + s, part).T for s in range(pair)], axis=0)
+        mixed = jnp.dot(vals, grown, preferred_element_type=F32)
+        inverse = 1.0 / sums
+        parts = []
+        for i in range(len(heads)):
+            cols = slice(i * columns, (i + 1) * columns)
+            chosen = mixed[:HEAD_DIM, cols]
+            for s in range(1, pair):
+                chosen = jnp.where(lane == s, mixed[s * HEAD_DIM : (s + 1) * HEAD_DIM, cols], chosen)
+            parts.append(chosen * inverse[:, cols])
+        mixed = jnp.concatenate(parts, axis=0).astype(BF16).T
+        start = k * WIDE + heads[0] * HEAD_DIM
+        mix[p * pair : (p + 1) * pair, :, start : start + len(heads) * HEAD_DIM] = mixed.reshape(
+            pair, total, len(heads) * HEAD_DIM
+        )
+
+    units = [
+        (p, k, tuple(range(j, j + together)))
+        for p in range(local // pair)
+        for k in range(KV_HEADS)
+        for j in range(0, GROUPS, together)
+    ]
+    staggered(units, scores_of, grow, values_of)
+    order = one_hot((block, block), group, local)
     for b in range(rows // block):
         for c in range(0, width, COLS):
             cols = slice(c, c + COLS)
@@ -340,20 +400,29 @@
         q = to_blocks(q, agents, steps, local)
     swap = [(h, HALVES - 1 - h) for h in range(HALVES)]
     other = lax.ppermute(own, "half", swap)
+    total = rows // local
+    block = max(COLS, local) if rows % max(COLS, local) == 0 else rows
+    own = call(
+        functools.partial(keys_kernel, local, block),
+        [struct((local, total, 2 * KEYS), BF16)],
+        [own],
+        flops=2 * rows * block * 2 * KEYS,
+    )
+    q, own = lax.optimization_barrier((q, own))
     q = lax.all_to_all(q, spread, split_axis=0, concat_axis=0, tiled=True)
 
-    block = max(COLS, local) if rows % max(COLS, local) == 0 else rows
+    pair = LANES // total if total < LANES and local % (LANES // total) == 0 else 1
     mix = call(
-        functools.partial(space_kernel, local, block, tiles),
+        functools.partial(space_kernel, local, block, tiles, pair),
         [struct((rows, width), BF16)],
         [q.reshape(rows, width + LANES), own, other],
         scratch=[
-            pltpu.VMEM((local, rows // local, width), BF16),
-            pltpu.VMEM((local, HALVES * rows // local, 2 * KEYS), BF16),
-            pltpu.VMEM((local, rows // local, width), BF16),
+            pltpu.VMEM((local, total, width), BF16),
+            pltpu.VMEM((local, total, 2 * KEYS), BF16),
+            pltpu.VMEM((local, total, width), BF16),
         ],
-        flops=8 * rows * rows // local * width,
-        mib=16 + 16 * GROUPS * HALVES * (rows // local) ** 2 // MIB,
+        flops=8 * rows * total * width,
+        mib=16 + 16 * GROUPS * HALVES * total**2 // MIB,
     )
     mix = lax.all_to_all(
         mix.reshape(parts, agents * local, width), spread, split_axis=0, concat_axis=0, tiled=True

time: 92.8 us -> 86.3 us (0.930)
  Pallas kernels: 25.5 us -> 19 us
  waiting for transfers between devices: 31 us -> 32.6 us
  local copies, waits for them, and re-layouts: 2.91 us -> 1.32 us
    pallas_call x4 -> x5, Pallas kernels: 25.5 us -> 19 us  [call(): pl.pallas_call(kernel, out_shape=list(shapes), in_specs=specs(len(args),...]
    unnamed x16, local copies, waits for them, and re-layouts: 2.83 us -> 1.25 us
    all_to_all x1, waiting for transfers between devices: 4.9 us -> 6.46 us  [per_device(): own = lax.all_to_all(kv, spread, split_axis=0, concat_axis=0, tiled=True)]
where the time goes in v4:
time: 86.3 us; the launch traced here: 85.9 us
  waiting for transfers between devices  32.6 us (38%)
  blocking collectives  20 us (23%)
  Pallas kernels  19 us (22%)
  starting transfers between devices  12.7 us (15%)
  local copies, waits for them, and re-layouts  1.32 us (2%)
    ppermute x1, waiting for transfers between devices, per_device(): other = lax.ppermute(own, 'half', swap)  23 us
    all_to_all x1, blocking collectives, per_device(): lax.all_to_all(mix.reshape(parts, agents * local, width), spread, split_a...  20 us
    pallas_call x5, Pallas kernels, call(): pl.pallas_call(kernel, out_shape=list(shapes), in_specs=specs(len(args),...  19 us
    all_to_all x1, waiting for transfers between devices, per_device(): own = lax.all_to_all(kv, spread, split_axis=0, concat_axis=0, tiled=True)  6.46 us
    all_to_all x1, starting transfers between devices, per_device(): own = lax.all_to_all(kv, spread, split_axis=0, concat_axis=0, tiled=True)  6.32 us
    all_to_all x1, starting transfers between devices, per_device(): q = lax.all_to_all(q, spread, split_axis=0, concat_axis=0, tiled=True)  3.71 us
    all_to_all x1, waiting for transfers between devices, per_device(): q = lax.all_to_all(q, spread, split_axis=0, concat_axis=0, tiled=True)  3.12 us
    ppermute x1, starting transfers between devices, per_device(): other = lax.ppermute(own, 'half', swap)  2.66 us
  transfers between devices with their start and end apart: 3, of which 3 were waited for; matrix products, arithmetic and copies ran while one was open for 0% of the time, Pallas kernels for 3%

profile of v4, /device:TPU:0, one launch (start us, length us, event | category | flops | bytes accessed | tf_op | source)
XLA Modules:
  0.0 85.9 jit_solution(710541461878465043)
XLA Ops:
  0.0 0.0 copy-start.6
  0.0 0.0 copy-start.7
  0.0 0.0 copy-start.5
  0.0 0.0 copy-start.2
  0.0 0.0 copy-start.4
  0.0 10.7 %shard_map.118 = (bf16[512,1024]{1,0:T(8,128)(2,1)}, bf16[16,32,512]{2,1,0:T(8,128)(2,1)}) custom-call(bf16[512,1024]{1,0:T(8,128)(2,1)} %bitcast.23, f32[1,1024]{1,0:T(1,128)} %bitcast.24, f32[1,1024]{1,0:T(1,128)} %bitcast.21, bf16[1024,1024]{1,0:T(8,128)(2,1)} %wq_hbm.1, bf16[1024,512]{1,0:T(8,128)(2,1)} %wkv_hbm.1, bf16[1024,1024]{1,0:T(8,128)(2,1)} %wo_hbm.1, ...), custom_call_target="tpu_custom_call" | custom-call | flops 3221225472 | bytes 8921088 | tf_op jit(solution)/shard_map/pallas_call | solution.py:314
  10.7 6.3 %all-to-all-start = ((bf16[16,32,512]{2,1,0:T(8,128)(2,1)}), bf16[16,32,512]{2,1,0:T(8,128)(2,1)S(1)}, u32[]{:S(2)}, u32[]{:S(2)}) async-start(bf16[16,32,512]{2,1,0:T(8,128)(2,1)} %get-tuple-element.10), calls=%async_computation | async-start | bytes 1048576 | tf_op jit(solution)/shard_map/all_to_all | solution.py:389
  17.0 0.0 copy-done.6
  17.0 0.0 copy-done.7
  17.1 0.1 select_reduce_fusion
  17.1 0.0 copy-done.5
  17.1 0.1 slice_bitcast_fusion.1
  17.2 0.1 broadcast_select_fusion
  17.3 0.1 pad_add_fusion
  17.4 0.0 copy-done.2
  17.4 0.0 copy-done.4
  17.4 0.0 copy-start
  17.4 1.2 %copy-done = bf16[512,1024]{1,0:T(8,128)(2,1)S(1)} copy-done((bf16[512,1024]{1,0:T(8,128)(2,1)S(1)}, bf16[512,1024]{1,0:T(8,128)(2,1)}, u32[]{:S(2)}) %copy-start) | copy-done | bytes 1048600
  18.6 2.5 %shard_map.119 = bf16[16,32,1152]{2,1,0:T(8,128)(2,1)} custom-call(bf16[512,1024]{1,0:T(8,128)(2,1)S(1)} %copy-done, f32[1,1024]{1,0:T(1,128)S(1)} %bitcast.22, bf16[1024,1024]{1,0:T(8,128)(2,1)S(1)} %copy-done.2, f32[8,128]{1,0:T(8,128)S(1)} %broadcast_in_dim.33.meta), custom_call_target="tpu_custom_call" | custom-call | flops 1073741824 | bytes 4333568 | tf_op jit(solution)/shard_map/pallas_call | solution.py:314
  21.1 6.5 %all-to-all-done = bf16[16,32,512]{2,1,0:T(8,128)(2,1)S(1)} async-done(((bf16[16,32,512]{2,1,0:T(8,128)(2,1)}), bf16[16,32,512]{2,1,0:T(8,128)(2,1)S(1)}, u32[]{:S(2)}, u32[]{:S(2)}) %all-to-all-start) | async-done | bytes 524320 | tf_op jit(solution)/shard_map/all_to_all | solution.py:389
  27.6 0.3 shard_map.120.own
  27.9 3.7 %all-to-all-start.1 = ((bf16[16,32,1152]{2,1,0:T(8,128)(2,1)}), bf16[16,32,1152]{2,1,0:T(8,128)(2,1)S(1)}, u32[]{:S(2)}, u32[]{:S(2)}) async-start(bf16[16,32,1152]{2,1,0:T(8,128)(2,1)} %shard_map.119), calls=%async_computation.1 | async-start | bytes 2359296 | tf_op jit(solution)/shard_map/all_to_all | solution.py:412
  31.6 2.7 %collective-permute-start = (bf16[512,512]{1,0:T(8,128)(2,1)S(1)}, bf16[512,512]{1,0:T(8,128)(2,1)S(1)}, u32[]{:S(2)}, u32[]{:S(2)}) collective-permute-start(bf16[512,512]{1,0:T(8,128)(2,1)S(1)} %bitcast.20), channel_id=1, source_target_pairs={{0,4},{4,0},{1,5},{5,1},{2,6},{6,2},{3,7},{7,3},{8,12},{12,8},{9,1... | collective-permute-start | bytes 1572872 | tf_op jit(solution)/shard_map/ppermute | solution.py:402
  34.3 23.0 %collective-permute-done.other_in = bf16[512,512]{1,0:T(8,128)(2,1)S(1)} collective-permute-done((bf16[512,512]{1,0:T(8,128)(2,1)S(1)}, bf16[512,512]{1,0:T(8,128)(2,1)S(1)}, u32[]{:S(2)}, u32[]{:S(2)}) %collective-permute-start) | collective-permute-done | bytes 524320 | tf_op jit(solution)/shard_map/ppermute | solution.py:402
  57.3 3.1 %all-to-all-done.1 = bf16[16,32,1152]{2,1,0:T(8,128)(2,1)S(1)} async-done(((bf16[16,32,1152]{2,1,0:T(8,128)(2,1)}), bf16[16,32,1152]{2,1,0:T(8,128)(2,1)S(1)}, u32[]{:S(2)}, u32[]{:S(2)}) %all-to-all-start.1) | async-done | bytes 1179680 | tf_op jit(solution)/shard_map/all_to_all | solution.py:412
  60.4 0.0 copy-start.1
  60.4 0.0 copy-start.3
  60.4 3.3 %shard_map.121 = bf16[512,1024]{1,0:T(8,128)(2,1)S(1)} custom-call(bf16[512,1152]{1,0:T(8,128)(2,1)S(1)} %bitcast.16, bf16[8,64,512]{2,1,0:T(8,128)(2,1)S(1)} %shard_map.120.own, bf16[512,512]{1,0:T(8,128)(2,1)S(1)} %collective-permute-done.other_in), custom_call_target="tpu_custom_call" | custom-call | flops 268435456 | bytes 3276800 | tf_op jit(solution)/shard_map/pallas_call | solution.py:314
  63.6 20.0 %all_to_all.15 = bf16[16,32,1024]{2,1,0:T(8,128)(2,1)S(1)} all-to-all(bf16[16,32,1024]{2,1,0:T(8,128)(2,1)S(1)} %bitcast.17), channel_id=1, replica_groups=mesh['tile'=4,'half'=2,'rest'=4] {'tile','rest'}, dimensions={0} | all-to-all | bytes 2097152 | tf_op jit(solution)/shard_map/all_to_all | solution.py:427
  83.6 0.0 copy-done.1
  83.6 0.0 copy-done.3
  83.6 2.2 %shard_map.122 = bf16[512,1024]{1,0:T(8,128)(2,1)} custom-call(bf16[512,1024]{1,0:T(8,128)(2,1)S(1)} %bitcast.18, bf16[512,1024]{1,0:T(8,128)(2,1)S(1)} %copy-done.1, bf16[1024,1024]{1,0:T(8,128)(2,1)S(1)} %copy-done.3), custom_call_target="tpu_custom_call" | custom-call | flops 1073741824 | bytes 5242880 | tf_op jit(solution)/shard_map/pallas_call | solution.py:314
  (2 shorter events, 0.0 us)
Async XLA Ops:
  0.0 17.0 %copy-start.6 = (s32[1,4]{1,0:T(1,128)S(1)}, s32[1,4]{1,0:T(1,128)}, u32[]{:S(2)}) copy-start(s32[1,4]{1,0:T(1,128)} %param.22) | copy-start | bytes 52
  0.0 17.0 %copy-start.7 = (s32[1,4]{1,0:T(1,128)S(1)}, s32[1,4]{1,0:T(1,128)}, u32[]{:S(2)}) copy-start(s32[1,4]{1,0:T(1,128)} %param.21) | copy-start | bytes 52
  0.0 17.1 %copy-start.5 = (s32[1,32]{1,0:T(1,128)S(1)}, s32[1,32]{1,0:T(1,128)}, u32[]{:S(2)}) copy-start(s32[1,32]{1,0:T(1,128)} %param.23) | copy-start | bytes 388
  0.0 17.4 %copy-start.2 = (bf16[1024,1024]{1,0:T(8,128)(2,1)S(1)}, bf16[1024,1024]{1,0:T(8,128)(2,1)}, u32[]{:S(2)}) copy-start(bf16[1024,1024]{1,0:T(8,128)(2,1)} %wq.1) | copy-start | bytes 6291460
  0.0 17.4 %copy-start.4 = (f32[1024]{0:T(1024)S(1)}, f32[1024]{0:T(1024)}, u32[]{:S(2)}) copy-start(f32[1024]{0:T(1024)} %param.17) | copy-start | bytes 12292
  10.7 16.9 %all-to-all-start = ((bf16[16,32,512]{2,1,0:T(8,128)(2,1)}), bf16[16,32,512]{2,1,0:T(8,128)(2,1)S(1)}, u32[]{:S(2)}, u32[]{:S(2)}) async-start(bf16[16,32,512]{2,1,0:T(8,128)(2,1)} %get-tuple-element.10), calls=%async_computation | async-start | bytes 1048576 | tf_op jit(solution)/shard_map/all_to_all | solution.py:389
  17.4 1.2 %copy-start = (bf16[512,1024]{1,0:T(8,128)(2,1)S(1)}, bf16[512,1024]{1,0:T(8,128)(2,1)}, u32[]{:S(2)}) copy-start(bf16[512,1024]{1,0:T(8,128)(2,1)} %get-tuple-element.9.mid) | copy-start | bytes 3145732
  27.9 32.5 %all-to-all-start.1 = ((bf16[16,32,1152]{2,1,0:T(8,128)(2,1)}), bf16[16,32,1152]{2,1,0:T(8,128)(2,1)S(1)}, u32[]{:S(2)}, u32[]{:S(2)}) async-start(bf16[16,32,1152]{2,1,0:T(8,128)(2,1)} %shard_map.119), calls=%async_computation.1 | async-start | bytes 2359296 | tf_op jit(solution)/shard_map/all_to_all | solution.py:412
  31.6 25.7 %collective-permute-start = (bf16[512,512]{1,0:T(8,128)(2,1)S(1)}, bf16[512,512]{1,0:T(8,128)(2,1)S(1)}, u32[]{:S(2)}, u32[]{:S(2)}) collective-permute-start(bf16[512,512]{1,0:T(8,128)(2,1)S(1)} %bitcast.20), channel_id=1, source_target_pairs={{0,4},{4,0},{1,5},{5,1},{2,6},{6,2},{3,7},{7,3},{8,12},{12,8},{9,1... | collective-permute-start | bytes 1572872 | tf_op jit(solution)/shard_map/ppermute | solution.py:402
  60.4 23.3 %copy-start.1 = (bf16[512,1024]{1,0:T(8,128)(2,1)S(1)}, bf16[512,1024]{1,0:T(8,128)(2,1)}, u32[]{:S(2)}) copy-start(bf16[512,1024]{1,0:T(8,128)(2,1)} %get-tuple-element.9.mid) | copy-start | bytes 3145732
  60.4 23.3 %copy-start.3 = (bf16[1024,1024]{1,0:T(8,128)(2,1)S(1)}, bf16[1024,1024]{1,0:T(8,128)(2,1)}, u32[]{:S(2)}) copy-start(bf16[1024,1024]{1,0:T(8,128)(2,1)} %wo.1) | copy-start | bytes 6291460

commit v5 on v4

--- a/solution.py
+++ b/solution.py
@@ -22,6 +22,7 @@
 COLS = 256
 HALVES = 2
 DEPTH = 2
+SHADOW = 10000
 MIB = 1024 * 1024
 F32 = jnp.float32
 BF16 = jnp.bfloat16
@@ -402,13 +403,13 @@
     other = lax.ppermute(own, "half", swap)
     total = rows // local
     block = max(COLS, local) if rows % max(COLS, local) == 0 else rows
+    q, own = lax.optimization_barrier((q, own))
     own = call(
         functools.partial(keys_kernel, local, block),
         [struct((local, total, 2 * KEYS), BF16)],
         [own],
-        flops=2 * rows * block * 2 * KEYS,
-    )
-    q, own = lax.optimization_barrier((q, own))
+        flops=SHADOW * rows * block * 2 * KEYS,
+    )
     q = lax.all_to_all(q, spread, split_axis=0, concat_axis=0, tiled=True)
 
     pair = LANES // total if total < LANES and local % (LANES // total) == 0 else 1

time: 86.3 us -> 89.7 us (1.039)
  Pallas kernels: 19 us -> 21.6 us
  waiting for transfers between devices: 32.6 us -> 33.9 us
  blocking collectives: 20 us -> 18.8 us
    all_to_all x1, waiting for transfers between devices: 3.12 us -> 10.2 us  [per_device(): q = lax.all_to_all(q, spread, split_axis=0, concat_axis=0, tiled=True)]
    ppermute x1, waiting for transfers between devices: 23 us -> 17.1 us  [per_device(): other = lax.ppermute(own, 'half', swap)]
    pallas_call x5, Pallas kernels: 19 us -> 21.6 us  [call(): pl.pallas_call(kernel, out_shape=list(shapes), in_specs=specs(len(args),...]
    all_to_all x1, blocking collectives: 20 us -> 18.8 us  [per_device(): lax.all_to_all(mix.reshape(parts, agents * local, width), spread, split_a...]
  transfers between devices with their start and end apart: 3 -> 3, of which waited for: 3 -> 3; matrix products, arithmetic and copies ran while one was open for 0% -> 0% of each run, Pallas kernels for 3% -> 4%
where the time goes in v5:
time: 89.7 us; the launch traced here: 89.2 us
  waiting for transfers between devices  33.9 us (38%)
  Pallas kernels  21.6 us (24%)
  blocking collectives  18.8 us (21%)
  starting transfers between devices  13.4 us (15%)
  local copies, waits for them, and re-layouts  1.32 us (1%)
    pallas_call x5, Pallas kernels, call(): pl.pallas_call(kernel, out_shape=list(shapes), in_specs=specs(len(args),...  21.6 us
    all_to_all x1, blocking collectives, per_device(): lax.all_to_all(mix.reshape(parts, agents * local, width), spread, split_a...  18.8 us
    ppermute x1, waiting for transfers between devices, per_device(): other = lax.ppermute(own, 'half', swap)  17.1 us
    all_to_all x1, waiting for transfers between devices, per_device(): q = lax.all_to_all(q, spread, split_axis=0, concat_axis=0, tiled=True)  10.2 us
    all_to_all x1, waiting for transfers between devices, per_device(): own = lax.all_to_all(kv, spread, split_axis=0, concat_axis=0, tiled=True)  6.54 us
    all_to_all x1, starting transfers between devices, per_device(): own = lax.all_to_all(kv, spread, split_axis=0, concat_axis=0, tiled=True)  6.37 us
    all_to_all x1, starting transfers between devices, per_device(): q = lax.all_to_all(q, spread, split_axis=0, concat_axis=0, tiled=True)  4.39 us
    ppermute x1, starting transfers between devices, per_device(): other = lax.ppermute(own, 'half', swap)  2.6 us
  transfers between devices with their start and end apart: 3, of which 3 were waited for; matrix products, arithmetic and copies ran while one was open for 0% of the time, Pallas kernels for 4%

profile of v5, /device:TPU:0, one launch (start us, length us, event | category | flops | bytes accessed | tf_op | source)
XLA Modules:
  0.0 89.2 jit_solution(2078542646321682021)
XLA Ops:
  0.0 0.0 copy-start.6
  0.0 0.0 copy-start.7
  0.0 0.0 copy-start.5
  0.0 0.0 copy-start.2
  0.0 0.0 copy-start.4
  0.0 10.7 %shard_map.118 = (bf16[512,1024]{1,0:T(8,128)(2,1)}, bf16[16,32,512]{2,1,0:T(8,128)(2,1)}) custom-call(bf16[512,1024]{1,0:T(8,128)(2,1)} %bitcast.20, f32[1,1024]{1,0:T(1,128)} %bitcast.21, f32[1,1024]{1,0:T(1,128)} %bitcast.18, bf16[1024,1024]{1,0:T(8,128)(2,1)} %wq_hbm.1, bf16[1024,512]{1,0:T(8,128)(2,1)} %wkv_hbm.1, bf16[1024,1024]{1,0:T(8,128)(2,1)} %wo_hbm.1, ...), custom_call_target="tpu_custom_call" | custom-call | flops 3221225472 | bytes 8921088 | tf_op jit(solution)/shard_map/pallas_call | solution.py:315
  10.7 6.4 %all-to-all-start = ((bf16[16,32,512]{2,1,0:T(8,128)(2,1)}), bf16[16,32,512]{2,1,0:T(8,128)(2,1)}, u32[]{:S(2)}, u32[]{:S(2)}) async-start(bf16[16,32,512]{2,1,0:T(8,128)(2,1)} %get-tuple-element.10), calls=%async_computation | async-start | bytes 1048576 | tf_op jit(solution)/shard_map/all_to_all | solution.py:390
  17.1 0.0 copy-done.6
  17.1 0.0 copy-done.7
  17.1 0.1 select_reduce_fusion
  17.2 0.0 copy-done.5
  17.2 0.1 slice_bitcast_fusion.1
  17.3 0.1 broadcast_select_fusion
  17.3 0.1 pad_add_fusion
  17.4 0.0 copy-done.2
  17.4 0.0 copy-done.4
  17.4 0.0 copy-start
  17.5 1.2 %copy-done = bf16[512,1024]{1,0:T(8,128)(2,1)S(1)} copy-done((bf16[512,1024]{1,0:T(8,128)(2,1)S(1)}, bf16[512,1024]{1,0:T(8,128)(2,1)}, u32[]{:S(2)}) %copy-start) | copy-done | bytes 1048600
  18.7 2.5 %shard_map.119 = bf16[16,32,1152]{2,1,0:T(8,128)(2,1)} custom-call(bf16[512,1024]{1,0:T(8,128)(2,1)S(1)} %copy-done, f32[1,1024]{1,0:T(1,128)S(1)} %bitcast.19, bf16[1024,1024]{1,0:T(8,128)(2,1)S(1)} %copy-done.2, f32[8,128]{1,0:T(8,128)S(1)} %broadcast_in_dim.33.meta), custom_call_target="tpu_custom_call" | custom-call | flops 1073741824 | bytes 4333568 | tf_op jit(solution)/shard_map/pallas_call | solution.py:315
  21.1 6.5 %all-to-all-done = bf16[16,32,512]{2,1,0:T(8,128)(2,1)} async-done(((bf16[16,32,512]{2,1,0:T(8,128)(2,1)}), bf16[16,32,512]{2,1,0:T(8,128)(2,1)}, u32[]{:S(2)}, u32[]{:S(2)}) %all-to-all-start) | async-done | bytes 524320 | tf_op jit(solution)/shard_map/all_to_all | solution.py:390
  27.7 2.6 %collective-permute-start = (bf16[512,512]{1,0:T(8,128)(2,1)}, bf16[512,512]{1,0:T(8,128)(2,1)}, u32[]{:S(2)}, u32[]{:S(2)}) collective-permute-start(bf16[512,512]{1,0:T(8,128)(2,1)} %bitcast.8.source), channel_id=1, source_target_pairs={{0,4},{4,0},{1,5},{5,1},{2,6},{6,2},{3,7},{7,3},{8,12},{12,8},{9,1... | collective-permute-start | bytes 1572872 | tf_op jit(solution)/shard_map/ppermute | solution.py:403
  30.3 4.4 %all-to-all-start.1 = ((bf16[16,32,1152]{2,1,0:T(8,128)(2,1)}), bf16[16,32,1152]{2,1,0:T(8,128)(2,1)}, u32[]{:S(2)}, u32[]{:S(2)}) async-start(bf16[16,32,1152]{2,1,0:T(8,128)(2,1)} %shard_map.119), calls=%async_computation.1 | async-start | bytes 2359296 | tf_op jit(solution)/shard_map/all_to_all | solution.py:413
  34.7 1.3 %shard_map.120.own = bf16[8,64,512]{2,1,0:T(8,128)(2,1)S(1)} custom-call(bf16[512,512]{1,0:T(8,128)(2,1)} %bitcast.8.source), custom_call_target="tpu_custom_call" | custom-call | flops 671088640000 | bytes 1048576 | tf_op jit(solution)/shard_map/pallas_call | solution.py:315
  36.0 17.1 %collective-permute-done.other_in = bf16[512,512]{1,0:T(8,128)(2,1)} collective-permute-done((bf16[512,512]{1,0:T(8,128)(2,1)}, bf16[512,512]{1,0:T(8,128)(2,1)}, u32[]{:S(2)}, u32[]{:S(2)}) %collective-permute-start) | collective-permute-done | bytes 524320 | tf_op jit(solution)/shard_map/ppermute | solution.py:403
  53.1 10.2 %all-to-all-done.1 = bf16[16,32,1152]{2,1,0:T(8,128)(2,1)} async-done(((bf16[16,32,1152]{2,1,0:T(8,128)(2,1)}), bf16[16,32,1152]{2,1,0:T(8,128)(2,1)}, u32[]{:S(2)}, u32[]{:S(2)}) %all-to-all-start.1) | async-done | bytes 1179680 | tf_op jit(solution)/shard_map/all_to_all | solution.py:413
  63.3 0.0 copy-start.1
  63.4 0.0 copy-start.3
  63.4 4.8 %shard_map.121 = bf16[512,1024]{1,0:T(8,128)(2,1)S(1)} custom-call(bf16[512,1152]{1,0:T(8,128)(2,1)} %bitcast.9.q_in, bf16[8,64,512]{2,1,0:T(8,128)(2,1)S(1)} %shard_map.120.own, bf16[512,512]{1,0:T(8,128)(2,1)} %collective-permute-done.other_in), custom_call_target="tpu_custom_call" | custom-call | flops 268435456 | bytes 3276800 | tf_op jit(solution)/shard_map/pallas_call | solution.py:315
  68.2 18.8 %all_to_all.15 = bf16[16,32,1024]{2,1,0:T(8,128)(2,1)S(1)} all-to-all(bf16[16,32,1024]{2,1,0:T(8,128)(2,1)S(1)} %bitcast.16), channel_id=1, replica_groups=mesh['tile'=4,'half'=2,'rest'=4] {'tile','rest'}, dimensions={0} | all-to-all | bytes 2097152 | tf_op jit(solution)/shard_map/all_to_all | solution.py:428
  87.0 0.0 copy-done.1
  87.0 0.0 copy-done.3
  87.0 2.2 %shard_map.122 = bf16[512,1024]{1,0:T(8,128)(2,1)} custom-call(bf16[512,1024]{1,0:T(8,128)(2,1)S(1)} %bitcast.17, bf16[512,1024]{1,0:T(8,128)(2,1)S(1)} %copy-done.1, bf16[1024,1024]{1,0:T(8,128)(2,1)S(1)} %copy-done.3), custom_call_target="tpu_custom_call" | custom-call | flops 1073741824 | bytes 5242880 | tf_op jit(solution)/shard_map/pallas_call | solution.py:315
  (2 shorter events, 0.0 us)
Async XLA Ops:
  0.0 17.1 %copy-start.6 = (s32[1,4]{1,0:T(1,128)S(1)}, s32[1,4]{1,0:T(1,128)}, u32[]{:S(2)}) copy-start(s32[1,4]{1,0:T(1,128)} %param.22) | copy-start | bytes 52
  0.0 17.1 %copy-start.7 = (s32[1,4]{1,0:T(1,128)S(1)}, s32[1,4]{1,0:T(1,128)}, u32[]{:S(2)}) copy-start(s32[1,4]{1,0:T(1,128)} %param.21) | copy-start | bytes 52
  0.0 17.2 %copy-start.5 = (s32[1,32]{1,0:T(1,128)S(1)}, s32[1,32]{1,0:T(1,128)}, u32[]{:S(2)}) copy-start(s32[1,32]{1,0:T(1,128)} %param.23) | copy-start | bytes 388
  0.0 17.4 %copy-start.2 = (bf16[1024,1024]{1,0:T(8,128)(2,1)S(1)}, bf16[1024,1024]{1,0:T(8,128)(2,1)}, u32[]{:S(2)}) copy-start(bf16[1024,1024]{1,0:T(8,128)(2,1)} %wq.1) | copy-start | bytes 6291460
  0.0 17.4 %copy-start.4 = (f32[1024]{0:T(1024)S(1)}, f32[1024]{0:T(1024)}, u32[]{:S(2)}) copy-start(f32[1024]{0:T(1024)} %param.17) | copy-start | bytes 12292
  10.7 17.0 %all-to-all-start = ((bf16[16,32,512]{2,1,0:T(8,128)(2,1)}), bf16[16,32,512]{2,1,0:T(8,128)(2,1)}, u32[]{:S(2)}, u32[]{:S(2)}) async-start(bf16[16,32,512]{2,1,0:T(8,128)(2,1)} %get-tuple-element.10), calls=%async_computation | async-start | bytes 1048576 | tf_op jit(solution)/shard_map/all_to_all | solution.py:390
  17.4 1.2 %copy-start = (bf16[512,1024]{1,0:T(8,128)(2,1)S(1)}, bf16[512,1024]{1,0:T(8,128)(2,1)}, u32[]{:S(2)}) copy-start(bf16[512,1024]{1,0:T(8,128)(2,1)} %get-tuple-element.9.mid) | copy-start | bytes 3145732
  27.7 25.4 %collective-permute-start = (bf16[512,512]{1,0:T(8,128)(2,1)}, bf16[512,512]{1,0:T(8,128)(2,1)}, u32[]{:S(2)}, u32[]{:S(2)}) collective-permute-start(bf16[512,512]{1,0:T(8,128)(2,1)} %bitcast.8.source), channel_id=1, source_target_pairs={{0,4},{4,0},{1,5},{5,1},{2,6},{6,2},{3,7},{7,3},{8,12},{12,8},{9,1... | collective-permute-start | bytes 1572872 | tf_op jit(solution)/shard_map/ppermute | solution.py:403
  30.3 33.1 %all-to-all-start.1 = ((bf16[16,32,1152]{2,1,0:T(8,128)(2,1)}), bf16[16,32,1152]{2,1,0:T(8,128)(2,1)}, u32[]{:S(2)}, u32[]{:S(2)}) async-start(bf16[16,32,1152]{2,1,0:T(8,128)(2,1)} %shard_map.119), calls=%async_computation.1 | async-start | bytes 2359296 | tf_op jit(solution)/shard_map/all_to_all | solution.py:413
  63.3 23.6 %copy-start.1 = (bf16[512,1024]{1,0:T(8,128)(2,1)S(1)}, bf16[512,1024]{1,0:T(8,128)(2,1)}, u32[]{:S(2)}) copy-start(bf16[512,1024]{1,0:T(8,128)(2,1)} %get-tuple-element.9.mid) | copy-start | bytes 3145732
  63.4 23.6 %copy-start.3 = (bf16[1024,1024]{1,0:T(8,128)(2,1)S(1)}, bf16[1024,1024]{1,0:T(8,128)(2,1)}, u32[]{:S(2)}) copy-start(bf16[1024,1024]{1,0:T(8,128)(2,1)} %wo.1) | copy-start | bytes 6291460

commit v6 on v5

--- a/solution.py
+++ b/solution.py
@@ -21,6 +21,8 @@
 LANES = 128
 COLS = 256
 HALVES = 2
+PLANES = 2
+CORES = 2
 DEPTH = 2
 SHADOW = 10000
 MIB = 1024 * 1024
@@ -152,7 +154,13 @@
     keep.wait()
 
 
-def query_kernel(agents, steps, local, blocked, mid, gain, wq, meta, out, second):
+def query_kernel(agents, steps, local, blocked, cross, mid, gain, wq, meta, *rest):
+    if cross:
+        place, same, other, second = rest
+        outs, swapped = (same, other), place[0] == 1
+    else:
+        out, second = rest
+        outs = (out,)
     width = mid.shape[1]
     for a in range(agents):
         part = pl.ds(a * steps, steps)
@@ -160,15 +168,22 @@
     for c in range(0, width, COLS):
         cols = slice(c, c + COLS)
         result = jnp.dot(second[...], wq[:, cols], preferred_element_type=F32)
-        if blocked:
+        if cross:
+            result = to_blocks(result, agents, steps, local).astype(BF16)
+            result = result.reshape(-1, PLANES, CORES * result.shape[1], COLS)
+            low, high = result[:, 0], result[:, 1]
+            same[:, :, cols] = jnp.where(swapped, high, low).reshape(same.shape[:2] + (COLS,))
+            other[:, :, cols] = jnp.where(swapped, low, high).reshape(same.shape[:2] + (COLS,))
+        elif blocked:
             out[:, :, cols] = to_blocks(result, agents, steps, local).astype(BF16)
         else:
             out[:, cols] = result.astype(BF16)
-    lines = jnp.broadcast_to(meta[0:1, :], (out.shape[-2], LANES)).astype(BF16)
-    if blocked:
-        out[:, :, width:] = jnp.broadcast_to(lines[None], (out.shape[0], out.shape[1], LANES))
-    else:
-        out[:, width:] = lines
+    for out in outs:
+        lines = jnp.broadcast_to(meta[0:1, :], (out.shape[-2], LANES)).astype(BF16)
+        if blocked:
+            out[:, :, width:] = jnp.broadcast_to(lines[None], out.shape[:2] + (LANES,))
+        else:
+            out[:, width:] = lines
 
 
 def one_hot(shape, group, local, dtype=BF16):
@@ -178,7 +193,7 @@
     return jnp.where(col == wanted, 1.0, 0.0).astype(dtype)
 
 
-def key_weights(notes, local, tiles, total):
+def key_weights(notes, local, tiles, total, stride):
     rows = notes.shape[0]
     group = total // tiles
     shape = (total, rows)
@@ -194,39 +209,49 @@
     alive = jnp.dot(lines, spread, preferred_element_type=F32)
     shape = (total, HALVES * total)
     row, key = (lax.broadcasted_iota(jnp.int32, shape, d) for d in range(2))
-    first = row == key % total // group * group
+    first = row == key % total // group * stride
     alive = jnp.sum(jnp.where(first, alive, 0.0), axis=0, keepdims=True)
     return listed * alive
 
 
-def by_steps(source, target, local, block, total, offset=0):
-    rows, width = source.shape[0], target.shape[-1]
+def by_steps(source, target, local, block, rows, sources=1):
+    width = target.shape[-1]
     group = block // local
     order = one_hot((block, block), group, local)
     for c in range(0, width, COLS):
         cols = slice(c, c + COLS)
         for b in range(rows // block):
-            piece = source[b * block : (b + 1) * block, cols]
+            if sources > 1:
+                share = source.shape[1] // sources
+                piece = source[:, b * share : (b + 1) * share, cols].reshape(block, COLS)
+            else:
+                piece = source[b * block : (b + 1) * block, cols]
             if local > 1:
                 piece = jnp.dot(order, piece, preferred_element_type=F32).astype(BF16)
-            at = offset + b * group
-            target[:, at : at + group, cols] = piece.reshape(local, group, piece.shape[1])
+            target[:, b * group : (b + 1) * group, cols] = piece.reshape(local, group, piece.shape[1])
 
 
 def keys_kernel(local, block, source, out):
-    by_steps(source, out, local, block, out.shape[1])
+    by_steps(source, out, local, block, source.shape[0])
 
 
 def space_kernel(
-    local, block, tiles, pair, q_in, own, other_in, out, query, other, mix
+    local, block, tiles, pair, sources, q_in, own, other_in, *refs
 ):
-    rows, width = out.shape
+    *place, out, query, other, mix = refs
+    rows, width = other_in.shape[0], out.shape[-1]
     group = block // local
     total = rows // local
     columns = pair * total
-    by_steps(q_in, query, local, block, total)
-    by_steps(other_in, other, local, block, total)
-    weight = key_weights(q_in[:, width:], local, tiles, total)
+    by_steps(q_in, query, local, block, rows, sources)
+    by_steps(other_in, other, local, block, rows)
+    if sources > 1:
+        share = q_in.shape[1] // sources
+        notes = [q_in[:, i * share : (i + 1) * share, width:] for i in range(sources)]
+        notes = jnp.concatenate([part.reshape(block, LANES) for part in notes], axis=0)
+    else:
+        notes = q_in[:, width:]
+    weight = key_weights(notes, local, tiles, total, total // sources // tiles)
     together = GROUPS if columns <= LANES else 1
     weight = jnp.concatenate([weight.T] * (pair * together), axis=1)
     valid = weight > 0
@@ -290,7 +315,11 @@
                 piece = lax.dot_general(
                     order, piece, (((0,), (0,)), ((), ())), preferred_element_type=F32
                 ).astype(BF16)
-            out[b * block : (b + 1) * block, cols] = piece
+            if sources > 1:
+                plane = (place[0][0] + b) % PLANES
+                out[:, plane, :, cols] = piece.reshape(out.shape[0], out.shape[2], COLS)
+            else:
+                out[b * block : (b + 1) * block, cols] = piece
 
 
 def out_kernel(agents, steps, local, blocked, mix, mid, wo, out):
@@ -303,19 +332,21 @@
         out[:, cols] = (mid[:, cols].astype(F32) + projected).astype(BF16)
 
 
-def call(kernel, shapes, args, hbm=(), hbm_out=(), scratch=(), flops=0, mib=16):
+def call(kernel, shapes, args, hbm=(), hbm_out=(), smem=(), scratch=(), flops=0, mib=16):
     moved = sum(a.size * a.dtype.itemsize for a in args)
     moved += sum(s.size * s.dtype.itemsize for s in shapes)
 
-    def specs(count, far):
+    def specs(count, far, scalars=()):
+        spaces = [pl.ANY if i in far else pltpu.VMEM for i in range(count)]
         return [
-            pl.BlockSpec(memory_space=pl.ANY if i in far else pltpu.VMEM) for i in range(count)
+            pl.BlockSpec(memory_space=pltpu.SMEM if i in scalars else space)
+            for i, space in enumerate(spaces)
         ]
 
     results = pl.pallas_call(
         kernel,
         out_shape=list(shapes),
-        in_specs=specs(len(args), hbm),
+        in_specs=specs(len(args), hbm, smem),
         out_specs=specs(len(shapes), hbm_out),
         scratch_shapes=list(scratch),
         compiler_params=pltpu.CompilerParams(vmem_limit_bytes=mib * MIB),
@@ -339,12 +370,14 @@
     agent_valid,
 ):
     agents, steps, width = histories.shape[1:]
-    tiles, rest = lax.axis_size("tile"), lax.axis_size("rest")
-    spread = ("tile", "rest")
+    tiles, planes, cores = (lax.axis_size(name) for name in ("tile", "plane", "core"))
+    rest = planes * cores
+    spread = ("tile", "plane", "core")
     parts = tiles * rest
     local = steps // parts
     rows = agents * steps
     blocked = local % 8 == 0
+    cross = blocked and planes == PLANES and cores == CORES and rows == 2 * COLS
     struct = jax.ShapeDtypeStruct
 
     hist = histories.reshape(rows, width)
@@ -389,34 +422,47 @@
     meta = jnp.broadcast_to(meta[None], (8, LANES))
     own = lax.all_to_all(kv, spread, split_axis=0, concat_axis=0, tiled=True)
     own = own.reshape(rows, 2 * KEYS)
-    q_shape = (parts, agents * local, width + LANES) if blocked else (rows, width + LANES)
+    place = lax.axis_index("plane").astype(jnp.int32).reshape(1)
+    deep = width + LANES
+    if cross:
+        q_shapes = [(tiles * cores, agents * local, deep)] * 2
+    else:
+        q_shapes = [(parts, agents * local, deep) if blocked else (rows, deep)]
     q = call(
-        functools.partial(query_kernel, agents, steps, local, blocked),
-        [struct(q_shape, BF16)],
-        [mid, gain_space[None], wq_space, meta],
+        functools.partial(query_kernel, agents, steps, local, blocked, cross),
+        [struct(shape, BF16) for shape in q_shapes],
+        [mid, gain_space[None], wq_space, meta] + ([place] if cross else []),
+        smem=(4,),
         scratch=[pltpu.VMEM((rows, width), BF16)],
         flops=2 * rows * width * width,
     )
-    if not blocked:
-        q = to_blocks(q, agents, steps, local)
+    if cross:
+        turn = [(p, PLANES - 1 - p) for p in range(PLANES)]
+        q = [q[0], lax.ppermute(q[1], "plane", turn)]
+    else:
+        q = [q if blocked else to_blocks(q, agents, steps, local)]
     swap = [(h, HALVES - 1 - h) for h in range(HALVES)]
     other = lax.ppermute(own, "half", swap)
     total = rows // local
     block = max(COLS, local) if rows % max(COLS, local) == 0 else rows
-    q, own = lax.optimization_barrier((q, own))
+    *q, own = lax.optimization_barrier((*q, own))
     own = call(
         functools.partial(keys_kernel, local, block),
         [struct((local, total, 2 * KEYS), BF16)],
         [own],
         flops=SHADOW * rows * block * 2 * KEYS,
     )
-    q = lax.all_to_all(q, spread, split_axis=0, concat_axis=0, tiled=True)
+    if cross:
+        q = [jnp.concatenate(q, axis=1)]
+    within = ("tile", "core") if cross else spread
+    q = lax.all_to_all(q[0], within, split_axis=0, concat_axis=0, tiled=True)
 
     pair = LANES // total if total < LANES and local % (LANES // total) == 0 else 1
     mix = call(
-        functools.partial(space_kernel, local, block, tiles, pair),
-        [struct((rows, width), BF16)],
-        [q.reshape(rows, width + LANES), own, other],
+        functools.partial(space_kernel, local, block, tiles, pair, PLANES if cross else 1),
+        [struct((tiles, PLANES, rows // (tiles * PLANES), width) if cross else (rows, width), BF16)],
+        [q if cross else q.reshape(rows, deep), own, other] + ([place] if cross else []),
+        smem=(3,) if cross else (),
         scratch=[
             pltpu.VMEM((local, total, width), BF16),
             pltpu.VMEM((local, total, 2 * KEYS), BF16),
@@ -441,10 +487,10 @@
 
 def solution(mesh):
     tiles, members = mesh.devices.shape
-    split = Mesh(
-        mesh.devices.reshape(tiles, HALVES, members // HALVES), ("tile", "half", "rest")
-    )
-    states = P("tile", ("half", "rest"), None, None)
+    cores = CORES if members % (HALVES * CORES) == 0 else 1
+    shape = (tiles, HALVES, members // HALVES // cores, cores)
+    split = Mesh(mesh.devices.reshape(shape), ("tile", "half", "plane", "core"))
+    states = P("tile", ("half", "plane", "core"), None, None)
     listing = P("tile", None)
     return jax.shard_map(
         per_device,

time: 89.7 us -> 98.6 us (1.099)
  waiting for transfers between devices: 33.9 us -> 38.3 us
  starting transfers between devices: 13.4 us -> 16 us
  local copies, waits for them, and re-layouts: 1.32 us -> 3.17 us
  Pallas kernels: 21.6 us -> 20.4 us
  other arithmetic: 0.25 us -> 1.43 us
    ppermute x0 -> x1, waiting for transfers between devices: none -> 17.4 us  [per_device(): q = [q[0], lax.ppermute(q[1], 'plane', turn)]]
    ppermute x1, waiting for transfers between devices: 17.1 us -> 0.01 us  [per_device(): other = lax.ppermute(own, 'half', swap)]
    all_to_all x1, waiting for transfers between devices: 10.2 us -> 14.8 us  [per_device(): q = lax.all_to_all(q[0], within, split_axis=0, concat_axis=0, tiled=True)]
    ppermute x0 -> x1, starting transfers between devices: none -> 1.93 us  [per_device(): q = [q[0], lax.ppermute(q[1], 'plane', turn)]]
    unnamed x16 -> x20, local copies, waits for them, and re-layouts: 1.25 us -> 3.09 us
    pallas_call x5, Pallas kernels: 21.6 us -> 20.4 us  [call(): pl.pallas_call(kernel, out_shape=list(shapes), in_specs=specs(len(args),...]
    concatenate x0 -> x1, other arithmetic: none -> 1.18 us  [per_device(): q = [jnp.concatenate(q, axis=1)]]
  transfers between devices with their start and end apart: 3 -> 4, of which waited for: 3 -> 3; matrix products, arithmetic and copies ran while one was open for 0% -> 2% of each run, Pallas kernels for 4% -> 3%
where the time goes in v6:
time: 98.6 us; the launch traced here: 98.1 us
  waiting for transfers between devices  38.3 us (39%)
  Pallas kernels  20.4 us (21%)
  blocking collectives  18.8 us (19%)
  starting transfers between devices  16 us (16%)
  local copies, waits for them, and re-layouts  3.17 us (3%)
  other arithmetic  1.43 us (1%)
    pallas_call x5, Pallas kernels, call(): pl.pallas_call(kernel, out_shape=list(shapes), in_specs=specs(len(args),...  20.4 us
    all_to_all x1, blocking collectives, per_device(): lax.all_to_all(mix.reshape(parts, agents * local, width), spread, split_a...  18.8 us
    ppermute x1, waiting for transfers between devices, per_device(): q = [q[0], lax.ppermute(q[1], 'plane', turn)]  17.4 us
    all_to_all x1, waiting for transfers between devices, per_device(): q = lax.all_to_all(q[0], within, split_axis=0, concat_axis=0, tiled=True)  14.8 us
    all_to_all x1, starting transfers between devices, per_device(): own = lax.all_to_all(kv, spread, split_axis=0, concat_axis=0, tiled=True)  6.37 us
    all_to_all x1, waiting for transfers between devices, per_device(): own = lax.all_to_all(kv, spread, split_axis=0, concat_axis=0, tiled=True)  6.12 us
    all_to_all x1, starting transfers between devices, per_device(): q = lax.all_to_all(q[0], within, split_axis=0, concat_axis=0, tiled=True)  5.1 us
    unnamed x20, local copies, waits for them, and re-layouts  3.09 us
  transfers between devices with their start and end apart: 4, of which 3 were waited for; matrix products, arithmetic and copies ran while one was open for 2% of the time, Pallas kernels for 3%

profile of v6, /device:TPU:0, one launch (start us, length us, event | category | flops | bytes accessed | tf_op | source)
XLA Modules:
  0.0 98.1 jit_solution(3934406426577021412)
XLA Ops:
  0.0 0.0 copy-start.7
  0.0 0.0 copy-start.8
  0.0 0.0 copy-start.9
  0.0 0.0 copy-start.5
  0.0 0.0 copy-start.6
  0.0 10.7 %shard_map.118 = (bf16[512,1024]{1,0:T(8,128)(2,1)}, bf16[16,32,512]{2,1,0:T(8,128)(2,1)}) custom-call(bf16[512,1024]{1,0:T(8,128)(2,1)} %bitcast.20, f32[1,1024]{1,0:T(1,128)} %bitcast.21, f32[1,1024]{1,0:T(1,128)} %bitcast.18, bf16[1024,1024]{1,0:T(8,128)(2,1)} %wq_hbm.1, bf16[1024,512]{1,0:T(8,128)(2,1)} %wkv_hbm.1, bf16[1024,1024]{1,0:T(8,128)(2,1)} %wo_hbm.1, ...), custom_call_target="tpu_custom_call" | custom-call | flops 3221225472 | bytes 8921088 | tf_op jit(solution)/shard_map/pallas_call | solution.py:346
  10.7 6.4 %all-to-all-start = ((bf16[16,32,512]{2,1,0:T(8,128)(2,1)}), bf16[16,32,512]{2,1,0:T(8,128)(2,1)}, u32[]{:S(2)}, u32[]{:S(2)}) async-start(bf16[16,32,512]{2,1,0:T(8,128)(2,1)} %get-tuple-element.15), calls=%async_computation | async-start | bytes 1048576 | tf_op jit(solution)/shard_map/all_to_all | solution.py:423
  17.1 0.0 copy-done.7
  17.1 0.1 slice_bitcast_fusion.1
  17.1 0.1 broadcast_select_fusion
  17.2 0.0 copy-done.8
  17.2 0.0 copy-done.9
  17.2 0.1 select_reduce_fusion
  17.3 0.1 pad_add_fusion
  17.4 0.0 copy-done.5
  17.4 0.0 copy-done.6
  17.4 0.0 copy-start.1
  17.4 1.2 %copy-done.1 = bf16[512,1024]{1,0:T(8,128)(2,1)S(1)} copy-done((bf16[512,1024]{1,0:T(8,128)(2,1)S(1)}, bf16[512,1024]{1,0:T(8,128)(2,1)}, u32[]{:S(2)}) %copy-start.1) | copy-done | bytes 1048600
  18.6 1.4 %shard_map.119 = (bf16[8,32,1152]{2,1,0:T(8,128)(2,1)S(1)}, bf16[8,32,1152]{2,1,0:T(8,128)(2,1)S(1)}) custom-call(bf16[512,1024]{1,0:T(8,128)(2,1)S(1)} %copy-done.1, f32[1,1024]{1,0:T(1,128)S(1)} %bitcast.19, bf16[1024,1024]{1,0:T(8,128)(2,1)S(1)} %copy-done.5, f32[8,128]{1,0:T(8,128)S(1)} %broadcast_in_dim.33.meta, s32[1]{0:T(128)} %bitcast.8.rest_0_.refs_0_), custom_call_target="tpu_custom_call" | custom-call | flops 1073741824 | bytes 4333572 | tf_op jit(solution)/shard_map/pallas_call | solution.py:346
  20.1 1.9 %collective-permute-start = (bf16[8,32,1152]{2,1,0:T(8,128)(2,1)S(1)}, bf16[8,32,1152]{2,1,0:T(8,128)(2,1)S(1)}, u32[]{:S(2)}, u32[]{:S(2)}) collective-permute-start(bf16[8,32,1152]{2,1,0:T(8,128)(2,1)S(1)} %get-tuple-element.14), channel_id=1, source_target_pairs={{0,2},{2,0},{1,3},{3,1},{4,6},{6,4},{5,7},{7,5},{8,10},{10,8},{9,1... | collective-permute-start | bytes 1769480 | tf_op jit(solution)/shard_map/ppermute | solution.py:441
  22.0 6.1 %all-to-all-done = bf16[16,32,512]{2,1,0:T(8,128)(2,1)} async-done(((bf16[16,32,512]{2,1,0:T(8,128)(2,1)}), bf16[16,32,512]{2,1,0:T(8,128)(2,1)}, u32[]{:S(2)}, u32[]{:S(2)}) %all-to-all-start) | async-done | bytes 524320 | tf_op jit(solution)/shard_map/all_to_all | solution.py:423
  28.1 2.6 %collective-permute-start.1 = (bf16[512,512]{1,0:T(8,128)(2,1)}, bf16[512,512]{1,0:T(8,128)(2,1)}, u32[]{:S(2)}, u32[]{:S(2)}) collective-permute-start(bf16[512,512]{1,0:T(8,128)(2,1)} %bitcast.9.source), channel_id=1, source_target_pairs={{0,4},{4,0},{1,5},{5,1},{2,6},{6,2},{3,7},{7,3},{8,12},{12,8},{9,1... | collective-permute-start | bytes 1572872 | tf_op jit(solution)/shard_map/ppermute | solution.py:445
  30.7 17.4 %collective-permute-done = bf16[8,32,1152]{2,1,0:T(8,128)(2,1)S(1)} collective-permute-done((bf16[8,32,1152]{2,1,0:T(8,128)(2,1)S(1)}, bf16[8,32,1152]{2,1,0:T(8,128)(2,1)S(1)}, u32[]{:S(2)}, u32[]{:S(2)}) %collective-permute-start) | collective-permute-done | bytes 589856 | tf_op jit(solution)/shard_map/ppermute | solution.py:441
  48.2 1.2 %pad_maximum_fusion = bf16[8,64,1152]{2,1,0:T(8,128)(2,1)} fusion(bf16[8,32,1152]{2,1,0:T(8,128)(2,1)S(1)} %collective-permute-done, bf16[8,32,1152]{2,1,0:T(8,128)(2,1)S(1)} %get-tuple-element.16), kind=kLoop, calls=%fused_computation | loop fusion | flops 2359296 | bytes 2359296 | tf_op jit(solution)/shard_map/concatenate | solution.py:456
  49.3 5.1 %all-to-all-start.1 = ((bf16[8,64,1152]{2,1,0:T(8,128)(2,1)}), bf16[8,64,1152]{2,1,0:T(8,128)(2,1)}, u32[]{:S(2)}, u32[]{:S(2)}) async-start(bf16[8,64,1152]{2,1,0:T(8,128)(2,1)} %pad_maximum_fusion), calls=%async_computation.1 | async-start | bytes 2359296 | tf_op jit(solution)/shard_map/all_to_all | solution.py:458
  54.4 1.3 %shard_map.120.own = bf16[8,64,512]{2,1,0:T(8,128)(2,1)S(1)} custom-call(bf16[512,512]{1,0:T(8,128)(2,1)} %bitcast.9.source), custom_call_target="tpu_custom_call" | custom-call | flops 671088640000 | bytes 1048576 | tf_op jit(solution)/shard_map/pallas_call | solution.py:346
  55.8 0.0 copy-start.3
  55.8 0.8 copy-done.3
  56.6 0.0 copy-start
  56.6 0.0 copy-start.2
  56.6 0.0 collective-permute-done.1.other_in
  56.6 14.8 %all-to-all-done.1.q_in = bf16[8,64,1152]{2,1,0:T(8,128)(2,1)} async-done(((bf16[8,64,1152]{2,1,0:T(8,128)(2,1)}), bf16[8,64,1152]{2,1,0:T(8,128)(2,1)}, u32[]{:S(2)}, u32[]{:S(2)}) %all-to-all-start.1) | async-done | bytes 1179680 | tf_op jit(solution)/shard_map/all_to_all | solution.py:458
  71.4 0.0 copy-start.4
  71.4 1.0 %copy-done.4 = bf16[8,64,512]{2,1,0:T(8,128)(2,1)S(1)} copy-done((bf16[8,64,512]{2,1,0:T(8,128)(2,1)S(1)}, bf16[8,64,512]{2,1,0:T(8,128)(2,1)}, u32[]{:S(2)}) %copy-start.4) | copy-done | bytes 524312
  72.4 4.7 %shard_map.121 = bf16[4,2,64,1024]{3,2,1,0:T(8,128)(2,1)S(1)} custom-call(bf16[8,64,1152]{2,1,0:T(8,128)(2,1)} %all-to-all-done.1.q_in, bf16[8,64,512]{2,1,0:T(8,128)(2,1)S(1)} %copy-done.4, bf16[512,512]{1,0:T(8,128)(2,1)} %collective-permute-done.1.other_in, s32[1]{0:T(128)} %bitcast.8.rest_0_.refs_0_), custom_call_target="tpu_custom_call" | custom-call | flops 268435456 | bytes 3276804 | tf_op jit(solution)/shard_map/pallas_call | solution.py:346
  77.1 18.8 %all_to_all.15 = bf16[16,32,1024]{2,1,0:T(8,128)(2,1)S(1)} all-to-all(bf16[16,32,1024]{2,1,0:T(8,128)(2,1)S(1)} %bitcast.17), channel_id=1, replica_groups=mesh['tile'=4,'half'=2,'plane'=2,'core'=2] {'tile','plane','core'}, dimensions={0} | all-to-all | bytes 2097152 | tf_op jit(solution)/shard_map/all_to_all | solution.py:474
  95.9 0.0 copy-done
  95.9 0.0 copy-done.2
  95.9 2.2 %shard_map.122 = bf16[512,1024]{1,0:T(8,128)(2,1)} custom-call(bf16[512,1024]{1,0:T(8,128)(2,1)S(1)} %bitcast.16, bf16[512,1024]{1,0:T(8,128)(2,1)S(1)} %copy-done.2, bf16[1024,1024]{1,0:T(8,128)(2,1)S(1)} %copy-done), custom_call_target="tpu_custom_call" | custom-call | flops 1073741824 | bytes 5242880 | tf_op jit(solution)/shard_map/pallas_call | solution.py:346
  (2 shorter events, 0.0 us)
Async XLA Ops:
  0.0 17.1 %copy-start.7 = (s32[1,32]{1,0:T(1,128)S(1)}, s32[1,32]{1,0:T(1,128)}, u32[]{:S(2)}) copy-start(s32[1,32]{1,0:T(1,128)} %param.23) | copy-start | bytes 388
  0.0 17.2 %copy-start.8 = (s32[1,4]{1,0:T(1,128)S(1)}, s32[1,4]{1,0:T(1,128)}, u32[]{:S(2)}) copy-start(s32[1,4]{1,0:T(1,128)} %param.22) | copy-start | bytes 52
  0.0 17.2 %copy-start.9 = (s32[1,4]{1,0:T(1,128)S(1)}, s32[1,4]{1,0:T(1,128)}, u32[]{:S(2)}) copy-start(s32[1,4]{1,0:T(1,128)} %param.21) | copy-start | bytes 52
  0.0 17.4 %copy-start.5 = (bf16[1024,1024]{1,0:T(8,128)(2,1)S(1)}, bf16[1024,1024]{1,0:T(8,128)(2,1)}, u32[]{:S(2)}) copy-start(bf16[1024,1024]{1,0:T(8,128)(2,1)} %wq.1) | copy-start | bytes 6291460
  0.0 17.4 %copy-start.6 = (f32[1024]{0:T(1024)S(1)}, f32[1024]{0:T(1024)}, u32[]{:S(2)}) copy-start(f32[1024]{0:T(1024)} %param.17) | copy-start | bytes 12292
  10.7 17.4 %all-to-all-start = ((bf16[16,32,512]{2,1,0:T(8,128)(2,1)}), bf16[16,32,512]{2,1,0:T(8,128)(2,1)}, u32[]{:S(2)}, u32[]{:S(2)}) async-start(bf16[16,32,512]{2,1,0:T(8,128)(2,1)} %get-tuple-element.15), calls=%async_computation | async-start | bytes 1048576 | tf_op jit(solution)/shard_map/all_to_all | solution.py:423
  17.4 1.2 %copy-start.1 = (bf16[512,1024]{1,0:T(8,128)(2,1)S(1)}, bf16[512,1024]{1,0:T(8,128)(2,1)}, u32[]{:S(2)}) copy-start(bf16[512,1024]{1,0:T(8,128)(2,1)} %get-tuple-element.12.mid) | copy-start | bytes 3145732
  20.1 28.1 %collective-permute-start = (bf16[8,32,1152]{2,1,0:T(8,128)(2,1)S(1)}, bf16[8,32,1152]{2,1,0:T(8,128)(2,1)S(1)}, u32[]{:S(2)}, u32[]{:S(2)}) collective-permute-start(bf16[8,32,1152]{2,1,0:T(8,128)(2,1)S(1)} %get-tuple-element.14), channel_id=1, source_target_pairs={{0,2},{2,0},{1,3},{3,1},{4,6},{6,4},{5,7},{7,5},{8,10},{10,8},{9,1... | collective-permute-start | bytes 1769480 | tf_op jit(solution)/shard_map/ppermute | solution.py:441
  28.1 28.5 %collective-permute-start.1 = (bf16[512,512]{1,0:T(8,128)(2,1)}, bf16[512,512]{1,0:T(8,128)(2,1)}, u32[]{:S(2)}, u32[]{:S(2)}) collective-permute-start(bf16[512,512]{1,0:T(8,128)(2,1)} %bitcast.9.source), channel_id=1, source_target_pairs={{0,4},{4,0},{1,5},{5,1},{2,6},{6,2},{3,7},{7,3},{8,12},{12,8},{9,1... | collective-permute-start | bytes 1572872 | tf_op jit(solution)/shard_map/ppermute | solution.py:445
  49.3 22.0 %all-to-all-start.1 = ((bf16[8,64,1152]{2,1,0:T(8,128)(2,1)}), bf16[8,64,1152]{2,1,0:T(8,128)(2,1)}, u32[]{:S(2)}, u32[]{:S(2)}) async-start(bf16[8,64,1152]{2,1,0:T(8,128)(2,1)} %pad_maximum_fusion), calls=%async_computation.1 | async-start | bytes 2359296 | tf_op jit(solution)/shard_map/all_to_all | solution.py:458
  55.8 0.8 copy-start.3
  56.6 39.3 %copy-start = (bf16[1024,1024]{1,0:T(8,128)(2,1)S(1)}, bf16[1024,1024]{1,0:T(8,128)(2,1)}, u32[]{:S(2)}) copy-start(bf16[1024,1024]{1,0:T(8,128)(2,1)} %wo.1) | copy-start | bytes 6291460
  56.6 39.3 %copy-start.2 = (bf16[512,1024]{1,0:T(8,128)(2,1)S(1)}, bf16[512,1024]{1,0:T(8,128)(2,1)}, u32[]{:S(2)}) copy-start(bf16[512,1024]{1,0:T(8,128)(2,1)} %get-tuple-element.12.mid) | copy-start | bytes 3145732
  71.4 1.0 %copy-start.4 = (bf16[8,64,512]{2,1,0:T(8,128)(2,1)S(1)}, bf16[8,64,512]{2,1,0:T(8,128)(2,1)}, u32[]{:S(2)}) copy-start(bf16[8,64,512]{2,1,0:T(8,128)(2,1)} %copy-done.3) | copy-start | bytes 1572868

commit v7 on v4

--- a/solution.py
+++ b/solution.py
@@ -22,6 +22,7 @@
 COLS = 256
 HALVES = 2
 DEPTH = 2
+SHADOW = 400
 MIB = 1024 * 1024
 F32 = jnp.float32
 BF16 = jnp.bfloat16
@@ -57,7 +58,7 @@
 
 def time_kernel(
     agents, steps, local, blocked,
-    hist_hbm, gain_t, gain_s, wq_hbm, wkv_hbm, wo_hbm, wkv2_hbm,
+    hist_hbm, gain_t, gain_s, wq_hbm, wkv_hbm, wo_hbm, wkv2_hbm, neighbours, nbr_valid, alive,
     mid_hbm, kv_out,
     hist, wq, wkv, wo, wkv2, normed, query, keyval, mix, mid, hist_sems, wq_sems, sems, out_sem,
 ):
@@ -148,10 +149,19 @@
             kv_out[:, :, cols] = to_blocks(result, agents, steps, local).astype(BF16)
         else:
             kv_out[:, cols] = result.astype(BF16)
+    lane = lax.broadcasted_iota(jnp.int32, (1, LANES), 1)
+    notes = jnp.zeros((1, LANES), F32)
+    for i in range(alive.shape[1]):
+        notes = jnp.where(lane == i, alive[0, i].astype(F32), notes)
+    for i in range(neighbours.shape[1]):
+        listed = lane == alive.shape[1] + neighbours[0, i]
+        notes = notes + jnp.where(listed, nbr_valid[0, i].astype(F32), 0.0)
+    notes = jnp.broadcast_to(notes, (kv_out.shape[-2], LANES)).astype(BF16)
+    kv_out[..., 2 * KEYS :] = jnp.broadcast_to(notes, kv_out.shape[:-1] + (LANES,))
     keep.wait()
 
 
-def query_kernel(agents, steps, local, blocked, mid, gain, wq, meta, out, second):
+def query_kernel(agents, steps, local, blocked, mid, gain, wq, out, second):
     width = mid.shape[1]
     for a in range(agents):
         part = pl.ds(a * steps, steps)
@@ -163,11 +173,6 @@
             out[:, :, cols] = to_blocks(result, agents, steps, local).astype(BF16)
         else:
             out[:, cols] = result.astype(BF16)
-    lines = jnp.broadcast_to(meta[0:1, :], (out.shape[-2], LANES)).astype(BF16)
-    if blocked:
-        out[:, :, width:] = jnp.broadcast_to(lines[None], (out.shape[0], out.shape[1], LANES))
-    else:
-        out[:, width:] = lines
 
 
 def one_hot(shape, group, local, dtype=BF16):
@@ -177,28 +182,30 @@
     return jnp.where(col == wanted, 1.0, 0.0).astype(dtype)
 
 
-def key_weights(notes, local, tiles, total):
-    rows = notes.shape[0]
+def weight_kernel(local, tiles, half, kv_in, out):
+    rows = kv_in.shape[0]
+    total = rows // local
     group = total // tiles
+    notes = kv_in[:, 2 * KEYS :]
     shape = (total, rows)
     row, col = (lax.broadcasted_iota(jnp.int32, shape, d) for d in range(2))
     pick = jnp.where(col == row * local, 1.0, 0.0).astype(BF16)
     lines = jnp.dot(pick, notes, preferred_element_type=F32).astype(BF16)
-    shape = (LANES, HALVES * total)
-    lane, key = (lax.broadcasted_iota(jnp.int32, shape, d) for d in range(2))
-    half, tile, agent = key // total, key % total // group, key % group
+    shape = (HALVES * total, LANES)
+    key, lane = (lax.broadcasted_iota(jnp.int32, shape, d) for d in range(2))
+    side, tile, agent = (key // total + half[0]) % HALVES, key % total // group, key % group
     spread = jnp.where(lane == HALVES * group + tile, 1.0, 0.0).astype(BF16)
-    listed = jnp.dot(lines, spread, preferred_element_type=F32)
-    spread = jnp.where(lane == half * group + agent, 1.0, 0.0).astype(BF16)
-    alive = jnp.dot(lines, spread, preferred_element_type=F32)
-    shape = (total, HALVES * total)
-    row, key = (lax.broadcasted_iota(jnp.int32, shape, d) for d in range(2))
-    first = row == key % total // group * group
-    alive = jnp.sum(jnp.where(first, alive, 0.0), axis=0, keepdims=True)
-    return listed * alive
-
-
-def by_steps(source, target, local, block, total, offset=0):
+    listed = lax.dot_general(spread, lines, ROWS_BY_COLS, preferred_element_type=F32)
+    spread = jnp.where(lane == side * group + agent, 1.0, 0.0).astype(BF16)
+    alive = lax.dot_general(spread, lines, ROWS_BY_COLS, preferred_element_type=F32)
+    shape = (HALVES * total, total)
+    key, query = (lax.broadcasted_iota(jnp.int32, shape, d) for d in range(2))
+    first = query == key % total // group * group
+    alive = jnp.sum(jnp.where(first, alive, 0.0), axis=1, keepdims=True)
+    out[...] = listed * alive
+
+
+def by_steps(source, target, local, block):
     rows, width = source.shape[0], target.shape[-1]
     group = block // local
     order = one_hot((block, block), group, local)
@@ -208,26 +215,23 @@
             piece = source[b * block : (b + 1) * block, cols]
             if local > 1:
                 piece = jnp.dot(order, piece, preferred_element_type=F32).astype(BF16)
-            at = offset + b * group
-            target[:, at : at + group, cols] = piece.reshape(local, group, piece.shape[1])
+            target[:, b * group : (b + 1) * group, cols] = piece.reshape(local, group, piece.shape[1])
 
 
 def keys_kernel(local, block, source, out):
-    by_steps(source, out, local, block, out.shape[1])
+    by_steps(source, out, local, block)
 
 
 def space_kernel(
-    local, block, tiles, pair, q_in, own, other_in, out, query, other, mix
+    local, block, pair, q_in, own, other, weights, out, query, mix
 ):
     rows, width = out.shape
     group = block // local
     total = rows // local
     columns = pair * total
-    by_steps(q_in, query, local, block, total)
-    by_steps(other_in, other, local, block, total)
-    weight = key_weights(q_in[:, width:], local, tiles, total)
+    by_steps(q_in, query, local, block)
     together = GROUPS if columns <= LANES else 1
-    weight = jnp.concatenate([weight.T] * (pair * together), axis=1)
+    weight = jnp.concatenate([weights[...]] * (pair * together), axis=1)
     valid = weight > 0
     lane = lax.broadcasted_iota(jnp.int32, (HEAD_DIM, columns), 1) // total
 
@@ -302,19 +306,21 @@
         out[:, cols] = (mid[:, cols].astype(F32) + projected).astype(BF16)
 
 
-def call(kernel, shapes, args, hbm=(), hbm_out=(), scratch=(), flops=0, mib=16):
+def call(kernel, shapes, args, hbm=(), hbm_out=(), smem=(), scratch=(), flops=0, mib=16):
     moved = sum(a.size * a.dtype.itemsize for a in args)
     moved += sum(s.size * s.dtype.itemsize for s in shapes)
 
-    def specs(count, far):
+    def specs(count, far, scalars=()):
+        spaces = [pl.ANY if i in far else pltpu.VMEM for i in range(count)]
         return [
-            pl.BlockSpec(memory_space=pl.ANY if i in far else pltpu.VMEM) for i in range(count)
+            pl.BlockSpec(memory_space=pltpu.SMEM if i in scalars else space)
+            for i, space in enumerate(spaces)
         ]
 
     results = pl.pallas_call(
         kernel,
         out_shape=list(shapes),
-        in_specs=specs(len(args), hbm),
+        in_specs=specs(len(args), hbm, smem),
         out_specs=specs(len(shapes), hbm_out),
         scratch_shapes=list(scratch),
         compiler_params=pltpu.CompilerParams(vmem_limit_bytes=mib * MIB),
@@ -347,12 +353,15 @@
     struct = jax.ShapeDtypeStruct
 
     hist = histories.reshape(rows, width)
-    kv_shape = (parts, agents * local, 2 * KEYS) if blocked else (rows, 2 * KEYS)
+    deep = 2 * KEYS + LANES
+    kv_shape = (parts, agents * local, deep) if blocked else (rows, deep)
     mid, kv = call(
         functools.partial(time_kernel, agents, steps, local, blocked),
         [struct((rows, width), BF16), struct(kv_shape, BF16)],
-        [hist, gain_time[None], gain_space[None], wq_time, wkv_time, wo_time, wkv_space],
+        [hist, gain_time[None], gain_space[None], wq_time, wkv_time, wo_time, wkv_space]
+        + [neighbours, nbr_valid, agent_valid],
         hbm=(0, 3, 4, 5, 6),
+        smem=(7, 8, 9),
         hbm_out=(0,),
         scratch=[
             pltpu.VMEM((rows, width), BF16),
@@ -375,50 +384,46 @@
     )
     if not blocked:
         kv = to_blocks(kv, agents, steps, local)
-    listed = jnp.sum(
-        jnp.where(
-            neighbours[0][:, None] == jnp.arange(tiles)[None, :], nbr_valid[0][:, None], 0
-        ),
-        axis=0,
-    )
-    group = rest * agents
-    alive = jnp.where(lax.axis_index("half") == 0, agent_valid[0], jnp.roll(agent_valid[0], -group))
-    meta = jnp.concatenate([alive, listed])
-    meta = jnp.pad(meta, (0, LANES - meta.shape[0])).astype(F32)
-    meta = jnp.broadcast_to(meta[None], (8, LANES))
-    own = lax.all_to_all(kv, spread, split_axis=0, concat_axis=0, tiled=True)
-    own = own.reshape(rows, 2 * KEYS)
-    q_shape = (parts, agents * local, width + LANES) if blocked else (rows, width + LANES)
+    kv = lax.all_to_all(kv, spread, split_axis=0, concat_axis=0, tiled=True)
+    kv = kv.reshape(rows, deep)
+    q_shape = (parts, agents * local, width) if blocked else (rows, width)
     q = call(
         functools.partial(query_kernel, agents, steps, local, blocked),
         [struct(q_shape, BF16)],
-        [mid, gain_space[None], wq_space, meta],
+        [mid, gain_space[None], wq_space],
         scratch=[pltpu.VMEM((rows, width), BF16)],
         flops=2 * rows * width * width,
     )
     if not blocked:
         q = to_blocks(q, agents, steps, local)
-    swap = [(h, HALVES - 1 - h) for h in range(HALVES)]
-    other = lax.ppermute(own, "half", swap)
     total = rows // local
     block = max(COLS, local) if rows % max(COLS, local) == 0 else rows
     own = call(
         functools.partial(keys_kernel, local, block),
         [struct((local, total, 2 * KEYS), BF16)],
-        [own],
+        [kv],
         flops=2 * rows * block * 2 * KEYS,
     )
-    q, own = lax.optimization_barrier((q, own))
+    swap = [(h, HALVES - 1 - h) for h in range(HALVES)]
+    other = lax.ppermute(own, "half", swap)
+    q, own, kv = lax.optimization_barrier((q, own, kv))
+    half = lax.axis_index("half").astype(jnp.int32).reshape(1)
+    weight = call(
+        functools.partial(weight_kernel, local, tiles),
+        [struct((HALVES * total, total), F32)],
+        [half, kv],
+        smem=(0,),
+        flops=SHADOW * rows * block * 2 * KEYS,
+    )
     q = lax.all_to_all(q, spread, split_axis=0, concat_axis=0, tiled=True)
 
     pair = LANES // total if total < LANES and local % (LANES // total) == 0 else 1
     mix = call(
-        functools.partial(space_kernel, local, block, tiles, pair),
+        functools.partial(space_kernel, local, block, pair),
         [struct((rows, width), BF16)],
-        [q.reshape(rows, width + LANES), own, other],
+        [q.reshape(rows, width), own, other, weight],
         scratch=[
             pltpu.VMEM((local, total, width), BF16),
-            pltpu.VMEM((local, total, 2 * KEYS), BF16),
             pltpu.VMEM((local, total, width), BF16),
         ],
         flops=8 * rows * total * width,

time: 86.3 us -> 86.9 us (level)
  local copies, waits for them, and re-layouts: 1.32 us -> 2.82 us
  blocking collectives: 20 us -> 18.8 us
    all_to_all x1, waiting for transfers between devices: 3.12 us -> 7.76 us  [per_device(): q = lax.all_to_all(q, spread, split_axis=0, concat_axis=0, tiled=True)]
    ppermute x1, waiting for transfers between devices: 23 us -> 18.7 us  [per_device(): other = lax.ppermute(own, 'half', swap)]
    unnamed x16 -> x10, local copies, waits for them, and re-layouts: 1.25 us -> 2.82 us
    all_to_all x1, blocking collectives: 20 us -> 18.8 us  [per_device(): lax.all_to_all(mix.reshape(parts, agents * local, width), spread, split_a...]
    pallas_call x5 -> x6, Pallas kernels: 19 us -> 18.9 us  [call(): pl.pallas_call(kernel, out_shape=list(shapes), in_specs=specs(len(args),...]
where the time goes in v7:
time: 86.9 us; the launch traced here: 86.4 us
  waiting for transfers between devices  33.2 us (38%)
  Pallas kernels  18.9 us (22%)
  blocking collectives  18.8 us (22%)
  starting transfers between devices  12.6 us (14%)
  local copies, waits for them, and re-layouts  2.82 us (3%)
    pallas_call x6, Pallas kernels, call(): pl.pallas_call(kernel, out_shape=list(shapes), in_specs=specs(len(args),...  18.9 us
    all_to_all x1, blocking collectives, per_device(): lax.all_to_all(mix.reshape(parts, agents * local, width), spread, split_a...  18.8 us
    ppermute x1, waiting for transfers between devices, per_device(): other = lax.ppermute(own, 'half', swap)  18.7 us
    all_to_all x1, waiting for transfers between devices, per_device(): q = lax.all_to_all(q, spread, split_axis=0, concat_axis=0, tiled=True)  7.76 us
    all_to_all x1, waiting for transfers between devices, per_device(): kv = lax.all_to_all(kv, spread, split_axis=0, concat_axis=0, tiled=True)  6.71 us
    all_to_all x1, starting transfers between devices, per_device(): kv = lax.all_to_all(kv, spread, split_axis=0, concat_axis=0, tiled=True)  6.29 us
    all_to_all x1, starting transfers between devices, per_device(): q = lax.all_to_all(q, spread, split_axis=0, concat_axis=0, tiled=True)  3.65 us
    unnamed x10, local copies, waits for them, and re-layouts  2.82 us
  transfers between devices with their start and end apart: 3, of which 3 were waited for; matrix products, arithmetic and copies ran while one was open for 0% of the time, Pallas kernels for 3%

profile of v7, /device:TPU:0, one launch (start us, length us, event | category | flops | bytes accessed | tf_op | source)
XLA Modules:
  0.0 86.4 jit_solution(8223276957523291261)
XLA Ops:
  0.0 0.0 copy-start.4
  0.0 10.7 %shard_map.118 = (bf16[512,1024]{1,0:T(8,128)(2,1)}, bf16[16,32,640]{2,1,0:T(8,128)(2,1)}) custom-call(bf16[512,1024]{1,0:T(8,128)(2,1)} %bitcast.16, f32[1,1024]{1,0:T(1,128)} %bitcast.17, f32[1,1024]{1,0:T(1,128)} %bitcast.14, bf16[1024,1024]{1,0:T(8,128)(2,1)} %wq_hbm.1, bf16[1024,512]{1,0:T(8,128)(2,1)} %wkv_hbm.1, bf16[1024,1024]{1,0:T(8,128)(2,1)} %wo_hbm.1, ...), custom_call_target="tpu_custom_call" | custom-call | flops 3221225472 | bytes 9052320 | tf_op jit(solution)/shard_map/pallas_call | solution.py:320
  10.7 6.3 %all-to-all-start = ((bf16[16,32,640]{2,1,0:T(8,128)(2,1)}), bf16[16,32,640]{2,1,0:T(8,128)(2,1)S(1)}, u32[]{:S(2)}, u32[]{:S(2)}) async-start(bf16[16,32,640]{2,1,0:T(8,128)(2,1)} %get-tuple-element.11), calls=%async_computation | async-start | bytes 1310720 | tf_op jit(solution)/shard_map/all_to_all | solution.py:387
  17.0 0.0 copy-done.4
  17.0 0.0 copy-start
  17.1 1.2 %copy-done = bf16[512,1024]{1,0:T(8,128)(2,1)S(1)} copy-done((bf16[512,1024]{1,0:T(8,128)(2,1)S(1)}, bf16[512,1024]{1,0:T(8,128)(2,1)}, u32[]{:S(2)}) %copy-start) | copy-done | bytes 1048600
  18.3 0.0 copy-start.2
  18.3 1.6 %copy-done.2 = bf16[1024,1024]{1,0:T(8,128)(2,1)S(1)} copy-done((bf16[1024,1024]{1,0:T(8,128)(2,1)S(1)}, bf16[1024,1024]{1,0:T(8,128)(2,1)}, u32[]{:S(2)}) %copy-start.2) | copy-done | bytes 2097176
  19.9 2.4 %shard_map.119 = bf16[16,32,1024]{2,1,0:T(8,128)(2,1)} custom-call(bf16[512,1024]{1,0:T(8,128)(2,1)S(1)} %copy-done, f32[1,1024]{1,0:T(1,128)S(1)} %bitcast.15, bf16[1024,1024]{1,0:T(8,128)(2,1)S(1)} %copy-done.2), custom_call_target="tpu_custom_call" | custom-call | flops 1073741824 | bytes 4198400 | tf_op jit(solution)/shard_map/pallas_call | solution.py:320
  22.3 6.7 %all-to-all-done = bf16[16,32,640]{2,1,0:T(8,128)(2,1)S(1)} async-done(((bf16[16,32,640]{2,1,0:T(8,128)(2,1)}), bf16[16,32,640]{2,1,0:T(8,128)(2,1)S(1)}, u32[]{:S(2)}, u32[]{:S(2)}) %all-to-all-start) | async-done | bytes 655392 | tf_op jit(solution)/shard_map/all_to_all | solution.py:387
  29.0 0.3 shard_map.120.own
  29.3 2.7 %collective-permute-start = (bf16[8,64,512]{2,1,0:T(8,128)(2,1)S(1)}, bf16[8,64,512]{2,1,0:T(8,128)(2,1)S(1)}, u32[]{:S(2)}, u32[]{:S(2)}) collective-permute-start(bf16[8,64,512]{2,1,0:T(8,128)(2,1)S(1)} %shard_map.120.own), channel_id=1, source_target_pairs={{0,4},{4,0},{1,5},{5,1},{2,6},{6,2},{3,7},{7,3},{8,12},{12,8},{9,1... | collective-permute-start | bytes 1572872 | tf_op jit(solution)/shard_map/ppermute | solution.py:408
  32.0 3.7 %all-to-all-start.1 = ((bf16[16,32,1024]{2,1,0:T(8,128)(2,1)}), bf16[16,32,1024]{2,1,0:T(8,128)(2,1)S(1)}, u32[]{:S(2)}, u32[]{:S(2)}) async-start(bf16[16,32,1024]{2,1,0:T(8,128)(2,1)} %shard_map.119), calls=%async_computation.1 | async-start | bytes 2097152 | tf_op jit(solution)/shard_map/all_to_all | solution.py:418
  35.6 0.4 shard_map.121.weights
  36.0 18.7 %collective-permute-done.other = bf16[8,64,512]{2,1,0:T(8,128)(2,1)S(1)} collective-permute-done((bf16[8,64,512]{2,1,0:T(8,128)(2,1)S(1)}, bf16[8,64,512]{2,1,0:T(8,128)(2,1)S(1)}, u32[]{:S(2)}, u32[]{:S(2)}) %collective-permute-start) | collective-permute-done | bytes 524320 | tf_op jit(solution)/shard_map/ppermute | solution.py:408
  54.7 7.8 %all-to-all-done.1 = bf16[16,32,1024]{2,1,0:T(8,128)(2,1)S(1)} async-done(((bf16[16,32,1024]{2,1,0:T(8,128)(2,1)}), bf16[16,32,1024]{2,1,0:T(8,128)(2,1)S(1)}, u32[]{:S(2)}, u32[]{:S(2)}) %all-to-all-start.1) | async-done | bytes 1048608 | tf_op jit(solution)/shard_map/all_to_all | solution.py:418
  62.5 0.0 copy-start.1
  62.5 0.0 copy-start.3
  62.5 2.9 %shard_map.122 = bf16[512,1024]{1,0:T(8,128)(2,1)S(1)} custom-call(bf16[512,1024]{1,0:T(8,128)(2,1)S(1)} %bitcast.9, bf16[8,64,512]{2,1,0:T(8,128)(2,1)S(1)} %shard_map.120.own, bf16[8,64,512]{2,1,0:T(8,128)(2,1)S(1)} %collective-permute-done.other, f32[128,64]{1,0:T(8,128)S(1)} %shard_map.121.weights), custom_call_target="tpu_custom_call" | custom-call | flops 268435456 | bytes 3178496 | tf_op jit(solution)/shard_map/pallas_call | solution.py:320
  65.4 18.8 %all_to_all.15 = bf16[16,32,1024]{2,1,0:T(8,128)(2,1)S(1)} all-to-all(bf16[16,32,1024]{2,1,0:T(8,128)(2,1)S(1)} %bitcast.10), channel_id=1, replica_groups=mesh['tile'=4,'half'=2,'rest'=4] {'tile','rest'}, dimensions={0} | all-to-all | bytes 2097152 | tf_op jit(solution)/shard_map/all_to_all | solution.py:432
  84.2 0.0 copy-done.1
  84.2 0.0 copy-done.3
  84.2 2.2 %shard_map.123 = bf16[512,1024]{1,0:T(8,128)(2,1)} custom-call(bf16[512,1024]{1,0:T(8,128)(2,1)S(1)} %bitcast.11, bf16[512,1024]{1,0:T(8,128)(2,1)S(1)} %copy-done.1, bf16[1024,1024]{1,0:T(8,128)(2,1)S(1)} %copy-done.3), custom_call_target="tpu_custom_call" | custom-call | flops 1073741824 | bytes 5242880 | tf_op jit(solution)/shard_map/pallas_call | solution.py:320
Async XLA Ops:
  0.0 17.0 %copy-start.4 = (f32[1024]{0:T(1024)S(1)}, f32[1024]{0:T(1024)}, u32[]{:S(2)}) copy-start(f32[1024]{0:T(1024)} %param.17) | copy-start | bytes 12292
  10.7 18.3 %all-to-all-start = ((bf16[16,32,640]{2,1,0:T(8,128)(2,1)}), bf16[16,32,640]{2,1,0:T(8,128)(2,1)S(1)}, u32[]{:S(2)}, u32[]{:S(2)}) async-start(bf16[16,32,640]{2,1,0:T(8,128)(2,1)} %get-tuple-element.11), calls=%async_computation | async-start | bytes 1310720 | tf_op jit(solution)/shard_map/all_to_all | solution.py:387
  17.0 1.2 %copy-start = (bf16[512,1024]{1,0:T(8,128)(2,1)S(1)}, bf16[512,1024]{1,0:T(8,128)(2,1)}, u32[]{:S(2)}) copy-start(bf16[512,1024]{1,0:T(8,128)(2,1)} %get-tuple-element.10.mid) | copy-start | bytes 3145732
  18.3 1.6 %copy-start.2 = (bf16[1024,1024]{1,0:T(8,128)(2,1)S(1)}, bf16[1024,1024]{1,0:T(8,128)(2,1)}, u32[]{:S(2)}) copy-start(bf16[1024,1024]{1,0:T(8,128)(2,1)} %wq.1) | copy-start | bytes 6291460
  29.3 25.4 %collective-permute-start = (bf16[8,64,512]{2,1,0:T(8,128)(2,1)S(1)}, bf16[8,64,512]{2,1,0:T(8,128)(2,1)S(1)}, u32[]{:S(2)}, u32[]{:S(2)}) collective-permute-start(bf16[8,64,512]{2,1,0:T(8,128)(2,1)S(1)} %shard_map.120.own), channel_id=1, source_target_pairs={{0,4},{4,0},{1,5},{5,1},{2,6},{6,2},{3,7},{7,3},{8,12},{12,8},{9,1... | collective-permute-start | bytes 1572872 | tf_op jit(solution)/shard_map/ppermute | solution.py:408
  32.0 30.5 %all-to-all-start.1 = ((bf16[16,32,1024]{2,1,0:T(8,128)(2,1)}), bf16[16,32,1024]{2,1,0:T(8,128)(2,1)S(1)}, u32[]{:S(2)}, u32[]{:S(2)}) async-start(bf16[16,32,1024]{2,1,0:T(8,128)(2,1)} %shard_map.119), calls=%async_computation.1 | async-start | bytes 2097152 | tf_op jit(solution)/shard_map/all_to_all | solution.py:418
  62.5 21.7 %copy-start.1 = (bf16[512,1024]{1,0:T(8,128)(2,1)S(1)}, bf16[512,1024]{1,0:T(8,128)(2,1)}, u32[]{:S(2)}) copy-start(bf16[512,1024]{1,0:T(8,128)(2,1)} %get-tuple-element.10.mid) | copy-start | bytes 3145732
  62.5 21.7 %copy-start.3 = (bf16[1024,1024]{1,0:T(8,128)(2,1)S(1)}, bf16[1024,1024]{1,0:T(8,128)(2,1)}, u32[]{:S(2)}) copy-start(bf16[1024,1024]{1,0:T(8,128)(2,1)} %wo.1) | copy-start | bytes 6291460

commit v8 on v0

v8 whole, which is shorter than its diff:
```python
import functools
import math

import jax
import jax.numpy as jnp
from jax import lax
from jax.experimental import pallas as pl
from jax.experimental.pallas import tpu as pltpu
from jax.sharding import Mesh
from jax.sharding import PartitionSpec as P

HEADS = 16
KV_HEADS = 4
HEAD_DIM = 64
GROUPS = HEADS // KV_HEADS
KEYS = KV_HEADS * HEAD_DIM
WIDE = GROUPS * HEAD_DIM
SCALE = HEAD_DIM ** (-0.5)
EXP2_SCALE = SCALE * math.log2(math.e)
NEG = -1e30
LANES = 128
COLS = 256
HALVES = 2
CHUNKS = 2
DEPTH = 2
MIB = 1024 * 1024
F32 = jnp.float32
BF16 = jnp.bfloat16
ROWS_BY_COLS = (((1,), (1,)), ((), ()))


def norm_rows(values, gain):
    wide = values.astype(F32)
    meansq = jnp.mean(wide * wide, axis=-1, keepdims=True)
    return (wide * lax.rsqrt(meansq + 1e-05) * gain).astype(BF16)


def one_hot(rows, source, turned=False):
    row = lax.broadcasted_iota(jnp.int32, (rows, rows), 1 if turned else 0)
    col = lax.broadcasted_iota(jnp.int32, (rows, rows), 0 if turned else 1)
    return jnp.where(col == source(row), 1.0, 0.0).astype(BF16)


def block_source(agents, span, local):
    return lambda row: row // local % agents * span + row // (local * agents) * local + row % local


def step_source(total, local):
    return lambda row: row % total * local + row // total


def moved(order, piece):
    return jnp.dot(order, piece, preferred_element_type=F32).astype(BF16)


def staggered(units, first, second, third):
    scores, grown = {}, {}
    for i in range(len(units) + 2 * DEPTH):
        if i < len(units):
            scores[i] = first(*units[i])
        if 0 <= i - DEPTH < len(units):
            grown[i - DEPTH] = second(scores.pop(i - DEPTH))
        if 0 <= i - 2 * DEPTH < len(units):
            third(units[i - 2 * DEPTH], *grown.pop(i - 2 * DEPTH))


def attend(members, pair, size, query, keyval, store, valid, weight=None):
    columns = pair * size
    together = GROUPS if columns <= LANES else 1
    valid = jnp.concatenate([valid] * together, axis=1)
    if weight is not None:
        weight = jnp.concatenate([weight] * together, axis=1)
    lane = lax.broadcasted_iota(jnp.int32, (HEAD_DIM, columns), 1) // size

    def scores_of(m, k, heads):
        turned = [query(m + s, slice(k * WIDE, (k + 1) * WIDE)) for s in range(pair)]
        turned = jnp.concatenate(turned, axis=0).T
        turned = [turned[j * HEAD_DIM : (j + 1) * HEAD_DIM] for j in heads]
        if pair > 1:
            zero = jnp.zeros((HEAD_DIM, columns), BF16)
            turned = [
                jnp.concatenate([jnp.where(lane == s, t, zero) for s in range(pair)], axis=0)
                for t in turned
            ]
        part = slice(k * HEAD_DIM, (k + 1) * HEAD_DIM)
        keys = jnp.concatenate([keyval(m + s, part) for s in range(pair)], axis=1)
        return jnp.dot(keys, jnp.concatenate(turned, axis=1), preferred_element_type=F32)

    def grow(scores):
        scores = jnp.where(valid, scores, NEG)
        top = jnp.max(scores, axis=0, keepdims=True)
        grown = jnp.exp2((scores - top) * EXP2_SCALE)
        if weight is not None:
            grown = grown * weight
        return grown.astype(BF16), jnp.sum(grown, axis=0, keepdims=True)

    def values_of(unit, grown, sums):
        m, k, heads = unit
        part = slice(KEYS + k * HEAD_DIM, KEYS + (k + 1) * HEAD_DIM)
        vals = jnp.concatenate([keyval(m + s, part).T for s in range(pair)], axis=0)
        mixed = jnp.dot(vals, grown, preferred_element_type=F32)
        inverse = 1.0 / sums
        parts = []
        for i in range(len(heads)):
            cols = slice(i * columns, (i + 1) * columns)
            chosen = mixed[:HEAD_DIM, cols]
            for s in range(1, pair):
                chosen = jnp.where(lane == s, mixed[s * HEAD_DIM : (s + 1) * HEAD_DIM, cols], chosen)
            parts.append(chosen * inverse[:, cols])
        mixed = jnp.concatenate(parts, axis=0).astype(BF16).T
        start = k * WIDE + heads[0] * HEAD_DIM
        store(m, slice(start, start + len(heads) * HEAD_DIM), mixed)

    units = [
        (m, k, tuple(range(j, j + together)))
        for m in range(0, members, pair)
        for k in range(KV_HEADS)
        for j in range(0, GROUPS, together)
    ]
    staggered(units, scores_of, grow, values_of)


def time_kernel(agents, steps, span, chunk, local, pair, *refs):
    hist_hbm, gain, wq_hbm, wkv_hbm, wo_hbm, *refs = refs
    before, refs = refs[:chunk], refs[chunk:]
    listing, refs = (refs[:3], refs[3:]) if chunk == 0 else ((), refs)
    mid, sent, keyval, *refs = refs
    hist, wq, wkv, wo, normed, query, mix, hist_sems, wq_sems, sems = refs
    rows, width = hist.shape
    hist_loads, wq_loads = [], []
    for a in range(agents):
        source = hist_hbm.at[pl.ds(a * steps + chunk * span, span), :]
        hist_loads.append(
            pltpu.make_async_copy(source, hist.at[pl.ds(a * span, span), :], hist_sems.at[a])
        )
    for c in range(0, width, COLS):
        cols = pl.ds(c, COLS)
        wq_loads.append(
            pltpu.make_async_copy(wq_hbm.at[:, cols], wq.at[:, cols], wq_sems.at[c // COLS])
        )
    loads = [
        pltpu.make_async_copy(wkv_hbm, wkv, sems.at[0]),
        pltpu.make_async_copy(wo_hbm, wo, sems.at[1]),
    ]
    for load in hist_loads + loads[:1]:
        load.start()
    for a in range(agents):
        part = pl.ds(a * span, span)
        hist_loads[a].wait()
        if a == 0:
            for load in wq_loads:
                load.start()
        normed[part, :] = norm_rows(hist[part, :], gain[...])
    loads[0].wait()
    for c in range(0, 2 * KEYS, COLS):
        keyval[:, c : c + COLS] = jnp.dot(
            normed[...], wkv[:, c : c + COLS], preferred_element_type=F32
        ).astype(BF16)
    loads[1].start()
    for c in range(0, width, COLS):
        wq_loads[c // COLS].wait()
        query[:, c : c + COLS] = jnp.dot(
            normed[...], wq[:, c : c + COLS], preferred_element_type=F32
        ).astype(BF16)

    keys = (chunk + 1) * span
    shape = (keys, pair * span)
    valid = lax.broadcasted_iota(jnp.int32, shape, 0) <= chunk * span + (
        lax.broadcasted_iota(jnp.int32, shape, 1) % span
    )

    def keyvals(a, cols):
        part = slice(a * span, (a + 1) * span)
        pieces = [ref[part, cols] for ref in (*before, keyval)]
        return jnp.concatenate(pieces, axis=0) if before else pieces[0]

    def store(a, cols, values):
        mix[a * span : (a + pair) * span, cols] = values

    attend(
        agents, pair, span, lambda a, cols: query[a * span : (a + 1) * span, cols],
        keyvals, store, valid,
    )
    order = one_hot(rows, block_source(agents, span, local))
    loads[1].wait()
    for c in range(0, width, COLS):
        cols = slice(c, c + COLS)
        projected = jnp.dot(mix[...], wo[:, cols], preferred_element_type=F32)
        piece = (hist[:, cols].astype(F32) + projected).astype(BF16)
        mid[:, cols] = piece
        sent[:, cols] = moved(order, piece)
    if listing:
        neighbours, nbr_valid, alive = listing
        lane = lax.broadcasted_iota(jnp.int32, (1, LANES), 1)
        notes = jnp.zeros((1, LANES), F32)
        for i in range(alive.shape[1]):
            notes = jnp.where(lane == i, alive[0, i].astype(F32), notes)
        for i in range(neighbours.shape[1]):
            listed = lane == alive.shape[1] + neighbours[0, i]
            notes = notes + jnp.where(listed, nbr_valid[0, i].astype(F32), 0.0)
        sent[:, width:] = jnp.broadcast_to(notes, (rows, LANES)).astype(BF16)


def keys_kernel(local, mid, gain, wkv, second, out):
    rows, width = second.shape
    total = rows // local
    second[...] = norm_rows(mid[:, :width], gain[...])
    if local > 1:
        order = one_hot(rows, step_source(total, local))
        for c in range(0, width, COLS):
            second[:, c : c + COLS] = moved(order, second[:, c : c + COLS])
    for c in range(0, 2 * KEYS, COLS):
        result = jnp.dot(second[...], wkv[:, c : c + COLS], preferred_element_type=F32)
        out[:, :, c : c + COLS] = result.astype(BF16).reshape(local, total, COLS)


def query_kernel(second, wq, out):
    local, total, width = out.shape
    for c in range(0, width, COLS):
        result = jnp.dot(second[...], wq[:, c : c + COLS], preferred_element_type=F32)
        out[:, :, c : c + COLS] = result.astype(BF16).reshape(local, total, COLS)


def weight_kernel(local, tiles, width, half, mid, out):
    rows = mid.shape[0]
    total = rows // local
    group = total // tiles
    notes = mid[:, width:]
    shape = (total, rows)
    row, col = (lax.broadcasted_iota(jnp.int32, shape, d) for d in range(2))
    pick = jnp.where(col == row * local, 1.0, 0.0).astype(BF16)
    lines = moved(pick, notes)
    shape = (HALVES * total, LANES)
    key, lane = (lax.broadcasted_iota(jnp.int32, shape, d) for d in range(2))
    side, tile, agent = (key // total + half[0]) % HALVES, key % total // group, key % group
    spread = jnp.where(lane == HALVES * group + tile, 1.0, 0.0).astype(BF16)
    listed = lax.dot_general(spread, lines, ROWS_BY_COLS, preferred_element_type=F32)
    spread = jnp.where(lane == side * group + agent, 1.0, 0.0).astype(BF16)
    alive = lax.dot_general(spread, lines, ROWS_BY_COLS, preferred_element_type=F32)
    shape = (HALVES * total, total)
    key, query = (lax.broadcasted_iota(jnp.int32, shape, d) for d in range(2))
    first = query == key % total // group * group
    alive = jnp.sum(jnp.where(first, alive, 0.0), axis=1, keepdims=True)
    out[...] = listed * alive


def space_kernel(pair, query, own, other, weights, out, mix):
    local, total, width = query.shape
    rows = local * total
    weight = jnp.concatenate([weights[...]] * pair, axis=1)

    def keyvals(s, cols):
        return jnp.concatenate([own[s, :, cols], other[s, :, cols]], axis=0)

    def store(s, cols, values):
        mix[s * total : (s + pair) * total, cols] = values

    attend(
        local, pair, total, lambda s, cols: query[s, :, cols], keyvals, store, weight > 0, weight
    )
    if local > 1:
        order = one_hot(rows, step_source(total, local), turned=True)
    for c in range(0, width, COLS):
        piece = mix[:, c : c + COLS]
        out[:, c : c + COLS] = moved(order, piece) if local > 1 else piece


def out_kernel(agents, span, local, chunks, *refs):
    mixes, mids, (wo, out, mix) = refs[:chunks], refs[chunks : 2 * chunks], refs[2 * chunks :]
    rows, width = mids[0].shape
    order = one_hot(rows, block_source(agents, span, local), turned=True)
    for c in range(0, width, COLS):
        for i in range(chunks):
            mix[i * rows : (i + 1) * rows, c : c + COLS] = moved(order, mixes[i][:, c : c + COLS])
    for c in range(0, width, COLS):
        cols = slice(c, c + COLS)
        projected = jnp.dot(mix[...], wo[:, cols], preferred_element_type=F32)
        for i in range(chunks):
            piece = mids[i][:, cols].astype(F32) + projected[i * rows : (i + 1) * rows]
            out[:, i * span : (i + 1) * span, cols] = piece.astype(BF16).reshape(agents, span, COLS)


def call(kernel, shapes, args, hbm=(), smem=(), scratch=(), flops=0, mib=16):
    touched = sum(a.size * a.dtype.itemsize for a in args)
    touched += sum(s.size * s.dtype.itemsize for s in shapes)
    spaces = [pl.ANY if i in hbm else pltpu.VMEM for i in range(len(args))]
    results = pl.pallas_call(
        kernel,
        out_shape=list(shapes),
        in_specs=[
            pl.BlockSpec(memory_space=pltpu.SMEM if i in smem else space)
            for i, space in enumerate(spaces)
        ],
        out_specs=[pl.BlockSpec(memory_space=pltpu.VMEM)] * len(shapes),
        scratch_shapes=list(scratch),
        compiler_params=pltpu.CompilerParams(vmem_limit_bytes=mib * MIB),
        cost_estimate=pl.CostEstimate(flops=flops, bytes_accessed=touched, transcendentals=0),
    )(*args)
    return results if len(shapes) > 1 else results[0]


def per_device(
    histories,
    gain_time,
    wq_time,
    wkv_time,
    wo_time,
    gain_space,
    wq_space,
    wkv_space,
    wo_space,
    neighbours,
    nbr_valid,
    agent_valid,
):
    agents, steps, width = histories.shape[1:]
    tiles, rest = lax.axis_size("tile"), lax.axis_size("rest")
    spread = ("tile", "rest")
    parts = tiles * rest
    chunks = CHUNKS if steps % (CHUNKS * parts) == 0 else 1
    span = steps // chunks
    local = span // parts
    rows = agents * span
    total = parts * agents
    struct = jax.ShapeDtypeStruct

    def beside(size, members):
        return LANES // size if size < LANES and members % (LANES // size) == 0 else 1

    hist = histories.reshape(agents * steps, width)
    mids, sents, before = [], [], []
    for i in range(chunks):
        deep = width + LANES if i == 0 else width
        mid, sent, keyval = call(
            functools.partial(time_kernel, agents, steps, span, i, local, beside(span, agents)),
            [struct((rows, width), BF16), struct((rows, deep), BF16), struct((rows, 2 * KEYS), BF16)],
            [hist, gain_time[None], wq_time, wkv_time, wo_time]
            + before
            + ([neighbours, nbr_valid, agent_valid] if i == 0 else []),
            hbm=(0, 2, 3, 4),
            smem=(5, 6, 7) if i == 0 else (),
            scratch=[
                pltpu.VMEM((rows, width), BF16),
                pltpu.VMEM(wq_time.shape, BF16),
                pltpu.VMEM(wkv_time.shape, BF16),
                pltpu.VMEM(wo_time.shape, BF16),
                pltpu.VMEM((rows, width), BF16),
                pltpu.VMEM((rows, width), BF16),
                pltpu.VMEM((rows, width), BF16),
                pltpu.SemaphoreType.DMA((agents,)),
                pltpu.SemaphoreType.DMA((width // COLS,)),
                pltpu.SemaphoreType.DMA((2,)),
            ],
            flops=2 * rows * width * (2 * width + 2 * KEYS),
            mib=56,
        )
        mids.append(mid)
        sents.append(sent.reshape(parts, agents * local, deep))
        before.append(keyval)

    swap = [(h, HALVES - 1 - h) for h in range(HALVES)]
    half = lax.axis_index("half").astype(jnp.int32).reshape(1)
    big = 16 + 16 * GROUPS * HALVES * total**2 // MIB
    mixes = []
    for i, sent in enumerate(sents):
        deep = sent.shape[-1]
        there = lax.all_to_all(sent, spread, split_axis=0, concat_axis=0, tiled=True)
        there = there.reshape(rows, deep)
        second, own = call(
            functools.partial(keys_kernel, local),
            [struct((rows, width), BF16), struct((local, total, 2 * KEYS), BF16)],
            [there, gain_space[None], wkv_space],
            flops=2 * rows * width * 2 * KEYS,
        )
        other = lax.ppermute(own, "half", swap)
        if i == 0:
            weight = call(
                functools.partial(weight_kernel, local, tiles, width),
                [struct((HALVES * total, total), F32)],
                [half, there],
                smem=(0,),
            )
        query = call(
            query_kernel,
            [struct((local, total, width), BF16)],
            [second, wq_space],
            flops=2 * rows * width * width,
        )
        mix = call(
            functools.partial(space_kernel, beside(total, local)),
            [struct((rows, width), BF16)],
            [query, own, other, weight],
            scratch=[pltpu.VMEM((rows, width), BF16)],
            flops=8 * rows * total * width,
            mib=big,
        )
        mix = mix.reshape(parts, agents * local, width)
        mix = lax.all_to_all(mix, spread, split_axis=0, concat_axis=0, tiled=True)
        mixes.append(mix.reshape(rows, width))
    out = call(
        functools.partial(out_kernel, agents, span, local, chunks),
        [struct((agents, steps, width), BF16)],
        mixes + mids + [wo_space],
        scratch=[pltpu.VMEM((agents * steps, width), BF16)],
        flops=2 * rows * width * width,
    )
    return out[None]


def solution(mesh):
    tiles, members = mesh.devices.shape
    split = Mesh(
        mesh.devices.reshape(tiles, HALVES, members // HALVES), ("tile", "half", "rest")
    )
    states = P("tile", ("half", "rest"), None, None)
    listing = P("tile", None)
    return jax.shard_map(
        per_device,
        mesh=split,
        in_specs=(states,) + (P(),) * 8 + (listing,) * 3,
        out_specs=states,
        check_vma=False,
    )
```

time: 212 us -> 102 us (0.48)
  local copies, waits for them, and re-layouts: 51 us -> 6.69 us
  blocking collectives: 71.6 us -> 31.4 us
  matrix products: 40.1 us -> 0 us
  Pallas kernels: 0 us -> 26.9 us
  other arithmetic: 19.2 us -> 0 us
  starting transfers between devices: 0.01 us -> 13.7 us
  between operations: 13.7 us -> 0.17 us
  waiting for transfers between devices: 14.7 us -> 22.3 us
    dot_general x16 -> x0, matrix products: 40.1 us -> none  [the longest x4 13.4 us: tile_update(): jnp.einsum('sakgd,bskd->skgab', queries, key_values[:, :, 0], preferred_e...]
    all_to_all x2, blocking collectives: 63.7 us -> 31.4 us  [the longest x1 17 us: per_device(): lax.all_to_all(sent, spread, split_axis=0, concat_axis=0, tiled=True)]
    pallas_call x0 -> x10, Pallas kernels: none -> 26.9 us  [call(): pl.pallas_call(kernel, out_shape=list(shapes), in_specs=[pl.BlockSpec(mem...]
    all_gather x1 -> x0, waiting for transfers between devices: 14.6 us -> none  [per_device(): lax.all_gather(keyval, 'tile', axis=0, tiled=True)]
    ppermute x0 -> x2, waiting for transfers between devices: none -> 13.6 us  [per_device(): other = lax.ppermute(own, 'half', swap)]
    reshape x8 -> x0, local copies, waits for them, and re-layouts: 13.6 us -> none  [the longest x2 7.89 us: per_device(): queries = queries.reshape(agents, local_steps, KV_HEADS, groups, HEAD_DIM)]
    while x28 -> x0, local copies, waits for them, and re-layouts: 13 us -> none
    reduce_sum x6 -> x0, other arithmetic: 8.8 us -> none  [the longest x4 6.75 us: tile_update(): denominator = denominator * factor + jnp.sum(expd, axis=-1)]
  transfers between devices with their start and end apart: 1 -> 4, of which waited for: 1 -> 3; matrix products, arithmetic and copies ran while one was open for 6% -> 0% of each run, Pallas kernels for 0% -> 5%
where the time goes in v8:
time: 102 us; the launch traced here: 101 us
  blocking collectives  31.4 us (31%)
  Pallas kernels  26.9 us (26%)
  waiting for transfers between devices  22.3 us (22%)
  starting transfers between devices  13.7 us (13%)
  local copies, waits for them, and re-layouts  6.69 us (7%)
    pallas_call x10, Pallas kernels, call(): pl.pallas_call(kernel, out_shape=list(shapes), in_specs=[pl.BlockSpec(mem...  26.9 us
    all_to_all x1, blocking collectives, per_device(): lax.all_to_all(sent, spread, split_axis=0, concat_axis=0, tiled=True)  17 us
    all_to_all x1, blocking collectives, per_device(): mix = lax.all_to_all(mix, spread, split_axis=0, concat_axis=0, tiled=True)  14.4 us
    ppermute x2, waiting for transfers between devices, per_device(): other = lax.ppermute(own, 'half', swap)  13.6 us
    all_to_all x1, waiting for transfers between devices, per_device(): lax.all_to_all(sent, spread, split_axis=0, concat_axis=0, tiled=True)  8.67 us
    unnamed x20, local copies, waits for them, and re-layouts  6.69 us
    ppermute x2, starting transfers between devices, per_device(): other = lax.ppermute(own, 'half', swap)  6.12 us
    all_to_all x1, starting transfers between devices, per_device(): mix = lax.all_to_all(mix, spread, split_axis=0, concat_axis=0, tiled=True)  4.03 us
  transfers between devices with their start and end apart: 4, of which 3 were waited for; matrix products, arithmetic and copies ran while one was open for 0% of the time, Pallas kernels for 5%

profile of v8, /device:TPU:0, one launch (start us, length us, event | category | flops | bytes accessed | tf_op | source)
XLA Modules:
  0.0 101.2 jit_solution(6181082432267273213)
XLA Ops:
  0.0 8.4 %shard_map.118 = (bf16[256,1024]{1,0:T(8,128)(2,1)}, bf16[256,1152]{1,0:T(8,128)(2,1)}, bf16[256,512]{1,0:T(8,128)(2,1)}) custom-call(bf16[512,1024]{1,0:T(8,128)(2,1)} %bitcast.22, f32[1,1024]{1,0:T(1,128)} %bitcast.26, bf16[1024,1024]{1,0:T(8,128)(2,1)} %refs_2_.3, bf16[1024,512]{1,0:T(8,128)(2,1)} %refs_3_.3, bf16[1024,1024]{1,0:T(8,128)(2,1)} %refs_4_.4, ...), custom_call_target="tpu_custom_call" | custom-call | flops 1342177280 | bytes 7671968 | tf_op jit(solution)/shard_map/pallas_call | solution.py:287
  8.4 8.7 %shard_map.123 = (bf16[256,1024]{1,0:T(8,128)(2,1)}, bf16[256,1024]{1,0:T(8,128)(2,1)}, bf16[256,512]{1,0:T(8,128)(2,1)}) custom-call(bf16[512,1024]{1,0:T(8,128)(2,1)} %bitcast.23, f32[1,1024]{1,0:T(1,128)} %bitcast.27, bf16[1024,1024]{1,0:T(8,128)(2,1)} %refs_2_.3, bf16[1024,512]{1,0:T(8,128)(2,1)} %refs_3_.3, bf16[1024,1024]{1,0:T(8,128)(2,1)} %refs_4_.4, ...), custom_call_target="tpu_custom_call" | custom-call | flops 1342177280 | bytes 7868416 | tf_op jit(solution)/shard_map/pallas_call | solution.py:287
  17.1 0.0 copy-start.9
  17.1 0.0 copy-start
  17.1 17.0 %all_to_all.20 = bf16[16,16,1024]{2,1,0:T(8,128)(2,1)S(1)} all-to-all(bf16[16,16,1024]{2,1,0:T(8,128)(2,1)} %bitcast.25), channel_id=1, replica_groups=mesh['tile'=4,'half'=2,'rest'=4] {'tile','rest'}, dimensions={0} | all-to-all | bytes 1048576 | tf_op jit(solution)/shard_map/all_to_all | solution.py:367
  34.1 3.6 %all-to-all-start = ((bf16[16,16,1152]{2,1,0:T(8,128)(2,1)}), bf16[16,16,1152]{2,1,0:T(8,128)(2,1)S(1)}, u32[]{:S(2)}, u32[]{:S(2)}) async-start(bf16[16,16,1152]{2,1,0:T(8,128)(2,1)} %bitcast.24), calls=%async_computation | async-start | bytes 1179648 | tf_op jit(solution)/shard_map/all_to_all | solution.py:367
  37.7 0.0 copy-done.9
  37.7 0.0 copy-start.1
  37.7 1.2 %copy-done.1 = bf16[1024,512]{1,0:T(8,128)(2,1)S(1)} copy-done((bf16[1024,512]{1,0:T(8,128)(2,1)S(1)}, bf16[1024,512]{1,0:T(8,128)(2,1)}, u32[]{:S(2)}) %copy-start.1) | copy-done | bytes 1048600
  38.9 0.8 shard_map.124
  39.7 0.0 copy-start.7
  39.7 0.8 copy-done.7
  40.5 2.6 %collective-permute-start.1 = (bf16[4,64,512]{2,1,0:T(8,128)(2,1)S(1)}, bf16[4,64,512]{2,1,0:T(8,128)(2,1)}, u32[]{:S(2)}, u32[]{:S(2)}) collective-permute-start(bf16[4,64,512]{2,1,0:T(8,128)(2,1)S(1)} %get-tuple-element.20.own), channel_id=1, source_target_pairs={{0,4},{4,0},{1,5},{5,1},{2,6},{6,2},{3,7},{7,3},{8,12},{12,8},{9,1... | collective-permute-start | bytes 786440 | tf_op jit(solution)/shard_map/ppermute | solution.py:375
  43.1 0.0 copy-done
  43.1 0.0 copy-start.8
  43.1 1.0 %copy-done.8 = bf16[256,1024]{1,0:T(8,128)(2,1)S(1)} copy-done((bf16[256,1024]{1,0:T(8,128)(2,1)S(1)}, bf16[256,1024]{1,0:T(8,128)(2,1)}, u32[]{:S(2)}) %copy-start.8) | copy-done | bytes 524312
  44.2 0.7 shard_map.125.query
  44.9 8.7 %all-to-all-done = bf16[16,16,1152]{2,1,0:T(8,128)(2,1)S(1)} async-done(((bf16[16,16,1152]{2,1,0:T(8,128)(2,1)}), bf16[16,16,1152]{2,1,0:T(8,128)(2,1)S(1)}, u32[]{:S(2)}, u32[]{:S(2)}) %all-to-all-start) | async-done | bytes 589856 | tf_op jit(solution)/shard_map/all_to_all | solution.py:367
  53.5 0.4 shard_map.121.weights
  53.9 1.8 %collective-permute-done.1.other = bf16[4,64,512]{2,1,0:T(8,128)(2,1)} collective-permute-done((bf16[4,64,512]{2,1,0:T(8,128)(2,1)S(1)}, bf16[4,64,512]{2,1,0:T(8,128)(2,1)}, u32[]{:S(2)}, u32[]{:S(2)}) %collective-permute-start.1) | collective-permute-done | bytes 262176 | tf_op jit(solution)/shard_map/ppermute | solution.py:375
  55.7 2.5 %shard_map.126 = bf16[256,1024]{1,0:T(8,128)(2,1)S(1)} custom-call(bf16[4,64,1024]{2,1,0:T(8,128)(2,1)S(1)} %shard_map.125.query, bf16[4,64,512]{2,1,0:T(8,128)(2,1)S(1)} %get-tuple-element.20.own, bf16[4,64,512]{2,1,0:T(8,128)(2,1)} %collective-permute-done.1.other, f32[128,64]{1,0:T(8,128)S(1)} %shard_map.121.weights), custom_call_target="tpu_custom_call" | custom-call | flops 134217728 | bytes 1605632 | tf_op jit(solution)/shard_map/pallas_call | solution.py:287
  58.2 0.0 copy-start.3
  58.2 0.8 copy-done.3
  59.0 4.0 %all-to-all-start.3 = ((bf16[16,16,1024]{2,1,0:T(8,128)(2,1)}), bf16[16,16,1024]{2,1,0:T(8,128)(2,1)S(1)}, u32[]{:S(2)}, u32[]{:S(2)}) async-start(bf16[16,16,1024]{2,1,0:T(8,128)(2,1)} %bitcast.16), calls=%async_computation.3 | async-start | bytes 1048576 | tf_op jit(solution)/shard_map/all_to_all | solution.py:398
  63.0 0.0 copy-start.2
  63.1 1.2 %copy-done.2 = bf16[1024,512]{1,0:T(8,128)(2,1)S(1)} copy-done((bf16[1024,512]{1,0:T(8,128)(2,1)S(1)}, bf16[1024,512]{1,0:T(8,128)(2,1)}, u32[]{:S(2)}) %copy-start.2) | copy-done | bytes 1048600
  64.3 0.8 shard_map.119
  65.0 3.5 %collective-permute-start = (bf16[4,64,512]{2,1,0:T(8,128)(2,1)S(1)}, bf16[4,64,512]{2,1,0:T(8,128)(2,1)S(1)}, u32[]{:S(2)}, u32[]{:S(2)}) collective-permute-start(bf16[4,64,512]{2,1,0:T(8,128)(2,1)S(1)} %get-tuple-element.16.own), channel_id=1, source_target_pairs={{0,4},{4,0},{1,5},{5,1},{2,6},{6,2},{3,7},{7,3},{8,12},{12,8},{9,1... | collective-permute-start | bytes 786440 | tf_op jit(solution)/shard_map/ppermute | solution.py:375
  68.6 0.7 shard_map.120.query
  69.3 0.0 copy-start.5
  69.3 0.0 copy-start.6
  69.3 11.8 %collective-permute-done.other = bf16[4,64,512]{2,1,0:T(8,128)(2,1)S(1)} collective-permute-done((bf16[4,64,512]{2,1,0:T(8,128)(2,1)S(1)}, bf16[4,64,512]{2,1,0:T(8,128)(2,1)S(1)}, u32[]{:S(2)}, u32[]{:S(2)}) %collective-permute-start) | collective-permute-done | bytes 262176 | tf_op jit(solution)/shard_map/ppermute | solution.py:375
  81.1 1.6 %shard_map.122 = bf16[256,1024]{1,0:T(8,128)(2,1)S(1)} custom-call(bf16[4,64,1024]{2,1,0:T(8,128)(2,1)S(1)} %shard_map.120.query, bf16[4,64,512]{2,1,0:T(8,128)(2,1)S(1)} %get-tuple-element.16.own, bf16[4,64,512]{2,1,0:T(8,128)(2,1)S(1)} %collective-permute-done.other, f32[128,64]{1,0:T(8,128)S(1)} %shard_map.121.weights), custom_call_target="tpu_custom_call" | custom-call | flops 134217728 | bytes 1605632 | tf_op jit(solution)/shard_map/pallas_call | solution.py:287
  82.7 0.0 all-to-all-done.3
  82.7 14.4 %all_to_all.21 = bf16[16,16,1024]{2,1,0:T(8,128)(2,1)S(1)} all-to-all(bf16[16,16,1024]{2,1,0:T(8,128)(2,1)S(1)} %bitcast.17), channel_id=1, replica_groups=mesh['tile'=4,'half'=2,'rest'=4] {'tile','rest'}, dimensions={0} | all-to-all | bytes 1048576 | tf_op jit(solution)/shard_map/all_to_all | solution.py:398
  97.1 0.0 copy-done.5
  97.1 0.0 copy-done.6
  97.1 0.0 copy-start.4
  97.1 1.6 %copy-done.4 = bf16[1024,1024]{1,0:T(8,128)(2,1)S(1)} copy-done((bf16[1024,1024]{1,0:T(8,128)(2,1)S(1)}, bf16[1024,1024]{1,0:T(8,128)(2,1)}, u32[]{:S(2)}) %copy-start.4) | copy-done | bytes 2097176
  98.7 2.5 %shard_map.127 = bf16[4,128,1024]{2,1,0:T(8,128)(2,1)} custom-call(bf16[256,1024]{1,0:T(8,128)(2,1)S(1)} %bitcast.19, bf16[256,1024]{1,0:T(8,128)(2,1)S(1)} %bitcast.15, bf16[256,1024]{1,0:T(8,128)(2,1)S(1)} %copy-done.5, bf16[256,1024]{1,0:T(8,128)(2,1)S(1)} %copy-done.6, bf16[1024,1024]{1,0:T(8,128)(2,1)S(1)} %copy-done.4), custom_call_target="tpu_custom_call" | custom-call | flops 536870912 | bytes 5242880 | tf_op jit(solution)/shard_map/pallas_call | solution.py:287
Async XLA Ops:
  17.1 20.6 %copy-start.9 = (f32[1024]{0:T(1024)S(1)}, f32[1024]{0:T(1024)}, u32[]{:S(2)}) copy-start(f32[1024]{0:T(1024)} %param.17) | copy-start | bytes 12292
  17.1 26.0 %copy-start = (bf16[1024,1024]{1,0:T(8,128)(2,1)S(1)}, bf16[1024,1024]{1,0:T(8,128)(2,1)}, u32[]{:S(2)}) copy-start(bf16[1024,1024]{1,0:T(8,128)(2,1)} %wq.3) | copy-start | bytes 6291460
  34.1 19.4 %all-to-all-start = ((bf16[16,16,1152]{2,1,0:T(8,128)(2,1)}), bf16[16,16,1152]{2,1,0:T(8,128)(2,1)S(1)}, u32[]{:S(2)}, u32[]{:S(2)}) async-start(bf16[16,16,1152]{2,1,0:T(8,128)(2,1)} %bitcast.24), calls=%async_computation | async-start | bytes 1179648 | tf_op jit(solution)/shard_map/all_to_all | solution.py:367
  37.7 1.2 %copy-start.1 = (bf16[1024,512]{1,0:T(8,128)(2,1)S(1)}, bf16[1024,512]{1,0:T(8,128)(2,1)}, u32[]{:S(2)}) copy-start(bf16[1024,512]{1,0:T(8,128)(2,1)} %wkv.3) | copy-start | bytes 3145732
  39.7 0.8 copy-start.7
  40.5 15.2 %collective-permute-start.1 = (bf16[4,64,512]{2,1,0:T(8,128)(2,1)S(1)}, bf16[4,64,512]{2,1,0:T(8,128)(2,1)}, u32[]{:S(2)}, u32[]{:S(2)}) collective-permute-start(bf16[4,64,512]{2,1,0:T(8,128)(2,1)S(1)} %get-tuple-element.20.own), channel_id=1, source_target_pairs={{0,4},{4,0},{1,5},{5,1},{2,6},{6,2},{3,7},{7,3},{8,12},{12,8},{9,1... | collective-permute-start | bytes 786440 | tf_op jit(solution)/shard_map/ppermute | solution.py:375
  43.1 1.0 %copy-start.8 = (bf16[256,1024]{1,0:T(8,128)(2,1)S(1)}, bf16[256,1024]{1,0:T(8,128)(2,1)}, u32[]{:S(2)}) copy-start(bf16[256,1024]{1,0:T(8,128)(2,1)} %copy-done.7) | copy-start | bytes 1572868
  58.2 0.8 copy-start.3
  59.0 23.7 %all-to-all-start.3 = ((bf16[16,16,1024]{2,1,0:T(8,128)(2,1)}), bf16[16,16,1024]{2,1,0:T(8,128)(2,1)S(1)}, u32[]{:S(2)}, u32[]{:S(2)}) async-start(bf16[16,16,1024]{2,1,0:T(8,128)(2,1)} %bitcast.16), calls=%async_computation.3 | async-start | bytes 1048576 | tf_op jit(solution)/shard_map/all_to_all | solution.py:398
  63.0 1.2 %copy-start.2 = (bf16[1024,512]{1,0:T(8,128)(2,1)S(1)}, bf16[1024,512]{1,0:T(8,128)(2,1)}, u32[]{:S(2)}) copy-start(bf16[1024,512]{1,0:T(8,128)(2,1)} %wkv.3) | copy-start | bytes 3145732
  65.0 16.1 %collective-permute-start = (bf16[4,64,512]{2,1,0:T(8,128)(2,1)S(1)}, bf16[4,64,512]{2,1,0:T(8,128)(2,1)S(1)}, u32[]{:S(2)}, u32[]{:S(2)}) collective-permute-start(bf16[4,64,512]{2,1,0:T(8,128)(2,1)S(1)} %get-tuple-element.16.own), channel_id=1, source_target_pairs={{0,4},{4,0},{1,5},{5,1},{2,6},{6,2},{3,7},{7,3},{8,12},{12,8},{9,1... | collective-permute-start | bytes 786440 | tf_op jit(solution)/shard_map/ppermute | solution.py:375
  69.3 27.8 %copy-start.5 = (bf16[256,1024]{1,0:T(8,128)(2,1)S(1)}, bf16[256,1024]{1,0:T(8,128)(2,1)}, u32[]{:S(2)}) copy-start(bf16[256,1024]{1,0:T(8,128)(2,1)} %get-tuple-element.21.refs_2_) | copy-start | bytes 1572868
  69.3 27.8 %copy-start.6 = (bf16[256,1024]{1,0:T(8,128)(2,1)S(1)}, bf16[256,1024]{1,0:T(8,128)(2,1)}, u32[]{:S(2)}) copy-start(bf16[256,1024]{1,0:T(8,128)(2,1)} %get-tuple-element.22.refs_3_) | copy-start | bytes 1572868
  97.1 1.6 %copy-start.4 = (bf16[1024,1024]{1,0:T(8,128)(2,1)S(1)}, bf16[1024,1024]{1,0:T(8,128)(2,1)}, u32[]{:S(2)}) copy-start(bf16[1024,1024]{1,0:T(8,128)(2,1)} %refs_4_.5) | copy-start | bytes 6291460

commit v9 on v8

--- a/solution.py
+++ b/solution.py
@@ -23,6 +23,7 @@
 HALVES = 2
 CHUNKS = 2
 DEPTH = 2
+SHADOW = 100
 MIB = 1024 * 1024
 F32 = jnp.float32
 BF16 = jnp.bfloat16
@@ -361,11 +362,13 @@
     swap = [(h, HALVES - 1 - h) for h in range(HALVES)]
     half = lax.axis_index("half").astype(jnp.int32).reshape(1)
     big = 16 + 16 * GROUPS * HALVES * total**2 // MIB
-    mixes = []
+    homes, mixes = [], []
     for i, sent in enumerate(sents):
         deep = sent.shape[-1]
         there = lax.all_to_all(sent, spread, split_axis=0, concat_axis=0, tiled=True)
         there = there.reshape(rows, deep)
+        if i + 1 < chunks:
+            there, sents[i + 1] = lax.optimization_barrier((there, sents[i + 1]))
         second, own = call(
             functools.partial(keys_kernel, local),
             [struct((rows, width), BF16), struct((local, total, 2 * KEYS), BF16)],
@@ -384,8 +387,14 @@
             query_kernel,
             [struct((local, total, width), BF16)],
             [second, wq_space],
-            flops=2 * rows * width * width,
-        )
+            flops=(2 if i == 0 else SHADOW) * rows * width * width,
+        )
+        homes.append((query, own, other))
+    for i in range(chunks - 1):
+        (query, own, other), (later, *held) = homes[i], homes[i + 1]
+        own, held[0] = lax.optimization_barrier((own, held[0]))
+        homes[i], homes[i + 1] = (query, own, other), (later, *held)
+    for query, own, other in homes:
         mix = call(
             functools.partial(space_kernel, beside(total, local)),
             [struct((rows, width), BF16)],

time: 102 us -> 85.7 us (0.84)
  blocking collectives: 31.4 us -> 13.2 us
  starting transfers between devices: 13.7 us -> 16.3 us
  Pallas kernels: 26.9 us -> 28.6 us
  local copies, waits for them, and re-layouts: 6.69 us -> 5.55 us
  waiting for transfers between devices: 22.3 us -> 21.2 us
    all_to_all x1 -> x0, blocking collectives: 17 us -> none  [per_device(): lax.all_to_all(sent, spread, split_axis=0, concat_axis=0, tiled=True)]
    ppermute x2, waiting for transfers between devices: 13.6 us -> 4.1 us  [per_device(): other = lax.ppermute(own, 'half', swap)]
    all_to_all x1 -> x2, starting transfers between devices: 3.58 us -> 9.87 us  [per_device(): lax.all_to_all(sent, spread, split_axis=0, concat_axis=0, tiled=True)]
    all_to_all x1, waiting for transfers between devices: 0.01 us -> 4.71 us  [per_device(): mix = lax.all_to_all(mix, spread, split_axis=0, concat_axis=0, tiled=True)]
    all_to_all x1 -> x2, waiting for transfers between devices: 8.67 us -> 12.4 us  [per_device(): lax.all_to_all(sent, spread, split_axis=0, concat_axis=0, tiled=True)]
    ppermute x2, starting transfers between devices: 6.12 us -> 2.66 us  [per_device(): other = lax.ppermute(own, 'half', swap)]
    pallas_call x10, Pallas kernels: 26.9 us -> 28.6 us  [call(): pl.pallas_call(kernel, out_shape=list(shapes), in_specs=[pl.BlockSpec(mem...]
    all_to_all x1, blocking collectives: 14.4 us -> 13.2 us  [per_device(): mix = lax.all_to_all(mix, spread, split_axis=0, concat_axis=0, tiled=True)]
  transfers between devices with their start and end apart: 4 -> 5, of which waited for: 3 -> 4; matrix products, arithmetic and copies ran while one was open for 0% -> 0% of each run, Pallas kernels for 5% -> 21%
where the time goes in v9:
time: 85.7 us; the launch traced here: 85 us
  Pallas kernels  28.6 us (33%)
  waiting for transfers between devices  21.2 us (25%)
  starting transfers between devices  16.3 us (19%)
  blocking collectives  13.2 us (15%)
  local copies, waits for them, and re-layouts  5.55 us (6%)
    pallas_call x10, Pallas kernels, call(): pl.pallas_call(kernel, out_shape=list(shapes), in_specs=[pl.BlockSpec(mem...  28.6 us
    all_to_all x1, blocking collectives, per_device(): mix = lax.all_to_all(mix, spread, split_axis=0, concat_axis=0, tiled=True)  13.2 us
    all_to_all x2, waiting for transfers between devices, per_device(): lax.all_to_all(sent, spread, split_axis=0, concat_axis=0, tiled=True)  12.4 us
    all_to_all x2, starting transfers between devices, per_device(): lax.all_to_all(sent, spread, split_axis=0, concat_axis=0, tiled=True)  9.87 us
    unnamed x18, local copies, waits for them, and re-layouts  5.55 us
    all_to_all x1, waiting for transfers between devices, per_device(): mix = lax.all_to_all(mix, spread, split_axis=0, concat_axis=0, tiled=True)  4.71 us
    ppermute x2, waiting for transfers between devices, per_device(): other = lax.ppermute(own, 'half', swap)  4.1 us
    all_to_all x1, starting transfers between devices, per_device(): mix = lax.all_to_all(mix, spread, split_axis=0, concat_axis=0, tiled=True)  3.75 us
  transfers between devices with their start and end apart: 5, of which 4 were waited for; matrix products, arithmetic and copies ran while one was open for 0% of the time, Pallas kernels for 21%

profile of v9, /device:TPU:0, one launch (start us, length us, event | category | flops | bytes accessed | tf_op | source)
XLA Modules:
  0.0 85.0 jit_solution(7254407073372611733)
XLA Ops:
  0.0 8.4 %shard_map.118 = (bf16[256,1024]{1,0:T(8,128)(2,1)}, bf16[256,1152]{1,0:T(8,128)(2,1)}, bf16[256,512]{1,0:T(8,128)(2,1)}) custom-call(bf16[512,1024]{1,0:T(8,128)(2,1)} %bitcast.21, f32[1,1024]{1,0:T(1,128)} %bitcast.25, bf16[1024,1024]{1,0:T(8,128)(2,1)} %refs_2_.3, bf16[1024,512]{1,0:T(8,128)(2,1)} %refs_3_.3, bf16[1024,1024]{1,0:T(8,128)(2,1)} %refs_4_.4, ...), custom_call_target="tpu_custom_call" | custom-call | flops 1342177280 | bytes 7671968 | tf_op jit(solution)/shard_map/pallas_call | solution.py:288
  8.4 6.3 %all-to-all-start = ((bf16[16,16,1152]{2,1,0:T(8,128)(2,1)}), bf16[16,16,1152]{2,1,0:T(8,128)(2,1)S(1)}, u32[]{:S(2)}, u32[]{:S(2)}) async-start(bf16[16,16,1152]{2,1,0:T(8,128)(2,1)} %bitcast.23), calls=%async_computation | async-start | bytes 1179648 | tf_op jit(solution)/shard_map/all_to_all | solution.py:368
  14.7 0.0 copy-start
  14.7 0.0 copy-start.6
  14.7 8.8 %shard_map.119 = (bf16[256,1024]{1,0:T(8,128)(2,1)}, bf16[256,1024]{1,0:T(8,128)(2,1)}, bf16[256,512]{1,0:T(8,128)(2,1)}) custom-call(bf16[512,1024]{1,0:T(8,128)(2,1)} %bitcast.22, f32[1,1024]{1,0:T(1,128)} %bitcast.26, bf16[1024,1024]{1,0:T(8,128)(2,1)} %refs_2_.3, bf16[1024,512]{1,0:T(8,128)(2,1)} %refs_3_.3, bf16[1024,1024]{1,0:T(8,128)(2,1)} %refs_4_.4, ...), custom_call_target="tpu_custom_call" | custom-call | flops 1342177280 | bytes 7868416 | tf_op jit(solution)/shard_map/pallas_call | solution.py:288
  23.5 2.4 %all-to-all-done = bf16[16,16,1152]{2,1,0:T(8,128)(2,1)S(1)} async-done(((bf16[16,16,1152]{2,1,0:T(8,128)(2,1)}), bf16[16,16,1152]{2,1,0:T(8,128)(2,1)S(1)}, u32[]{:S(2)}, u32[]{:S(2)}) %all-to-all-start) | async-done | bytes 589856 | tf_op jit(solution)/shard_map/all_to_all | solution.py:368
  25.9 3.6 %all-to-all-start.1 = ((bf16[16,16,1024]{2,1,0:T(8,128)(2,1)}), bf16[16,16,1024]{2,1,0:T(8,128)(2,1)S(1)}, u32[]{:S(2)}, u32[]{:S(2)}) async-start(bf16[16,16,1024]{2,1,0:T(8,128)(2,1)} %bitcast.24), calls=%async_computation.1 | async-start | bytes 1048576 | tf_op jit(solution)/shard_map/all_to_all | solution.py:368
  29.5 0.0 copy-done
  29.5 0.0 copy-done.6
  29.5 0.8 shard_map.120
  30.3 2.7 %collective-permute-start = (bf16[4,64,512]{2,1,0:T(8,128)(2,1)S(1)}, bf16[4,64,512]{2,1,0:T(8,128)(2,1)S(1)}, u32[]{:S(2)}, u32[]{:S(2)}) collective-permute-start(bf16[4,64,512]{2,1,0:T(8,128)(2,1)S(1)} %get-tuple-element.26.own), channel_id=1, source_target_pairs={{0,4},{4,0},{1,5},{5,1},{2,6},{6,2},{3,7},{7,3},{8,12},{12,8},{9,1... | collective-permute-start | bytes 786440 | tf_op jit(solution)/shard_map/ppermute | solution.py:378
  33.0 0.4 shard_map.123.weights
  33.3 0.0 copy-start.1
  33.4 1.6 %copy-done.1 = bf16[1024,1024]{1,0:T(8,128)(2,1)S(1)} copy-done((bf16[1024,1024]{1,0:T(8,128)(2,1)S(1)}, bf16[1024,1024]{1,0:T(8,128)(2,1)}, u32[]{:S(2)}) %copy-start.1) | copy-done | bytes 2097176
  34.9 0.7 shard_map.121.query
  35.6 10.0 %all-to-all-done.1 = bf16[16,16,1024]{2,1,0:T(8,128)(2,1)S(1)} async-done(((bf16[16,16,1024]{2,1,0:T(8,128)(2,1)}), bf16[16,16,1024]{2,1,0:T(8,128)(2,1)S(1)}, u32[]{:S(2)}, u32[]{:S(2)}) %all-to-all-start.1) | async-done | bytes 524320 | tf_op jit(solution)/shard_map/all_to_all | solution.py:368
  45.6 1.5 %shard_map.122 = (bf16[256,1024]{1,0:T(8,128)(2,1)S(1)}, bf16[4,64,512]{2,1,0:T(8,128)(2,1)}) custom-call(bf16[256,1024]{1,0:T(8,128)(2,1)S(1)} %bitcast.15, f32[1,1024]{1,0:T(1,128)S(1)} %bitcast.20, bf16[1024,512]{1,0:T(8,128)(2,1)S(1)} %copy-done), custom_call_target="tpu_custom_call" | custom-call | flops 268435456 | bytes 2363392 | tf_op jit(solution)/shard_map/pallas_call | solution.py:288
  47.1 0.0 copy-start.7
  47.1 0.8 copy-done.7
  47.9 0.0 copy-start.2
  47.9 0.0 collective-permute-start.1
  47.9 0.0 collective-permute-done.other
  47.9 2.3 %shard_map.124 = bf16[256,1024]{1,0:T(8,128)(2,1)} custom-call(bf16[4,64,1024]{2,1,0:T(8,128)(2,1)S(1)} %shard_map.121.query, bf16[4,64,512]{2,1,0:T(8,128)(2,1)S(1)} %get-tuple-element.26.own, bf16[4,64,512]{2,1,0:T(8,128)(2,1)S(1)} %collective-permute-done.other, f32[128,64]{1,0:T(8,128)S(1)} %shard_map.123.weights), custom_call_target="tpu_custom_call" | custom-call | flops 134217728 | bytes 1605632 | tf_op jit(solution)/shard_map/pallas_call | solution.py:288
  50.3 3.8 %all-to-all-start.2 = ((bf16[16,16,1024]{2,1,0:T(8,128)(2,1)}), bf16[16,16,1024]{2,1,0:T(8,128)(2,1)S(1)}, u32[]{:S(2)}, u32[]{:S(2)}) async-start(bf16[16,16,1024]{2,1,0:T(8,128)(2,1)} %bitcast.8), calls=%async_computation.2 | async-start | bytes 1048576 | tf_op jit(solution)/shard_map/all_to_all | solution.py:407
  54.0 0.0 copy-done.2
  54.0 0.0 copy-start.8
  54.1 1.0 %copy-done.8 = bf16[256,1024]{1,0:T(8,128)(2,1)S(1)} copy-done((bf16[256,1024]{1,0:T(8,128)(2,1)S(1)}, bf16[256,1024]{1,0:T(8,128)(2,1)}, u32[]{:S(2)}) %copy-start.8) | copy-done | bytes 524312
  55.1 0.7 shard_map.125.query
  55.8 0.0 copy-start.3
  55.8 4.1 %collective-permute-done.1.other = bf16[4,64,512]{2,1,0:T(8,128)(2,1)} collective-permute-done((bf16[4,64,512]{2,1,0:T(8,128)(2,1)}, bf16[4,64,512]{2,1,0:T(8,128)(2,1)}, u32[]{:S(2)}, u32[]{:S(2)}) %collective-permute-start.1) | collective-permute-done | bytes 262176 | tf_op jit(solution)/shard_map/ppermute | solution.py:378
  59.9 2.6 %shard_map.126 = bf16[256,1024]{1,0:T(8,128)(2,1)S(1)} custom-call(bf16[4,64,1024]{2,1,0:T(8,128)(2,1)S(1)} %shard_map.125.query, bf16[4,64,512]{2,1,0:T(8,128)(2,1)} %get-tuple-element.28.own, bf16[4,64,512]{2,1,0:T(8,128)(2,1)} %collective-permute-done.1.other, f32[128,64]{1,0:T(8,128)S(1)} %shard_map.123.weights), custom_call_target="tpu_custom_call" | custom-call | flops 134217728 | bytes 1605632 | tf_op jit(solution)/shard_map/pallas_call | solution.py:288
  62.5 4.7 %all-to-all-done.2 = bf16[16,16,1024]{2,1,0:T(8,128)(2,1)S(1)} async-done(((bf16[16,16,1024]{2,1,0:T(8,128)(2,1)}), bf16[16,16,1024]{2,1,0:T(8,128)(2,1)S(1)}, u32[]{:S(2)}, u32[]{:S(2)}) %all-to-all-start.2) | async-done | bytes 524320 | tf_op jit(solution)/shard_map/all_to_all | solution.py:407
  67.2 13.2 %all_to_all.20 = bf16[16,16,1024]{2,1,0:T(8,128)(2,1)S(1)} all-to-all(bf16[16,16,1024]{2,1,0:T(8,128)(2,1)S(1)} %bitcast.17), channel_id=1, replica_groups=mesh['tile'=4,'half'=2,'rest'=4] {'tile','rest'}, dimensions={0} | all-to-all | bytes 1048576 | tf_op jit(solution)/shard_map/all_to_all | solution.py:407
  80.4 0.0 copy-done.3
  80.4 0.0 copy-start.4
  80.4 1.0 %copy-done.4 = bf16[256,1024]{1,0:T(8,128)(2,1)S(1)} copy-done((bf16[256,1024]{1,0:T(8,128)(2,1)S(1)}, bf16[256,1024]{1,0:T(8,128)(2,1)}, u32[]{:S(2)}) %copy-start.4) | copy-done | bytes 524312
  81.4 0.0 copy-start.5
  81.4 1.0 %copy-done.5 = bf16[256,1024]{1,0:T(8,128)(2,1)S(1)} copy-done((bf16[256,1024]{1,0:T(8,128)(2,1)S(1)}, bf16[256,1024]{1,0:T(8,128)(2,1)}, u32[]{:S(2)}) %copy-start.5) | copy-done | bytes 524312
  82.5 2.5 %shard_map.127 = bf16[4,128,1024]{2,1,0:T(8,128)(2,1)} custom-call(bf16[256,1024]{1,0:T(8,128)(2,1)S(1)} %bitcast.16, bf16[256,1024]{1,0:T(8,128)(2,1)S(1)} %bitcast.18, bf16[256,1024]{1,0:T(8,128)(2,1)S(1)} %copy-done.4, bf16[256,1024]{1,0:T(8,128)(2,1)S(1)} %copy-done.5, bf16[1024,1024]{1,0:T(8,128)(2,1)S(1)} %copy-done.3), custom_call_target="tpu_custom_call" | custom-call | flops 536870912 | bytes 5242880 | tf_op jit(solution)/shard_map/pallas_call | solution.py:288
Async XLA Ops:
  8.4 17.6 %all-to-all-start = ((bf16[16,16,1152]{2,1,0:T(8,128)(2,1)}), bf16[16,16,1152]{2,1,0:T(8,128)(2,1)S(1)}, u32[]{:S(2)}, u32[]{:S(2)}) async-start(bf16[16,16,1152]{2,1,0:T(8,128)(2,1)} %bitcast.23), calls=%async_computation | async-start | bytes 1179648 | tf_op jit(solution)/shard_map/all_to_all | solution.py:368
  14.7 14.8 %copy-start = (bf16[1024,512]{1,0:T(8,128)(2,1)S(1)}, bf16[1024,512]{1,0:T(8,128)(2,1)}, u32[]{:S(2)}) copy-start(bf16[1024,512]{1,0:T(8,128)(2,1)} %wkv.3) | copy-start | bytes 3145732
  14.7 14.8 %copy-start.6 = (f32[1024]{0:T(1024)S(1)}, f32[1024]{0:T(1024)}, u32[]{:S(2)}) copy-start(f32[1024]{0:T(1024)} %param.17) | copy-start | bytes 12292
  25.9 19.7 %all-to-all-start.1 = ((bf16[16,16,1024]{2,1,0:T(8,128)(2,1)}), bf16[16,16,1024]{2,1,0:T(8,128)(2,1)S(1)}, u32[]{:S(2)}, u32[]{:S(2)}) async-start(bf16[16,16,1024]{2,1,0:T(8,128)(2,1)} %bitcast.24), calls=%async_computation.1 | async-start | bytes 1048576 | tf_op jit(solution)/shard_map/all_to_all | solution.py:368
  30.3 17.6 %collective-permute-start = (bf16[4,64,512]{2,1,0:T(8,128)(2,1)S(1)}, bf16[4,64,512]{2,1,0:T(8,128)(2,1)S(1)}, u32[]{:S(2)}, u32[]{:S(2)}) collective-permute-start(bf16[4,64,512]{2,1,0:T(8,128)(2,1)S(1)} %get-tuple-element.26.own), channel_id=1, source_target_pairs={{0,4},{4,0},{1,5},{5,1},{2,6},{6,2},{3,7},{7,3},{8,12},{12,8},{9,1... | collective-permute-start | bytes 786440 | tf_op jit(solution)/shard_map/ppermute | solution.py:378
  33.3 1.6 %copy-start.1 = (bf16[1024,1024]{1,0:T(8,128)(2,1)S(1)}, bf16[1024,1024]{1,0:T(8,128)(2,1)}, u32[]{:S(2)}) copy-start(bf16[1024,1024]{1,0:T(8,128)(2,1)} %wq.3) | copy-start | bytes 6291460
  47.1 0.8 copy-start.7
  47.9 6.1 %copy-start.2 = (bf16[1024,1024]{1,0:T(8,128)(2,1)S(1)}, bf16[1024,1024]{1,0:T(8,128)(2,1)}, u32[]{:S(2)}) copy-start(bf16[1024,1024]{1,0:T(8,128)(2,1)} %wq.3) | copy-start | bytes 6291460
  47.9 12.0 %collective-permute-start.1 = (bf16[4,64,512]{2,1,0:T(8,128)(2,1)}, bf16[4,64,512]{2,1,0:T(8,128)(2,1)}, u32[]{:S(2)}, u32[]{:S(2)}) collective-permute-start(bf16[4,64,512]{2,1,0:T(8,128)(2,1)} %get-tuple-element.28.own), channel_id=1, source_target_pairs={{0,4},{4,0},{1,5},{5,1},{2,6},{6,2},{3,7},{7,3},{8,12},{12,8},{9,1... | collective-permute-start | bytes 786440 | tf_op jit(solution)/shard_map/ppermute | solution.py:378
  50.3 16.9 %all-to-all-start.2 = ((bf16[16,16,1024]{2,1,0:T(8,128)(2,1)}), bf16[16,16,1024]{2,1,0:T(8,128)(2,1)S(1)}, u32[]{:S(2)}, u32[]{:S(2)}) async-start(bf16[16,16,1024]{2,1,0:T(8,128)(2,1)} %bitcast.8), calls=%async_computation.2 | async-start | bytes 1048576 | tf_op jit(solution)/shard_map/all_to_all | solution.py:407
  54.0 1.0 %copy-start.8 = (bf16[256,1024]{1,0:T(8,128)(2,1)S(1)}, bf16[256,1024]{1,0:T(8,128)(2,1)}, u32[]{:S(2)}) copy-start(bf16[256,1024]{1,0:T(8,128)(2,1)} %copy-done.7) | copy-start | bytes 1572868
  55.8 24.6 %copy-start.3 = (bf16[1024,1024]{1,0:T(8,128)(2,1)S(1)}, bf16[1024,1024]{1,0:T(8,128)(2,1)}, u32[]{:S(2)}) copy-start(bf16[1024,1024]{1,0:T(8,128)(2,1)} %refs_4_.5) | copy-start | bytes 6291460
  80.4 1.0 %copy-start.4 = (bf16[256,1024]{1,0:T(8,128)(2,1)S(1)}, bf16[256,1024]{1,0:T(8,128)(2,1)}, u32[]{:S(2)}) copy-start(bf16[256,1024]{1,0:T(8,128)(2,1)} %get-tuple-element.29.refs_2_) | copy-start | bytes 1572868
  81.4 1.0 %copy-start.5 = (bf16[256,1024]{1,0:T(8,128)(2,1)S(1)}, bf16[256,1024]{1,0:T(8,128)(2,1)}, u32[]{:S(2)}) copy-start(bf16[256,1024]{1,0:T(8,128)(2,1)} %get-tuple-element.30.refs_3_) | copy-start | bytes 1572868

commit v10 on v9

--- a/solution.py
+++ b/solution.py
@@ -36,18 +36,15 @@
     return (wide * lax.rsqrt(meansq + 1e-05) * gain).astype(BF16)
 
 
-def one_hot(rows, source, turned=False):
-    row = lax.broadcasted_iota(jnp.int32, (rows, rows), 1 if turned else 0)
-    col = lax.broadcasted_iota(jnp.int32, (rows, rows), 0 if turned else 1)
-    return jnp.where(col == source(row), 1.0, 0.0).astype(BF16)
-
-
-def block_source(agents, span, local):
-    return lambda row: row // local % agents * span + row // (local * agents) * local + row % local
-
-
-def step_source(total, local):
-    return lambda row: row % total * local + row // total
+def one_hot(rows, target):
+    row = lax.broadcasted_iota(jnp.int32, (rows, rows), 0)
+    wanted = target(lax.broadcasted_iota(jnp.int32, (1, rows), 1))
+    return jnp.where(row == wanted, 1.0, 0.0).astype(BF16)
+
+
+def regroup(row, first, second, third):
+    i, j, k = row // (second * third), row // third % second, row % third
+    return (j * first + i) * third + k
 
 
 def moved(order, piece):
@@ -124,9 +121,11 @@
 def time_kernel(agents, steps, span, chunk, local, pair, *refs):
     hist_hbm, gain, wq_hbm, wkv_hbm, wo_hbm, *refs = refs
     before, refs = refs[:chunk], refs[chunk:]
+    refs = refs[1:] if chunk else refs
     listing, refs = (refs[:3], refs[3:]) if chunk == 0 else ((), refs)
-    mid, sent, keyval, *refs = refs
-    hist, wq, wkv, wo, normed, query, mix, hist_sems, wq_sems, sems = refs
+    mid_hbm, sent_hbm, keyval_hbm, *refs = refs
+    mid, sent, keyval, hist, wq, wkv, wo, normed, query, mix, *refs = refs
+    hist_sems, wq_sems, sems, mid_sems, sent_sems, keyval_sem = refs
     rows, width = hist.shape
     hist_loads, wq_loads = [], []
     for a in range(agents):
@@ -157,6 +156,8 @@
         keyval[:, c : c + COLS] = jnp.dot(
             normed[...], wkv[:, c : c + COLS], preferred_element_type=F32
         ).astype(BF16)
+    keeps = [pltpu.make_async_copy(keyval, keyval_hbm, keyval_sem)]
+    keeps[0].start()
     loads[1].start()
     for c in range(0, width, COLS):
         wq_loads[c // COLS].wait()
@@ -182,7 +183,7 @@
         agents, pair, span, lambda a, cols: query[a * span : (a + 1) * span, cols],
         keyvals, store, valid,
     )
-    order = one_hot(rows, block_source(agents, span, local))
+    order = one_hot(rows, lambda row: regroup(row, agents, span // local, local))
     loads[1].wait()
     for c in range(0, width, COLS):
         cols = slice(c, c + COLS)
@@ -190,6 +191,17 @@
         piece = (hist[:, cols].astype(F32) + projected).astype(BF16)
         mid[:, cols] = piece
         sent[:, cols] = moved(order, piece)
+        part = pl.ds(c, COLS)
+        keeps.append(
+            pltpu.make_async_copy(sent.at[:, part], sent_hbm.at[:, part], sent_sems.at[c // COLS])
+        )
+        keeps[-1].start()
+    for a in range(agents):
+        goal = mid_hbm.at[a, pl.ds(chunk * span, span), :]
+        keeps.append(
+            pltpu.make_async_copy(mid.at[pl.ds(a * span, span), :], goal, mid_sems.at[a])
+        )
+        keeps[-1].start()
     if listing:
         neighbours, nbr_valid, alive = listing
         lane = lax.broadcasted_iota(jnp.int32, (1, LANES), 1)
@@ -200,6 +212,15 @@
             listed = lane == alive.shape[1] + neighbours[0, i]
             notes = notes + jnp.where(listed, nbr_valid[0, i].astype(F32), 0.0)
         sent[:, width:] = jnp.broadcast_to(notes, (rows, LANES)).astype(BF16)
+        part = pl.ds(width, LANES)
+        keeps.append(
+            pltpu.make_async_copy(
+                sent.at[:, part], sent_hbm.at[:, part], sent_sems.at[width // COLS]
+            )
+        )
+        keeps[-1].start()
+    for keep in keeps:
+        keep.wait()
 
 
 def keys_kernel(local, mid, gain, wkv, second, out):
@@ -207,7 +228,7 @@
     total = rows // local
     second[...] = norm_rows(mid[:, :width], gain[...])
     if local > 1:
-        order = one_hot(rows, step_source(total, local))
+        order = one_hot(rows, lambda row: regroup(row, total, local, 1))
         for c in range(0, width, COLS):
             second[:, c : c + COLS] = moved(order, second[:, c : c + COLS])
     for c in range(0, 2 * KEYS, COLS):
@@ -260,28 +281,46 @@
         local, pair, total, lambda s, cols: query[s, :, cols], keyvals, store, weight > 0, weight
     )
     if local > 1:
-        order = one_hot(rows, step_source(total, local), turned=True)
+        order = one_hot(rows, lambda row: regroup(row, local, total, 1))
     for c in range(0, width, COLS):
         piece = mix[:, c : c + COLS]
         out[:, c : c + COLS] = moved(order, piece) if local > 1 else piece
 
 
 def out_kernel(agents, span, local, chunks, *refs):
-    mixes, mids, (wo, out, mix) = refs[:chunks], refs[chunks : 2 * chunks], refs[2 * chunks :]
-    rows, width = mids[0].shape
-    order = one_hot(rows, block_source(agents, span, local), turned=True)
+    mixes, (mid_hbm, wo, out_hbm, mix, mids, sems, out_sems) = refs[:chunks], refs[chunks:]
+    rows, width = mixes[0].shape
+    loads = [
+        pltpu.make_async_copy(mid_hbm.at[:, pl.ds(i * span, span), :], mids.at[i], sems.at[i])
+        for i in range(chunks)
+    ]
+    for load in loads:
+        load.start()
+    order = one_hot(rows, lambda row: regroup(row, span // local, agents, local))
     for c in range(0, width, COLS):
         for i in range(chunks):
             mix[i * rows : (i + 1) * rows, c : c + COLS] = moved(order, mixes[i][:, c : c + COLS])
+    for load in loads:
+        load.wait()
     for c in range(0, width, COLS):
         cols = slice(c, c + COLS)
         projected = jnp.dot(mix[...], wo[:, cols], preferred_element_type=F32)
         for i in range(chunks):
-            piece = mids[i][:, cols].astype(F32) + projected[i * rows : (i + 1) * rows]
-            out[:, i * span : (i + 1) * span, cols] = piece.astype(BF16).reshape(agents, span, COLS)
-
-
-def call(kernel, shapes, args, hbm=(), smem=(), scratch=(), flops=0, mib=16):
+            piece = projected[i * rows : (i + 1) * rows].reshape(agents, span, COLS)
+            mids[i, :, :, cols] = (mids[i, :, :, cols].astype(F32) + piece).astype(BF16)
+    keeps = [
+        pltpu.make_async_copy(mids.at[i], out_hbm.at[:, pl.ds(i * span, span), :], out_sems.at[i])
+        for i in range(chunks)
+    ]
+    for keep in keeps:
+        keep.start()
+    for keep in keeps:
+        keep.wait()
+
+
+def call(
+    kernel, shapes, args, hbm=(), hbm_out=(), smem=(), aliases=None, scratch=(), flops=0, mib=16
+):
     touched = sum(a.size * a.dtype.itemsize for a in args)
     touched += sum(s.size * s.dtype.itemsize for s in shapes)
     spaces = [pl.ANY if i in hbm else pltpu.VMEM for i in range(len(args))]
@@ -292,8 +331,12 @@
             pl.BlockSpec(memory_space=pltpu.SMEM if i in smem else space)
             for i, space in enumerate(spaces)
         ],
-        out_specs=[pl.BlockSpec(memory_space=pltpu.VMEM)] * len(shapes),
+        out_specs=[
+            pl.BlockSpec(memory_space=pl.ANY if i in hbm_out else pltpu.VMEM)
+            for i in range(len(shapes))
+        ],
         scratch_shapes=list(scratch),
+        input_output_aliases=aliases or {},
         compiler_params=pltpu.CompilerParams(vmem_limit_bytes=mib * MIB),
         cost_estimate=pl.CostEstimate(flops=flops, bytes_accessed=touched, transcendentals=0),
     )(*args)
@@ -330,17 +373,24 @@
 
     hist = histories.reshape(agents * steps, width)
     mids, sents, before = [], [], []
+    whole = struct((agents, steps, width), BF16)
     for i in range(chunks):
         deep = width + LANES if i == 0 else width
         mid, sent, keyval = call(
             functools.partial(time_kernel, agents, steps, span, i, local, beside(span, agents)),
-            [struct((rows, width), BF16), struct((rows, deep), BF16), struct((rows, 2 * KEYS), BF16)],
+            [whole, struct((rows, deep), BF16), struct((rows, 2 * KEYS), BF16)],
             [hist, gain_time[None], wq_time, wkv_time, wo_time]
             + before
+            + mids
             + ([neighbours, nbr_valid, agent_valid] if i == 0 else []),
-            hbm=(0, 2, 3, 4),
+            hbm=(0, 2, 3, 4) + ((5 + i,) if i else ()),
+            aliases={5 + i: 0} if i else None,
             smem=(5, 6, 7) if i == 0 else (),
+            hbm_out=(0, 1, 2),
             scratch=[
+                pltpu.VMEM((rows, width), BF16),
+                pltpu.VMEM((rows, deep), BF16),
+                pltpu.VMEM((rows, 2 * KEYS), BF16),
                 pltpu.VMEM((rows, width), BF16),
                 pltpu.VMEM(wq_time.shape, BF16),
                 pltpu.VMEM(wkv_time.shape, BF16),
@@ -351,11 +401,14 @@
                 pltpu.SemaphoreType.DMA((agents,)),
                 pltpu.SemaphoreType.DMA((width // COLS,)),
                 pltpu.SemaphoreType.DMA((2,)),
+                pltpu.SemaphoreType.DMA((agents,)),
+                pltpu.SemaphoreType.DMA((width // COLS + 1,)),
+                pltpu.SemaphoreType.DMA,
             ],
             flops=2 * rows * width * (2 * width + 2 * KEYS),
             mib=56,
         )
-        mids.append(mid)
+        mids = [mid]
         sents.append(sent.reshape(parts, agents * local, deep))
         before.append(keyval)
 
@@ -408,9 +461,17 @@
         mixes.append(mix.reshape(rows, width))
     out = call(
         functools.partial(out_kernel, agents, span, local, chunks),
-        [struct((agents, steps, width), BF16)],
+        [whole],
         mixes + mids + [wo_space],
-        scratch=[pltpu.VMEM((agents * steps, width), BF16)],
+        hbm=(chunks,),
+        hbm_out=(0,),
+        aliases={chunks: 0},
+        scratch=[
+            pltpu.VMEM((agents * steps, width), BF16),
+            pltpu.VMEM((chunks, agents, span, width), BF16),
+            pltpu.SemaphoreType.DMA((chunks,)),
+            pltpu.SemaphoreType.DMA((chunks,)),
+        ],
         flops=2 * rows * width * width,
     )
     return out[None]

time: 85.7 us -> 84.7 us (0.988)
  local copies, waits for them, and re-layouts: 5.55 us -> 3.45 us
  Pallas kernels: 28.6 us -> 29.5 us
    unnamed x18 -> x14, local copies, waits for them, and re-layouts: 5.55 us -> 3.45 us
where the time goes in v10:
time: 84.7 us; the launch traced here: 84 us
  Pallas kernels  29.5 us (35%)
  waiting for transfers between devices  21.4 us (25%)
  starting transfers between devices  16.3 us (19%)
  blocking collectives  13.2 us (16%)
  local copies, waits for them, and re-layouts  3.45 us (4%)
    pallas_call x10, Pallas kernels, call(): pl.pallas_call(kernel, out_shape=list(shapes), in_specs=[pl.BlockSpec(mem...  29.5 us
    all_to_all x1, blocking collectives, per_device(): mix = lax.all_to_all(mix, spread, split_axis=0, concat_axis=0, tiled=True)  13.2 us
    all_to_all x2, waiting for transfers between devices, per_device(): lax.all_to_all(sent, spread, split_axis=0, concat_axis=0, tiled=True)  12.6 us
    all_to_all x2, starting transfers between devices, per_device(): lax.all_to_all(sent, spread, split_axis=0, concat_axis=0, tiled=True)  9.87 us
    all_to_all x1, waiting for transfers between devices, per_device(): mix = lax.all_to_all(mix, spread, split_axis=0, concat_axis=0, tiled=True)  4.7 us
    ppermute x2, waiting for transfers between devices, per_device(): other = lax.ppermute(own, 'half', swap)  4.08 us
    all_to_all x1, starting transfers between devices, per_device(): mix = lax.all_to_all(mix, spread, split_axis=0, concat_axis=0, tiled=True)  3.75 us
    unnamed x14, local copies, waits for them, and re-layouts  3.45 us
  transfers between devices with their start and end apart: 5, of which 4 were waited for; matrix products, arithmetic and copies ran while one was open for 0% of the time, Pallas kernels for 21%

profile of v10, /device:TPU:0, one launch (start us, length us, event | category | flops | bytes accessed | tf_op | source)
XLA Modules:
  0.0 84.0 jit_solution(5227224617939047199)
XLA Ops:
  0.0 8.2 %shard_map.118 = (bf16[4,128,1024]{2,1,0:T(8,128)(2,1)}, bf16[256,1152]{1,0:T(8,128)(2,1)}, bf16[256,512]{1,0:T(8,128)(2,1)}) custom-call(bf16[512,1024]{1,0:T(8,128)(2,1)} %bitcast.21, f32[1,1024]{1,0:T(1,128)} %bitcast.25, bf16[1024,1024]{1,0:T(8,128)(2,1)} %refs_2_.3, bf16[1024,512]{1,0:T(8,128)(2,1)} %refs_3_.4, bf16[1024,1024]{1,0:T(8,128)(2,1)} %refs_4_.3, ...), custom_call_target="tpu_custom_call" | custom-call | flops 1342177280 | bytes 8196256 | tf_op jit(solution)/shard_map/pallas_call | solution.py:327
  8.2 6.3 %all-to-all-start = ((bf16[16,16,1152]{2,1,0:T(8,128)(2,1)}), bf16[16,16,1152]{2,1,0:T(8,128)(2,1)S(1)}, u32[]{:S(2)}, u32[]{:S(2)}) async-start(bf16[16,16,1152]{2,1,0:T(8,128)(2,1)} %bitcast.23), calls=%async_computation | async-start | bytes 1179648 | tf_op jit(solution)/shard_map/all_to_all | solution.py:421
  14.5 0.0 copy-start
  14.6 0.0 copy-start.4
  14.6 8.6 %shard_map.119 = (bf16[4,128,1024]{2,1,0:T(8,128)(2,1)}, bf16[256,1024]{1,0:T(8,128)(2,1)}, bf16[256,512]{1,0:T(8,128)(2,1)}) custom-call(bf16[512,1024]{1,0:T(8,128)(2,1)} %bitcast.22, f32[1,1024]{1,0:T(1,128)} %bitcast.26, bf16[1024,1024]{1,0:T(8,128)(2,1)} %refs_2_.3, bf16[1024,512]{1,0:T(8,128)(2,1)} %refs_3_.4, ...), custom_call_target="tpu_custom_call", output_to_operand_aliasing={{0}: (6, {})} | custom-call | flops 1342177280 | bytes 9441280 | tf_op jit(solution)/shard_map/pallas_call | solution.py:327
  23.2 2.6 %all-to-all-done = bf16[16,16,1152]{2,1,0:T(8,128)(2,1)S(1)} async-done(((bf16[16,16,1152]{2,1,0:T(8,128)(2,1)}), bf16[16,16,1152]{2,1,0:T(8,128)(2,1)S(1)}, u32[]{:S(2)}, u32[]{:S(2)}) %all-to-all-start) | async-done | bytes 589856 | tf_op jit(solution)/shard_map/all_to_all | solution.py:421
  25.8 3.6 %all-to-all-start.1 = ((bf16[16,16,1024]{2,1,0:T(8,128)(2,1)}), bf16[16,16,1024]{2,1,0:T(8,128)(2,1)S(1)}, u32[]{:S(2)}, u32[]{:S(2)}) async-start(bf16[16,16,1024]{2,1,0:T(8,128)(2,1)} %bitcast.24), calls=%async_computation.1 | async-start | bytes 1048576 | tf_op jit(solution)/shard_map/all_to_all | solution.py:421
  29.4 0.0 copy-done
  29.4 0.0 copy-done.4
  29.4 0.7 shard_map.120
  30.1 2.6 %collective-permute-start = (bf16[4,64,512]{2,1,0:T(8,128)(2,1)S(1)}, bf16[4,64,512]{2,1,0:T(8,128)(2,1)S(1)}, u32[]{:S(2)}, u32[]{:S(2)}) collective-permute-start(bf16[4,64,512]{2,1,0:T(8,128)(2,1)S(1)} %get-tuple-element.27.own), channel_id=1, source_target_pairs={{0,4},{4,0},{1,5},{5,1},{2,6},{6,2},{3,7},{7,3},{8,12},{12,8},{9,1... | collective-permute-start | bytes 786440 | tf_op jit(solution)/shard_map/ppermute | solution.py:431
  32.8 0.4 shard_map.123.weights
  33.2 0.0 copy-start.1
  33.2 1.6 %copy-done.1 = bf16[1024,1024]{1,0:T(8,128)(2,1)S(1)} copy-done((bf16[1024,1024]{1,0:T(8,128)(2,1)S(1)}, bf16[1024,1024]{1,0:T(8,128)(2,1)}, u32[]{:S(2)}) %copy-start.1) | copy-done | bytes 2097176
  34.8 0.7 shard_map.121.query
  35.5 10.0 %all-to-all-done.1 = bf16[16,16,1024]{2,1,0:T(8,128)(2,1)S(1)} async-done(((bf16[16,16,1024]{2,1,0:T(8,128)(2,1)}), bf16[16,16,1024]{2,1,0:T(8,128)(2,1)S(1)}, u32[]{:S(2)}, u32[]{:S(2)}) %all-to-all-start.1) | async-done | bytes 524320 | tf_op jit(solution)/shard_map/all_to_all | solution.py:421
  45.5 1.4 %shard_map.122 = (bf16[256,1024]{1,0:T(8,128)(2,1)S(1)}, bf16[4,64,512]{2,1,0:T(8,128)(2,1)}) custom-call(bf16[256,1024]{1,0:T(8,128)(2,1)S(1)} %bitcast.15, f32[1,1024]{1,0:T(1,128)S(1)} %bitcast.20, bf16[1024,512]{1,0:T(8,128)(2,1)S(1)} %copy-done), custom_call_target="tpu_custom_call" | custom-call | flops 268435456 | bytes 2363392 | tf_op jit(solution)/shard_map/pallas_call | solution.py:327
  47.0 0.0 copy-start.5
  47.0 0.8 copy-done.5
  47.8 0.0 copy-start.2
  47.8 0.0 collective-permute-start.1
  47.8 0.0 collective-permute-done.other
  47.8 2.4 %shard_map.124 = bf16[256,1024]{1,0:T(8,128)(2,1)} custom-call(bf16[4,64,1024]{2,1,0:T(8,128)(2,1)S(1)} %shard_map.121.query, bf16[4,64,512]{2,1,0:T(8,128)(2,1)S(1)} %get-tuple-element.27.own, bf16[4,64,512]{2,1,0:T(8,128)(2,1)S(1)} %collective-permute-done.other, f32[128,64]{1,0:T(8,128)S(1)} %shard_map.123.weights), custom_call_target="tpu_custom_call" | custom-call | flops 134217728 | bytes 1605632 | tf_op jit(solution)/shard_map/pallas_call | solution.py:327
  50.1 3.8 %all-to-all-start.2 = ((bf16[16,16,1024]{2,1,0:T(8,128)(2,1)}), bf16[16,16,1024]{2,1,0:T(8,128)(2,1)S(1)}, u32[]{:S(2)}, u32[]{:S(2)}) async-start(bf16[16,16,1024]{2,1,0:T(8,128)(2,1)} %bitcast.8), calls=%async_computation.2 | async-start | bytes 1048576 | tf_op jit(solution)/shard_map/all_to_all | solution.py:460
  53.9 0.0 copy-done.2
  53.9 0.0 copy-start.6
  53.9 1.0 %copy-done.6 = bf16[256,1024]{1,0:T(8,128)(2,1)S(1)} copy-done((bf16[256,1024]{1,0:T(8,128)(2,1)S(1)}, bf16[256,1024]{1,0:T(8,128)(2,1)}, u32[]{:S(2)}) %copy-start.6) | copy-done | bytes 524312
  54.9 0.7 shard_map.125.query
  55.6 0.0 copy-start.3
  55.7 4.1 %collective-permute-done.1.other = bf16[4,64,512]{2,1,0:T(8,128)(2,1)} collective-permute-done((bf16[4,64,512]{2,1,0:T(8,128)(2,1)}, bf16[4,64,512]{2,1,0:T(8,128)(2,1)}, u32[]{:S(2)}, u32[]{:S(2)}) %collective-permute-start.1) | collective-permute-done | bytes 262176 | tf_op jit(solution)/shard_map/ppermute | solution.py:431
  59.7 2.6 %shard_map.126 = bf16[256,1024]{1,0:T(8,128)(2,1)S(1)} custom-call(bf16[4,64,1024]{2,1,0:T(8,128)(2,1)S(1)} %shard_map.125.query, bf16[4,64,512]{2,1,0:T(8,128)(2,1)} %get-tuple-element.29.own, bf16[4,64,512]{2,1,0:T(8,128)(2,1)} %collective-permute-done.1.other, f32[128,64]{1,0:T(8,128)S(1)} %shard_map.123.weights), custom_call_target="tpu_custom_call" | custom-call | flops 134217728 | bytes 1605632 | tf_op jit(solution)/shard_map/pallas_call | solution.py:327
  62.3 4.7 %all-to-all-done.2 = bf16[16,16,1024]{2,1,0:T(8,128)(2,1)S(1)} async-done(((bf16[16,16,1024]{2,1,0:T(8,128)(2,1)}), bf16[16,16,1024]{2,1,0:T(8,128)(2,1)S(1)}, u32[]{:S(2)}, u32[]{:S(2)}) %all-to-all-start.2) | async-done | bytes 524320 | tf_op jit(solution)/shard_map/all_to_all | solution.py:460
  67.0 13.2 %all_to_all.20 = bf16[16,16,1024]{2,1,0:T(8,128)(2,1)S(1)} all-to-all(bf16[16,16,1024]{2,1,0:T(8,128)(2,1)S(1)} %bitcast.17), channel_id=1, replica_groups=mesh['tile'=4,'half'=2,'rest'=4] {'tile','rest'}, dimensions={0} | all-to-all | bytes 1048576 | tf_op jit(solution)/shard_map/all_to_all | solution.py:460
  80.2 0.0 copy-done.3
  80.2 3.7 %shard_map.127 = bf16[4,128,1024]{2,1,0:T(8,128)(2,1)} custom-call(bf16[256,1024]{1,0:T(8,128)(2,1)S(1)} %bitcast.16, bf16[256,1024]{1,0:T(8,128)(2,1)S(1)} %bitcast.18, bf16[4,128,1024]{2,1,0:T(8,128)(2,1)} %get-tuple-element.30.refs_2_, bf16[1024,1024]{1,0:T(8,128)(2,1)S(1)} %copy-done.3), custom_call_target="tpu_custom_call", output_to_operand_aliasing={{}: (2, {})} | custom-call | flops 536870912 | bytes 5242880 | tf_op jit(solution)/shard_map/pallas_call | solution.py:327
Async XLA Ops:
  8.2 17.6 %all-to-all-start = ((bf16[16,16,1152]{2,1,0:T(8,128)(2,1)}), bf16[16,16,1152]{2,1,0:T(8,128)(2,1)S(1)}, u32[]{:S(2)}, u32[]{:S(2)}) async-start(bf16[16,16,1152]{2,1,0:T(8,128)(2,1)} %bitcast.23), calls=%async_computation | async-start | bytes 1179648 | tf_op jit(solution)/shard_map/all_to_all | solution.py:421
  14.5 14.8 %copy-start = (bf16[1024,512]{1,0:T(8,128)(2,1)S(1)}, bf16[1024,512]{1,0:T(8,128)(2,1)}, u32[]{:S(2)}) copy-start(bf16[1024,512]{1,0:T(8,128)(2,1)} %wkv.3) | copy-start | bytes 3145732
  14.6 14.8 %copy-start.4 = (f32[1024]{0:T(1024)S(1)}, f32[1024]{0:T(1024)}, u32[]{:S(2)}) copy-start(f32[1024]{0:T(1024)} %param.17) | copy-start | bytes 12292
  25.8 19.7 %all-to-all-start.1 = ((bf16[16,16,1024]{2,1,0:T(8,128)(2,1)}), bf16[16,16,1024]{2,1,0:T(8,128)(2,1)S(1)}, u32[]{:S(2)}, u32[]{:S(2)}) async-start(bf16[16,16,1024]{2,1,0:T(8,128)(2,1)} %bitcast.24), calls=%async_computation.1 | async-start | bytes 1048576 | tf_op jit(solution)/shard_map/all_to_all | solution.py:421
  30.1 17.6 %collective-permute-start = (bf16[4,64,512]{2,1,0:T(8,128)(2,1)S(1)}, bf16[4,64,512]{2,1,0:T(8,128)(2,1)S(1)}, u32[]{:S(2)}, u32[]{:S(2)}) collective-permute-start(bf16[4,64,512]{2,1,0:T(8,128)(2,1)S(1)} %get-tuple-element.27.own), channel_id=1, source_target_pairs={{0,4},{4,0},{1,5},{5,1},{2,6},{6,2},{3,7},{7,3},{8,12},{12,8},{9,1... | collective-permute-start | bytes 786440 | tf_op jit(solution)/shard_map/ppermute | solution.py:431
  33.2 1.6 %copy-start.1 = (bf16[1024,1024]{1,0:T(8,128)(2,1)S(1)}, bf16[1024,1024]{1,0:T(8,128)(2,1)}, u32[]{:S(2)}) copy-start(bf16[1024,1024]{1,0:T(8,128)(2,1)} %wq.3) | copy-start | bytes 6291460
  47.0 0.8 copy-start.5
  47.8 6.1 %copy-start.2 = (bf16[1024,1024]{1,0:T(8,128)(2,1)S(1)}, bf16[1024,1024]{1,0:T(8,128)(2,1)}, u32[]{:S(2)}) copy-start(bf16[1024,1024]{1,0:T(8,128)(2,1)} %wq.3) | copy-start | bytes 6291460
  47.8 12.0 %collective-permute-start.1 = (bf16[4,64,512]{2,1,0:T(8,128)(2,1)}, bf16[4,64,512]{2,1,0:T(8,128)(2,1)}, u32[]{:S(2)}, u32[]{:S(2)}) collective-permute-start(bf16[4,64,512]{2,1,0:T(8,128)(2,1)} %get-tuple-element.29.own), channel_id=1, source_target_pairs={{0,4},{4,0},{1,5},{5,1},{2,6},{6,2},{3,7},{7,3},{8,12},{12,8},{9,1... | collective-permute-start | bytes 786440 | tf_op jit(solution)/shard_map/ppermute | solution.py:431
  50.1 16.9 %all-to-all-start.2 = ((bf16[16,16,1024]{2,1,0:T(8,128)(2,1)}), bf16[16,16,1024]{2,1,0:T(8,128)(2,1)S(1)}, u32[]{:S(2)}, u32[]{:S(2)}) async-start(bf16[16,16,1024]{2,1,0:T(8,128)(2,1)} %bitcast.8), calls=%async_computation.2 | async-start | bytes 1048576 | tf_op jit(solution)/shard_map/all_to_all | solution.py:460
  53.9 1.0 %copy-start.6 = (bf16[256,1024]{1,0:T(8,128)(2,1)S(1)}, bf16[256,1024]{1,0:T(8,128)(2,1)}, u32[]{:S(2)}) copy-start(bf16[256,1024]{1,0:T(8,128)(2,1)} %copy-done.5) | copy-start | bytes 1572868
  55.6 24.5 %copy-start.3 = (bf16[1024,1024]{1,0:T(8,128)(2,1)S(1)}, bf16[1024,1024]{1,0:T(8,128)(2,1)}, u32[]{:S(2)}) copy-start(bf16[1024,1024]{1,0:T(8,128)(2,1)} %refs_3_.5) | copy-start | bytes 6291460

commit v11 on v10

--- a/solution.py
+++ b/solution.py
@@ -190,7 +190,8 @@
         projected = jnp.dot(mix[...], wo[:, cols], preferred_element_type=F32)
         piece = (hist[:, cols].astype(F32) + projected).astype(BF16)
         mid[:, cols] = piece
-        sent[:, cols] = moved(order, piece)
+    for c in range(0, width, COLS):
+        sent[:, c : c + COLS] = moved(order, mid[:, c : c + COLS])
         part = pl.ds(c, COLS)
         keeps.append(
             pltpu.make_async_copy(sent.at[:, part], sent_hbm.at[:, part], sent_sems.at[c // COLS])
@@ -302,18 +303,20 @@
             mix[i * rows : (i + 1) * rows, c : c + COLS] = moved(order, mixes[i][:, c : c + COLS])
     for load in loads:
         load.wait()
+    keeps = []
     for c in range(0, width, COLS):
         cols = slice(c, c + COLS)
         projected = jnp.dot(mix[...], wo[:, cols], preferred_element_type=F32)
         for i in range(chunks):
             piece = projected[i * rows : (i + 1) * rows].reshape(agents, span, COLS)
             mids[i, :, :, cols] = (mids[i, :, :, cols].astype(F32) + piece).astype(BF16)
-    keeps = [
-        pltpu.make_async_copy(mids.at[i], out_hbm.at[:, pl.ds(i * span, span), :], out_sems.at[i])
-        for i in range(chunks)
-    ]
-    for keep in keeps:
-        keep.start()
+            goal = out_hbm.at[:, pl.ds(i * span, span), pl.ds(c, COLS)]
+            keeps.append(
+                pltpu.make_async_copy(
+                    mids.at[i, :, :, pl.ds(c, COLS)], goal, out_sems.at[i, c // COLS]
+                )
+            )
+            keeps[-1].start()
     for keep in keeps:
         keep.wait()
 
@@ -470,7 +473,7 @@
             pltpu.VMEM((agents * steps, width), BF16),
             pltpu.VMEM((chunks, agents, span, width), BF16),
             pltpu.SemaphoreType.DMA((chunks,)),
-            pltpu.SemaphoreType.DMA((chunks,)),
+            pltpu.SemaphoreType.DMA((chunks, width // COLS)),
         ],
         flops=2 * rows * width * width,
     )

time: 84.7 us -> 84.8 us (level)
  waiting for transfers between devices: 21.4 us -> 22.5 us
    all_to_all x2, waiting for transfers between devices: 12.6 us -> 13.6 us  [per_device(): lax.all_to_all(sent, spread, split_axis=0, concat_axis=0, tiled=True)]
  transfers between devices with their start and end apart: 5 -> 5, of which waited for: 4 -> 4; matrix products, arithmetic and copies ran while one was open for 0% -> 0% of each run, Pallas kernels for 21% -> 20%
where the time goes in v11:
time: 84.8 us; the launch traced here: 84.2 us
  Pallas kernels  28.8 us (34%)
  waiting for transfers between devices  22.5 us (27%)
  starting transfers between devices  16.1 us (19%)
  blocking collectives  13.2 us (16%)
  local copies, waits for them, and re-layouts  3.45 us (4%)
    pallas_call x10, Pallas kernels, call(): pl.pallas_call(kernel, out_shape=list(shapes), in_specs=[pl.BlockSpec(mem...  28.8 us
    all_to_all x2, waiting for transfers between devices, per_device(): lax.all_to_all(sent, spread, split_axis=0, concat_axis=0, tiled=True)  13.6 us
    all_to_all x1, blocking collectives, per_device(): mix = lax.all_to_all(mix, spread, split_axis=0, concat_axis=0, tiled=True)  13.2 us
    all_to_all x2, starting transfers between devices, per_device(): lax.all_to_all(sent, spread, split_axis=0, concat_axis=0, tiled=True)  9.87 us
    all_to_all x1, waiting for transfers between devices, per_device(): mix = lax.all_to_all(mix, spread, split_axis=0, concat_axis=0, tiled=True)  4.7 us
    ppermute x2, waiting for transfers between devices, per_device(): other = lax.ppermute(own, 'half', swap)  4.27 us
    all_to_all x1, starting transfers between devices, per_device(): mix = lax.all_to_all(mix, spread, split_axis=0, concat_axis=0, tiled=True)  3.57 us
    unnamed x14, local copies, waits for them, and re-layouts  3.45 us
  transfers between devices with their start and end apart: 5, of which 4 were waited for; matrix products, arithmetic and copies ran while one was open for 0% of the time, Pallas kernels for 20%

profile of v11, /device:TPU:0, one launch (start us, length us, event | category | flops | bytes accessed | tf_op | source)
XLA Modules:
  0.0 84.2 jit_solution(15827697967934520348)
XLA Ops:
  0.0 7.3 %shard_map.118 = (bf16[4,128,1024]{2,1,0:T(8,128)(2,1)}, bf16[256,1152]{1,0:T(8,128)(2,1)}, bf16[256,512]{1,0:T(8,128)(2,1)}) custom-call(bf16[512,1024]{1,0:T(8,128)(2,1)} %bitcast.21, f32[1,1024]{1,0:T(1,128)} %bitcast.25, bf16[1024,1024]{1,0:T(8,128)(2,1)} %refs_2_.3, bf16[1024,512]{1,0:T(8,128)(2,1)} %refs_3_.4, bf16[1024,1024]{1,0:T(8,128)(2,1)} %refs_4_.3, ...), custom_call_target="tpu_custom_call" | custom-call | flops 1342177280 | bytes 8196256 | tf_op jit(solution)/shard_map/pallas_call | solution.py:330
  7.3 6.3 %all-to-all-start = ((bf16[16,16,1152]{2,1,0:T(8,128)(2,1)}), bf16[16,16,1152]{2,1,0:T(8,128)(2,1)S(1)}, u32[]{:S(2)}, u32[]{:S(2)}) async-start(bf16[16,16,1152]{2,1,0:T(8,128)(2,1)} %bitcast.23), calls=%async_computation | async-start | bytes 1179648 | tf_op jit(solution)/shard_map/all_to_all | solution.py:424
  13.6 0.0 copy-start
  13.6 0.0 copy-start.4
  13.6 7.7 %shard_map.119 = (bf16[4,128,1024]{2,1,0:T(8,128)(2,1)}, bf16[256,1024]{1,0:T(8,128)(2,1)}, bf16[256,512]{1,0:T(8,128)(2,1)}) custom-call(bf16[512,1024]{1,0:T(8,128)(2,1)} %bitcast.22, f32[1,1024]{1,0:T(1,128)} %bitcast.26, bf16[1024,1024]{1,0:T(8,128)(2,1)} %refs_2_.3, bf16[1024,512]{1,0:T(8,128)(2,1)} %refs_3_.4, ...), custom_call_target="tpu_custom_call", output_to_operand_aliasing={{0}: (6, {})} | custom-call | flops 1342177280 | bytes 9441280 | tf_op jit(solution)/shard_map/pallas_call | solution.py:330
  21.3 3.5 %all-to-all-done = bf16[16,16,1152]{2,1,0:T(8,128)(2,1)S(1)} async-done(((bf16[16,16,1152]{2,1,0:T(8,128)(2,1)}), bf16[16,16,1152]{2,1,0:T(8,128)(2,1)S(1)}, u32[]{:S(2)}, u32[]{:S(2)}) %all-to-all-start) | async-done | bytes 589856 | tf_op jit(solution)/shard_map/all_to_all | solution.py:424
  24.8 3.6 %all-to-all-start.1 = ((bf16[16,16,1024]{2,1,0:T(8,128)(2,1)}), bf16[16,16,1024]{2,1,0:T(8,128)(2,1)S(1)}, u32[]{:S(2)}, u32[]{:S(2)}) async-start(bf16[16,16,1024]{2,1,0:T(8,128)(2,1)} %bitcast.24), calls=%async_computation.1 | async-start | bytes 1048576 | tf_op jit(solution)/shard_map/all_to_all | solution.py:424
  28.4 0.0 copy-done
  28.4 0.0 copy-done.4
  28.4 0.7 shard_map.120
  29.2 2.7 %collective-permute-start = (bf16[4,64,512]{2,1,0:T(8,128)(2,1)S(1)}, bf16[4,64,512]{2,1,0:T(8,128)(2,1)S(1)}, u32[]{:S(2)}, u32[]{:S(2)}) collective-permute-start(bf16[4,64,512]{2,1,0:T(8,128)(2,1)S(1)} %get-tuple-element.27.own), channel_id=1, source_target_pairs={{0,4},{4,0},{1,5},{5,1},{2,6},{6,2},{3,7},{7,3},{8,12},{12,8},{9,1... | collective-permute-start | bytes 786440 | tf_op jit(solution)/shard_map/ppermute | solution.py:434
  31.8 0.4 shard_map.123.weights
  32.2 0.0 copy-start.1
  32.2 1.6 %copy-done.1 = bf16[1024,1024]{1,0:T(8,128)(2,1)S(1)} copy-done((bf16[1024,1024]{1,0:T(8,128)(2,1)S(1)}, bf16[1024,1024]{1,0:T(8,128)(2,1)}, u32[]{:S(2)}) %copy-start.1) | copy-done | bytes 2097176
  33.8 0.7 shard_map.121.query
  34.5 10.0 %all-to-all-done.1 = bf16[16,16,1024]{2,1,0:T(8,128)(2,1)S(1)} async-done(((bf16[16,16,1024]{2,1,0:T(8,128)(2,1)}), bf16[16,16,1024]{2,1,0:T(8,128)(2,1)S(1)}, u32[]{:S(2)}, u32[]{:S(2)}) %all-to-all-start.1) | async-done | bytes 524320 | tf_op jit(solution)/shard_map/all_to_all | solution.py:424
  44.5 1.4 %shard_map.122 = (bf16[256,1024]{1,0:T(8,128)(2,1)S(1)}, bf16[4,64,512]{2,1,0:T(8,128)(2,1)}) custom-call(bf16[256,1024]{1,0:T(8,128)(2,1)S(1)} %bitcast.15, f32[1,1024]{1,0:T(1,128)S(1)} %bitcast.20, bf16[1024,512]{1,0:T(8,128)(2,1)S(1)} %copy-done), custom_call_target="tpu_custom_call" | custom-call | flops 268435456 | bytes 2363392 | tf_op jit(solution)/shard_map/pallas_call | solution.py:330
  46.0 0.0 copy-start.5
  46.0 0.8 copy-done.5
  46.8 0.0 copy-start.2
  46.8 0.0 collective-permute-start.1
  46.8 0.0 collective-permute-done.other
  46.8 2.4 %shard_map.124 = bf16[256,1024]{1,0:T(8,128)(2,1)} custom-call(bf16[4,64,1024]{2,1,0:T(8,128)(2,1)S(1)} %shard_map.121.query, bf16[4,64,512]{2,1,0:T(8,128)(2,1)S(1)} %get-tuple-element.27.own, bf16[4,64,512]{2,1,0:T(8,128)(2,1)S(1)} %collective-permute-done.other, f32[128,64]{1,0:T(8,128)S(1)} %shard_map.123.weights), custom_call_target="tpu_custom_call" | custom-call | flops 134217728 | bytes 1605632 | tf_op jit(solution)/shard_map/pallas_call | solution.py:330
  49.2 3.6 %all-to-all-start.2 = ((bf16[16,16,1024]{2,1,0:T(8,128)(2,1)}), bf16[16,16,1024]{2,1,0:T(8,128)(2,1)S(1)}, u32[]{:S(2)}, u32[]{:S(2)}) async-start(bf16[16,16,1024]{2,1,0:T(8,128)(2,1)} %bitcast.8), calls=%async_computation.2 | async-start | bytes 1048576 | tf_op jit(solution)/shard_map/all_to_all | solution.py:463
  52.7 0.0 copy-done.2
  52.7 0.0 copy-start.6
  52.8 1.0 %copy-done.6 = bf16[256,1024]{1,0:T(8,128)(2,1)S(1)} copy-done((bf16[256,1024]{1,0:T(8,128)(2,1)S(1)}, bf16[256,1024]{1,0:T(8,128)(2,1)}, u32[]{:S(2)}) %copy-start.6) | copy-done | bytes 524312
  53.8 0.7 shard_map.125.query
  54.5 0.0 copy-start.3
  54.5 4.3 %collective-permute-done.1.other = bf16[4,64,512]{2,1,0:T(8,128)(2,1)} collective-permute-done((bf16[4,64,512]{2,1,0:T(8,128)(2,1)}, bf16[4,64,512]{2,1,0:T(8,128)(2,1)}, u32[]{:S(2)}, u32[]{:S(2)}) %collective-permute-start.1) | collective-permute-done | bytes 262176 | tf_op jit(solution)/shard_map/ppermute | solution.py:434
  58.8 2.6 %shard_map.126 = bf16[256,1024]{1,0:T(8,128)(2,1)S(1)} custom-call(bf16[4,64,1024]{2,1,0:T(8,128)(2,1)S(1)} %shard_map.125.query, bf16[4,64,512]{2,1,0:T(8,128)(2,1)} %get-tuple-element.29.own, bf16[4,64,512]{2,1,0:T(8,128)(2,1)} %collective-permute-done.1.other, f32[128,64]{1,0:T(8,128)S(1)} %shard_map.123.weights), custom_call_target="tpu_custom_call" | custom-call | flops 134217728 | bytes 1605632 | tf_op jit(solution)/shard_map/pallas_call | solution.py:330
  61.4 4.7 %all-to-all-done.2 = bf16[16,16,1024]{2,1,0:T(8,128)(2,1)S(1)} async-done(((bf16[16,16,1024]{2,1,0:T(8,128)(2,1)}), bf16[16,16,1024]{2,1,0:T(8,128)(2,1)S(1)}, u32[]{:S(2)}, u32[]{:S(2)}) %all-to-all-start.2) | async-done | bytes 524320 | tf_op jit(solution)/shard_map/all_to_all | solution.py:463
  66.1 13.2 %all_to_all.20 = bf16[16,16,1024]{2,1,0:T(8,128)(2,1)S(1)} all-to-all(bf16[16,16,1024]{2,1,0:T(8,128)(2,1)S(1)} %bitcast.17), channel_id=1, replica_groups=mesh['tile'=4,'half'=2,'rest'=4] {'tile','rest'}, dimensions={0} | all-to-all | bytes 1048576 | tf_op jit(solution)/shard_map/all_to_all | solution.py:463
  79.2 0.0 copy-done.3
  79.2 4.9 %shard_map.127 = bf16[4,128,1024]{2,1,0:T(8,128)(2,1)} custom-call(bf16[256,1024]{1,0:T(8,128)(2,1)S(1)} %bitcast.16, bf16[256,1024]{1,0:T(8,128)(2,1)S(1)} %bitcast.18, bf16[4,128,1024]{2,1,0:T(8,128)(2,1)} %get-tuple-element.30.refs_2_, bf16[1024,1024]{1,0:T(8,128)(2,1)S(1)} %copy-done.3), custom_call_target="tpu_custom_call", output_to_operand_aliasing={{}: (2, {})} | custom-call | flops 536870912 | bytes 5242880 | tf_op jit(solution)/shard_map/pallas_call | solution.py:330
Async XLA Ops:
  7.3 17.6 %all-to-all-start = ((bf16[16,16,1152]{2,1,0:T(8,128)(2,1)}), bf16[16,16,1152]{2,1,0:T(8,128)(2,1)S(1)}, u32[]{:S(2)}, u32[]{:S(2)}) async-start(bf16[16,16,1152]{2,1,0:T(8,128)(2,1)} %bitcast.23), calls=%async_computation | async-start | bytes 1179648 | tf_op jit(solution)/shard_map/all_to_all | solution.py:424
  13.6 14.8 %copy-start = (bf16[1024,512]{1,0:T(8,128)(2,1)S(1)}, bf16[1024,512]{1,0:T(8,128)(2,1)}, u32[]{:S(2)}) copy-start(bf16[1024,512]{1,0:T(8,128)(2,1)} %wkv.3) | copy-start | bytes 3145732
  13.6 14.8 %copy-start.4 = (f32[1024]{0:T(1024)S(1)}, f32[1024]{0:T(1024)}, u32[]{:S(2)}) copy-start(f32[1024]{0:T(1024)} %param.17) | copy-start | bytes 12292
  24.8 19.7 %all-to-all-start.1 = ((bf16[16,16,1024]{2,1,0:T(8,128)(2,1)}), bf16[16,16,1024]{2,1,0:T(8,128)(2,1)S(1)}, u32[]{:S(2)}, u32[]{:S(2)}) async-start(bf16[16,16,1024]{2,1,0:T(8,128)(2,1)} %bitcast.24), calls=%async_computation.1 | async-start | bytes 1048576 | tf_op jit(solution)/shard_map/all_to_all | solution.py:424
  29.2 17.6 %collective-permute-start = (bf16[4,64,512]{2,1,0:T(8,128)(2,1)S(1)}, bf16[4,64,512]{2,1,0:T(8,128)(2,1)S(1)}, u32[]{:S(2)}, u32[]{:S(2)}) collective-permute-start(bf16[4,64,512]{2,1,0:T(8,128)(2,1)S(1)} %get-tuple-element.27.own), channel_id=1, source_target_pairs={{0,4},{4,0},{1,5},{5,1},{2,6},{6,2},{3,7},{7,3},{8,12},{12,8},{9,1... | collective-permute-start | bytes 786440 | tf_op jit(solution)/shard_map/ppermute | solution.py:434
  32.2 1.6 %copy-start.1 = (bf16[1024,1024]{1,0:T(8,128)(2,1)S(1)}, bf16[1024,1024]{1,0:T(8,128)(2,1)}, u32[]{:S(2)}) copy-start(bf16[1024,1024]{1,0:T(8,128)(2,1)} %wq.3) | copy-start | bytes 6291460
  46.0 0.8 copy-start.5
  46.8 6.0 %copy-start.2 = (bf16[1024,1024]{1,0:T(8,128)(2,1)S(1)}, bf16[1024,1024]{1,0:T(8,128)(2,1)}, u32[]{:S(2)}) copy-start(bf16[1024,1024]{1,0:T(8,128)(2,1)} %wq.3) | copy-start | bytes 6291460
  46.8 12.0 %collective-permute-start.1 = (bf16[4,64,512]{2,1,0:T(8,128)(2,1)}, bf16[4,64,512]{2,1,0:T(8,128)(2,1)}, u32[]{:S(2)}, u32[]{:S(2)}) collective-permute-start(bf16[4,64,512]{2,1,0:T(8,128)(2,1)} %get-tuple-element.29.own), channel_id=1, source_target_pairs={{0,4},{4,0},{1,5},{5,1},{2,6},{6,2},{3,7},{7,3},{8,12},{12,8},{9,1... | collective-permute-start | bytes 786440 | tf_op jit(solution)/shard_map/ppermute | solution.py:434
  49.2 16.9 %all-to-all-start.2 = ((bf16[16,16,1024]{2,1,0:T(8,128)(2,1)}), bf16[16,16,1024]{2,1,0:T(8,128)(2,1)S(1)}, u32[]{:S(2)}, u32[]{:S(2)}) async-start(bf16[16,16,1024]{2,1,0:T(8,128)(2,1)} %bitcast.8), calls=%async_computation.2 | async-start | bytes 1048576 | tf_op jit(solution)/shard_map/all_to_all | solution.py:463
  52.7 1.0 %copy-start.6 = (bf16[256,1024]{1,0:T(8,128)(2,1)S(1)}, bf16[256,1024]{1,0:T(8,128)(2,1)}, u32[]{:S(2)}) copy-start(bf16[256,1024]{1,0:T(8,128)(2,1)} %copy-done.5) | copy-start | bytes 1572868
  54.5 24.7 %copy-start.3 = (bf16[1024,1024]{1,0:T(8,128)(2,1)S(1)}, bf16[1024,1024]{1,0:T(8,128)(2,1)}, u32[]{:S(2)}) copy-start(bf16[1024,1024]{1,0:T(8,128)(2,1)} %refs_3_.5) | copy-start | bytes 6291460

commit v12 on v10

--- a/solution.py
+++ b/solution.py
@@ -190,12 +190,6 @@
         projected = jnp.dot(mix[...], wo[:, cols], preferred_element_type=F32)
         piece = (hist[:, cols].astype(F32) + projected).astype(BF16)
         mid[:, cols] = piece
-        sent[:, cols] = moved(order, piece)
-        part = pl.ds(c, COLS)
-        keeps.append(
-            pltpu.make_async_copy(sent.at[:, part], sent_hbm.at[:, part], sent_sems.at[c // COLS])
-        )
-        keeps[-1].start()
     for a in range(agents):
         goal = mid_hbm.at[a, pl.ds(chunk * span, span), :]
         keeps.append(
@@ -212,10 +206,15 @@
             listed = lane == alive.shape[1] + neighbours[0, i]
             notes = notes + jnp.where(listed, nbr_valid[0, i].astype(F32), 0.0)
         sent[:, width:] = jnp.broadcast_to(notes, (rows, LANES)).astype(BF16)
-        part = pl.ds(width, LANES)
+    for r in range(0, rows, rows // 2):
+        for c in range(0, width, COLS):
+            sent[r : r + rows // 2, c : c + COLS] = moved(
+                order[r : r + rows // 2], mid[:, c : c + COLS]
+            )
+        part = pl.ds(r, rows // 2)
         keeps.append(
             pltpu.make_async_copy(
-                sent.at[:, part], sent_hbm.at[:, part], sent_sems.at[width // COLS]
+                sent.at[part, :], sent_hbm.at[part, :], sent_sems.at[r // (rows // 2)]
             )
         )
         keeps[-1].start()
@@ -287,35 +286,23 @@
         out[:, c : c + COLS] = moved(order, piece) if local > 1 else piece
 
 
-def out_kernel(agents, span, local, chunks, *refs):
-    mixes, (mid_hbm, wo, out_hbm, mix, mids, sems, out_sems) = refs[:chunks], refs[chunks:]
-    rows, width = mixes[0].shape
-    loads = [
-        pltpu.make_async_copy(mid_hbm.at[:, pl.ds(i * span, span), :], mids.at[i], sems.at[i])
-        for i in range(chunks)
-    ]
-    for load in loads:
-        load.start()
+def out_kernel(agents, span, chunk, local, arrived, mid_hbm, wo, out_hbm, mix, mid, sems):
+    rows, width = arrived.shape
+    part = pl.ds(chunk * span, span)
+    load = pltpu.make_async_copy(mid_hbm.at[:, part, :], mid, sems.at[0])
+    load.start()
     order = one_hot(rows, lambda row: regroup(row, span // local, agents, local))
     for c in range(0, width, COLS):
-        for i in range(chunks):
-            mix[i * rows : (i + 1) * rows, c : c + COLS] = moved(order, mixes[i][:, c : c + COLS])
-    for load in loads:
-        load.wait()
+        mix[:, c : c + COLS] = moved(order, arrived[:, c : c + COLS])
+    load.wait()
     for c in range(0, width, COLS):
         cols = slice(c, c + COLS)
         projected = jnp.dot(mix[...], wo[:, cols], preferred_element_type=F32)
-        for i in range(chunks):
-            piece = projected[i * rows : (i + 1) * rows].reshape(agents, span, COLS)
-            mids[i, :, :, cols] = (mids[i, :, :, cols].astype(F32) + piece).astype(BF16)
-    keeps = [
-        pltpu.make_async_copy(mids.at[i], out_hbm.at[:, pl.ds(i * span, span), :], out_sems.at[i])
-        for i in range(chunks)
-    ]
-    for keep in keeps:
-        keep.start()
-    for keep in keeps:
-        keep.wait()
+        piece = projected.reshape(agents, span, COLS)
+        mid[:, :, cols] = (mid[:, :, cols].astype(F32) + piece).astype(BF16)
+    keep = pltpu.make_async_copy(mid, out_hbm.at[:, part, :], sems.at[1])
+    keep.start()
+    keep.wait()
 
 
 def call(
@@ -402,7 +389,7 @@
                 pltpu.SemaphoreType.DMA((width // COLS,)),
                 pltpu.SemaphoreType.DMA((2,)),
                 pltpu.SemaphoreType.DMA((agents,)),
-                pltpu.SemaphoreType.DMA((width // COLS + 1,)),
+                pltpu.SemaphoreType.DMA((2,)),
                 pltpu.SemaphoreType.DMA,
             ],
             flops=2 * rows * width * (2 * width + 2 * KEYS),
@@ -459,21 +446,22 @@
         mix = mix.reshape(parts, agents * local, width)
         mix = lax.all_to_all(mix, spread, split_axis=0, concat_axis=0, tiled=True)
         mixes.append(mix.reshape(rows, width))
-    out = call(
-        functools.partial(out_kernel, agents, span, local, chunks),
-        [whole],
-        mixes + mids + [wo_space],
-        hbm=(chunks,),
-        hbm_out=(0,),
-        aliases={chunks: 0},
-        scratch=[
-            pltpu.VMEM((agents * steps, width), BF16),
-            pltpu.VMEM((chunks, agents, span, width), BF16),
-            pltpu.SemaphoreType.DMA((chunks,)),
-            pltpu.SemaphoreType.DMA((chunks,)),
-        ],
-        flops=2 * rows * width * width,
-    )
+    out = mids[0]
+    for i, mix in enumerate(mixes):
+        out = call(
+            functools.partial(out_kernel, agents, span, i, local),
+            [whole],
+            [mix, out, wo_space],
+            hbm=(1,),
+            hbm_out=(0,),
+            aliases={1: 0},
+            scratch=[
+                pltpu.VMEM((rows, width), BF16),
+                pltpu.VMEM((agents, span, width), BF16),
+                pltpu.SemaphoreType.DMA((2,)),
+            ],
+            flops=2 * rows * width * width,
+        )
     return out[None]
 
 

time: 84.7 us -> 86.4 us (1.020)
  blocking collectives: 13.2 us -> 0 us
  starting transfers between devices: 16.3 us -> 25.3 us
  waiting for transfers between devices: 21.4 us -> 27.9 us
    all_to_all x1 -> x0, blocking collectives: 13.2 us -> none  [per_device(): mix = lax.all_to_all(mix, spread, split_axis=0, concat_axis=0, tiled=True)]
    all_to_all x1 -> x2, waiting for transfers between devices: 4.7 us -> 14.3 us  [per_device(): mix = lax.all_to_all(mix, spread, split_axis=0, concat_axis=0, tiled=True)]
    all_to_all x1 -> x2, starting transfers between devices: 3.75 us -> 12.7 us  [per_device(): mix = lax.all_to_all(mix, spread, split_axis=0, concat_axis=0, tiled=True)]
    ppermute x2, waiting for transfers between devices: 4.08 us -> 0.01 us  [per_device(): other = lax.ppermute(own, 'half', swap)]
    all_to_all x2, waiting for transfers between devices: 12.6 us -> 13.6 us  [per_device(): lax.all_to_all(sent, spread, split_axis=0, concat_axis=0, tiled=True)]
    pallas_call x10 -> x11, Pallas kernels: 29.5 us -> 29.4 us  [call(): pl.pallas_call(kernel, out_shape=list(shapes), in_specs=[pl.BlockSpec(mem...]
  transfers between devices with their start and end apart: 5 -> 6, of which waited for: 4 -> 4; matrix products, arithmetic and copies ran while one was open for 0% -> 0% of each run, Pallas kernels for 21% -> 23%
where the time goes in v12:
time: 86.4 us; the launch traced here: 85.5 us
  Pallas kernels  29.4 us (34%)
  waiting for transfers between devices  27.9 us (32%)
  starting transfers between devices  25.3 us (29%)
  local copies, waits for them, and re-layouts  2.66 us (3%)
    pallas_call x11, Pallas kernels, call(): pl.pallas_call(kernel, out_shape=list(shapes), in_specs=[pl.BlockSpec(mem...  29.4 us
    all_to_all x2, waiting for transfers between devices, per_device(): mix = lax.all_to_all(mix, spread, split_axis=0, concat_axis=0, tiled=True)  14.3 us
    all_to_all x2, waiting for transfers between devices, per_device(): lax.all_to_all(sent, spread, split_axis=0, concat_axis=0, tiled=True)  13.6 us
    all_to_all x2, starting transfers between devices, per_device(): mix = lax.all_to_all(mix, spread, split_axis=0, concat_axis=0, tiled=True)  12.7 us
    all_to_all x2, starting transfers between devices, per_device(): lax.all_to_all(sent, spread, split_axis=0, concat_axis=0, tiled=True)  9.87 us
    ppermute x2, starting transfers between devices, per_device(): other = lax.ppermute(own, 'half', swap)  2.72 us
    unnamed x14, local copies, waits for them, and re-layouts  2.66 us
  transfers between devices with their start and end apart: 6, of which 4 were waited for; matrix products, arithmetic and copies ran while one was open for 0% of the time, Pallas kernels for 23%

profile of v12, /device:TPU:0, one launch (start us, length us, event | category | flops | bytes accessed | tf_op | source)
XLA Modules:
  0.0 85.5 jit_solution(15805143211106319369)
XLA Ops:
  0.0 7.3 %shard_map.118 = (bf16[4,128,1024]{2,1,0:T(8,128)(2,1)}, bf16[256,1152]{1,0:T(8,128)(2,1)}, bf16[256,512]{1,0:T(8,128)(2,1)}) custom-call(bf16[512,1024]{1,0:T(8,128)(2,1)} %bitcast.20, f32[1,1024]{1,0:T(1,128)} %bitcast.24, bf16[1024,1024]{1,0:T(8,128)(2,1)} %refs_2_.3, bf16[1024,512]{1,0:T(8,128)(2,1)} %refs_3_.3, bf16[1024,1024]{1,0:T(8,128)(2,1)} %refs_4_.3, ...), custom_call_target="tpu_custom_call" | custom-call | flops 1342177280 | bytes 8196256 | tf_op jit(solution)/shard_map/pallas_call | solution.py:314
  7.3 6.3 %all-to-all-start = ((bf16[16,16,1152]{2,1,0:T(8,128)(2,1)}), bf16[16,16,1152]{2,1,0:T(8,128)(2,1)S(1)}, u32[]{:S(2)}, u32[]{:S(2)}) async-start(bf16[16,16,1152]{2,1,0:T(8,128)(2,1)} %bitcast.22), calls=%async_computation | async-start | bytes 1179648 | tf_op jit(solution)/shard_map/all_to_all | solution.py:408
  13.6 0.0 copy-start.1
  13.7 0.0 copy-start.4
  13.7 7.6 %shard_map.119 = (bf16[4,128,1024]{2,1,0:T(8,128)(2,1)}, bf16[256,1024]{1,0:T(8,128)(2,1)}, bf16[256,512]{1,0:T(8,128)(2,1)}) custom-call(bf16[512,1024]{1,0:T(8,128)(2,1)} %bitcast.21, f32[1,1024]{1,0:T(1,128)} %bitcast.25, bf16[1024,1024]{1,0:T(8,128)(2,1)} %refs_2_.3, bf16[1024,512]{1,0:T(8,128)(2,1)} %refs_3_.3, ...), custom_call_target="tpu_custom_call", output_to_operand_aliasing={{0}: (6, {})} | custom-call | flops 1342177280 | bytes 9441280 | tf_op jit(solution)/shard_map/pallas_call | solution.py:314
  21.3 3.6 %all-to-all-done = bf16[16,16,1152]{2,1,0:T(8,128)(2,1)S(1)} async-done(((bf16[16,16,1152]{2,1,0:T(8,128)(2,1)}), bf16[16,16,1152]{2,1,0:T(8,128)(2,1)S(1)}, u32[]{:S(2)}, u32[]{:S(2)}) %all-to-all-start) | async-done | bytes 589856 | tf_op jit(solution)/shard_map/all_to_all | solution.py:408
  24.9 3.6 %all-to-all-start.1 = ((bf16[16,16,1024]{2,1,0:T(8,128)(2,1)}), bf16[16,16,1024]{2,1,0:T(8,128)(2,1)S(1)}, u32[]{:S(2)}, u32[]{:S(2)}) async-start(bf16[16,16,1024]{2,1,0:T(8,128)(2,1)} %bitcast.23), calls=%async_computation.1 | async-start | bytes 1048576 | tf_op jit(solution)/shard_map/all_to_all | solution.py:408
  28.5 0.0 copy-done.1
  28.5 0.0 copy-done.4
  28.5 0.7 shard_map.122
  29.2 2.7 %collective-permute-start.1 = (bf16[4,64,512]{2,1,0:T(8,128)(2,1)S(1)}, bf16[4,64,512]{2,1,0:T(8,128)(2,1)}, u32[]{:S(2)}, u32[]{:S(2)}) collective-permute-start(bf16[4,64,512]{2,1,0:T(8,128)(2,1)S(1)} %get-tuple-element.29.own), channel_id=1, source_target_pairs={{0,4},{4,0},{1,5},{5,1},{2,6},{6,2},{3,7},{7,3},{8,12},{12,8},{9,1... | collective-permute-start | bytes 786440 | tf_op jit(solution)/shard_map/ppermute | solution.py:418
  31.9 0.4 shard_map.123.weights
  32.3 0.0 copy-start.2
  32.3 1.6 %copy-done.2 = bf16[1024,1024]{1,0:T(8,128)(2,1)S(1)} copy-done((bf16[1024,1024]{1,0:T(8,128)(2,1)S(1)}, bf16[1024,1024]{1,0:T(8,128)(2,1)}, u32[]{:S(2)}) %copy-start.2) | copy-done | bytes 2097176
  33.9 0.7 shard_map.125.query
  34.6 10.0 %all-to-all-done.1 = bf16[16,16,1024]{2,1,0:T(8,128)(2,1)S(1)} async-done(((bf16[16,16,1024]{2,1,0:T(8,128)(2,1)}), bf16[16,16,1024]{2,1,0:T(8,128)(2,1)S(1)}, u32[]{:S(2)}, u32[]{:S(2)}) %all-to-all-start.1) | async-done | bytes 524320 | tf_op jit(solution)/shard_map/all_to_all | solution.py:408
  44.6 0.7 shard_map.120
  45.3 0.0 copy-start.5
  45.4 0.0 copy-start.3
  45.4 0.1 collective-permute-start
  45.4 0.0 collective-permute-done.1.other
  45.5 3.6 %shard_map.126 = bf16[256,1024]{1,0:T(8,128)(2,1)} custom-call(bf16[4,64,1024]{2,1,0:T(8,128)(2,1)S(1)} %shard_map.125.query, bf16[4,64,512]{2,1,0:T(8,128)(2,1)S(1)} %get-tuple-element.29.own, bf16[4,64,512]{2,1,0:T(8,128)(2,1)} %collective-permute-done.1.other, f32[128,64]{1,0:T(8,128)S(1)} %shard_map.123.weights), custom_call_target="tpu_custom_call" | custom-call | flops 134217728 | bytes 1605632 | tf_op jit(solution)/shard_map/pallas_call | solution.py:314
  49.0 0.0 copy-done.5
  49.0 9.1 %all-to-all-start.3 = ((bf16[16,16,1024]{2,1,0:T(8,128)(2,1)}), bf16[16,16,1024]{2,1,0:T(8,128)(2,1)S(1)}, u32[]{:S(2)}, u32[]{:S(2)}) async-start(bf16[16,16,1024]{2,1,0:T(8,128)(2,1)} %bitcast.10), calls=%async_computation.3 | async-start | bytes 1048576 | tf_op jit(solution)/shard_map/all_to_all | solution.py:447
  58.1 0.0 copy-done.3
  58.1 0.0 copy-start.6
  58.1 1.0 %copy-done.6 = bf16[256,1024]{1,0:T(8,128)(2,1)S(1)} copy-done((bf16[256,1024]{1,0:T(8,128)(2,1)S(1)}, bf16[256,1024]{1,0:T(8,128)(2,1)}, u32[]{:S(2)}) %copy-start.6) | copy-done | bytes 524312
  59.2 0.7 shard_map.121.query
  59.9 0.0 copy-start
  59.9 0.0 collective-permute-done.other
  59.9 2.3 %shard_map.124 = bf16[256,1024]{1,0:T(8,128)(2,1)} custom-call(bf16[4,64,1024]{2,1,0:T(8,128)(2,1)S(1)} %shard_map.121.query, bf16[4,64,512]{2,1,0:T(8,128)(2,1)S(1)} %get-tuple-element.27.own, bf16[4,64,512]{2,1,0:T(8,128)(2,1)S(1)} %collective-permute-done.other, f32[128,64]{1,0:T(8,128)S(1)} %shard_map.123.weights), custom_call_target="tpu_custom_call" | custom-call | flops 134217728 | bytes 1605632 | tf_op jit(solution)/shard_map/pallas_call | solution.py:314
  62.2 6.4 %all-to-all-done.3 = bf16[16,16,1024]{2,1,0:T(8,128)(2,1)S(1)} async-done(((bf16[16,16,1024]{2,1,0:T(8,128)(2,1)}), bf16[16,16,1024]{2,1,0:T(8,128)(2,1)S(1)}, u32[]{:S(2)}, u32[]{:S(2)}) %all-to-all-start.3) | async-done | bytes 524320 | tf_op jit(solution)/shard_map/all_to_all | solution.py:447
  68.7 3.6 %all-to-all-start.2 = ((bf16[16,16,1024]{2,1,0:T(8,128)(2,1)}), bf16[16,16,1024]{2,1,0:T(8,128)(2,1)S(1)}, u32[]{:S(2)}, u32[]{:S(2)}) async-start(bf16[16,16,1024]{2,1,0:T(8,128)(2,1)} %bitcast.8), calls=%async_computation.2 | async-start | bytes 1048576 | tf_op jit(solution)/shard_map/all_to_all | solution.py:447
  72.2 0.0 copy-done
  72.2 2.6 %shard_map.127.mid_hbm = bf16[4,128,1024]{2,1,0:T(8,128)(2,1)} custom-call(bf16[256,1024]{1,0:T(8,128)(2,1)S(1)} %bitcast.16, bf16[4,128,1024]{2,1,0:T(8,128)(2,1)} %get-tuple-element.30.mid_hbm, bf16[1024,1024]{1,0:T(8,128)(2,1)S(1)} %copy-done), custom_call_target="tpu_custom_call", output_to_operand_aliasing={{}: (1, {})} | custom-call | flops 536870912 | bytes 4718592 | tf_op jit(solution)/shard_map/pallas_call | solution.py:314
  74.9 7.9 %all-to-all-done.2 = bf16[16,16,1024]{2,1,0:T(8,128)(2,1)S(1)} async-done(((bf16[16,16,1024]{2,1,0:T(8,128)(2,1)}), bf16[16,16,1024]{2,1,0:T(8,128)(2,1)S(1)}, u32[]{:S(2)}, u32[]{:S(2)}) %all-to-all-start.2) | async-done | bytes 524320 | tf_op jit(solution)/shard_map/all_to_all | solution.py:447
  82.7 2.6 %shard_map.128 = bf16[4,128,1024]{2,1,0:T(8,128)(2,1)} custom-call(bf16[256,1024]{1,0:T(8,128)(2,1)S(1)} %bitcast.17, bf16[4,128,1024]{2,1,0:T(8,128)(2,1)} %shard_map.127.mid_hbm, bf16[1024,1024]{1,0:T(8,128)(2,1)S(1)} %copy-done), custom_call_target="tpu_custom_call", output_to_operand_aliasing={{}: (1, {})} | custom-call | flops 536870912 | bytes 4718592 | tf_op jit(solution)/shard_map/pallas_call | solution.py:314
Async XLA Ops:
  7.3 17.6 %all-to-all-start = ((bf16[16,16,1152]{2,1,0:T(8,128)(2,1)}), bf16[16,16,1152]{2,1,0:T(8,128)(2,1)S(1)}, u32[]{:S(2)}, u32[]{:S(2)}) async-start(bf16[16,16,1152]{2,1,0:T(8,128)(2,1)} %bitcast.22), calls=%async_computation | async-start | bytes 1179648 | tf_op jit(solution)/shard_map/all_to_all | solution.py:408
  13.6 14.8 %copy-start.1 = (bf16[1024,512]{1,0:T(8,128)(2,1)S(1)}, bf16[1024,512]{1,0:T(8,128)(2,1)}, u32[]{:S(2)}) copy-start(bf16[1024,512]{1,0:T(8,128)(2,1)} %wkv.3) | copy-start | bytes 3145732
  13.7 14.8 %copy-start.4 = (f32[1024]{0:T(1024)S(1)}, f32[1024]{0:T(1024)}, u32[]{:S(2)}) copy-start(f32[1024]{0:T(1024)} %param.17) | copy-start | bytes 12292
  24.9 19.7 %all-to-all-start.1 = ((bf16[16,16,1024]{2,1,0:T(8,128)(2,1)}), bf16[16,16,1024]{2,1,0:T(8,128)(2,1)S(1)}, u32[]{:S(2)}, u32[]{:S(2)}) async-start(bf16[16,16,1024]{2,1,0:T(8,128)(2,1)} %bitcast.23), calls=%async_computation.1 | async-start | bytes 1048576 | tf_op jit(solution)/shard_map/all_to_all | solution.py:408
  29.2 16.2 %collective-permute-start.1 = (bf16[4,64,512]{2,1,0:T(8,128)(2,1)S(1)}, bf16[4,64,512]{2,1,0:T(8,128)(2,1)}, u32[]{:S(2)}, u32[]{:S(2)}) collective-permute-start(bf16[4,64,512]{2,1,0:T(8,128)(2,1)S(1)} %get-tuple-element.29.own), channel_id=1, source_target_pairs={{0,4},{4,0},{1,5},{5,1},{2,6},{6,2},{3,7},{7,3},{8,12},{12,8},{9,1... | collective-permute-start | bytes 786440 | tf_op jit(solution)/shard_map/ppermute | solution.py:418
  32.3 1.6 %copy-start.2 = (bf16[1024,1024]{1,0:T(8,128)(2,1)S(1)}, bf16[1024,1024]{1,0:T(8,128)(2,1)}, u32[]{:S(2)}) copy-start(bf16[1024,1024]{1,0:T(8,128)(2,1)} %wq.3) | copy-start | bytes 6291460
  45.3 3.7 %copy-start.5 = (bf16[256,1024]{1,0:T(8,128)(2,1)}, bf16[256,1024]{1,0:T(8,128)(2,1)S(1)}, u32[]{:S(2)}) copy-start(bf16[256,1024]{1,0:T(8,128)(2,1)S(1)} %get-tuple-element.23.second) | copy-start | bytes 1572868
  45.4 12.8 %copy-start.3 = (bf16[1024,1024]{1,0:T(8,128)(2,1)S(1)}, bf16[1024,1024]{1,0:T(8,128)(2,1)}, u32[]{:S(2)}) copy-start(bf16[1024,1024]{1,0:T(8,128)(2,1)} %wq.3) | copy-start | bytes 6291460
  45.4 14.5 %collective-permute-start = (bf16[4,64,512]{2,1,0:T(8,128)(2,1)S(1)}, bf16[4,64,512]{2,1,0:T(8,128)(2,1)S(1)}, u32[]{:S(2)}, u32[]{:S(2)}) collective-permute-start(bf16[4,64,512]{2,1,0:T(8,128)(2,1)S(1)} %get-tuple-element.27.own), channel_id=1, source_target_pairs={{0,4},{4,0},{1,5},{5,1},{2,6},{6,2},{3,7},{7,3},{8,12},{12,8},{9,1... | collective-permute-start | bytes 786440 | tf_op jit(solution)/shard_map/ppermute | solution.py:418
  49.0 19.6 %all-to-all-start.3 = ((bf16[16,16,1024]{2,1,0:T(8,128)(2,1)}), bf16[16,16,1024]{2,1,0:T(8,128)(2,1)S(1)}, u32[]{:S(2)}, u32[]{:S(2)}) async-start(bf16[16,16,1024]{2,1,0:T(8,128)(2,1)} %bitcast.10), calls=%async_computation.3 | async-start | bytes 1048576 | tf_op jit(solution)/shard_map/all_to_all | solution.py:447
  58.1 1.0 %copy-start.6 = (bf16[256,1024]{1,0:T(8,128)(2,1)S(1)}, bf16[256,1024]{1,0:T(8,128)(2,1)}, u32[]{:S(2)}) copy-start(bf16[256,1024]{1,0:T(8,128)(2,1)} %copy-done.5) | copy-start | bytes 1572868
  59.9 12.4 %copy-start = (bf16[1024,1024]{1,0:T(8,128)(2,1)S(1)}, bf16[1024,1024]{1,0:T(8,128)(2,1)}, u32[]{:S(2)}) copy-start(bf16[1024,1024]{1,0:T(8,128)(2,1)} %wo.3) | copy-start | bytes 6291460
  68.7 14.1 %all-to-all-start.2 = ((bf16[16,16,1024]{2,1,0:T(8,128)(2,1)}), bf16[16,16,1024]{2,1,0:T(8,128)(2,1)S(1)}, u32[]{:S(2)}, u32[]{:S(2)}) async-start(bf16[16,16,1024]{2,1,0:T(8,128)(2,1)} %bitcast.8), calls=%async_computation.2 | async-start | bytes 1048576 | tf_op jit(solution)/shard_map/all_to_all | solution.py:447

commit v13 on v12

--- a/solution.py
+++ b/solution.py
@@ -23,7 +23,7 @@
 HALVES = 2
 CHUNKS = 2
 DEPTH = 2
-SHADOW = 100
+SHADOW = 500
 MIB = 1024 * 1024
 F32 = jnp.float32
 BF16 = jnp.bfloat16
@@ -409,12 +409,20 @@
         there = there.reshape(rows, deep)
         if i + 1 < chunks:
             there, sents[i + 1] = lax.optimization_barrier((there, sents[i + 1]))
+        if homes:
+            first, *held = homes[-1]
+            there, first, weight = lax.optimization_barrier((there, first, weight))
+            homes[-1] = (first, *held)
         second, own = call(
             functools.partial(keys_kernel, local),
             [struct((rows, width), BF16), struct((local, total, 2 * KEYS), BF16)],
             [there, gain_space[None], wkv_space],
             flops=2 * rows * width * 2 * KEYS,
         )
+        if homes:
+            *held, last = homes[-1]
+            own, last = lax.optimization_barrier((own, last))
+            homes[-1] = (*held, last)
         other = lax.ppermute(own, "half", swap)
         if i == 0:
             weight = call(
@@ -427,20 +435,16 @@
             query_kernel,
             [struct((local, total, width), BF16)],
             [second, wq_space],
-            flops=(2 if i == 0 else SHADOW) * rows * width * width,
+            flops=2 * rows * width * width,
         )
         homes.append((query, own, other))
-    for i in range(chunks - 1):
-        (query, own, other), (later, *held) = homes[i], homes[i + 1]
-        own, held[0] = lax.optimization_barrier((own, held[0]))
-        homes[i], homes[i + 1] = (query, own, other), (later, *held)
-    for query, own, other in homes:
+    for i, (query, own, other) in enumerate(homes):
         mix = call(
             functools.partial(space_kernel, beside(total, local)),
             [struct((rows, width), BF16)],
             [query, own, other, weight],
             scratch=[pltpu.VMEM((rows, width), BF16)],
-            flops=8 * rows * total * width,
+            flops=(8 if i == 0 else SHADOW) * rows * total * width,
             mib=big,
         )
         mix = mix.reshape(parts, agents * local, width)

time: 86.4 us -> 87.3 us (1.010)
  local copies, waits for them, and re-layouts: 2.66 us -> 6.57 us
  waiting for transfers between devices: 27.9 us -> 24 us
  Pallas kernels: 29.4 us -> 31.2 us
  starting transfers between devices: 25.3 us -> 24.2 us
    unnamed x14 -> x24, local copies, waits for them, and re-layouts: 2.66 us -> 6.57 us
    all_to_all x2, waiting for transfers between devices: 13.6 us -> 9.83 us  [per_device(): lax.all_to_all(sent, spread, split_axis=0, concat_axis=0, tiled=True)]
    all_to_all x2, waiting for transfers between devices: 14.3 us -> 12.3 us  [per_device(): mix = lax.all_to_all(mix, spread, split_axis=0, concat_axis=0, tiled=True)]
    ppermute x2, waiting for transfers between devices: 0.01 us -> 1.88 us  [per_device(): other = lax.ppermute(own, 'half', swap)]
    pallas_call x11, Pallas kernels: 29.4 us -> 31.2 us  [call(): pl.pallas_call(kernel, out_shape=list(shapes), in_specs=[pl.BlockSpec(mem...]
    all_to_all x2, starting transfers between devices: 12.7 us -> 11 us  [per_device(): mix = lax.all_to_all(mix, spread, split_axis=0, concat_axis=0, tiled=True)]
  transfers between devices with their start and end apart: 6 -> 6, of which waited for: 4 -> 6; matrix products, arithmetic and copies ran while one was open for 0% -> 0% of each run, Pallas kernels for 23% -> 25%
where the time goes in v13:
time: 87.3 us; the launch traced here: 86.4 us
  Pallas kernels  31.2 us (36%)
  starting transfers between devices  24.2 us (28%)
  waiting for transfers between devices  24 us (27%)
  local copies, waits for them, and re-layouts  6.57 us (8%)
    pallas_call x11, Pallas kernels, call(): pl.pallas_call(kernel, out_shape=list(shapes), in_specs=[pl.BlockSpec(mem...  31.2 us
    all_to_all x2, waiting for transfers between devices, per_device(): mix = lax.all_to_all(mix, spread, split_axis=0, concat_axis=0, tiled=True)  12.3 us
    all_to_all x2, starting transfers between devices, per_device(): mix = lax.all_to_all(mix, spread, split_axis=0, concat_axis=0, tiled=True)  11 us
    all_to_all x2, starting transfers between devices, per_device(): lax.all_to_all(sent, spread, split_axis=0, concat_axis=0, tiled=True)  10.5 us
    all_to_all x2, waiting for transfers between devices, per_device(): lax.all_to_all(sent, spread, split_axis=0, concat_axis=0, tiled=True)  9.83 us
    unnamed x24, local copies, waits for them, and re-layouts  6.57 us
    ppermute x2, starting transfers between devices, per_device(): other = lax.ppermute(own, 'half', swap)  2.59 us
    ppermute x2, waiting for transfers between devices, per_device(): other = lax.ppermute(own, 'half', swap)  1.88 us
  transfers between devices with their start and end apart: 6, of which 6 were waited for; matrix products, arithmetic and copies ran while one was open for 0% of the time, Pallas kernels for 25%

profile of v13, /device:TPU:0, one launch (start us, length us, event | category | flops | bytes accessed | tf_op | source)
XLA Modules:
  0.0 86.4 jit_solution(17169807884700240365)
XLA Ops:
  0.0 7.3 %shard_map.118 = (bf16[4,128,1024]{2,1,0:T(8,128)(2,1)}, bf16[256,1152]{1,0:T(8,128)(2,1)}, bf16[256,512]{1,0:T(8,128)(2,1)}) custom-call(bf16[512,1024]{1,0:T(8,128)(2,1)} %bitcast.20, f32[1,1024]{1,0:T(1,128)} %bitcast.24, bf16[1024,1024]{1,0:T(8,128)(2,1)} %refs_2_.3, bf16[1024,512]{1,0:T(8,128)(2,1)} %refs_3_.3, bf16[1024,1024]{1,0:T(8,128)(2,1)} %refs_4_.3, ...), custom_call_target="tpu_custom_call" | custom-call | flops 1342177280 | bytes 8196256 | tf_op jit(solution)/shard_map/pallas_call | solution.py:314
  7.3 6.3 %all-to-all-start = ((bf16[16,16,1152]{2,1,0:T(8,128)(2,1)}), bf16[16,16,1152]{2,1,0:T(8,128)(2,1)S(1)}, u32[]{:S(2)}, u32[]{:S(2)}) async-start(bf16[16,16,1152]{2,1,0:T(8,128)(2,1)} %bitcast.22), calls=%async_computation | async-start | bytes 1179648 | tf_op jit(solution)/shard_map/all_to_all | solution.py:408
  13.6 0.0 copy-start.11
  13.6 7.5 %shard_map.119 = (bf16[4,128,1024]{2,1,0:T(8,128)(2,1)}, bf16[256,1024]{1,0:T(8,128)(2,1)}, bf16[256,512]{1,0:T(8,128)(2,1)}) custom-call(bf16[512,1024]{1,0:T(8,128)(2,1)} %bitcast.21, f32[1,1024]{1,0:T(1,128)} %bitcast.25, bf16[1024,1024]{1,0:T(8,128)(2,1)} %refs_2_.3, bf16[1024,512]{1,0:T(8,128)(2,1)} %refs_3_.3, ...), custom_call_target="tpu_custom_call", output_to_operand_aliasing={{0}: (6, {})} | custom-call | flops 1342177280 | bytes 9441280 | tf_op jit(solution)/shard_map/pallas_call | solution.py:314
  21.2 0.0 copy-start
  21.2 3.7 %all-to-all-done = bf16[16,16,1152]{2,1,0:T(8,128)(2,1)S(1)} async-done(((bf16[16,16,1152]{2,1,0:T(8,128)(2,1)}), bf16[16,16,1152]{2,1,0:T(8,128)(2,1)S(1)}, u32[]{:S(2)}, u32[]{:S(2)}) %all-to-all-start) | async-done | bytes 589856 | tf_op jit(solution)/shard_map/all_to_all | solution.py:408
  24.9 4.2 %all-to-all-start.1 = ((bf16[16,16,1024]{2,1,0:T(8,128)(2,1)}), bf16[16,16,1024]{2,1,0:T(8,128)(2,1)}, u32[]{:S(2)}, u32[]{:S(2)}) async-start(bf16[16,16,1024]{2,1,0:T(8,128)(2,1)} %bitcast.23), calls=%async_computation.1 | async-start | bytes 1048576 | tf_op jit(solution)/shard_map/all_to_all | solution.py:408
  29.1 0.0 copy-done.11
  29.1 0.0 copy-start.2
  29.2 1.2 %copy-done.2 = bf16[1024,512]{1,0:T(8,128)(2,1)S(1)} copy-done((bf16[1024,512]{1,0:T(8,128)(2,1)S(1)}, bf16[1024,512]{1,0:T(8,128)(2,1)}, u32[]{:S(2)}) %copy-start.2) | copy-done | bytes 1048600
  30.4 0.7 shard_map.120
  31.1 0.0 copy-start.9
  31.1 0.8 copy-done.9
  31.9 2.6 %collective-permute-start = (bf16[4,64,512]{2,1,0:T(8,128)(2,1)S(1)}, bf16[4,64,512]{2,1,0:T(8,128)(2,1)}, u32[]{:S(2)}, u32[]{:S(2)}) collective-permute-start(bf16[4,64,512]{2,1,0:T(8,128)(2,1)S(1)} %get-tuple-element.31.own), channel_id=1, source_target_pairs={{0,4},{4,0},{1,5},{5,1},{2,6},{6,2},{3,7},{7,3},{8,12},{12,8},{9,1... | collective-permute-start | bytes 786440 | tf_op jit(solution)/shard_map/ppermute | solution.py:426
  34.5 0.4 shard_map.122.weights
  34.9 0.0 copy-start.3
  34.9 0.0 copy-done
  34.9 0.0 copy-start.10
  34.9 1.1 %copy-done.10 = bf16[256,1024]{1,0:T(8,128)(2,1)S(1)} copy-done((bf16[256,1024]{1,0:T(8,128)(2,1)S(1)}, bf16[256,1024]{1,0:T(8,128)(2,1)}, u32[]{:S(2)}) %copy-start.10) | copy-done | bytes 524312
  36.0 0.7 shard_map.121.query
  36.7 0.0 copy-start.4
  36.7 0.8 copy-done.4
  37.5 6.1 %all-to-all-done.1 = bf16[16,16,1024]{2,1,0:T(8,128)(2,1)} async-done(((bf16[16,16,1024]{2,1,0:T(8,128)(2,1)}), bf16[16,16,1024]{2,1,0:T(8,128)(2,1)}, u32[]{:S(2)}, u32[]{:S(2)}) %all-to-all-start.1) | async-done | bytes 524320 | tf_op jit(solution)/shard_map/all_to_all | solution.py:408
  43.7 0.0 copy-done.3
  43.7 2.5 %shard_map.123 = (bf16[256,1024]{1,0:T(8,128)(2,1)S(1)}, bf16[4,64,512]{2,1,0:T(8,128)(2,1)}) custom-call(bf16[256,1024]{1,0:T(8,128)(2,1)} %bitcast.5.mid, f32[1,1024]{1,0:T(1,128)S(1)} %bitcast.19, bf16[1024,512]{1,0:T(8,128)(2,1)S(1)} %copy-done.3), custom_call_target="tpu_custom_call" | custom-call | flops 268435456 | bytes 2363392 | tf_op jit(solution)/shard_map/pallas_call | solution.py:314
  46.1 0.0 copy-start.7
  46.1 0.8 copy-done.7
  47.0 0.1 collective-permute-done.other
  47.0 0.0 collective-permute-start.1
  47.0 0.0 copy-start.5
  47.0 1.0 %copy-done.5 = bf16[4,64,1024]{2,1,0:T(8,128)(2,1)S(1)} copy-done((bf16[4,64,1024]{2,1,0:T(8,128)(2,1)S(1)}, bf16[4,64,1024]{2,1,0:T(8,128)(2,1)}, u32[]{:S(2)}) %copy-start.5) | copy-done | bytes 524312
  48.1 0.0 copy-start.8
  48.1 3.4 %shard_map.126 = bf16[256,1024]{1,0:T(8,128)(2,1)} custom-call(bf16[4,64,1024]{2,1,0:T(8,128)(2,1)S(1)} %copy-done.5, bf16[4,64,512]{2,1,0:T(8,128)(2,1)S(1)} %get-tuple-element.31.own, bf16[4,64,512]{2,1,0:T(8,128)(2,1)} %collective-permute-done.other, f32[128,64]{1,0:T(8,128)S(1)} %shard_map.122.weights), custom_call_target="tpu_custom_call" | custom-call | flops 134217728 | bytes 1605632 | tf_op jit(solution)/shard_map/pallas_call | solution.py:314
  51.4 7.5 %all-to-all-start.3 = ((bf16[16,16,1024]{2,1,0:T(8,128)(2,1)}), bf16[16,16,1024]{2,1,0:T(8,128)(2,1)S(1)}, u32[]{:S(2)}, u32[]{:S(2)}) async-start(bf16[16,16,1024]{2,1,0:T(8,128)(2,1)} %bitcast.10), calls=%async_computation.3 | async-start | bytes 1048576 | tf_op jit(solution)/shard_map/all_to_all | solution.py:451
  58.9 0.0 copy-done.8
  58.9 0.7 shard_map.124.query
  59.6 1.8 %collective-permute-done.1.other = bf16[4,64,512]{2,1,0:T(8,128)(2,1)} collective-permute-done((bf16[4,64,512]{2,1,0:T(8,128)(2,1)}, bf16[4,64,512]{2,1,0:T(8,128)(2,1)}, u32[]{:S(2)}, u32[]{:S(2)}) %collective-permute-start.1) | collective-permute-done | bytes 262176 | tf_op jit(solution)/shard_map/ppermute | solution.py:426
  61.5 0.0 copy-start.1
  61.5 2.7 %shard_map.125 = bf16[256,1024]{1,0:T(8,128)(2,1)S(1)} custom-call(bf16[4,64,1024]{2,1,0:T(8,128)(2,1)S(1)} %shard_map.124.query, bf16[4,64,512]{2,1,0:T(8,128)(2,1)} %get-tuple-element.32.own, bf16[4,64,512]{2,1,0:T(8,128)(2,1)} %collective-permute-done.1.other, f32[128,64]{1,0:T(8,128)S(1)} %shard_map.122.weights), custom_call_target="tpu_custom_call" | custom-call | flops 8388608000 | bytes 1605632 | tf_op jit(solution)/shard_map/pallas_call | solution.py:314
  64.2 0.0 copy-start.6
  64.2 0.8 copy-done.6
  65.0 4.5 %all-to-all-done.3 = bf16[16,16,1024]{2,1,0:T(8,128)(2,1)S(1)} async-done(((bf16[16,16,1024]{2,1,0:T(8,128)(2,1)}), bf16[16,16,1024]{2,1,0:T(8,128)(2,1)S(1)}, u32[]{:S(2)}, u32[]{:S(2)}) %all-to-all-start.3) | async-done | bytes 524320 | tf_op jit(solution)/shard_map/all_to_all | solution.py:451
  69.5 3.6 %all-to-all-start.2 = ((bf16[16,16,1024]{2,1,0:T(8,128)(2,1)}), bf16[16,16,1024]{2,1,0:T(8,128)(2,1)S(1)}, u32[]{:S(2)}, u32[]{:S(2)}) async-start(bf16[16,16,1024]{2,1,0:T(8,128)(2,1)} %bitcast.17), calls=%async_computation.2 | async-start | bytes 1048576 | tf_op jit(solution)/shard_map/all_to_all | solution.py:451
  73.0 0.0 copy-done.1
  73.1 2.6 %shard_map.127.mid_hbm = bf16[4,128,1024]{2,1,0:T(8,128)(2,1)} custom-call(bf16[256,1024]{1,0:T(8,128)(2,1)S(1)} %bitcast.15, bf16[4,128,1024]{2,1,0:T(8,128)(2,1)} %get-tuple-element.36.mid_hbm, bf16[1024,1024]{1,0:T(8,128)(2,1)S(1)} %copy-done.1), custom_call_target="tpu_custom_call", output_to_operand_aliasing={{}: (1, {})} | custom-call | flops 536870912 | bytes 4718592 | tf_op jit(solution)/shard_map/pallas_call | solution.py:314
  75.7 7.9 %all-to-all-done.2 = bf16[16,16,1024]{2,1,0:T(8,128)(2,1)S(1)} async-done(((bf16[16,16,1024]{2,1,0:T(8,128)(2,1)}), bf16[16,16,1024]{2,1,0:T(8,128)(2,1)S(1)}, u32[]{:S(2)}, u32[]{:S(2)}) %all-to-all-start.2) | async-done | bytes 524320 | tf_op jit(solution)/shard_map/all_to_all | solution.py:451
  83.6 2.6 %shard_map.128 = bf16[4,128,1024]{2,1,0:T(8,128)(2,1)} custom-call(bf16[256,1024]{1,0:T(8,128)(2,1)S(1)} %bitcast.16, bf16[4,128,1024]{2,1,0:T(8,128)(2,1)} %shard_map.127.mid_hbm, bf16[1024,1024]{1,0:T(8,128)(2,1)S(1)} %copy-done.1), custom_call_target="tpu_custom_call", output_to_operand_aliasing={{}: (1, {})} | custom-call | flops 536870912 | bytes 4718592 | tf_op jit(solution)/shard_map/pallas_call | solution.py:314
Async XLA Ops:
  7.3 17.6 %all-to-all-start = ((bf16[16,16,1152]{2,1,0:T(8,128)(2,1)}), bf16[16,16,1152]{2,1,0:T(8,128)(2,1)S(1)}, u32[]{:S(2)}, u32[]{:S(2)}) async-start(bf16[16,16,1152]{2,1,0:T(8,128)(2,1)} %bitcast.22), calls=%async_computation | async-start | bytes 1179648 | tf_op jit(solution)/shard_map/all_to_all | solution.py:408
  13.6 15.5 %copy-start.11 = (f32[1024]{0:T(1024)S(1)}, f32[1024]{0:T(1024)}, u32[]{:S(2)}) copy-start(f32[1024]{0:T(1024)} %param.17) | copy-start | bytes 12292
  21.2 13.7 %copy-start = (bf16[1024,1024]{1,0:T(8,128)(2,1)S(1)}, bf16[1024,1024]{1,0:T(8,128)(2,1)}, u32[]{:S(2)}) copy-start(bf16[1024,1024]{1,0:T(8,128)(2,1)} %wq.3) | copy-start | bytes 6291460
  24.9 18.8 %all-to-all-start.1 = ((bf16[16,16,1024]{2,1,0:T(8,128)(2,1)}), bf16[16,16,1024]{2,1,0:T(8,128)(2,1)}, u32[]{:S(2)}, u32[]{:S(2)}) async-start(bf16[16,16,1024]{2,1,0:T(8,128)(2,1)} %bitcast.23), calls=%async_computation.1 | async-start | bytes 1048576 | tf_op jit(solution)/shard_map/all_to_all | solution.py:408
  29.1 1.2 %copy-start.2 = (bf16[1024,512]{1,0:T(8,128)(2,1)S(1)}, bf16[1024,512]{1,0:T(8,128)(2,1)}, u32[]{:S(2)}) copy-start(bf16[1024,512]{1,0:T(8,128)(2,1)} %wkv.3) | copy-start | bytes 3145732
  31.1 0.8 copy-start.9
  31.9 15.1 %collective-permute-start = (bf16[4,64,512]{2,1,0:T(8,128)(2,1)S(1)}, bf16[4,64,512]{2,1,0:T(8,128)(2,1)}, u32[]{:S(2)}, u32[]{:S(2)}) collective-permute-start(bf16[4,64,512]{2,1,0:T(8,128)(2,1)S(1)} %get-tuple-element.31.own), channel_id=1, source_target_pairs={{0,4},{4,0},{1,5},{5,1},{2,6},{6,2},{3,7},{7,3},{8,12},{12,8},{9,1... | collective-permute-start | bytes 786440 | tf_op jit(solution)/shard_map/ppermute | solution.py:426
  34.9 8.8 %copy-start.3 = (bf16[1024,512]{1,0:T(8,128)(2,1)S(1)}, bf16[1024,512]{1,0:T(8,128)(2,1)}, u32[]{:S(2)}) copy-start(bf16[1024,512]{1,0:T(8,128)(2,1)} %wkv.3) | copy-start | bytes 3145732
  34.9 1.1 %copy-start.10 = (bf16[256,1024]{1,0:T(8,128)(2,1)S(1)}, bf16[256,1024]{1,0:T(8,128)(2,1)}, u32[]{:S(2)}) copy-start(bf16[256,1024]{1,0:T(8,128)(2,1)} %copy-done.9) | copy-start | bytes 1572868
  36.7 0.8 copy-start.4
  46.1 0.8 copy-start.7
  47.0 14.4 %collective-permute-start.1 = (bf16[4,64,512]{2,1,0:T(8,128)(2,1)}, bf16[4,64,512]{2,1,0:T(8,128)(2,1)}, u32[]{:S(2)}, u32[]{:S(2)}) collective-permute-start(bf16[4,64,512]{2,1,0:T(8,128)(2,1)} %get-tuple-element.32.own), channel_id=1, source_target_pairs={{0,4},{4,0},{1,5},{5,1},{2,6},{6,2},{3,7},{7,3},{8,12},{12,8},{9,1... | collective-permute-start | bytes 786440 | tf_op jit(solution)/shard_map/ppermute | solution.py:426
  47.0 1.0 %copy-start.5 = (bf16[4,64,1024]{2,1,0:T(8,128)(2,1)S(1)}, bf16[4,64,1024]{2,1,0:T(8,128)(2,1)}, u32[]{:S(2)}) copy-start(bf16[4,64,1024]{2,1,0:T(8,128)(2,1)} %copy-done.4) | copy-start | bytes 1572868
  48.1 10.9 %copy-start.8 = (bf16[256,1024]{1,0:T(8,128)(2,1)S(1)}, bf16[256,1024]{1,0:T(8,128)(2,1)}, u32[]{:S(2)}) copy-start(bf16[256,1024]{1,0:T(8,128)(2,1)} %copy-done.7) | copy-start | bytes 1572868
  51.4 18.0 %all-to-all-start.3 = ((bf16[16,16,1024]{2,1,0:T(8,128)(2,1)}), bf16[16,16,1024]{2,1,0:T(8,128)(2,1)S(1)}, u32[]{:S(2)}, u32[]{:S(2)}) async-start(bf16[16,16,1024]{2,1,0:T(8,128)(2,1)} %bitcast.10), calls=%async_computation.3 | async-start | bytes 1048576 | tf_op jit(solution)/shard_map/all_to_all | solution.py:451
  61.5 11.6 %copy-start.1 = (bf16[1024,1024]{1,0:T(8,128)(2,1)S(1)}, bf16[1024,1024]{1,0:T(8,128)(2,1)}, u32[]{:S(2)}) copy-start(bf16[1024,1024]{1,0:T(8,128)(2,1)} %wo.3) | copy-start | bytes 6291460
  64.2 0.8 copy-start.6
  69.5 14.1 %all-to-all-start.2 = ((bf16[16,16,1024]{2,1,0:T(8,128)(2,1)}), bf16[16,16,1024]{2,1,0:T(8,128)(2,1)S(1)}, u32[]{:S(2)}, u32[]{:S(2)}) async-start(bf16[16,16,1024]{2,1,0:T(8,128)(2,1)} %bitcast.17), calls=%async_computation.2 | async-start | bytes 1048576 | tf_op jit(solution)/shard_map/all_to_all | solution.py:451

commit v14 on v10

--- a/solution.py
+++ b/solution.py
@@ -190,12 +190,6 @@
         projected = jnp.dot(mix[...], wo[:, cols], preferred_element_type=F32)
         piece = (hist[:, cols].astype(F32) + projected).astype(BF16)
         mid[:, cols] = piece
-        sent[:, cols] = moved(order, piece)
-        part = pl.ds(c, COLS)
-        keeps.append(
-            pltpu.make_async_copy(sent.at[:, part], sent_hbm.at[:, part], sent_sems.at[c // COLS])
-        )
-        keeps[-1].start()
     for a in range(agents):
         goal = mid_hbm.at[a, pl.ds(chunk * span, span), :]
         keeps.append(
@@ -212,10 +206,15 @@
             listed = lane == alive.shape[1] + neighbours[0, i]
             notes = notes + jnp.where(listed, nbr_valid[0, i].astype(F32), 0.0)
         sent[:, width:] = jnp.broadcast_to(notes, (rows, LANES)).astype(BF16)
-        part = pl.ds(width, LANES)
+    for r in range(0, rows, rows // 2):
+        for c in range(0, width, COLS):
+            sent[r : r + rows // 2, c : c + COLS] = moved(
+                order[r : r + rows // 2], mid[:, c : c + COLS]
+            )
+        part = pl.ds(r, rows // 2)
         keeps.append(
             pltpu.make_async_copy(
-                sent.at[:, part], sent_hbm.at[:, part], sent_sems.at[width // COLS]
+                sent.at[part, :], sent_hbm.at[part, :], sent_sems.at[r // (rows // 2)]
             )
         )
         keeps[-1].start()
@@ -300,20 +299,18 @@
     for c in range(0, width, COLS):
         for i in range(chunks):
             mix[i * rows : (i + 1) * rows, c : c + COLS] = moved(order, mixes[i][:, c : c + COLS])
-    for load in loads:
-        load.wait()
-    for c in range(0, width, COLS):
-        cols = slice(c, c + COLS)
-        projected = jnp.dot(mix[...], wo[:, cols], preferred_element_type=F32)
-        for i in range(chunks):
-            piece = projected[i * rows : (i + 1) * rows].reshape(agents, span, COLS)
+    keeps = []
+    for i in range(chunks):
+        loads[i].wait()
+        for c in range(0, width, COLS):
+            cols = slice(c, c + COLS)
+            part = mix[i * rows : (i + 1) * rows, :]
+            projected = jnp.dot(part, wo[:, cols], preferred_element_type=F32)
+            piece = projected.reshape(agents, span, COLS)
             mids[i, :, :, cols] = (mids[i, :, :, cols].astype(F32) + piece).astype(BF16)
-    keeps = [
-        pltpu.make_async_copy(mids.at[i], out_hbm.at[:, pl.ds(i * span, span), :], out_sems.at[i])
-        for i in range(chunks)
-    ]
-    for keep in keeps:
-        keep.start()
+        goal = out_hbm.at[:, pl.ds(i * span, span), :]
+        keeps.append(pltpu.make_async_copy(mids.at[i], goal, out_sems.at[i]))
+        keeps[-1].start()
     for keep in keeps:
         keep.wait()
 
@@ -402,7 +399,7 @@
                 pltpu.SemaphoreType.DMA((width // COLS,)),
                 pltpu.SemaphoreType.DMA((2,)),
                 pltpu.SemaphoreType.DMA((agents,)),
-                pltpu.SemaphoreType.DMA((width // COLS + 1,)),
+                pltpu.SemaphoreType.DMA((2,)),
                 pltpu.SemaphoreType.DMA,
             ],
             flops=2 * rows * width * (2 * width + 2 * KEYS),

time: 84.7 us -> 83.7 us (0.988)
  Pallas kernels: 29.5 us -> 27.4 us
  waiting for transfers between devices: 21.4 us -> 22.4 us
    pallas_call x10, Pallas kernels: 29.5 us -> 27.4 us  [call(): pl.pallas_call(kernel, out_shape=list(shapes), in_specs=[pl.BlockSpec(mem...]
    all_to_all x2, waiting for transfers between devices: 12.6 us -> 13.6 us  [per_device(): lax.all_to_all(sent, spread, split_axis=0, concat_axis=0, tiled=True)]
  transfers between devices with their start and end apart: 5 -> 5, of which waited for: 4 -> 4; matrix products, arithmetic and copies ran while one was open for 0% -> 0% of each run, Pallas kernels for 21% -> 20%
where the time goes in v14:
time: 83.7 us; the launch traced here: 83 us
  Pallas kernels  27.4 us (33%)
  waiting for transfers between devices  22.4 us (27%)
  starting transfers between devices  16.3 us (19%)
  blocking collectives  13.2 us (16%)
  local copies, waits for them, and re-layouts  3.45 us (4%)
    pallas_call x10, Pallas kernels, call(): pl.pallas_call(kernel, out_shape=list(shapes), in_specs=[pl.BlockSpec(mem...  27.4 us
    all_to_all x2, waiting for transfers between devices, per_device(): lax.all_to_all(sent, spread, split_axis=0, concat_axis=0, tiled=True)  13.6 us
    all_to_all x1, blocking collectives, per_device(): mix = lax.all_to_all(mix, spread, split_axis=0, concat_axis=0, tiled=True)  13.2 us
    all_to_all x2, starting transfers between devices, per_device(): lax.all_to_all(sent, spread, split_axis=0, concat_axis=0, tiled=True)  9.87 us
    all_to_all x1, waiting for transfers between devices, per_device(): mix = lax.all_to_all(mix, spread, split_axis=0, concat_axis=0, tiled=True)  4.69 us
    ppermute x2, waiting for transfers between devices, per_device(): other = lax.ppermute(own, 'half', swap)  4.1 us
    all_to_all x1, starting transfers between devices, per_device(): mix = lax.all_to_all(mix, spread, split_axis=0, concat_axis=0, tiled=True)  3.75 us
    unnamed x14, local copies, waits for them, and re-layouts  3.45 us
  transfers between devices with their start and end apart: 5, of which 4 were waited for; matrix products, arithmetic and copies ran while one was open for 0% of the time, Pallas kernels for 20%

profile of v14, /device:TPU:0, one launch (start us, length us, event | category | flops | bytes accessed | tf_op | source)
XLA Modules:
  0.0 83.0 jit_solution(17265004309196498492)
XLA Ops:
  0.0 7.3 %shard_map.118 = (bf16[4,128,1024]{2,1,0:T(8,128)(2,1)}, bf16[256,1152]{1,0:T(8,128)(2,1)}, bf16[256,512]{1,0:T(8,128)(2,1)}) custom-call(bf16[512,1024]{1,0:T(8,128)(2,1)} %bitcast.21, f32[1,1024]{1,0:T(1,128)} %bitcast.25, bf16[1024,1024]{1,0:T(8,128)(2,1)} %refs_2_.3, bf16[1024,512]{1,0:T(8,128)(2,1)} %refs_3_.4, bf16[1024,1024]{1,0:T(8,128)(2,1)} %refs_4_.3, ...), custom_call_target="tpu_custom_call" | custom-call | flops 1342177280 | bytes 8196256 | tf_op jit(solution)/shard_map/pallas_call | solution.py:324
  7.3 6.3 %all-to-all-start = ((bf16[16,16,1152]{2,1,0:T(8,128)(2,1)}), bf16[16,16,1152]{2,1,0:T(8,128)(2,1)S(1)}, u32[]{:S(2)}, u32[]{:S(2)}) async-start(bf16[16,16,1152]{2,1,0:T(8,128)(2,1)} %bitcast.23), calls=%async_computation | async-start | bytes 1179648 | tf_op jit(solution)/shard_map/all_to_all | solution.py:418
  13.7 0.0 copy-start
  13.7 0.0 copy-start.4
  13.7 7.6 %shard_map.119 = (bf16[4,128,1024]{2,1,0:T(8,128)(2,1)}, bf16[256,1024]{1,0:T(8,128)(2,1)}, bf16[256,512]{1,0:T(8,128)(2,1)}) custom-call(bf16[512,1024]{1,0:T(8,128)(2,1)} %bitcast.22, f32[1,1024]{1,0:T(1,128)} %bitcast.26, bf16[1024,1024]{1,0:T(8,128)(2,1)} %refs_2_.3, bf16[1024,512]{1,0:T(8,128)(2,1)} %refs_3_.4, ...), custom_call_target="tpu_custom_call", output_to_operand_aliasing={{0}: (6, {})} | custom-call | flops 1342177280 | bytes 9441280 | tf_op jit(solution)/shard_map/pallas_call | solution.py:324
  21.3 3.6 %all-to-all-done = bf16[16,16,1152]{2,1,0:T(8,128)(2,1)S(1)} async-done(((bf16[16,16,1152]{2,1,0:T(8,128)(2,1)}), bf16[16,16,1152]{2,1,0:T(8,128)(2,1)S(1)}, u32[]{:S(2)}, u32[]{:S(2)}) %all-to-all-start) | async-done | bytes 589856 | tf_op jit(solution)/shard_map/all_to_all | solution.py:418
  24.9 3.6 %all-to-all-start.1 = ((bf16[16,16,1024]{2,1,0:T(8,128)(2,1)}), bf16[16,16,1024]{2,1,0:T(8,128)(2,1)S(1)}, u32[]{:S(2)}, u32[]{:S(2)}) async-start(bf16[16,16,1024]{2,1,0:T(8,128)(2,1)} %bitcast.24), calls=%async_computation.1 | async-start | bytes 1048576 | tf_op jit(solution)/shard_map/all_to_all | solution.py:418
  28.5 0.0 copy-done
  28.5 0.0 copy-done.4
  28.5 0.7 shard_map.120
  29.2 2.7 %collective-permute-start = (bf16[4,64,512]{2,1,0:T(8,128)(2,1)S(1)}, bf16[4,64,512]{2,1,0:T(8,128)(2,1)S(1)}, u32[]{:S(2)}, u32[]{:S(2)}) collective-permute-start(bf16[4,64,512]{2,1,0:T(8,128)(2,1)S(1)} %get-tuple-element.27.own), channel_id=1, source_target_pairs={{0,4},{4,0},{1,5},{5,1},{2,6},{6,2},{3,7},{7,3},{8,12},{12,8},{9,1... | collective-permute-start | bytes 786440 | tf_op jit(solution)/shard_map/ppermute | solution.py:428
  31.9 0.4 shard_map.123.weights
  32.3 0.0 copy-start.1
  32.3 1.6 %copy-done.1 = bf16[1024,1024]{1,0:T(8,128)(2,1)S(1)} copy-done((bf16[1024,1024]{1,0:T(8,128)(2,1)S(1)}, bf16[1024,1024]{1,0:T(8,128)(2,1)}, u32[]{:S(2)}) %copy-start.1) | copy-done | bytes 2097176
  33.9 0.7 shard_map.121.query
  34.6 10.0 %all-to-all-done.1 = bf16[16,16,1024]{2,1,0:T(8,128)(2,1)S(1)} async-done(((bf16[16,16,1024]{2,1,0:T(8,128)(2,1)}), bf16[16,16,1024]{2,1,0:T(8,128)(2,1)S(1)}, u32[]{:S(2)}, u32[]{:S(2)}) %all-to-all-start.1) | async-done | bytes 524320 | tf_op jit(solution)/shard_map/all_to_all | solution.py:418
  44.6 1.4 %shard_map.122 = (bf16[256,1024]{1,0:T(8,128)(2,1)S(1)}, bf16[4,64,512]{2,1,0:T(8,128)(2,1)}) custom-call(bf16[256,1024]{1,0:T(8,128)(2,1)S(1)} %bitcast.15, f32[1,1024]{1,0:T(1,128)S(1)} %bitcast.20, bf16[1024,512]{1,0:T(8,128)(2,1)S(1)} %copy-done), custom_call_target="tpu_custom_call" | custom-call | flops 268435456 | bytes 2363392 | tf_op jit(solution)/shard_map/pallas_call | solution.py:324
  46.1 0.0 copy-start.5
  46.1 0.8 copy-done.5
  46.9 0.0 copy-start.2
  46.9 0.0 collective-permute-start.1
  46.9 0.0 collective-permute-done.other
  46.9 2.3 %shard_map.124 = bf16[256,1024]{1,0:T(8,128)(2,1)} custom-call(bf16[4,64,1024]{2,1,0:T(8,128)(2,1)S(1)} %shard_map.121.query, bf16[4,64,512]{2,1,0:T(8,128)(2,1)S(1)} %get-tuple-element.27.own, bf16[4,64,512]{2,1,0:T(8,128)(2,1)S(1)} %collective-permute-done.other, f32[128,64]{1,0:T(8,128)S(1)} %shard_map.123.weights), custom_call_target="tpu_custom_call" | custom-call | flops 134217728 | bytes 1605632 | tf_op jit(solution)/shard_map/pallas_call | solution.py:324
  49.2 3.8 %all-to-all-start.2 = ((bf16[16,16,1024]{2,1,0:T(8,128)(2,1)}), bf16[16,16,1024]{2,1,0:T(8,128)(2,1)S(1)}, u32[]{:S(2)}, u32[]{:S(2)}) async-start(bf16[16,16,1024]{2,1,0:T(8,128)(2,1)} %bitcast.8), calls=%async_computation.2 | async-start | bytes 1048576 | tf_op jit(solution)/shard_map/all_to_all | solution.py:457
  53.0 0.0 copy-done.2
  53.0 0.0 copy-start.6
  53.0 1.0 %copy-done.6 = bf16[256,1024]{1,0:T(8,128)(2,1)S(1)} copy-done((bf16[256,1024]{1,0:T(8,128)(2,1)S(1)}, bf16[256,1024]{1,0:T(8,128)(2,1)}, u32[]{:S(2)}) %copy-start.6) | copy-done | bytes 524312
  54.0 0.7 shard_map.125.query
  54.7 0.0 copy-start.3
  54.8 4.1 %collective-permute-done.1.other = bf16[4,64,512]{2,1,0:T(8,128)(2,1)} collective-permute-done((bf16[4,64,512]{2,1,0:T(8,128)(2,1)}, bf16[4,64,512]{2,1,0:T(8,128)(2,1)}, u32[]{:S(2)}, u32[]{:S(2)}) %collective-permute-start.1) | collective-permute-done | bytes 262176 | tf_op jit(solution)/shard_map/ppermute | solution.py:428
  58.9 2.6 %shard_map.126 = bf16[256,1024]{1,0:T(8,128)(2,1)S(1)} custom-call(bf16[4,64,1024]{2,1,0:T(8,128)(2,1)S(1)} %shard_map.125.query, bf16[4,64,512]{2,1,0:T(8,128)(2,1)} %get-tuple-element.29.own, bf16[4,64,512]{2,1,0:T(8,128)(2,1)} %collective-permute-done.1.other, f32[128,64]{1,0:T(8,128)S(1)} %shard_map.123.weights), custom_call_target="tpu_custom_call" | custom-call | flops 134217728 | bytes 1605632 | tf_op jit(solution)/shard_map/pallas_call | solution.py:324
  61.5 4.7 %all-to-all-done.2 = bf16[16,16,1024]{2,1,0:T(8,128)(2,1)S(1)} async-done(((bf16[16,16,1024]{2,1,0:T(8,128)(2,1)}), bf16[16,16,1024]{2,1,0:T(8,128)(2,1)S(1)}, u32[]{:S(2)}, u32[]{:S(2)}) %all-to-all-start.2) | async-done | bytes 524320 | tf_op jit(solution)/shard_map/all_to_all | solution.py:457
  66.2 13.2 %all_to_all.20 = bf16[16,16,1024]{2,1,0:T(8,128)(2,1)S(1)} all-to-all(bf16[16,16,1024]{2,1,0:T(8,128)(2,1)S(1)} %bitcast.17), channel_id=1, replica_groups=mesh['tile'=4,'half'=2,'rest'=4] {'tile','rest'}, dimensions={0} | all-to-all | bytes 1048576 | tf_op jit(solution)/shard_map/all_to_all | solution.py:457
  79.3 0.0 copy-done.3
  79.3 3.5 %shard_map.127 = bf16[4,128,1024]{2,1,0:T(8,128)(2,1)} custom-call(bf16[256,1024]{1,0:T(8,128)(2,1)S(1)} %bitcast.16, bf16[256,1024]{1,0:T(8,128)(2,1)S(1)} %bitcast.18, bf16[4,128,1024]{2,1,0:T(8,128)(2,1)} %get-tuple-element.30.refs_2_, bf16[1024,1024]{1,0:T(8,128)(2,1)S(1)} %copy-done.3), custom_call_target="tpu_custom_call", output_to_operand_aliasing={{}: (2, {})} | custom-call | flops 536870912 | bytes 5242880 | tf_op jit(solution)/shard_map/pallas_call | solution.py:324
Async XLA Ops:
  7.3 17.6 %all-to-all-start = ((bf16[16,16,1152]{2,1,0:T(8,128)(2,1)}), bf16[16,16,1152]{2,1,0:T(8,128)(2,1)S(1)}, u32[]{:S(2)}, u32[]{:S(2)}) async-start(bf16[16,16,1152]{2,1,0:T(8,128)(2,1)} %bitcast.23), calls=%async_computation | async-start | bytes 1179648 | tf_op jit(solution)/shard_map/all_to_all | solution.py:418
  13.7 14.8 %copy-start = (bf16[1024,512]{1,0:T(8,128)(2,1)S(1)}, bf16[1024,512]{1,0:T(8,128)(2,1)}, u32[]{:S(2)}) copy-start(bf16[1024,512]{1,0:T(8,128)(2,1)} %wkv.3) | copy-start | bytes 3145732
  13.7 14.8 %copy-start.4 = (f32[1024]{0:T(1024)S(1)}, f32[1024]{0:T(1024)}, u32[]{:S(2)}) copy-start(f32[1024]{0:T(1024)} %param.17) | copy-start | bytes 12292
  24.9 19.7 %all-to-all-start.1 = ((bf16[16,16,1024]{2,1,0:T(8,128)(2,1)}), bf16[16,16,1024]{2,1,0:T(8,128)(2,1)S(1)}, u32[]{:S(2)}, u32[]{:S(2)}) async-start(bf16[16,16,1024]{2,1,0:T(8,128)(2,1)} %bitcast.24), calls=%async_computation.1 | async-start | bytes 1048576 | tf_op jit(solution)/shard_map/all_to_all | solution.py:418
  29.2 17.6 %collective-permute-start = (bf16[4,64,512]{2,1,0:T(8,128)(2,1)S(1)}, bf16[4,64,512]{2,1,0:T(8,128)(2,1)S(1)}, u32[]{:S(2)}, u32[]{:S(2)}) collective-permute-start(bf16[4,64,512]{2,1,0:T(8,128)(2,1)S(1)} %get-tuple-element.27.own), channel_id=1, source_target_pairs={{0,4},{4,0},{1,5},{5,1},{2,6},{6,2},{3,7},{7,3},{8,12},{12,8},{9,1... | collective-permute-start | bytes 786440 | tf_op jit(solution)/shard_map/ppermute | solution.py:428
  32.3 1.6 %copy-start.1 = (bf16[1024,1024]{1,0:T(8,128)(2,1)S(1)}, bf16[1024,1024]{1,0:T(8,128)(2,1)}, u32[]{:S(2)}) copy-start(bf16[1024,1024]{1,0:T(8,128)(2,1)} %wq.3) | copy-start | bytes 6291460
  46.1 0.8 copy-start.5
  46.9 6.1 %copy-start.2 = (bf16[1024,1024]{1,0:T(8,128)(2,1)S(1)}, bf16[1024,1024]{1,0:T(8,128)(2,1)}, u32[]{:S(2)}) copy-start(bf16[1024,1024]{1,0:T(8,128)(2,1)} %wq.3) | copy-start | bytes 6291460
  46.9 12.0 %collective-permute-start.1 = (bf16[4,64,512]{2,1,0:T(8,128)(2,1)}, bf16[4,64,512]{2,1,0:T(8,128)(2,1)}, u32[]{:S(2)}, u32[]{:S(2)}) collective-permute-start(bf16[4,64,512]{2,1,0:T(8,128)(2,1)} %get-tuple-element.29.own), channel_id=1, source_target_pairs={{0,4},{4,0},{1,5},{5,1},{2,6},{6,2},{3,7},{7,3},{8,12},{12,8},{9,1... | collective-permute-start | bytes 786440 | tf_op jit(solution)/shard_map/ppermute | solution.py:428
  49.2 16.9 %all-to-all-start.2 = ((bf16[16,16,1024]{2,1,0:T(8,128)(2,1)}), bf16[16,16,1024]{2,1,0:T(8,128)(2,1)S(1)}, u32[]{:S(2)}, u32[]{:S(2)}) async-start(bf16[16,16,1024]{2,1,0:T(8,128)(2,1)} %bitcast.8), calls=%async_computation.2 | async-start | bytes 1048576 | tf_op jit(solution)/shard_map/all_to_all | solution.py:457
  53.0 1.0 %copy-start.6 = (bf16[256,1024]{1,0:T(8,128)(2,1)S(1)}, bf16[256,1024]{1,0:T(8,128)(2,1)}, u32[]{:S(2)}) copy-start(bf16[256,1024]{1,0:T(8,128)(2,1)} %copy-done.5) | copy-start | bytes 1572868
  54.7 24.6 %copy-start.3 = (bf16[1024,1024]{1,0:T(8,128)(2,1)S(1)}, bf16[1024,1024]{1,0:T(8,128)(2,1)}, u32[]{:S(2)}) copy-start(bf16[1024,1024]{1,0:T(8,128)(2,1)} %refs_3_.5) | copy-start | bytes 6291460

commit v15 on v14

--- a/solution.py
+++ b/solution.py
@@ -222,7 +222,7 @@
         keep.wait()
 
 
-def keys_kernel(local, mid, gain, wkv, second, out):
+def keys_kernel(local, mid, gain, wkv, out, second):
     rows, width = second.shape
     total = rows // local
     second[...] = norm_rows(mid[:, :width], gain[...])
@@ -235,8 +235,14 @@
         out[:, :, c : c + COLS] = result.astype(BF16).reshape(local, total, COLS)
 
 
-def query_kernel(second, wq, out):
+def query_kernel(mid, gain, wq, out, second):
     local, total, width = out.shape
+    rows = local * total
+    second[...] = norm_rows(mid[:, :width], gain[...])
+    if local > 1:
+        order = one_hot(rows, lambda row: regroup(row, total, local, 1))
+        for c in range(0, width, COLS):
+            second[:, c : c + COLS] = moved(order, second[:, c : c + COLS])
     for c in range(0, width, COLS):
         result = jnp.dot(second[...], wq[:, c : c + COLS], preferred_element_type=F32)
         out[:, :, c : c + COLS] = result.astype(BF16).reshape(local, total, COLS)
@@ -419,10 +425,11 @@
         there = there.reshape(rows, deep)
         if i + 1 < chunks:
             there, sents[i + 1] = lax.optimization_barrier((there, sents[i + 1]))
-        second, own = call(
+        own = call(
             functools.partial(keys_kernel, local),
-            [struct((rows, width), BF16), struct((local, total, 2 * KEYS), BF16)],
+            [struct((local, total, 2 * KEYS), BF16)],
             [there, gain_space[None], wkv_space],
+            scratch=[pltpu.VMEM((rows, width), BF16)],
             flops=2 * rows * width * 2 * KEYS,
         )
         other = lax.ppermute(own, "half", swap)
@@ -436,7 +443,8 @@
         query = call(
             query_kernel,
             [struct((local, total, width), BF16)],
-            [second, wq_space],
+            [there, gain_space[None], wq_space],
+            scratch=[pltpu.VMEM((rows, width), BF16)],
             flops=(2 if i == 0 else SHADOW) * rows * width * width,
         )
         homes.append((query, own, other))

time: 83.7 us -> 86.1 us (1.029)
  starting transfers between devices: 16.3 us -> 21.9 us
  waiting for transfers between devices: 22.4 us -> 18 us
  local copies, waits for them, and re-layouts: 3.45 us -> 4.85 us
    all_to_all x1, starting transfers between devices: 3.75 us -> 9.33 us  [per_device(): mix = lax.all_to_all(mix, spread, split_axis=0, concat_axis=0, tiled=True)]
    ppermute x2, waiting for transfers between devices: 4.1 us -> 0.01 us  [per_device(): other = lax.ppermute(own, 'half', swap)]
    unnamed x14, local copies, waits for them, and re-layouts: 3.45 us -> 4.85 us
  transfers between devices with their start and end apart: 5 -> 5, of which waited for: 4 -> 3; matrix products, arithmetic and copies ran while one was open for 0% -> 0% of each run, Pallas kernels for 20% -> 19%
where the time goes in v15:
time: 86.1 us; the launch traced here: 85.5 us
  Pallas kernels  27.2 us (32%)
  starting transfers between devices  21.9 us (25%)
  waiting for transfers between devices  18 us (21%)
  blocking collectives  13.2 us (15%)
  local copies, waits for them, and re-layouts  4.85 us (6%)
    pallas_call x10, Pallas kernels, call(): pl.pallas_call(kernel, out_shape=list(shapes), in_specs=[pl.BlockSpec(mem...  27.2 us
    all_to_all x2, waiting for transfers between devices, per_device(): lax.all_to_all(sent, spread, split_axis=0, concat_axis=0, tiled=True)  13.3 us
    all_to_all x1, blocking collectives, per_device(): mix = lax.all_to_all(mix, spread, split_axis=0, concat_axis=0, tiled=True)  13.2 us
    all_to_all x2, starting transfers between devices, per_device(): lax.all_to_all(sent, spread, split_axis=0, concat_axis=0, tiled=True)  9.87 us
    all_to_all x1, starting transfers between devices, per_device(): mix = lax.all_to_all(mix, spread, split_axis=0, concat_axis=0, tiled=True)  9.33 us
    unnamed x14, local copies, waits for them, and re-layouts  4.85 us
    all_to_all x1, waiting for transfers between devices, per_device(): mix = lax.all_to_all(mix, spread, split_axis=0, concat_axis=0, tiled=True)  4.69 us
    ppermute x2, starting transfers between devices, per_device(): other = lax.ppermute(own, 'half', swap)  2.73 us
  transfers between devices with their start and end apart: 5, of which 3 were waited for; matrix products, arithmetic and copies ran while one was open for 0% of the time, Pallas kernels for 19%

profile of v15, /device:TPU:0, one launch (start us, length us, event | category | flops | bytes accessed | tf_op | source)
XLA Modules:
  0.0 85.5 jit_solution(14044192524813745079)
XLA Ops:
  0.0 7.3 %shard_map.118 = (bf16[4,128,1024]{2,1,0:T(8,128)(2,1)}, bf16[256,1152]{1,0:T(8,128)(2,1)}, bf16[256,512]{1,0:T(8,128)(2,1)}) custom-call(bf16[512,1024]{1,0:T(8,128)(2,1)} %bitcast.25, f32[1,1024]{1,0:T(1,128)} %bitcast.29, bf16[1024,1024]{1,0:T(8,128)(2,1)} %refs_2_.3, bf16[1024,512]{1,0:T(8,128)(2,1)} %refs_3_.4, bf16[1024,1024]{1,0:T(8,128)(2,1)} %refs_4_.3, ...), custom_call_target="tpu_custom_call" | custom-call | flops 1342177280 | bytes 8196256 | tf_op jit(solution)/shard_map/pallas_call | solution.py:330
  7.3 6.3 %all-to-all-start = ((bf16[16,16,1152]{2,1,0:T(8,128)(2,1)}), bf16[16,16,1152]{2,1,0:T(8,128)(2,1)S(1)}, u32[]{:S(2)}, u32[]{:S(2)}) async-start(bf16[16,16,1152]{2,1,0:T(8,128)(2,1)} %bitcast.27), calls=%async_computation | async-start | bytes 1179648 | tf_op jit(solution)/shard_map/all_to_all | solution.py:424
  13.6 0.0 copy-start
  13.6 0.0 copy-start.6
  13.7 7.6 %shard_map.119 = (bf16[4,128,1024]{2,1,0:T(8,128)(2,1)}, bf16[256,1024]{1,0:T(8,128)(2,1)}, bf16[256,512]{1,0:T(8,128)(2,1)}) custom-call(bf16[512,1024]{1,0:T(8,128)(2,1)} %bitcast.26, f32[1,1024]{1,0:T(1,128)} %bitcast.30, bf16[1024,1024]{1,0:T(8,128)(2,1)} %refs_2_.3, bf16[1024,512]{1,0:T(8,128)(2,1)} %refs_3_.4, ...), custom_call_target="tpu_custom_call", output_to_operand_aliasing={{0}: (6, {})} | custom-call | flops 1342177280 | bytes 9441280 | tf_op jit(solution)/shard_map/pallas_call | solution.py:330
  21.3 3.6 %all-to-all-done = bf16[16,16,1152]{2,1,0:T(8,128)(2,1)S(1)} async-done(((bf16[16,16,1152]{2,1,0:T(8,128)(2,1)}), bf16[16,16,1152]{2,1,0:T(8,128)(2,1)S(1)}, u32[]{:S(2)}, u32[]{:S(2)}) %all-to-all-start) | async-done | bytes 589856 | tf_op jit(solution)/shard_map/all_to_all | solution.py:424
  24.9 3.6 %all-to-all-start.1 = ((bf16[16,16,1024]{2,1,0:T(8,128)(2,1)}), bf16[16,16,1024]{2,1,0:T(8,128)(2,1)S(1)}, u32[]{:S(2)}, u32[]{:S(2)}) async-start(bf16[16,16,1024]{2,1,0:T(8,128)(2,1)} %bitcast.28), calls=%async_computation.1 | async-start | bytes 1048576 | tf_op jit(solution)/shard_map/all_to_all | solution.py:424
  28.5 0.0 copy-done
  28.5 0.0 copy-done.6
  28.5 0.7 shard_map.121.own
  29.2 2.7 %collective-permute-start = (bf16[4,64,512]{2,1,0:T(8,128)(2,1)S(1)}, bf16[4,64,512]{2,1,0:T(8,128)(2,1)}, u32[]{:S(2)}, u32[]{:S(2)}) collective-permute-start(bf16[4,64,512]{2,1,0:T(8,128)(2,1)S(1)} %shard_map.121.own), channel_id=1, source_target_pairs={{0,4},{4,0},{1,5},{5,1},{2,6},{6,2},{3,7},{7,3},{8,12},{12,8},{9,1... | collective-permute-start | bytes 786440 | tf_op jit(solution)/shard_map/ppermute | solution.py:435
  31.9 0.4 shard_map.123.weights
  32.2 0.0 copy-start.1
  32.3 1.6 %copy-done.1 = bf16[1024,1024]{1,0:T(8,128)(2,1)S(1)} copy-done((bf16[1024,1024]{1,0:T(8,128)(2,1)S(1)}, bf16[1024,1024]{1,0:T(8,128)(2,1)}, u32[]{:S(2)}) %copy-start.1) | copy-done | bytes 2097176
  33.8 1.0 %shard_map.120.query = bf16[4,64,1024]{2,1,0:T(8,128)(2,1)S(1)} custom-call(bf16[256,1152]{1,0:T(8,128)(2,1)S(1)} %bitcast.15, f32[1,1024]{1,0:T(1,128)S(1)} %bitcast.22, bf16[1024,1024]{1,0:T(8,128)(2,1)S(1)} %copy-done.1), custom_call_target="tpu_custom_call" | custom-call | flops 536870912 | bytes 3215360 | tf_op jit(solution)/shard_map/pallas_call | solution.py:330
  34.9 9.7 %all-to-all-done.1 = bf16[16,16,1024]{2,1,0:T(8,128)(2,1)S(1)} async-done(((bf16[16,16,1024]{2,1,0:T(8,128)(2,1)}), bf16[16,16,1024]{2,1,0:T(8,128)(2,1)S(1)}, u32[]{:S(2)}, u32[]{:S(2)}) %all-to-all-start.1) | async-done | bytes 524320 | tf_op jit(solution)/shard_map/all_to_all | solution.py:424
  44.6 0.7 shard_map.122.own
  45.3 0.1 collective-permute-start.1
  45.4 0.0 collective-permute-done.other
  45.4 3.3 %shard_map.124 = bf16[256,1024]{1,0:T(8,128)(2,1)} custom-call(bf16[4,64,1024]{2,1,0:T(8,128)(2,1)S(1)} %shard_map.120.query, bf16[4,64,512]{2,1,0:T(8,128)(2,1)S(1)} %shard_map.121.own, bf16[4,64,512]{2,1,0:T(8,128)(2,1)} %collective-permute-done.other, f32[128,64]{1,0:T(8,128)S(1)} %shard_map.123.weights), custom_call_target="tpu_custom_call" | custom-call | flops 134217728 | bytes 1605632 | tf_op jit(solution)/shard_map/pallas_call | solution.py:330
  48.7 9.3 %all-to-all-start.2 = ((bf16[16,16,1024]{2,1,0:T(8,128)(2,1)}), bf16[16,16,1024]{2,1,0:T(8,128)(2,1)S(1)}, u32[]{:S(2)}, u32[]{:S(2)}) async-start(bf16[16,16,1024]{2,1,0:T(8,128)(2,1)} %bitcast.8), calls=%async_computation.2 | async-start | bytes 1048576 | tf_op jit(solution)/shard_map/all_to_all | solution.py:465
  58.1 0.0 copy-start.2
  58.1 1.6 %copy-done.2 = bf16[1024,1024]{1,0:T(8,128)(2,1)S(1)} copy-done((bf16[1024,1024]{1,0:T(8,128)(2,1)S(1)}, bf16[1024,1024]{1,0:T(8,128)(2,1)}, u32[]{:S(2)}) %copy-start.2) | copy-done | bytes 2097176
  59.7 1.0 %shard_map.125.query = bf16[4,64,1024]{2,1,0:T(8,128)(2,1)S(1)} custom-call(bf16[256,1024]{1,0:T(8,128)(2,1)S(1)} %bitcast.17, f32[1,1024]{1,0:T(1,128)S(1)} %bitcast.24, bf16[1024,1024]{1,0:T(8,128)(2,1)S(1)} %copy-done.2), custom_call_target="tpu_custom_call" | custom-call | flops 26843545600 | bytes 3149824 | tf_op jit(solution)/shard_map/pallas_call | solution.py:330
  60.7 0.0 copy-start.3
  60.7 0.0 collective-permute-done.1.other
  60.7 0.0 copy-start.4
  60.7 0.7 copy-done.4
  61.4 0.0 copy-start.5
  61.4 0.9 %copy-done.5 = bf16[4,64,512]{2,1,0:T(8,128)(2,1)S(1)} copy-done((bf16[4,64,512]{2,1,0:T(8,128)(2,1)S(1)}, bf16[4,64,512]{2,1,0:T(8,128)(2,1)}, u32[]{:S(2)}) %copy-start.5) | copy-done | bytes 262168
  62.4 1.5 %shard_map.126 = bf16[256,1024]{1,0:T(8,128)(2,1)S(1)} custom-call(bf16[4,64,1024]{2,1,0:T(8,128)(2,1)S(1)} %shard_map.125.query, bf16[4,64,512]{2,1,0:T(8,128)(2,1)S(1)} %shard_map.122.own, bf16[4,64,512]{2,1,0:T(8,128)(2,1)S(1)} %copy-done.5, f32[128,64]{1,0:T(8,128)S(1)} %shard_map.123.weights), custom_call_target="tpu_custom_call" | custom-call | flops 134217728 | bytes 1605632 | tf_op jit(solution)/shard_map/pallas_call | solution.py:330
  63.9 4.7 %all-to-all-done.2 = bf16[16,16,1024]{2,1,0:T(8,128)(2,1)S(1)} async-done(((bf16[16,16,1024]{2,1,0:T(8,128)(2,1)}), bf16[16,16,1024]{2,1,0:T(8,128)(2,1)S(1)}, u32[]{:S(2)}, u32[]{:S(2)}) %all-to-all-start.2) | async-done | bytes 524320 | tf_op jit(solution)/shard_map/all_to_all | solution.py:465
  68.6 13.2 %all_to_all.20 = bf16[16,16,1024]{2,1,0:T(8,128)(2,1)S(1)} all-to-all(bf16[16,16,1024]{2,1,0:T(8,128)(2,1)S(1)} %bitcast.19), channel_id=1, replica_groups=mesh['tile'=4,'half'=2,'rest'=4] {'tile','rest'}, dimensions={0} | all-to-all | bytes 1048576 | tf_op jit(solution)/shard_map/all_to_all | solution.py:465
  81.8 0.0 copy-done.3
  81.8 3.5 %shard_map.127 = bf16[4,128,1024]{2,1,0:T(8,128)(2,1)} custom-call(bf16[256,1024]{1,0:T(8,128)(2,1)S(1)} %bitcast.18, bf16[256,1024]{1,0:T(8,128)(2,1)S(1)} %bitcast.20, bf16[4,128,1024]{2,1,0:T(8,128)(2,1)} %get-tuple-element.22.refs_2_, bf16[1024,1024]{1,0:T(8,128)(2,1)S(1)} %copy-done.3), custom_call_target="tpu_custom_call", output_to_operand_aliasing={{}: (2, {})} | custom-call | flops 536870912 | bytes 5242880 | tf_op jit(solution)/shard_map/pallas_call | solution.py:330
Async XLA Ops:
  7.3 17.6 %all-to-all-start = ((bf16[16,16,1152]{2,1,0:T(8,128)(2,1)}), bf16[16,16,1152]{2,1,0:T(8,128)(2,1)S(1)}, u32[]{:S(2)}, u32[]{:S(2)}) async-start(bf16[16,16,1152]{2,1,0:T(8,128)(2,1)} %bitcast.27), calls=%async_computation | async-start | bytes 1179648 | tf_op jit(solution)/shard_map/all_to_all | solution.py:424
  13.6 14.8 %copy-start = (bf16[1024,512]{1,0:T(8,128)(2,1)S(1)}, bf16[1024,512]{1,0:T(8,128)(2,1)}, u32[]{:S(2)}) copy-start(bf16[1024,512]{1,0:T(8,128)(2,1)} %wkv.3) | copy-start | bytes 3145732
  13.6 14.8 %copy-start.6 = (f32[1024]{0:T(1024)S(1)}, f32[1024]{0:T(1024)}, u32[]{:S(2)}) copy-start(f32[1024]{0:T(1024)} %param.17) | copy-start | bytes 12292
  24.9 19.7 %all-to-all-start.1 = ((bf16[16,16,1024]{2,1,0:T(8,128)(2,1)}), bf16[16,16,1024]{2,1,0:T(8,128)(2,1)S(1)}, u32[]{:S(2)}, u32[]{:S(2)}) async-start(bf16[16,16,1024]{2,1,0:T(8,128)(2,1)} %bitcast.28), calls=%async_computation.1 | async-start | bytes 1048576 | tf_op jit(solution)/shard_map/all_to_all | solution.py:424
  29.2 16.2 %collective-permute-start = (bf16[4,64,512]{2,1,0:T(8,128)(2,1)S(1)}, bf16[4,64,512]{2,1,0:T(8,128)(2,1)}, u32[]{:S(2)}, u32[]{:S(2)}) collective-permute-start(bf16[4,64,512]{2,1,0:T(8,128)(2,1)S(1)} %shard_map.121.own), channel_id=1, source_target_pairs={{0,4},{4,0},{1,5},{5,1},{2,6},{6,2},{3,7},{7,3},{8,12},{12,8},{9,1... | collective-permute-start | bytes 786440 | tf_op jit(solution)/shard_map/ppermute | solution.py:435
  32.2 1.6 %copy-start.1 = (bf16[1024,1024]{1,0:T(8,128)(2,1)S(1)}, bf16[1024,1024]{1,0:T(8,128)(2,1)}, u32[]{:S(2)}) copy-start(bf16[1024,1024]{1,0:T(8,128)(2,1)} %wq.3) | copy-start | bytes 6291460
  45.3 15.4 %collective-permute-start.1 = (bf16[4,64,512]{2,1,0:T(8,128)(2,1)S(1)}, bf16[4,64,512]{2,1,0:T(8,128)(2,1)S(1)}, u32[]{:S(2)}, u32[]{:S(2)}) collective-permute-start(bf16[4,64,512]{2,1,0:T(8,128)(2,1)S(1)} %shard_map.122.own), channel_id=1, source_target_pairs={{0,4},{4,0},{1,5},{5,1},{2,6},{6,2},{3,7},{7,3},{8,12},{12,8},{9,1... | collective-permute-start | bytes 786440 | tf_op jit(solution)/shard_map/ppermute | solution.py:435
  48.7 19.9 %all-to-all-start.2 = ((bf16[16,16,1024]{2,1,0:T(8,128)(2,1)}), bf16[16,16,1024]{2,1,0:T(8,128)(2,1)S(1)}, u32[]{:S(2)}, u32[]{:S(2)}) async-start(bf16[16,16,1024]{2,1,0:T(8,128)(2,1)} %bitcast.8), calls=%async_computation.2 | async-start | bytes 1048576 | tf_op jit(solution)/shard_map/all_to_all | solution.py:465
  58.1 1.6 %copy-start.2 = (bf16[1024,1024]{1,0:T(8,128)(2,1)S(1)}, bf16[1024,1024]{1,0:T(8,128)(2,1)}, u32[]{:S(2)}) copy-start(bf16[1024,1024]{1,0:T(8,128)(2,1)} %wq.3) | copy-start | bytes 6291460
  60.7 21.1 %copy-start.3 = (bf16[1024,1024]{1,0:T(8,128)(2,1)S(1)}, bf16[1024,1024]{1,0:T(8,128)(2,1)}, u32[]{:S(2)}) copy-start(bf16[1024,1024]{1,0:T(8,128)(2,1)} %refs_3_.5) | copy-start | bytes 6291460
  60.7 0.7 copy-start.4
  61.4 0.9 %copy-start.5 = (bf16[4,64,512]{2,1,0:T(8,128)(2,1)S(1)}, bf16[4,64,512]{2,1,0:T(8,128)(2,1)}, u32[]{:S(2)}) copy-start(bf16[4,64,512]{2,1,0:T(8,128)(2,1)} %copy-done.4) | copy-start | bytes 786436

commit v16 on v14

--- a/solution.py
+++ b/solution.py
@@ -22,7 +22,7 @@
 COLS = 256
 HALVES = 2
 CHUNKS = 2
-DEPTH = 2
+DEPTH = 3
 SHADOW = 100
 MIB = 1024 * 1024
 F32 = jnp.float32

time: 83.7 us -> 83.6 us (level)
  no operation moved by 1% of the time
where the time goes in v16:
time: 83.6 us; the launch traced here: 83 us
  Pallas kernels  27.5 us (33%)
  waiting for transfers between devices  22.3 us (27%)
  starting transfers between devices  16.3 us (19%)
  blocking collectives  13.2 us (16%)
  local copies, waits for them, and re-layouts  3.45 us (4%)
    pallas_call x10, Pallas kernels, call(): pl.pallas_call(kernel, out_shape=list(shapes), in_specs=[pl.BlockSpec(mem...  27.5 us
    all_to_all x2, waiting for transfers between devices, per_device(): lax.all_to_all(sent, spread, split_axis=0, concat_axis=0, tiled=True)  13.7 us
    all_to_all x1, blocking collectives, per_device(): mix = lax.all_to_all(mix, spread, split_axis=0, concat_axis=0, tiled=True)  13.2 us
    all_to_all x2, starting transfers between devices, per_device(): lax.all_to_all(sent, spread, split_axis=0, concat_axis=0, tiled=True)  9.87 us
    all_to_all x1, waiting for transfers between devices, per_device(): mix = lax.all_to_all(mix, spread, split_axis=0, concat_axis=0, tiled=True)  4.64 us
    ppermute x2, waiting for transfers between devices, per_device(): other = lax.ppermute(own, 'half', swap)  4.03 us
    all_to_all x1, starting transfers between devices, per_device(): mix = lax.all_to_all(mix, spread, split_axis=0, concat_axis=0, tiled=True)  3.75 us
    unnamed x14, local copies, waits for them, and re-layouts  3.45 us
  transfers between devices with their start and end apart: 5, of which 4 were waited for; matrix products, arithmetic and copies ran while one was open for 0% of the time, Pallas kernels for 20%

profile of v16, /device:TPU:0, one launch (start us, length us, event | category | flops | bytes accessed | tf_op | source)
XLA Modules:
  0.0 83.0 jit_solution(2945841538605138393)
XLA Ops:
  0.0 7.3 %shard_map.118 = (bf16[4,128,1024]{2,1,0:T(8,128)(2,1)}, bf16[256,1152]{1,0:T(8,128)(2,1)}, bf16[256,512]{1,0:T(8,128)(2,1)}) custom-call(bf16[512,1024]{1,0:T(8,128)(2,1)} %bitcast.21, f32[1,1024]{1,0:T(1,128)} %bitcast.25, bf16[1024,1024]{1,0:T(8,128)(2,1)} %refs_2_.3, bf16[1024,512]{1,0:T(8,128)(2,1)} %refs_3_.4, bf16[1024,1024]{1,0:T(8,128)(2,1)} %refs_4_.3, ...), custom_call_target="tpu_custom_call" | custom-call | flops 1342177280 | bytes 8196256 | tf_op jit(solution)/shard_map/pallas_call | solution.py:324
  7.3 6.3 %all-to-all-start = ((bf16[16,16,1152]{2,1,0:T(8,128)(2,1)}), bf16[16,16,1152]{2,1,0:T(8,128)(2,1)S(1)}, u32[]{:S(2)}, u32[]{:S(2)}) async-start(bf16[16,16,1152]{2,1,0:T(8,128)(2,1)} %bitcast.23), calls=%async_computation | async-start | bytes 1179648 | tf_op jit(solution)/shard_map/all_to_all | solution.py:418
  13.7 0.0 copy-start
  13.7 0.0 copy-start.4
  13.7 7.6 %shard_map.119 = (bf16[4,128,1024]{2,1,0:T(8,128)(2,1)}, bf16[256,1024]{1,0:T(8,128)(2,1)}, bf16[256,512]{1,0:T(8,128)(2,1)}) custom-call(bf16[512,1024]{1,0:T(8,128)(2,1)} %bitcast.22, f32[1,1024]{1,0:T(1,128)} %bitcast.26, bf16[1024,1024]{1,0:T(8,128)(2,1)} %refs_2_.3, bf16[1024,512]{1,0:T(8,128)(2,1)} %refs_3_.4, ...), custom_call_target="tpu_custom_call", output_to_operand_aliasing={{0}: (6, {})} | custom-call | flops 1342177280 | bytes 9441280 | tf_op jit(solution)/shard_map/pallas_call | solution.py:324
  21.3 3.6 %all-to-all-done = bf16[16,16,1152]{2,1,0:T(8,128)(2,1)S(1)} async-done(((bf16[16,16,1152]{2,1,0:T(8,128)(2,1)}), bf16[16,16,1152]{2,1,0:T(8,128)(2,1)S(1)}, u32[]{:S(2)}, u32[]{:S(2)}) %all-to-all-start) | async-done | bytes 589856 | tf_op jit(solution)/shard_map/all_to_all | solution.py:418
  24.9 3.6 %all-to-all-start.1 = ((bf16[16,16,1024]{2,1,0:T(8,128)(2,1)}), bf16[16,16,1024]{2,1,0:T(8,128)(2,1)S(1)}, u32[]{:S(2)}, u32[]{:S(2)}) async-start(bf16[16,16,1024]{2,1,0:T(8,128)(2,1)} %bitcast.24), calls=%async_computation.1 | async-start | bytes 1048576 | tf_op jit(solution)/shard_map/all_to_all | solution.py:418
  28.5 0.0 copy-done
  28.5 0.0 copy-done.4
  28.5 0.7 shard_map.120
  29.3 2.6 %collective-permute-start = (bf16[4,64,512]{2,1,0:T(8,128)(2,1)S(1)}, bf16[4,64,512]{2,1,0:T(8,128)(2,1)S(1)}, u32[]{:S(2)}, u32[]{:S(2)}) collective-permute-start(bf16[4,64,512]{2,1,0:T(8,128)(2,1)S(1)} %get-tuple-element.27.own), channel_id=1, source_target_pairs={{0,4},{4,0},{1,5},{5,1},{2,6},{6,2},{3,7},{7,3},{8,12},{12,8},{9,1... | collective-permute-start | bytes 786440 | tf_op jit(solution)/shard_map/ppermute | solution.py:428
  31.9 0.4 shard_map.123.weights
  32.3 0.0 copy-start.1
  32.3 1.6 %copy-done.1 = bf16[1024,1024]{1,0:T(8,128)(2,1)S(1)} copy-done((bf16[1024,1024]{1,0:T(8,128)(2,1)S(1)}, bf16[1024,1024]{1,0:T(8,128)(2,1)}, u32[]{:S(2)}) %copy-start.1) | copy-done | bytes 2097176
  33.9 0.7 shard_map.121.query
  34.6 10.0 %all-to-all-done.1 = bf16[16,16,1024]{2,1,0:T(8,128)(2,1)S(1)} async-done(((bf16[16,16,1024]{2,1,0:T(8,128)(2,1)}), bf16[16,16,1024]{2,1,0:T(8,128)(2,1)S(1)}, u32[]{:S(2)}, u32[]{:S(2)}) %all-to-all-start.1) | async-done | bytes 524320 | tf_op jit(solution)/shard_map/all_to_all | solution.py:418
  44.6 1.4 %shard_map.122 = (bf16[256,1024]{1,0:T(8,128)(2,1)S(1)}, bf16[4,64,512]{2,1,0:T(8,128)(2,1)}) custom-call(bf16[256,1024]{1,0:T(8,128)(2,1)S(1)} %bitcast.15, f32[1,1024]{1,0:T(1,128)S(1)} %bitcast.20, bf16[1024,512]{1,0:T(8,128)(2,1)S(1)} %copy-done), custom_call_target="tpu_custom_call" | custom-call | flops 268435456 | bytes 2363392 | tf_op jit(solution)/shard_map/pallas_call | solution.py:324
  46.1 0.0 copy-start.5
  46.1 0.8 copy-done.5
  46.9 0.0 copy-start.2
  46.9 0.0 collective-permute-start.1
  46.9 0.0 collective-permute-done.other
  46.9 2.4 %shard_map.124 = bf16[256,1024]{1,0:T(8,128)(2,1)} custom-call(bf16[4,64,1024]{2,1,0:T(8,128)(2,1)S(1)} %shard_map.121.query, bf16[4,64,512]{2,1,0:T(8,128)(2,1)S(1)} %get-tuple-element.27.own, bf16[4,64,512]{2,1,0:T(8,128)(2,1)S(1)} %collective-permute-done.other, f32[128,64]{1,0:T(8,128)S(1)} %shard_map.123.weights), custom_call_target="tpu_custom_call" | custom-call | flops 134217728 | bytes 1605632 | tf_op jit(solution)/shard_map/pallas_call | solution.py:324
  49.3 3.8 %all-to-all-start.2 = ((bf16[16,16,1024]{2,1,0:T(8,128)(2,1)}), bf16[16,16,1024]{2,1,0:T(8,128)(2,1)S(1)}, u32[]{:S(2)}, u32[]{:S(2)}) async-start(bf16[16,16,1024]{2,1,0:T(8,128)(2,1)} %bitcast.8), calls=%async_computation.2 | async-start | bytes 1048576 | tf_op jit(solution)/shard_map/all_to_all | solution.py:457
  53.0 0.0 copy-done.2
  53.1 0.0 copy-start.6
  53.1 1.0 %copy-done.6 = bf16[256,1024]{1,0:T(8,128)(2,1)S(1)} copy-done((bf16[256,1024]{1,0:T(8,128)(2,1)S(1)}, bf16[256,1024]{1,0:T(8,128)(2,1)}, u32[]{:S(2)}) %copy-start.6) | copy-done | bytes 524312
  54.1 0.7 shard_map.125.query
  54.8 0.0 copy-start.3
  54.8 4.0 %collective-permute-done.1.other = bf16[4,64,512]{2,1,0:T(8,128)(2,1)} collective-permute-done((bf16[4,64,512]{2,1,0:T(8,128)(2,1)}, bf16[4,64,512]{2,1,0:T(8,128)(2,1)}, u32[]{:S(2)}, u32[]{:S(2)}) %collective-permute-start.1) | collective-permute-done | bytes 262176 | tf_op jit(solution)/shard_map/ppermute | solution.py:428
  58.8 2.6 %shard_map.126 = bf16[256,1024]{1,0:T(8,128)(2,1)S(1)} custom-call(bf16[4,64,1024]{2,1,0:T(8,128)(2,1)S(1)} %shard_map.125.query, bf16[4,64,512]{2,1,0:T(8,128)(2,1)} %get-tuple-element.29.own, bf16[4,64,512]{2,1,0:T(8,128)(2,1)} %collective-permute-done.1.other, f32[128,64]{1,0:T(8,128)S(1)} %shard_map.123.weights), custom_call_target="tpu_custom_call" | custom-call | flops 134217728 | bytes 1605632 | tf_op jit(solution)/shard_map/pallas_call | solution.py:324
  61.5 4.6 %all-to-all-done.2 = bf16[16,16,1024]{2,1,0:T(8,128)(2,1)S(1)} async-done(((bf16[16,16,1024]{2,1,0:T(8,128)(2,1)}), bf16[16,16,1024]{2,1,0:T(8,128)(2,1)S(1)}, u32[]{:S(2)}, u32[]{:S(2)}) %all-to-all-start.2) | async-done | bytes 524320 | tf_op jit(solution)/shard_map/all_to_all | solution.py:457
  66.1 13.2 %all_to_all.20 = bf16[16,16,1024]{2,1,0:T(8,128)(2,1)S(1)} all-to-all(bf16[16,16,1024]{2,1,0:T(8,128)(2,1)S(1)} %bitcast.17), channel_id=1, replica_groups=mesh['tile'=4,'half'=2,'rest'=4] {'tile','rest'}, dimensions={0} | all-to-all | bytes 1048576 | tf_op jit(solution)/shard_map/all_to_all | solution.py:457
  79.3 0.0 copy-done.3
  79.3 3.5 %shard_map.127 = bf16[4,128,1024]{2,1,0:T(8,128)(2,1)} custom-call(bf16[256,1024]{1,0:T(8,128)(2,1)S(1)} %bitcast.16, bf16[256,1024]{1,0:T(8,128)(2,1)S(1)} %bitcast.18, bf16[4,128,1024]{2,1,0:T(8,128)(2,1)} %get-tuple-element.30.refs_2_, bf16[1024,1024]{1,0:T(8,128)(2,1)S(1)} %copy-done.3), custom_call_target="tpu_custom_call", output_to_operand_aliasing={{}: (2, {})} | custom-call | flops 536870912 | bytes 5242880 | tf_op jit(solution)/shard_map/pallas_call | solution.py:324
Async XLA Ops:
  7.3 17.6 %all-to-all-start = ((bf16[16,16,1152]{2,1,0:T(8,128)(2,1)}), bf16[16,16,1152]{2,1,0:T(8,128)(2,1)S(1)}, u32[]{:S(2)}, u32[]{:S(2)}) async-start(bf16[16,16,1152]{2,1,0:T(8,128)(2,1)} %bitcast.23), calls=%async_computation | async-start | bytes 1179648 | tf_op jit(solution)/shard_map/all_to_all | solution.py:418
  13.7 14.8 %copy-start = (bf16[1024,512]{1,0:T(8,128)(2,1)S(1)}, bf16[1024,512]{1,0:T(8,128)(2,1)}, u32[]{:S(2)}) copy-start(bf16[1024,512]{1,0:T(8,128)(2,1)} %wkv.3) | copy-start | bytes 3145732
  13.7 14.8 %copy-start.4 = (f32[1024]{0:T(1024)S(1)}, f32[1024]{0:T(1024)}, u32[]{:S(2)}) copy-start(f32[1024]{0:T(1024)} %param.17) | copy-start | bytes 12292
  24.9 19.7 %all-to-all-start.1 = ((bf16[16,16,1024]{2,1,0:T(8,128)(2,1)}), bf16[16,16,1024]{2,1,0:T(8,128)(2,1)S(1)}, u32[]{:S(2)}, u32[]{:S(2)}) async-start(bf16[16,16,1024]{2,1,0:T(8,128)(2,1)} %bitcast.24), calls=%async_computation.1 | async-start | bytes 1048576 | tf_op jit(solution)/shard_map/all_to_all | solution.py:418
  29.3 17.6 %collective-permute-start = (bf16[4,64,512]{2,1,0:T(8,128)(2,1)S(1)}, bf16[4,64,512]{2,1,0:T(8,128)(2,1)S(1)}, u32[]{:S(2)}, u32[]{:S(2)}) collective-permute-start(bf16[4,64,512]{2,1,0:T(8,128)(2,1)S(1)} %get-tuple-element.27.own), channel_id=1, source_target_pairs={{0,4},{4,0},{1,5},{5,1},{2,6},{6,2},{3,7},{7,3},{8,12},{12,8},{9,1... | collective-permute-start | bytes 786440 | tf_op jit(solution)/shard_map/ppermute | solution.py:428
  32.3 1.6 %copy-start.1 = (bf16[1024,1024]{1,0:T(8,128)(2,1)S(1)}, bf16[1024,1024]{1,0:T(8,128)(2,1)}, u32[]{:S(2)}) copy-start(bf16[1024,1024]{1,0:T(8,128)(2,1)} %wq.3) | copy-start | bytes 6291460
  46.1 0.8 copy-start.5
  46.9 6.2 %copy-start.2 = (bf16[1024,1024]{1,0:T(8,128)(2,1)S(1)}, bf16[1024,1024]{1,0:T(8,128)(2,1)}, u32[]{:S(2)}) copy-start(bf16[1024,1024]{1,0:T(8,128)(2,1)} %wq.3) | copy-start | bytes 6291460
  46.9 12.0 %collective-permute-start.1 = (bf16[4,64,512]{2,1,0:T(8,128)(2,1)}, bf16[4,64,512]{2,1,0:T(8,128)(2,1)}, u32[]{:S(2)}, u32[]{:S(2)}) collective-permute-start(bf16[4,64,512]{2,1,0:T(8,128)(2,1)} %get-tuple-element.29.own), channel_id=1, source_target_pairs={{0,4},{4,0},{1,5},{5,1},{2,6},{6,2},{3,7},{7,3},{8,12},{12,8},{9,1... | collective-permute-start | bytes 786440 | tf_op jit(solution)/shard_map/ppermute | solution.py:428
  49.3 16.9 %all-to-all-start.2 = ((bf16[16,16,1024]{2,1,0:T(8,128)(2,1)}), bf16[16,16,1024]{2,1,0:T(8,128)(2,1)S(1)}, u32[]{:S(2)}, u32[]{:S(2)}) async-start(bf16[16,16,1024]{2,1,0:T(8,128)(2,1)} %bitcast.8), calls=%async_computation.2 | async-start | bytes 1048576 | tf_op jit(solution)/shard_map/all_to_all | solution.py:457
  53.1 1.0 %copy-start.6 = (bf16[256,1024]{1,0:T(8,128)(2,1)S(1)}, bf16[256,1024]{1,0:T(8,128)(2,1)}, u32[]{:S(2)}) copy-start(bf16[256,1024]{1,0:T(8,128)(2,1)} %copy-done.5) | copy-start | bytes 1572868
  54.8 24.5 %copy-start.3 = (bf16[1024,1024]{1,0:T(8,128)(2,1)S(1)}, bf16[1024,1024]{1,0:T(8,128)(2,1)}, u32[]{:S(2)}) copy-start(bf16[1024,1024]{1,0:T(8,128)(2,1)} %refs_3_.5) | copy-start | bytes 6291460
